TPU v7x, 32 devices: a whole 2x2x4 slice. The times are simulated.
32 devices in a mesh: img: 16 (over z, x, core), txt: 2 (over y).
Axes of the slice: x: 2, y: 2, z: 4, core: 2. Of those that a mesh axis runs over, the one named last changes fastest.
Arguments:
- image_emb: bfloat16 [512, 1152], P(('img', 'txt')), may hold values from -0.296875 to 0.296875
- text_emb: bfloat16 [512, 1152], P(('img', 'txt')), may hold values from -0.296875 to 0.296875
- pair_class: int32 [512], P(('img', 'txt')), may hold values from 0 to 255
- scale: float32 [], replicated, may hold values from 4 to 12
- shift: float32 [], replicated, may hold values from -2 to -0.5
Outputs:
- row_loss: float32 [512], P(('img', 'txt'))
- grad_image: float32 [512, 1152], P(('img', 'txt'))
- grad_text: float32 [512, 1152], P(('img', 'txt'))
All inputs are finite; a program needn't handle non-finite values.
Results may differ from a plain program's by a relative error of at most 0.0012.
Values may be sent and summed in bfloat16 or wider, within the bound.
No kernel may reach another device: no remote copies, remote signals or barrier semaphores. Data moves between devices by JAX's collectives and lax.ppermute only.
A program may use at most 64 MiB of HBM per device.

v0:
```python
import jax
import jax.numpy as jnp
from jax import lax
from jax.sharding import PartitionSpec as P


def unit_rows(rows):
    wide = rows.astype(jnp.float32)
    inverse = 1.0 / jnp.sqrt(jnp.sum(wide * wide, axis=1, keepdims=True) + 1e-06)
    return (wide * inverse, inverse)


def project_back(unit, inverse, pull):
    inner = jnp.sum(unit * pull, axis=1, keepdims=True)
    return (pull - unit * inner) * inverse


def tile_terms(rows_half, row_class, cols_half, col_class, scale, shift):
    logits = (
        scale
        * lax.dot_general(
            rows_half, cols_half, (((1,), (1,)), ((), ())), preferred_element_type=jnp.float32
        )
        + shift
    )
    sign = jnp.where(row_class[:, None] == col_class[None, :], 1.0, -1.0).astype(jnp.float32)
    margin = sign * logits
    loss_part = -jnp.sum(jax.nn.log_sigmoid(margin), axis=1)
    coef = (-sign * jax.nn.sigmoid(-margin) * scale).astype(jnp.bfloat16)
    return (coef, loss_part)


def local(image_emb, text_emb, pair_class, scale, shift):
    image_unit, image_inv = unit_rows(image_emb)
    text_unit, text_inv = unit_rows(text_emb)
    own_rows = text_emb.shape[0]
    pairs = own_rows * lax.axis_size("img") * lax.axis_size("txt")
    text_half = text_unit.astype(jnp.bfloat16)
    rows_half, row_class = (
        lax.all_gather(image_unit.astype(jnp.bfloat16), "txt", axis=0, tiled=True),
        lax.all_gather(pair_class, "txt", axis=0, tiled=True),
    )
    cols_half, col_class = (
        lax.all_gather(text_half, "img", axis=0, tiled=True),
        lax.all_gather(pair_class, "img", axis=0, tiled=True),
    )
    coef, loss_part = tile_terms(rows_half, row_class, cols_half, col_class, scale, shift)
    image_pull = jnp.dot(coef, cols_half, preferred_element_type=jnp.float32)
    text_pull = lax.psum_scatter(
        lax.dot_general(
            coef, rows_half, (((0,), (0,)), ((), ())), preferred_element_type=jnp.float32
        ),
        "img",
        scatter_dimension=0,
        tiled=True,
    )
    image_sum, loss_sum = (
        lax.psum_scatter(image_pull, "txt", scatter_dimension=0, tiled=True),
        lax.psum_scatter(loss_part, "txt", scatter_dimension=0, tiled=True),
    )
    row_loss = loss_sum / pairs
    grad_image = project_back(image_unit, image_inv, image_sum)
    grad_text = project_back(text_unit, text_inv, text_pull)
    return (row_loss, grad_image, grad_text)


def solution(mesh):
    in_specs = (P(("img", "txt"), None), P(("img", "txt"), None), P(("img", "txt")), P(), P())
    out_specs = (P(("img", "txt")), P(("img", "txt"), None), P(("img", "txt"), None))
    return jax.shard_map(local, mesh=mesh, in_specs=in_specs, out_specs=out_specs, check_vma=False)
```

profile of v0, /device:TPU:0, one launch (start us, length us, event | category | flops | bytes accessed | tf_op | source)
XLA Modules:
  0.0 140.8 jit_solution(15818215051196344280)
XLA Ops:
  7.2 0.0 reduce-scatter.3.cloned.1.call-start
  8.5 1.2 dynamic-slice.1
  10.4 1.3 fusion.24
  12.4 0.9 fusion.11
  13.3 0.9 fusion.15
  14.2 0.9 dynamic-update-slice
  15.0 5.2 %all-reduce = s32[32]{0:T(128)S(1)} all-reduce(s32[32]{0:T(128)S(1)} %dynamic-update-slice), channel_id=1, replica_groups=mesh['img'=16,'txt'=2] {'txt'}, use_global_device_ids=true, to_apply=%add | all-reduce | flops 32 | bytes 256
  20.3 0.8 dynamic-update-slice.1
  21.1 12.7 %all-reduce.1 = s32[256]{0:T(256)S(1)} all-reduce(s32[256]{0:T(256)S(1)} %dynamic-update-slice.1), channel_id=1, replica_groups=mesh['img'=16,'txt'=2] {'img'}, use_global_device_ids=true, to_apply=%add.1 | all-reduce | flops 256 | bytes 2048
  33.8 0.8 fusion.4
  34.7 0.8 fusion.7
  35.5 4.6 %all_gather.14 = bf16[32,1152]{1,0:T(8,128)(2,1)S(1)} all-gather(bf16[16,1152]{1,0:T(8,128)(2,1)S(1)} %fusion.7), channel_id=1, replica_groups=mesh['img'=16,'txt'=2] {'txt'}, dimensions={0}, use_global_device_ids=true | all-gather | bytes 110592 | tf_op jit(solution)/shard_map/all_gather | solution.py:40
  40.1 19.5 %all_gather.15 = bf16[256,1152]{1,0:T(8,128)(2,1)S(1)} all-gather(bf16[16,1152]{1,0:T(8,128)(2,1)S(1)} %fusion.4), channel_id=1, replica_groups=mesh['img'=16,'txt'=2] {'img'}, dimensions={0}, use_global_device_ids=true | all-gather | bytes 626688 | tf_op jit(solution)/shard_map/all_gather | solution.py:44
  59.7 0.4 fusion.19
  60.1 0.9 fusion.22
  61.1 0.0 reduce-scatter.3.cloned.1.call-update
  61.1 0.0 copy-start
  61.1 0.0 copy-start.1
  61.1 0.0 reduce-scatter.5.cloned.1.call-start
  61.2 1.4 %fusion.20 = f32[256,1152]{1,0:T(8,128)} fusion(bf16[32,1152]{1,0:T(8,128)(2,1)S(1)} %all_gather.14, f32[32,256]{1,0:T(8,128)S(1)} %get-tuple-element.6, f32[]{:T(128)S(6)} %copy.10, s32[256]{0:T(256)S(1)} %all-reduce.1, s32[32]{0:T(128)S(1)} %all-reduce), kind=kOutput, calls=%fused_computation.30 | convolution fusion | flops 18939904 | bytes 1287300 | tf_op jit(solution)/shard_map/dot_general | solution.py:50
  62.6 0.0 reduce-scatter.5.cloned.1.call-update
  63.3 4.9 %all-reduce.2 = f32[32]{0:T(128)S(1)} all-reduce(f32[32]{0:T(128)S(1)} %get-tuple-element.5), channel_id=2, replica_groups=mesh['img'=16,'txt'=2] {'txt'}, use_global_device_ids=true, to_apply=%region_3.4.clone | all-reduce | flops 32 | bytes 256
  68.2 0.6 dynamic-slice_multiply_fusion
  68.8 0.9 reduce-scatter.3.cloned.1.call-done
  69.7 0.0 copy-done
  69.7 1.1 fusion.8
  70.8 1.6 %fusion.10 = f32[16,1152]{1,0:T(8,128)} fusion(f32[16,1152]{1,0:T(8,128)} %reduce-scatter.3.cloned.1.call-done, bf16[16,1152]{1,0:T(8,128)(2,1)S(1)} %copy-done, f32[16]{0:T(128)S(1)} %fusion.8, f32[16]{0:T(128)S(1)} %add_rsqrt_fusion.1), kind=kLoop, calls=%fused_computation.16 | loop fusion | flops 92160 | bytes 184448 | tf_op jit(solution)/shard_map/mul | solution.py:15
  72.4 58.9 %reduce-scatter.5.cloned.1.call-done = f32[16,1152]{1,0:T(8,128)} async-done(((f32[256,1152]{1,0:T(8,128)}), f32[16,1152]{1,0:T(8,128)}) %reduce-scatter.5.cloned.1.call-update) | async-done | bytes 73744 | tf_op jit(solution)/shard_map/reduce_scatter | solution.py:49
  131.3 0.0 copy-done.1
  131.3 1.1 fusion.12
  132.4 1.6 %fusion.14 = f32[16,1152]{1,0:T(8,128)} fusion(f32[16,1152]{1,0:T(8,128)} %reduce-scatter.5.cloned.1.call-done, bf16[16,1152]{1,0:T(8,128)(2,1)S(1)} %copy-done.1, f32[16]{0:T(128)S(1)} %fusion.12, f32[16]{0:T(128)S(1)} %add_rsqrt_fusion), kind=kLoop, calls=%fused_computation.20 | loop fusion | flops 92160 | bytes 184448 | tf_op jit(solution)/shard_map/mul | solution.py:15
  (4 shorter events, 0.0 us)
Async XLA Ops:
  7.2 62.5 %reduce-scatter.3.cloned.1.call-start = ((), (), s32[]{:S(2)}) async-start(), calls=%async_computation.2 | async-start | bytes 221184 | tf_op jit(solution)/shard_map/reduce_scatter | solution.py:58
  61.1 8.6 %copy-start = (bf16[16,1152]{1,0:T(8,128)(2,1)S(1)}, bf16[16,1152]{1,0:T(8,128)(2,1)}, u32[]{:S(2)}) copy-start(bf16[16,1152]{1,0:T(8,128)(2,1)} %param.5) | copy-start | bytes 110596
  61.1 70.2 %copy-start.1 = (bf16[16,1152]{1,0:T(8,128)(2,1)S(1)}, bf16[16,1152]{1,0:T(8,128)(2,1)}, u32[]{:S(2)}) copy-start(bf16[16,1152]{1,0:T(8,128)(2,1)} %param.6) | copy-start | bytes 110596
  61.1 70.2 %reduce-scatter.5.cloned.1.call-start = ((), (), s32[]{:S(2)}) async-start(), calls=%async_computation.3 | async-start | bytes 1253376 | tf_op jit(solution)/shard_map/reduce_scatter | solution.py:49
Sparse Core Ops, SparseCore 0:
  61.2 8.4 reduce-scatter.2
  73.3 57.9 reduce-scatter.4
where the time goes:
time: 142 us; the launch traced here: 141 us
  waiting for transfers between devices  59.9 us (42%)
  blocking collectives  47.1 us (33%)
  between operations  17.3 us (12%)
  other arithmetic  9.42 us (7%)
  local copies, waits for them, and re-layouts  4.28 us (3%)
  matrix products  2.79 us (2%)
    reduce_scatter x1, waiting for transfers between devices, local(): lax.psum_scatter(lax.dot_general(coef, rows_half, (((0,), (0,)), ((), ())...  58.9 us
    unnamed x3, blocking collectives  22.9 us
    all_gather x1, blocking collectives, local(): lax.all_gather(text_half, 'img', axis=0, tiled=True)  19.5 us
    all_gather x1, blocking collectives, local(): lax.all_gather(image_unit.astype(jnp.bfloat16), 'txt', axis=0, tiled=True)  4.62 us
    unnamed x10, local copies, waits for them, and re-layouts  4.28 us
    mul x2, other arithmetic, project_back(): return (pull - unit * inner) * inverse  3.2 us
  transfers between devices with their start and end apart: 2, of which 2 were waited for; matrix products, arithmetic and copies ran while one was open for 3% of the time, Pallas kernels for 0%

commit v1 on v0

--- a/solution.py
+++ b/solution.py
@@ -1,7 +1,13 @@
 import jax
 import jax.numpy as jnp
 from jax import lax
+from jax.experimental import pallas as pl
+from jax.experimental.pallas import tpu as pltpu
 from jax.sharding import PartitionSpec as P
+
+GATHER_LIMIT_BYTES = 8 << 20
+DIGITS = 4
+LANES = 128
 
 
 def unit_rows(rows):
@@ -30,7 +36,7 @@
     return (coef, loss_part)
 
 
-def local(image_emb, text_emb, pair_class, scale, shift):
+def tile_plan(image_emb, text_emb, pair_class, scale, shift):
     image_unit, image_inv = unit_rows(image_emb)
     text_unit, text_inv = unit_rows(text_emb)
     own_rows = text_emb.shape[0]
@@ -64,6 +70,118 @@
     return (row_loss, grad_image, grad_text)
 
 
+def class_digits(class_ref, rows):
+    row = lax.broadcasted_iota(jnp.int32, (rows, LANES), 0)
+    lane = lax.broadcasted_iota(jnp.int32, (rows, LANES), 1)
+    spread = jnp.zeros((rows, LANES), jnp.int32)
+    for i in range(rows):
+        spread = jnp.where(row == i, class_ref[i], spread)
+    digit = lax.shift_right_logical(spread, 8 * jnp.minimum(lane, DIGITS - 1)) & 255
+    return jnp.where(lane < DIGITS, digit, 0).astype(jnp.float32)
+
+
+def pack_kernel(image_ref, text_ref, class_ref, packed_ref):
+    rows, depth = image_ref.shape
+    packed_ref[:, :depth] = unit_rows(image_ref[...])[0].astype(jnp.bfloat16)
+    packed_ref[:, depth : 2 * depth] = unit_rows(text_ref[...])[0].astype(jnp.bfloat16)
+    packed_ref[:, 2 * depth :] = class_digits(class_ref, rows).astype(jnp.bfloat16)
+
+
+def side(own_half, others, sign, scale, shift):
+    logits = (
+        scale
+        * lax.dot_general(
+            own_half, others, (((1,), (1,)), ((), ())), preferred_element_type=jnp.float32
+        )
+        + shift
+    )
+    margin = sign * logits
+    small = jnp.exp(-jnp.abs(margin))
+    over = 1.0 / (1.0 + small)
+    coef = -sign * jnp.where(margin >= 0, small * over, over) * scale
+    pull = jnp.dot(coef.astype(jnp.bfloat16), others, preferred_element_type=jnp.float32)
+    return margin, small, pull
+
+
+def main_kernel(
+    image_ref, text_ref, class_ref, scale_ref, shift_ref, all_ref, loss_ref, grad_image_ref, grad_text_ref
+):
+    rows, depth = image_ref.shape
+    pairs = all_ref.shape[0]
+    scale, shift = scale_ref[0], shift_ref[0]
+    image_unit, image_inv = unit_rows(image_ref[...])
+    text_unit, text_inv = unit_rows(text_ref[...])
+
+    own_digits = class_digits(class_ref, rows)
+    pick = (
+        lax.broadcasted_iota(jnp.int32, (8, LANES), 0)
+        == lax.broadcasted_iota(jnp.int32, (8, LANES), 1)
+    )
+    all_digits = lax.dot_general(
+        pick.astype(jnp.bfloat16),
+        all_ref[:, 2 * depth :],
+        (((1,), (1,)), ((), ())),
+        preferred_element_type=jnp.float32,
+    )
+    same = None
+    for k in range(DIGITS):
+        equal = own_digits[:, k : k + 1] == all_digits[k : k + 1, :]
+        same = equal if same is None else same & equal
+    sign = jnp.where(same, 1.0, -1.0).astype(jnp.float32)
+
+    margin, small, image_pull = side(
+        image_unit.astype(jnp.bfloat16), all_ref[:, depth : 2 * depth], sign, scale, shift
+    )
+    grad_image_ref[...] = project_back(image_unit, image_inv, image_pull)
+    loss = jnp.log1p(small) - jnp.minimum(margin, 0.0)
+    folded = loss[:, :LANES]
+    for start in range(LANES, pairs, LANES):
+        folded = folded + loss[:, start : start + LANES]
+    loss_ref[...] = jnp.sum(folded.T, axis=0, keepdims=True) / pairs
+
+    _, _, text_pull = side(
+        text_unit.astype(jnp.bfloat16), all_ref[:, :depth], sign, scale, shift
+    )
+    grad_text_ref[...] = project_back(text_unit, text_inv, text_pull)
+
+
+def gather_plan(image_emb, text_emb, pair_class, scale, shift):
+    rows, depth = image_emb.shape
+    pairs = rows * lax.axis_size("img") * lax.axis_size("txt")
+    vmem = pl.BlockSpec(memory_space=pltpu.VMEM)
+    smem = pl.BlockSpec(memory_space=pltpu.SMEM)
+    width = 2 * depth + LANES
+    packed = pl.pallas_call(
+        pack_kernel,
+        out_shape=jax.ShapeDtypeStruct((rows, width), jnp.bfloat16),
+        in_specs=[vmem, vmem, smem],
+        out_specs=vmem,
+        name="pack",
+    )(image_emb, text_emb, pair_class)
+    everything = lax.all_gather(packed, ("img", "txt"), axis=0, tiled=True)
+    loss, grad_image, grad_text = pl.pallas_call(
+        main_kernel,
+        out_shape=(
+            jax.ShapeDtypeStruct((1, rows), jnp.float32),
+            jax.ShapeDtypeStruct((rows, depth), jnp.float32),
+            jax.ShapeDtypeStruct((rows, depth), jnp.float32),
+        ),
+        in_specs=[vmem, vmem, smem, smem, smem, vmem],
+        out_specs=(vmem, vmem, vmem),
+        compiler_params=pltpu.CompilerParams(vmem_limit_bytes=32 << 20),
+        name="contrast",
+    )(image_emb, text_emb, pair_class, scale[None], shift[None], everything)
+    return (loss[0], grad_image, grad_text)
+
+
+def local(image_emb, text_emb, pair_class, scale, shift):
+    rows, depth = image_emb.shape
+    pairs = rows * lax.axis_size("img") * lax.axis_size("txt")
+    if 2 * pairs * depth * image_emb.dtype.itemsize <= GATHER_LIMIT_BYTES:
+        return gather_plan(image_emb, text_emb, pair_class, scale, shift)
+    return tile_plan(image_emb, text_emb, pair_class, scale, shift)
+
+
 def solution(mesh):
     in_specs = (P(("img", "txt"), None), P(("img", "txt"), None), P(("img", "txt")), P(), P())
     out_specs = (P(("img", "txt")), P(("img", "txt"), None), P(("img", "txt"), None))

time: 142 us -> 84.9 us (0.60)
  blocking collectives: 47.1 us -> 0 us
  other arithmetic: 9.42 us -> 0 us
  Pallas kernels: 0 us -> 4.1 us
  matrix products: 2.79 us -> 0 us
  between operations: 17.3 us -> 15.3 us
    all_gather x0 -> x1, waiting for transfers between devices: none -> 61.2 us  [gather_plan(): everything = lax.all_gather(packed, ('img', 'txt'), axis=0, tiled=True)]
    reduce_scatter x2 -> x0, waiting for transfers between devices: 59.8 us -> none  [the longest x1 58.9 us: local(): lax.psum_scatter(lax.dot_general(coef, rows_half, (((0,), (0,)), ((), ())...]
    all_gather x2 -> x0, blocking collectives: 24.2 us -> none  [the longest x1 19.5 us: local(): lax.all_gather(text_half, 'img', axis=0, tiled=True)]
    unnamed x3 -> x0, blocking collectives: 22.9 us -> none
    pallas_call x0 -> x2, Pallas kernels: none -> 4.1 us  [the longest x1 2.56 us: gather_plan(): pl.pallas_call(main_kernel, out_shape=(jax.ShapeDtypeStruct((1, rows), jn...]
    reduce_sum x4 -> x0, other arithmetic: 3.93 us -> none  [the longest x2 2.15 us: project_back(): inner = jnp.sum(unit * pull, axis=1, keepdims=True)]
    mul x2 -> x0, other arithmetic: 3.2 us -> none  [project_back(): return (pull - unit * inner) * inverse]
    dot_general x3 -> x0, matrix products: 2.79 us -> none  [the longest x1 1.42 us: local(): lax.dot_general(coef, rows_half, (((0,), (0,)), ((), ())), preferred_elem...]
  transfers between devices with their start and end apart: 2 -> 1, of which waited for: 2 -> 1; matrix products, arithmetic and copies ran while one was open for 3% -> 0% of each run, Pallas kernels for 0% -> 0%
where the time goes in v1:
time: 84.9 us; the launch traced here: 84.5 us
  waiting for transfers between devices  61.2 us (72%)
  between operations  15.3 us (18%)
  Pallas kernels  4.1 us (5%)
  local copies, waits for them, and re-layouts  3.89 us (5%)
    all_gather x1, waiting for transfers between devices, gather_plan(): everything = lax.all_gather(packed, ('img', 'txt'), axis=0, tiled=True)  61.2 us
    unnamed x8, local copies, waits for them, and re-layouts  3.89 us
    pallas_call x1, Pallas kernels, gather_plan(): pl.pallas_call(main_kernel, out_shape=(jax.ShapeDtypeStruct((1, rows), jn...  2.56 us
  transfers between devices with their start and end apart: 1, of which 1 were waited for; matrix products, arithmetic and copies ran while one was open for 0% of the time, Pallas kernels for 0%

profile of v1, /device:TPU:0, one launch (start us, length us, event | category | flops | bytes accessed | tf_op | source)
XLA Modules:
  0.0 84.5 jit_solution(11983252948986403024)
XLA Ops:
  7.2 0.0 all-gather.2.cloned.1.call-start
  7.2 1.5 %pack.1 = bf16[16,2432]{1,0:T(8,128)(2,1)} custom-call(bf16[16,1152]{1,0:T(8,128)(2,1)} %image_ref.3, bf16[16,1152]{1,0:T(8,128)(2,1)} %text_ref.3, s32[16]{0:T(128)} %class_ref.3), custom_call_target="tpu_custom_call" | custom-call | tf_op jit(solution)/shard_map/pack/pallas_call | solution.py:154
  8.8 0.0 all-gather.2.cloned.1.call-update
  10.1 61.2 %all-gather.2.cloned.1.call-done.all_ref = bf16[512,2432]{1,0:T(8,128)(2,1)} async-done(((bf16[16,2432]{1,0:T(8,128)(2,1)}), bf16[512,2432]{1,0:T(8,128)(2,1)}) %all-gather.2.cloned.1.call-update) | async-done | bytes 2490384 | tf_op jit(solution)/shard_map/all_gather | solution.py:161
  71.2 0.0 copy-start
  71.2 1.7 %copy-done = bf16[512,2432]{1,0:T(8,128)(2,1)S(1)} copy-done((bf16[512,2432]{1,0:T(8,128)(2,1)S(1)}, bf16[512,2432]{1,0:T(8,128)(2,1)}, u32[]{:S(2)}) %copy-start) | copy-done | bytes 2490392
  72.9 0.0 copy-start.1
  73.0 0.8 copy-done.1
  73.7 0.0 copy-start.2
  73.7 0.8 copy-done.2
  74.5 0.0 copy-start.3
  74.5 0.7 copy-done.3
  75.1 2.6 %contrast.1 = (f32[1,16]{1,0:T(1,128)}, f32[16,1152]{1,0:T(8,128)}, f32[16,1152]{1,0:T(8,128)}) custom-call(bf16[16,1152]{1,0:T(8,128)(2,1)S(1)} %copy-done.1, bf16[16,1152]{1,0:T(8,128)(2,1)S(1)} %copy-done.2, s32[16]{0:T(128)S(1)} %copy-done.3, f32[1]{0:T(128)} %bitcast.3.scale_ref, f32[1]{0:T(128)} %bitcast.4.shift_ref, bf16[512,2432]{1,0:T(8,128)(2,1)S(1)} %copy-done), custom_call_target="tpu_custom_call" | custom-call | tf_op jit(solution)/shard_map/contrast/pallas_call | solution.py:162
Async XLA Ops:
  7.2 64.1 %all-gather.2.cloned.1.call-start = ((), (), s32[]{:S(2)}) async-start(), calls=%async_computation | async-start | bytes 2568192 | tf_op jit(solution)/shard_map/all_gather | solution.py:161
  71.2 1.7 %copy-start = (bf16[512,2432]{1,0:T(8,128)(2,1)S(1)}, bf16[512,2432]{1,0:T(8,128)(2,1)}, u32[]{:S(2)}) copy-start(bf16[512,2432]{1,0:T(8,128)(2,1)} %all-gather.2.cloned.1.call-done.all_ref) | copy-start | bytes 7471108
  72.9 0.8 copy-start.1
  73.7 0.8 copy-start.2
  74.5 0.7 copy-start.3
Sparse Core Ops, SparseCore 0:
  10.8 60.3 all-gather.1

commit v2 on v1

--- a/solution.py
+++ b/solution.py
@@ -104,10 +104,15 @@
 
 
 def main_kernel(
-    image_ref, text_ref, class_ref, scale_ref, shift_ref, all_ref, loss_ref, grad_image_ref, grad_text_ref
+    image_ref, text_ref, class_ref, scale_ref, shift_ref, *refs
 ):
+    block_refs, (loss_ref, grad_image_ref, grad_text_ref, all_ref) = refs[:-4], refs[-4:]
     rows, depth = image_ref.shape
     pairs = all_ref.shape[0]
+    start = 0
+    for block_ref in block_refs:
+        all_ref[start : start + block_ref.shape[0], :] = block_ref[...]
+        start += block_ref.shape[0]
     scale, shift = scale_ref[0], shift_ref[0]
     image_unit, image_inv = unit_rows(image_ref[...])
     text_unit, text_inv = unit_rows(text_ref[...])
@@ -143,6 +148,18 @@
         text_unit.astype(jnp.bfloat16), all_ref[:, :depth], sign, scale, shift
     )
     grad_text_ref[...] = project_back(text_unit, text_inv, text_pull)
+
+
+def exchange(rows, n, stride):
+    return lax.ppermute(rows, ("img", "txt"), [(i, i ^ stride) for i in range(n)])
+
+
+def spread(rows, n):
+    quarter = n // 4
+    line = [rows] + [exchange(rows, n, k * quarter) for k in (1, 2, 3)]
+    line = jnp.concatenate(line, axis=0)
+    plane = [line] + [exchange(line, n, k) for k in (quarter // 2, 1, quarter // 2 + 1)]
+    return plane + [exchange(block, n, quarter // 4) for block in plane]
 
 
 def gather_plan(image_emb, text_emb, pair_class, scale, shift):
@@ -158,7 +175,7 @@
         out_specs=vmem,
         name="pack",
     )(image_emb, text_emb, pair_class)
-    everything = lax.all_gather(packed, ("img", "txt"), axis=0, tiled=True)
+    blocks = spread(packed, lax.axis_size("img") * lax.axis_size("txt"))
     loss, grad_image, grad_text = pl.pallas_call(
         main_kernel,
         out_shape=(
@@ -166,18 +183,21 @@
             jax.ShapeDtypeStruct((rows, depth), jnp.float32),
             jax.ShapeDtypeStruct((rows, depth), jnp.float32),
         ),
-        in_specs=[vmem, vmem, smem, smem, smem, vmem],
+        in_specs=[vmem, vmem, smem, smem, smem] + [vmem] * len(blocks),
         out_specs=(vmem, vmem, vmem),
+        scratch_shapes=[pltpu.VMEM((pairs, width), jnp.bfloat16)],
         compiler_params=pltpu.CompilerParams(vmem_limit_bytes=32 << 20),
         name="contrast",
-    )(image_emb, text_emb, pair_class, scale[None], shift[None], everything)
+    )(image_emb, text_emb, pair_class, scale[None], shift[None], *blocks)
     return (loss[0], grad_image, grad_text)
 
 
 def local(image_emb, text_emb, pair_class, scale, shift):
     rows, depth = image_emb.shape
     pairs = rows * lax.axis_size("img") * lax.axis_size("txt")
-    if 2 * pairs * depth * image_emb.dtype.itemsize <= GATHER_LIMIT_BYTES:
+    devices = lax.axis_size("img") * lax.axis_size("txt")
+    small = 2 * pairs * depth * image_emb.dtype.itemsize <= GATHER_LIMIT_BYTES
+    if small and devices == 32:
         return gather_plan(image_emb, text_emb, pair_class, scale, shift)
     return tile_plan(image_emb, text_emb, pair_class, scale, shift)
 

time: 84.9 us -> 36.7 us (0.43)
  waiting for transfers between devices: 61.2 us -> 19.3 us
  between operations: 15.3 us -> 1.97 us
  starting transfers between devices: 0.04 us -> 9.48 us
  local copies, waits for them, and re-layouts: 3.89 us -> 0.66 us
  other arithmetic: 0 us -> 0.91 us
    all_gather x1 -> x0, waiting for transfers between devices: 61.2 us -> none  [gather_plan(): everything = lax.all_gather(packed, ('img', 'txt'), axis=0, tiled=True)]
    ppermute x0 -> x10, waiting for transfers between devices: none -> 19.3 us  [exchange(): lax.ppermute(rows, ('img', 'txt'), [(i, i ^ stride) for i in range(n)])]
    ppermute x0 -> x10, starting transfers between devices: none -> 9.48 us  [exchange(): lax.ppermute(rows, ('img', 'txt'), [(i, i ^ stride) for i in range(n)])]
    unnamed x8 -> x6, local copies, waits for them, and re-layouts: 3.89 us -> 0.66 us
    concatenate x0 -> x1, other arithmetic: none -> 0.91 us  [spread(): line = jnp.concatenate(line, axis=0)]
  transfers between devices with their start and end apart: 1 -> 10, of which waited for: 1 -> 6; matrix products, arithmetic and copies ran while one was open for 0% -> 0% of each run, Pallas kernels for 0% -> 0%
where the time goes in v2:
time: 36.7 us; the launch traced here: 36.4 us
  waiting for transfers between devices  19.3 us (53%)
  starting transfers between devices  9.48 us (26%)
  Pallas kernels  4.12 us (11%)
  between operations  1.97 us (5%)
  other arithmetic  0.91 us (2%)
  local copies, waits for them, and re-layouts  0.66 us (2%)
    ppermute x10, waiting for transfers between devices, exchange(): lax.ppermute(rows, ('img', 'txt'), [(i, i ^ stride) for i in range(n)])  19.3 us
    ppermute x10, starting transfers between devices, exchange(): lax.ppermute(rows, ('img', 'txt'), [(i, i ^ stride) for i in range(n)])  9.48 us
    pallas_call x1, Pallas kernels, gather_plan(): pl.pallas_call(main_kernel, out_shape=(jax.ShapeDtypeStruct((1, rows), jn...  2.59 us
    pallas_call x1, Pallas kernels, gather_plan(): pl.pallas_call(pack_kernel, out_shape=jax.ShapeDtypeStruct((rows, width),...  1.54 us
    concatenate x1, other arithmetic, spread(): line = jnp.concatenate(line, axis=0)  0.91 us
  transfers between devices with their start and end apart: 10, of which 6 were waited for; matrix products, arithmetic and copies ran while one was open for 0% of the time, Pallas kernels for 0%

profile of v2, /device:TPU:0, one launch (start us, length us, event | category | flops | bytes accessed | tf_op | source)
XLA Modules:
  0.0 36.4 jit_solution(18047470303651439044)
XLA Ops:
  0.6 1.5 %pack.1 = bf16[16,2432]{1,0:T(8,128)(2,1)} custom-call(bf16[16,1152]{1,0:T(8,128)(2,1)} %image_ref.3, bf16[16,1152]{1,0:T(8,128)(2,1)} %text_ref.3, s32[16]{0:T(128)} %class_ref.3), custom_call_target="tpu_custom_call" | custom-call | tf_op jit(solution)/shard_map/pack/pallas_call | solution.py:171
  2.2 0.0 copy-start
  2.2 0.0 copy-start.1
  2.2 5.0 %collective-permute-start.2 = (bf16[16,2432]{1,0:T(8,128)(2,1)}, bf16[16,2432]{1,0:T(8,128)(2,1)S(1)}, u32[]{:S(2)}, u32[]{:S(2)}) collective-permute-start(bf16[16,2432]{1,0:T(8,128)(2,1)} %pack.1), channel_id=1, source_target_pairs={{0,24},{1,25},{2,26},{3,27},{4,28},{5,29},{6,30},{7,31},{8,16},{9,... | collective-permute-start | bytes 233480 | tf_op jit(solution)/shard_map/ppermute | solution.py:154
  7.2 0.0 collective-permute-start.1
  7.2 0.6 %collective-permute-start = (bf16[16,2432]{1,0:T(8,128)(2,1)}, bf16[16,2432]{1,0:T(8,128)(2,1)S(1)}, u32[]{:S(2)}, u32[]{:S(2)}) collective-permute-start(bf16[16,2432]{1,0:T(8,128)(2,1)} %pack.1), channel_id=1, source_target_pairs={{0,8},{1,9},{2,10},{3,11},{4,12},{5,13},{6,14},{7,15},{8,0},{9,1},... | collective-permute-start | bytes 233480 | tf_op jit(solution)/shard_map/ppermute | solution.py:154
  7.9 2.4 %collective-permute-done.2 = bf16[16,2432]{1,0:T(8,128)(2,1)S(1)} collective-permute-done((bf16[16,2432]{1,0:T(8,128)(2,1)}, bf16[16,2432]{1,0:T(8,128)(2,1)S(1)}, u32[]{:S(2)}, u32[]{:S(2)}) %collective-permute-start.2) | collective-permute-done | bytes 77856 | tf_op jit(solution)/shard_map/ppermute | solution.py:154
  10.3 3.7 %collective-permute-done.1 = bf16[16,2432]{1,0:T(8,128)(2,1)S(1)} collective-permute-done((bf16[16,2432]{1,0:T(8,128)(2,1)}, bf16[16,2432]{1,0:T(8,128)(2,1)S(1)}, u32[]{:S(2)}, u32[]{:S(2)}) %collective-permute-start.1) | collective-permute-done | bytes 77856 | tf_op jit(solution)/shard_map/ppermute | solution.py:154
  14.0 0.0 collective-permute-done
  14.0 0.9 %pad_maximum_fusion.refs_0_ = bf16[64,2432]{1,0:T(8,128)(2,1)S(1)} fusion(bf16[16,2432]{1,0:T(8,128)(2,1)S(1)} %collective-permute-done.2, bf16[16,2432]{1,0:T(8,128)(2,1)S(1)} %collective-permute-done.1, bf16[16,2432]{1,0:T(8,128)(2,1)S(1)} %collective-permute-done, bf16[16,2432]{1,0:T(8,128)(2,1)} %pack.1), kind=kLoop, calls=%fused_computation | loop fusion | flops 1245184 | bytes 622592 | tf_op jit(solution)/shard_map/concatenate | solution.py:160
  14.9 2.5 %collective-permute-start.5 = (bf16[64,2432]{1,0:T(8,128)(2,1)S(1)}, bf16[64,2432]{1,0:T(8,128)(2,1)S(1)}, u32[]{:S(2)}, u32[]{:S(2)}) collective-permute-start(bf16[64,2432]{1,0:T(8,128)(2,1)S(1)} %pad_maximum_fusion.refs_0_), channel_id=1, source_target_pairs={{0,5},{1,4},{2,7},{3,6},{4,1},{5,0},{6,3},{7,2},{8,13},{9,12},{10,... | collective-permute-start | bytes 933896 | tf_op jit(solution)/shard_map/ppermute | solution.py:154
  17.4 0.5 %collective-permute-start.4 = (bf16[64,2432]{1,0:T(8,128)(2,1)S(1)}, bf16[64,2432]{1,0:T(8,128)(2,1)S(1)}, u32[]{:S(2)}, u32[]{:S(2)}) collective-permute-start(bf16[64,2432]{1,0:T(8,128)(2,1)S(1)} %pad_maximum_fusion.refs_0_), channel_id=1, source_target_pairs={{0,1},{1,0},{2,3},{3,2},{4,5},{5,4},{6,7},{7,6},{8,9},{9,8},{10,11... | collective-permute-start | bytes 933896 | tf_op jit(solution)/shard_map/ppermute | solution.py:154
  17.9 0.5 %collective-permute-start.3 = (bf16[64,2432]{1,0:T(8,128)(2,1)S(1)}, bf16[64,2432]{1,0:T(8,128)(2,1)S(1)}, u32[]{:S(2)}, u32[]{:S(2)}) collective-permute-start(bf16[64,2432]{1,0:T(8,128)(2,1)S(1)} %pad_maximum_fusion.refs_0_), channel_id=1, source_target_pairs={{0,4},{1,5},{2,6},{3,7},{4,0},{5,1},{6,2},{7,3},{8,12},{9,13},{10,... | collective-permute-start | bytes 933896 | tf_op jit(solution)/shard_map/ppermute | solution.py:154
  18.4 0.0 collective-permute-start.6
  18.4 7.7 %collective-permute-done.5.refs_3_ = bf16[64,2432]{1,0:T(8,128)(2,1)S(1)} collective-permute-done((bf16[64,2432]{1,0:T(8,128)(2,1)S(1)}, bf16[64,2432]{1,0:T(8,128)(2,1)S(1)}, u32[]{:S(2)}, u32[]{:S(2)}) %collective-permute-start.5) | collective-permute-done | bytes 311328 | tf_op jit(solution)/shard_map/ppermute | solution.py:154
  26.2 0.0 collective-permute-start.9
  26.2 5.0 %collective-permute-done.4.refs_2_ = bf16[64,2432]{1,0:T(8,128)(2,1)S(1)} collective-permute-done((bf16[64,2432]{1,0:T(8,128)(2,1)S(1)}, bf16[64,2432]{1,0:T(8,128)(2,1)S(1)}, u32[]{:S(2)}, u32[]{:S(2)}) %collective-permute-start.4) | collective-permute-done | bytes 311328 | tf_op jit(solution)/shard_map/ppermute | solution.py:154
  31.1 0.0 collective-permute-start.8
  31.2 0.3 collective-permute-done.3.refs_1_
  31.4 0.2 collective-permute-start.7
  33.0 0.0 collective-permute-done.6.refs_4_
  33.0 0.0 collective-permute-done.9.refs_7_
  33.0 0.0 collective-permute-done.8.refs_6_
  33.0 0.2 collective-permute-done.7.refs_5_
  33.2 0.0 copy-start.2
  33.2 0.0 copy-done
  33.2 0.0 copy-done.1
  33.2 0.6 %copy-done.2 = s32[16]{0:T(128)S(1)} copy-done((s32[16]{0:T(128)S(1)}, s32[16]{0:T(128)}, u32[]{:S(2)}) %copy-start.2) | copy-done | bytes 88
  33.8 2.6 %contrast.1 = (f32[1,16]{1,0:T(1,128)}, f32[16,1152]{1,0:T(8,128)}, f32[16,1152]{1,0:T(8,128)}) custom-call(bf16[16,1152]{1,0:T(8,128)(2,1)S(1)} %copy-done, bf16[16,1152]{1,0:T(8,128)(2,1)S(1)} %copy-done.1, s32[16]{0:T(128)S(1)} %copy-done.2, f32[1]{0:T(128)} %bitcast.3.scale_ref, f32[1]{0:T(128)} %bitcast.4.shift_ref, ...), custom_call_target="tpu_custom_call" | custom-call | tf_op jit(solution)/shard_map/contrast/pallas_call | solution.py:179
Async XLA Ops:
  2.2 31.0 %copy-start = (bf16[16,1152]{1,0:T(8,128)(2,1)S(1)}, bf16[16,1152]{1,0:T(8,128)(2,1)}, u32[]{:S(2)}) copy-start(bf16[16,1152]{1,0:T(8,128)(2,1)} %image_ref.3) | copy-start | bytes 110596
  2.2 31.0 %copy-start.1 = (bf16[16,1152]{1,0:T(8,128)(2,1)S(1)}, bf16[16,1152]{1,0:T(8,128)(2,1)}, u32[]{:S(2)}) copy-start(bf16[16,1152]{1,0:T(8,128)(2,1)} %text_ref.3) | copy-start | bytes 110596
  2.2 8.1 %collective-permute-start.2 = (bf16[16,2432]{1,0:T(8,128)(2,1)}, bf16[16,2432]{1,0:T(8,128)(2,1)S(1)}, u32[]{:S(2)}, u32[]{:S(2)}) collective-permute-start(bf16[16,2432]{1,0:T(8,128)(2,1)} %pack.1), channel_id=1, source_target_pairs={{0,24},{1,25},{2,26},{3,27},{4,28},{5,29},{6,30},{7,31},{8,16},{9,... | collective-permute-start | bytes 233480 | tf_op jit(solution)/shard_map/ppermute | solution.py:154
  7.2 6.7 %collective-permute-start.1 = (bf16[16,2432]{1,0:T(8,128)(2,1)}, bf16[16,2432]{1,0:T(8,128)(2,1)S(1)}, u32[]{:S(2)}, u32[]{:S(2)}) collective-permute-start(bf16[16,2432]{1,0:T(8,128)(2,1)} %pack.1), channel_id=1, source_target_pairs={{0,16},{1,17},{2,18},{3,19},{4,20},{5,21},{6,22},{7,23},{8,24},{9,... | collective-permute-start | bytes 233480 | tf_op jit(solution)/shard_map/ppermute | solution.py:154
  7.2 6.7 %collective-permute-start = (bf16[16,2432]{1,0:T(8,128)(2,1)}, bf16[16,2432]{1,0:T(8,128)(2,1)S(1)}, u32[]{:S(2)}, u32[]{:S(2)}) collective-permute-start(bf16[16,2432]{1,0:T(8,128)(2,1)} %pack.1), channel_id=1, source_target_pairs={{0,8},{1,9},{2,10},{3,11},{4,12},{5,13},{6,14},{7,15},{8,0},{9,1},... | collective-permute-start | bytes 233480 | tf_op jit(solution)/shard_map/ppermute | solution.py:154
  14.9 11.3 %collective-permute-start.5 = (bf16[64,2432]{1,0:T(8,128)(2,1)S(1)}, bf16[64,2432]{1,0:T(8,128)(2,1)S(1)}, u32[]{:S(2)}, u32[]{:S(2)}) collective-permute-start(bf16[64,2432]{1,0:T(8,128)(2,1)S(1)} %pad_maximum_fusion.refs_0_), channel_id=1, source_target_pairs={{0,5},{1,4},{2,7},{3,6},{4,1},{5,0},{6,3},{7,2},{8,13},{9,12},{10,... | collective-permute-start | bytes 933896 | tf_op jit(solution)/shard_map/ppermute | solution.py:154
  17.4 13.8 %collective-permute-start.4 = (bf16[64,2432]{1,0:T(8,128)(2,1)S(1)}, bf16[64,2432]{1,0:T(8,128)(2,1)S(1)}, u32[]{:S(2)}, u32[]{:S(2)}) collective-permute-start(bf16[64,2432]{1,0:T(8,128)(2,1)S(1)} %pad_maximum_fusion.refs_0_), channel_id=1, source_target_pairs={{0,1},{1,0},{2,3},{3,2},{4,5},{5,4},{6,7},{7,6},{8,9},{9,8},{10,11... | collective-permute-start | bytes 933896 | tf_op jit(solution)/shard_map/ppermute | solution.py:154
  17.9 13.5 %collective-permute-start.3 = (bf16[64,2432]{1,0:T(8,128)(2,1)S(1)}, bf16[64,2432]{1,0:T(8,128)(2,1)S(1)}, u32[]{:S(2)}, u32[]{:S(2)}) collective-permute-start(bf16[64,2432]{1,0:T(8,128)(2,1)S(1)} %pad_maximum_fusion.refs_0_), channel_id=1, source_target_pairs={{0,4},{1,5},{2,6},{3,7},{4,0},{5,1},{6,2},{7,3},{8,12},{9,13},{10,... | collective-permute-start | bytes 933896 | tf_op jit(solution)/shard_map/ppermute | solution.py:154
  18.4 14.5 %collective-permute-start.6 = (bf16[64,2432]{1,0:T(8,128)(2,1)S(1)}, bf16[64,2432]{1,0:T(8,128)(2,1)S(1)}, u32[]{:S(2)}, u32[]{:S(2)}) collective-permute-start(bf16[64,2432]{1,0:T(8,128)(2,1)S(1)} %pad_maximum_fusion.refs_0_), channel_id=1, source_target_pairs={{0,2},{1,3},{2,0},{3,1},{4,6},{5,7},{6,4},{7,5},{8,10},{9,11},{10,... | collective-permute-start | bytes 933896 | tf_op jit(solution)/shard_map/ppermute | solution.py:154
  26.2 6.8 %collective-permute-start.9 = (bf16[64,2432]{1,0:T(8,128)(2,1)S(1)}, bf16[64,2432]{1,0:T(8,128)(2,1)S(1)}, u32[]{:S(2)}, u32[]{:S(2)}) collective-permute-start(bf16[64,2432]{1,0:T(8,128)(2,1)S(1)} %collective-permute-done.5.refs_3_), channel_id=1, source_target_pairs={{0,2},{1,3},{2,0},{3,1},{4,6},{5,7},{6,4},{7,5},{8,10},{9,11},{10,... | collective-permute-start | bytes 933896 | tf_op jit(solution)/shard_map/ppermute | solution.py:154
  31.1 1.8 %collective-permute-start.8 = (bf16[64,2432]{1,0:T(8,128)(2,1)S(1)}, bf16[64,2432]{1,0:T(8,128)(2,1)S(1)}, u32[]{:S(2)}, u32[]{:S(2)}) collective-permute-start(bf16[64,2432]{1,0:T(8,128)(2,1)S(1)} %collective-permute-done.4.refs_2_), channel_id=1, source_target_pairs={{0,2},{1,3},{2,0},{3,1},{4,6},{5,7},{6,4},{7,5},{8,10},{9,11},{10,... | collective-permute-start | bytes 933896 | tf_op jit(solution)/shard_map/ppermute | solution.py:154
  31.4 1.8 %collective-permute-start.7 = (bf16[64,2432]{1,0:T(8,128)(2,1)S(1)}, bf16[64,2432]{1,0:T(8,128)(2,1)S(1)}, u32[]{:S(2)}, u32[]{:S(2)}) collective-permute-start(bf16[64,2432]{1,0:T(8,128)(2,1)S(1)} %collective-permute-done.3.refs_1_), channel_id=1, source_target_pairs={{0,2},{1,3},{2,0},{3,1},{4,6},{5,7},{6,4},{7,5},{8,10},{9,11},{10,... | collective-permute-start | bytes 933896 | tf_op jit(solution)/shard_map/ppermute | solution.py:154
  33.2 0.7 %copy-start.2 = (s32[16]{0:T(128)S(1)}, s32[16]{0:T(128)}, u32[]{:S(2)}) copy-start(s32[16]{0:T(128)} %class_ref.3) | copy-start | bytes 196

commit v3 on v0

v3 whole, which is shorter than its diff:
```python
import jax
import jax.numpy as jnp
from jax import lax
from jax.experimental import pallas as pl
from jax.experimental.pallas import tpu as pltpu
from jax.sharding import PartitionSpec as P

AXES = ("img", "txt")
DIGITS = 4
LANES = 128
TOP = 32767.0


def unit_rows(rows):
    wide = rows.astype(jnp.float32)
    inverse = 1.0 / jnp.sqrt(jnp.sum(wide * wide, axis=1, keepdims=True) + 1e-06)
    return (wide * inverse, inverse)


def project_back(unit, inverse, pull):
    inner = jnp.sum(unit * pull, axis=1, keepdims=True)
    return (pull - unit * inner) * inverse


def class_digits(class_ref, rows):
    row = lax.broadcasted_iota(jnp.int32, (rows, LANES), 0)
    lane = lax.broadcasted_iota(jnp.int32, (rows, LANES), 1)
    spread = jnp.zeros((rows, LANES), jnp.int32)
    for i in range(rows):
        spread = jnp.where(row == i, class_ref[i], spread)
    digit = lax.shift_right_logical(spread, 8 * jnp.minimum(lane, DIGITS - 1)) & 255
    return jnp.where(lane < DIGITS, digit, 0).astype(jnp.float32).astype(jnp.bfloat16)


def pack_kernel(image_ref, text_ref, class_ref, image_out, text_out):
    rows, depth = image_ref.shape
    digits = class_digits(class_ref, rows)
    for source, out in ((image_ref, image_out), (text_ref, text_out)):
        half = unit_rows(source[...])[0].astype(jnp.bfloat16)
        for k in range(out.shape[0]):
            out[k, :, :depth] = half
            out[k, :, depth:] = digits


def power_above(size):
    return jnp.ceil(jnp.log2(jnp.maximum(size, 1e-30)) + 0.01)


def code(values, power):
    steps = jnp.clip(jnp.round(values * (TOP / jnp.exp2(power))), -TOP, TOP)
    return steps.astype(jnp.int32).astype(jnp.int16)


def decode(steps, power):
    return steps.astype(jnp.int32).astype(jnp.float32) * (jnp.exp2(power) * (1.0 / TOP))


def put_rows(out, pull, extra):
    blocks, rows, width = out.shape
    depth = width - LANES
    power = power_above(jnp.max(jnp.abs(pull), axis=1, keepdims=True))
    steps = code(pull, power)
    lane = lax.broadcasted_iota(jnp.int32, (blocks * rows, LANES), 1)
    tail = jnp.where(lane == 0, power, 0.0)
    if extra is not None:
        loss_power = power_above(extra)
        tail = jnp.where(lane == 1, loss_power, tail)
        tail = jnp.where(lane == 2, jnp.round(extra * (TOP / jnp.exp2(loss_power))), tail)
    tail = tail.astype(jnp.int32).astype(jnp.int16)
    for k in range(blocks):
        out[k, :, :depth] = steps[k * rows : (k + 1) * rows]
        out[k, :, depth:] = tail[k * rows : (k + 1) * rows]


def tile_kernel(image_ref, text_ref, scale_ref, shift_ref, image_out, text_out):
    a, rows, width = image_ref.shape
    b = text_ref.shape[0]
    depth = width - LANES
    scale, shift = scale_ref[0], shift_ref[0]
    image = image_ref[...].reshape(a * rows, width)
    text = text_ref[...].reshape(b * rows, width)
    logits = (
        scale
        * lax.dot_general(
            image[:, :depth],
            text[:, :depth],
            (((1,), (1,)), ((), ())),
            preferred_element_type=jnp.float32,
        )
        + shift
    )
    pick = (
        lax.broadcasted_iota(jnp.int32, (8, LANES), 0)
        == lax.broadcasted_iota(jnp.int32, (8, LANES), 1)
    )
    text_digits = lax.dot_general(
        pick.astype(jnp.bfloat16),
        text[:, depth:],
        (((1,), (1,)), ((), ())),
        preferred_element_type=jnp.float32,
    )
    image_digits = image[:, depth:].astype(jnp.float32)
    same = None
    for k in range(DIGITS):
        equal = image_digits[:, k : k + 1] == text_digits[k : k + 1, :]
        same = equal if same is None else same & equal
    sign = jnp.where(same, 1.0, -1.0).astype(jnp.float32)
    margin = sign * logits
    small = jnp.exp(-jnp.abs(margin))
    over = 1.0 / (1.0 + small)
    coef = -sign * jnp.where(margin >= 0, small * over, over) * scale
    image_pull = jnp.dot(
        coef.astype(jnp.bfloat16), text[:, :depth], preferred_element_type=jnp.float32
    )
    text_pull = jnp.dot(
        coef.T.astype(jnp.bfloat16), image[:, :depth], preferred_element_type=jnp.float32
    )
    loss = jnp.sum(jnp.log1p(small) - jnp.minimum(margin, 0.0), axis=1, keepdims=True)
    put_rows(image_out, image_pull, loss)
    put_rows(text_out, text_pull, None)


def final_kernel(image_ref, text_ref, image_parts, text_parts, loss_ref, grad_image_ref, grad_text_ref):
    rows, depth = image_ref.shape
    pairs = rows * image_parts.shape[0] * text_parts.shape[0]
    for source, parts, out in (
        (image_ref, image_parts, grad_image_ref),
        (text_ref, text_parts, grad_text_ref),
    ):
        unit, inverse = unit_rows(source[...])
        pull = jnp.zeros((rows, depth), jnp.float32)
        loss = jnp.zeros((rows, 1), jnp.float32)
        for k in range(parts.shape[0]):
            tail = parts[k, :, depth:].astype(jnp.int32).astype(jnp.float32)
            pull = pull + decode(parts[k, :, :depth], tail[:, 0:1])
            loss = loss + tail[:, 2:3] * (jnp.exp2(tail[:, 1:2]) * (1.0 / TOP))
        out[...] = project_back(unit, inverse, pull)
        if out is grad_image_ref:
            row = lax.broadcasted_iota(jnp.int32, (rows, rows), 0)
            column = lax.broadcasted_iota(jnp.int32, (rows, rows), 1)
            across = jnp.where(row == column, loss / pairs, 0.0)
            loss_ref[...] = jnp.sum(across, axis=0, keepdims=True)


def local(image_emb, text_emb, pair_class, scale, shift):
    rows, depth = image_emb.shape
    n = lax.axis_size("img") * lax.axis_size("txt")
    b = min(d for d in range(1, n + 1) if n % d == 0 and d * d >= n)
    a = n // b
    along_a = [[i * b + j for i in range(a)] for j in range(b)]
    along_b = [[i * b + j for j in range(b)] for i in range(a)]
    width = depth + LANES
    vmem = pl.BlockSpec(memory_space=pltpu.VMEM)
    smem = pl.BlockSpec(memory_space=pltpu.SMEM)
    params = pltpu.CompilerParams(vmem_limit_bytes=32 << 20)

    def swap(blocks, groups):
        return lax.all_to_all(blocks, AXES, 0, 0, axis_index_groups=groups)

    image_rows, text_rows = pl.pallas_call(
        pack_kernel,
        out_shape=(
            jax.ShapeDtypeStruct((a, rows, width), jnp.bfloat16),
            jax.ShapeDtypeStruct((b, rows, width), jnp.bfloat16),
        ),
        in_specs=[vmem, vmem, smem],
        out_specs=(vmem, vmem),
        compiler_params=params,
        name="pack",
    )(image_emb, text_emb, pair_class)
    image_parts, text_parts = pl.pallas_call(
        tile_kernel,
        out_shape=(
            jax.ShapeDtypeStruct((a, rows, width), jnp.int16),
            jax.ShapeDtypeStruct((b, rows, width), jnp.int16),
        ),
        in_specs=[vmem, vmem, smem, smem],
        out_specs=(vmem, vmem),
        compiler_params=params,
        name="tile",
    )(swap(image_rows, along_a), swap(text_rows, along_b), scale[None], shift[None])
    loss, grad_image, grad_text = pl.pallas_call(
        final_kernel,
        out_shape=(
            jax.ShapeDtypeStruct((1, rows), jnp.float32),
            jax.ShapeDtypeStruct((rows, depth), jnp.float32),
            jax.ShapeDtypeStruct((rows, depth), jnp.float32),
        ),
        in_specs=[vmem, vmem, vmem, vmem],
        out_specs=(vmem, vmem, vmem),
        compiler_params=params,
        name="final",
    )(image_emb, text_emb, swap(image_parts, along_a), swap(text_parts, along_b))
    return (loss[0], grad_image, grad_text)


def solution(mesh):
    in_specs = (P(AXES, None), P(AXES, None), P(AXES), P(), P())
    out_specs = (P(AXES), P(AXES, None), P(AXES, None))
    return jax.shard_map(local, mesh=mesh, in_specs=in_specs, out_specs=out_specs, check_vma=False)
```

time: 142 us -> 49.6 us (0.35)
  waiting for transfers between devices: 59.9 us -> 5.44 us
  between operations: 17.3 us -> 1.95 us
  blocking collectives: 47.1 us -> 32.7 us
  other arithmetic: 9.42 us -> 0 us
  starting transfers between devices: 0.08 us -> 3.72 us
  Pallas kernels: 0 us -> 3.07 us
  matrix products: 2.79 us -> 0 us
  local copies, waits for them, and re-layouts: 4.28 us -> 2.19 us
    reduce_scatter x2 -> x0, waiting for transfers between devices: 59.8 us -> none  [the longest x1 58.9 us: local(): lax.psum_scatter(lax.dot_general(coef, rows_half, (((0,), (0,)), ((), ())...]
    all_to_all x0 -> x3, blocking collectives: none -> 32.7 us  [swap(): return lax.all_to_all(blocks, AXES, 0, 0, axis_index_groups=groups)]
    all_gather x2 -> x0, blocking collectives: 24.2 us -> none  [the longest x1 19.5 us: local(): lax.all_gather(text_half, 'img', axis=0, tiled=True)]
    unnamed x3 -> x0, blocking collectives: 22.9 us -> none
    all_to_all x0 -> x1, waiting for transfers between devices: none -> 5.44 us  [swap(): return lax.all_to_all(blocks, AXES, 0, 0, axis_index_groups=groups)]
    reduce_sum x4 -> x0, other arithmetic: 3.93 us -> none  [the longest x2 2.15 us: project_back(): inner = jnp.sum(unit * pull, axis=1, keepdims=True)]
    all_to_all x0 -> x1, starting transfers between devices: none -> 3.72 us  [swap(): return lax.all_to_all(blocks, AXES, 0, 0, axis_index_groups=groups)]
    mul x2 -> x0, other arithmetic: 3.2 us -> none  [project_back(): return (pull - unit * inner) * inverse]
  transfers between devices with their start and end apart: 2 -> 1, of which waited for: 2 -> 1; matrix products, arithmetic and copies ran while one was open for 3% -> 0% of each run, Pallas kernels for 0% -> 0%
where the time goes in v3:
time: 49.6 us; the launch traced here: 49.1 us
  blocking collectives  32.7 us (66%)
  waiting for transfers between devices  5.44 us (11%)
  starting transfers between devices  3.72 us (8%)
  Pallas kernels  3.07 us (6%)
  local copies, waits for them, and re-layouts  2.19 us (4%)
  between operations  1.95 us (4%)
    all_to_all x3, blocking collectives, swap(): return lax.all_to_all(blocks, AXES, 0, 0, axis_index_groups=groups)  32.7 us
    all_to_all x1, waiting for transfers between devices, swap(): return lax.all_to_all(blocks, AXES, 0, 0, axis_index_groups=groups)  5.44 us
    all_to_all x1, starting transfers between devices, swap(): return lax.all_to_all(blocks, AXES, 0, 0, axis_index_groups=groups)  3.72 us
    unnamed x10, local copies, waits for them, and re-layouts  2.19 us
    pallas_call x1, Pallas kernels, local(): pl.pallas_call(pack_kernel, out_shape=(jax.ShapeDtypeStruct((a, rows, wid...  1.39 us
  transfers between devices with their start and end apart: 1, of which 1 were waited for; matrix products, arithmetic and copies ran while one was open for 0% of the time, Pallas kernels for 0%

profile of v3, /device:TPU:0, one launch (start us, length us, event | category | flops | bytes accessed | tf_op | source)
XLA Modules:
  0.0 49.1 jit_solution(1383074332987772326)
XLA Ops:
  0.6 0.0 copy-start
  0.6 0.8 %copy-done = bf16[16,1152]{1,0:T(8,128)(2,1)S(1)} copy-done((bf16[16,1152]{1,0:T(8,128)(2,1)S(1)}, bf16[16,1152]{1,0:T(8,128)(2,1)}, u32[]{:S(2)}) %copy-start) | copy-done | bytes 36888
  1.4 0.0 copy-start.2
  1.4 0.8 %copy-done.2 = bf16[16,1152]{1,0:T(8,128)(2,1)S(1)} copy-done((bf16[16,1152]{1,0:T(8,128)(2,1)S(1)}, bf16[16,1152]{1,0:T(8,128)(2,1)}, u32[]{:S(2)}) %copy-start.2) | copy-done | bytes 36888
  2.2 0.0 copy-start.4
  2.2 0.7 %copy-done.4 = s32[16]{0:T(128)S(1)} copy-done((s32[16]{0:T(128)S(1)}, s32[16]{0:T(128)}, u32[]{:S(2)}) %copy-start.4) | copy-done | bytes 88
  2.8 1.4 %pack.1 = (bf16[4,16,1280]{2,1,0:T(8,128)(2,1)S(1)}, bf16[8,16,1280]{2,1,0:T(8,128)(2,1)}) custom-call(bf16[16,1152]{1,0:T(8,128)(2,1)S(1)} %copy-done, bf16[16,1152]{1,0:T(8,128)(2,1)S(1)} %copy-done.2, s32[16]{0:T(128)S(1)} %copy-done.4), custom_call_target="tpu_custom_call" | custom-call | tf_op jit(solution)/shard_map/pack/pallas_call | solution.py:160
  4.2 13.1 %all_to_all.20.image_ref = bf16[4,16,1280]{2,1,0:T(8,128)(2,1)S(1)} all-to-all(bf16[4,16,1280]{2,1,0:T(8,128)(2,1)S(1)} %get-tuple-element.10), channel_id=1, replica_groups={{0,8,16,24},{1,9,17,25},{2,10,18,26},{3,11,19,27},{4,12,20,28},{5,13,21..., dimensions={0} | all-to-all | bytes 327680 | tf_op jit(solution)/shard_map/all_to_all | solution.py:158
  17.3 3.7 %all-to-all-start.1 = ((bf16[8,16,1280]{2,1,0:T(8,128)(2,1)}), bf16[8,16,1280]{2,1,0:T(8,128)(2,1)S(1)}, u32[]{:S(2)}, u32[]{:S(2)}) async-start(bf16[8,16,1280]{2,1,0:T(8,128)(2,1)} %get-tuple-element.11), calls=%async_computation.1 | async-start | bytes 655360 | tf_op jit(solution)/shard_map/all_to_all | solution.py:158
  22.3 5.4 %all-to-all-done.1.text_ref = bf16[8,16,1280]{2,1,0:T(8,128)(2,1)S(1)} async-done(((bf16[8,16,1280]{2,1,0:T(8,128)(2,1)}), bf16[8,16,1280]{2,1,0:T(8,128)(2,1)S(1)}, u32[]{:S(2)}, u32[]{:S(2)}) %all-to-all-start.1) | async-done | bytes 327712 | tf_op jit(solution)/shard_map/all_to_all | solution.py:158
  27.7 0.8 %tile.1 = (s16[4,16,1280]{2,1,0:T(8,128)(2,1)S(1)}, s16[8,16,1280]{2,1,0:T(8,128)(2,1)S(1)}) custom-call(bf16[4,16,1280]{2,1,0:T(8,128)(2,1)S(1)} %all_to_all.20.image_ref, bf16[8,16,1280]{2,1,0:T(8,128)(2,1)S(1)} %all-to-all-done.1.text_ref, f32[1]{0:T(128)} %bitcast.3.scale_ref, f32[1]{0:T(128)} %bitcast.4.shift_ref), custom_call_target="tpu_custom_call" | custom-call | tf_op jit(solution)/shard_map/tile/pallas_call | solution.py:171
  28.5 9.8 %all_to_all.21.image_parts = s16[4,16,1280]{2,1,0:T(8,128)(2,1)S(1)} all-to-all(s16[4,16,1280]{2,1,0:T(8,128)(2,1)S(1)} %get-tuple-element.12), channel_id=1, replica_groups={{0,8,16,24},{1,9,17,25},{2,10,18,26},{3,11,19,27},{4,12,20,28},{5,13,21..., dimensions={0} | all-to-all | bytes 327680 | tf_op jit(solution)/shard_map/all_to_all | solution.py:158
  38.3 0.0 copy-start.1
  38.3 0.0 copy-start.3
  38.3 9.9 %all_to_all.22.text_parts = s16[8,16,1280]{2,1,0:T(8,128)(2,1)S(1)} all-to-all(s16[8,16,1280]{2,1,0:T(8,128)(2,1)S(1)} %get-tuple-element.13), channel_id=1, replica_groups={{0,1,2,3,4,5,6,7},{8,9,10,11,12,13,14,15},{16,17,18,19,20,21,22,23},{24..., dimensions={0} | all-to-all | bytes 655360 | tf_op jit(solution)/shard_map/all_to_all | solution.py:158
  48.1 0.0 copy-done.1
  48.1 0.0 copy-done.3
  48.1 0.9 %final.1 = (f32[1,16]{1,0:T(1,128)}, f32[16,1152]{1,0:T(8,128)}, f32[16,1152]{1,0:T(8,128)}) custom-call(bf16[16,1152]{1,0:T(8,128)(2,1)S(1)} %copy-done.1, bf16[16,1152]{1,0:T(8,128)(2,1)S(1)} %copy-done.3, s16[4,16,1280]{2,1,0:T(8,128)(2,1)S(1)} %all_to_all.21.image_parts, s16[8,16,1280]{2,1,0:T(8,128)(2,1)S(1)} %all_to_all.22.text_parts), custom_call_target="tpu_custom_call" | custom-call | tf_op jit(solution)/shard_map/final/pallas_call | solution.py:182
Async XLA Ops:
  0.6 0.8 %copy-start = (bf16[16,1152]{1,0:T(8,128)(2,1)S(1)}, bf16[16,1152]{1,0:T(8,128)(2,1)}, u32[]{:S(2)}) copy-start(bf16[16,1152]{1,0:T(8,128)(2,1)} %image_ref.3) | copy-start | bytes 110596
  1.4 0.8 %copy-start.2 = (bf16[16,1152]{1,0:T(8,128)(2,1)S(1)}, bf16[16,1152]{1,0:T(8,128)(2,1)}, u32[]{:S(2)}) copy-start(bf16[16,1152]{1,0:T(8,128)(2,1)} %text_ref.3) | copy-start | bytes 110596
  2.2 0.7 %copy-start.4 = (s32[16]{0:T(128)S(1)}, s32[16]{0:T(128)}, u32[]{:S(2)}) copy-start(s32[16]{0:T(128)} %class_ref.1) | copy-start | bytes 196
  17.3 10.5 %all-to-all-start.1 = ((bf16[8,16,1280]{2,1,0:T(8,128)(2,1)}), bf16[8,16,1280]{2,1,0:T(8,128)(2,1)S(1)}, u32[]{:S(2)}, u32[]{:S(2)}) async-start(bf16[8,16,1280]{2,1,0:T(8,128)(2,1)} %get-tuple-element.11), calls=%async_computation.1 | async-start | bytes 655360 | tf_op jit(solution)/shard_map/all_to_all | solution.py:158
  38.3 9.9 %copy-start.1 = (bf16[16,1152]{1,0:T(8,128)(2,1)S(1)}, bf16[16,1152]{1,0:T(8,128)(2,1)}, u32[]{:S(2)}) copy-start(bf16[16,1152]{1,0:T(8,128)(2,1)} %image_ref.3) | copy-start | bytes 110596
  38.3 9.9 %copy-start.3 = (bf16[16,1152]{1,0:T(8,128)(2,1)S(1)}, bf16[16,1152]{1,0:T(8,128)(2,1)}, u32[]{:S(2)}) copy-start(bf16[16,1152]{1,0:T(8,128)(2,1)} %text_ref.3) | copy-start | bytes 110596

commit v4 on v3

--- a/solution.py
+++ b/solution.py
@@ -1,3 +1,5 @@
+import functools
+
 import jax
 import jax.numpy as jnp
 from jax import lax
@@ -37,9 +39,8 @@
     digits = class_digits(class_ref, rows)
     for source, out in ((image_ref, image_out), (text_ref, text_out)):
         half = unit_rows(source[...])[0].astype(jnp.bfloat16)
-        for k in range(out.shape[0]):
-            out[k, :, :depth] = half
-            out[k, :, depth:] = digits
+        out[:, :depth] = half
+        out[:, depth:] = digits
 
 
 def power_above(size):
@@ -55,8 +56,8 @@
     return steps.astype(jnp.int32).astype(jnp.float32) * (jnp.exp2(power) * (1.0 / TOP))
 
 
-def put_rows(out, pull, extra):
-    blocks, rows, width = out.shape
+def put_rows(outs, pull, extra):
+    blocks, (rows, width) = len(outs), outs[0].shape
     depth = width - LANES
     power = power_above(jnp.max(jnp.abs(pull), axis=1, keepdims=True))
     steps = code(pull, power)
@@ -67,18 +68,18 @@
         tail = jnp.where(lane == 1, loss_power, tail)
         tail = jnp.where(lane == 2, jnp.round(extra * (TOP / jnp.exp2(loss_power))), tail)
     tail = tail.astype(jnp.int32).astype(jnp.int16)
-    for k in range(blocks):
-        out[k, :, :depth] = steps[k * rows : (k + 1) * rows]
-        out[k, :, depth:] = tail[k * rows : (k + 1) * rows]
-
-
-def tile_kernel(image_ref, text_ref, scale_ref, shift_ref, image_out, text_out):
-    a, rows, width = image_ref.shape
-    b = text_ref.shape[0]
-    depth = width - LANES
+    for k, out in enumerate(outs):
+        out[:, :depth] = steps[k * rows : (k + 1) * rows]
+        out[:, depth:] = tail[k * rows : (k + 1) * rows]
+
+
+def tile_kernel(a, b, scale_ref, shift_ref, *refs):
+    image_refs, text_refs = refs[:a], refs[a : a + b]
+    image_outs, text_outs = refs[a + b : 2 * a + b], refs[2 * a + b :]
+    depth = image_refs[0].shape[1] - LANES
     scale, shift = scale_ref[0], shift_ref[0]
-    image = image_ref[...].reshape(a * rows, width)
-    text = text_ref[...].reshape(b * rows, width)
+    image = jnp.concatenate([ref[...] for ref in image_refs], axis=0)
+    text = jnp.concatenate([ref[...] for ref in text_refs], axis=0)
     logits = (
         scale
         * lax.dot_general(
@@ -116,13 +117,15 @@
         coef.T.astype(jnp.bfloat16), image[:, :depth], preferred_element_type=jnp.float32
     )
     loss = jnp.sum(jnp.log1p(small) - jnp.minimum(margin, 0.0), axis=1, keepdims=True)
-    put_rows(image_out, image_pull, loss)
-    put_rows(text_out, text_pull, None)
-
-
-def final_kernel(image_ref, text_ref, image_parts, text_parts, loss_ref, grad_image_ref, grad_text_ref):
+    put_rows(image_outs, image_pull, loss)
+    put_rows(text_outs, text_pull, None)
+
+
+def final_kernel(a, b, image_ref, text_ref, *refs):
+    image_parts, text_parts = refs[:a], refs[a : a + b]
+    loss_ref, grad_image_ref, grad_text_ref = refs[a + b :]
     rows, depth = image_ref.shape
-    pairs = rows * image_parts.shape[0] * text_parts.shape[0]
+    pairs = rows * a * b
     for source, parts, out in (
         (image_ref, image_parts, grad_image_ref),
         (text_ref, text_parts, grad_text_ref),
@@ -130,9 +133,9 @@
         unit, inverse = unit_rows(source[...])
         pull = jnp.zeros((rows, depth), jnp.float32)
         loss = jnp.zeros((rows, 1), jnp.float32)
-        for k in range(parts.shape[0]):
-            tail = parts[k, :, depth:].astype(jnp.int32).astype(jnp.float32)
-            pull = pull + decode(parts[k, :, :depth], tail[:, 0:1])
+        for part in parts:
+            tail = part[:, depth:].astype(jnp.int32).astype(jnp.float32)
+            pull = pull + decode(part[:, :depth], tail[:, 0:1])
             loss = loss + tail[:, 2:3] * (jnp.exp2(tail[:, 1:2]) * (1.0 / TOP))
         out[...] = project_back(unit, inverse, pull)
         if out is grad_image_ref:
@@ -142,55 +145,64 @@
             loss_ref[...] = jnp.sum(across, axis=0, keepdims=True)
 
 
+def partner(place, k, size):
+    return place ^ k if size & (size - 1) == 0 else (place + k) % size
+
+
 def local(image_emb, text_emb, pair_class, scale, shift):
     rows, depth = image_emb.shape
     n = lax.axis_size("img") * lax.axis_size("txt")
     b = min(d for d in range(1, n + 1) if n % d == 0 and d * d >= n)
     a = n // b
-    along_a = [[i * b + j for i in range(a)] for j in range(b)]
-    along_b = [[i * b + j for j in range(b)] for i in range(a)]
     width = depth + LANES
     vmem = pl.BlockSpec(memory_space=pltpu.VMEM)
     smem = pl.BlockSpec(memory_space=pltpu.SMEM)
     params = pltpu.CompilerParams(vmem_limit_bytes=32 << 20)
 
-    def swap(blocks, groups):
-        return lax.all_to_all(blocks, AXES, 0, 0, axis_index_groups=groups)
+    def along_a(i, k):
+        return partner(i // b, k, a) * b + i % b
+
+    def along_b(i, k):
+        return i // b * b + partner(i % b, k, b)
+
+    def collect(block, size, along):
+        pairs = [[(along(i, k), i) for i in range(n)] for k in range(1, size)]
+        return [block] + [lax.ppermute(block, AXES, pair) for pair in pairs]
+
+    def give_back(blocks, along):
+        pairs = [[(i, along(i, k)) for i in range(n)] for k in range(len(blocks))]
+        return blocks[:1] + [lax.ppermute(x, AXES, p) for x, p in zip(blocks[1:], pairs[1:])]
 
     image_rows, text_rows = pl.pallas_call(
         pack_kernel,
-        out_shape=(
-            jax.ShapeDtypeStruct((a, rows, width), jnp.bfloat16),
-            jax.ShapeDtypeStruct((b, rows, width), jnp.bfloat16),
-        ),
+        out_shape=(jax.ShapeDtypeStruct((rows, width), jnp.bfloat16),) * 2,
         in_specs=[vmem, vmem, smem],
         out_specs=(vmem, vmem),
         compiler_params=params,
         name="pack",
     )(image_emb, text_emb, pair_class)
-    image_parts, text_parts = pl.pallas_call(
-        tile_kernel,
-        out_shape=(
-            jax.ShapeDtypeStruct((a, rows, width), jnp.int16),
-            jax.ShapeDtypeStruct((b, rows, width), jnp.int16),
-        ),
-        in_specs=[vmem, vmem, smem, smem],
-        out_specs=(vmem, vmem),
+    images, texts = collect(image_rows, a, along_a), collect(text_rows, b, along_b)
+    parts = pl.pallas_call(
+        functools.partial(tile_kernel, a, b),
+        out_shape=(jax.ShapeDtypeStruct((rows, width), jnp.int16),) * (a + b),
+        in_specs=[smem, smem] + [vmem] * (a + b),
+        out_specs=(vmem,) * (a + b),
         compiler_params=params,
         name="tile",
-    )(swap(image_rows, along_a), swap(text_rows, along_b), scale[None], shift[None])
+    )(scale[None], shift[None], *images, *texts)
+    parts = give_back(list(parts[:a]), along_a) + give_back(list(parts[a:]), along_b)
     loss, grad_image, grad_text = pl.pallas_call(
-        final_kernel,
+        functools.partial(final_kernel, a, b),
         out_shape=(
             jax.ShapeDtypeStruct((1, rows), jnp.float32),
             jax.ShapeDtypeStruct((rows, depth), jnp.float32),
             jax.ShapeDtypeStruct((rows, depth), jnp.float32),
         ),
-        in_specs=[vmem, vmem, vmem, vmem],
+        in_specs=[vmem] * (2 + a + b),
         out_specs=(vmem, vmem, vmem),
         compiler_params=params,
         name="final",
-    )(image_emb, text_emb, swap(image_parts, along_a), swap(text_parts, along_b))
+    )(image_emb, text_emb, *parts)
     return (loss[0], grad_image, grad_text)
 
 

time: 49.6 us -> 38.1 us (0.77)
  blocking collectives: 32.7 us -> 0 us
  starting transfers between devices: 3.72 us -> 25 us
  waiting for transfers between devices: 5.44 us -> 6.34 us
  Pallas kernels: 3.07 us -> 2.34 us
    all_to_all x3 -> x0, blocking collectives: 32.7 us -> none  [swap(): return lax.all_to_all(blocks, AXES, 0, 0, axis_index_groups=groups)]
    ppermute x0 -> x20, starting transfers between devices: none -> 25 us  [the longest x10 13.6 us: collect(): return [block] + [lax.ppermute(block, AXES, pair) for pair in pairs]]
    ppermute x0 -> x20, waiting for transfers between devices: none -> 6.34 us  [the longest x10 4.15 us: give_back(): lax.ppermute(x, AXES, p)]
    all_to_all x1 -> x0, waiting for transfers between devices: 5.44 us -> none  [swap(): return lax.all_to_all(blocks, AXES, 0, 0, axis_index_groups=groups)]
    all_to_all x1 -> x0, starting transfers between devices: 3.72 us -> none  [swap(): return lax.all_to_all(blocks, AXES, 0, 0, axis_index_groups=groups)]
    pallas_call x3, Pallas kernels: 3.07 us -> 2.34 us  [the longest x1 0.93 us: local(): pl.pallas_call(functools.partial(final_kernel, a, b), out_shape=(jax.Shap...]
  transfers between devices with their start and end apart: 1 -> 20, of which waited for: 1 -> 5; matrix products, arithmetic and copies ran while one was open for 0% -> 0% of each run, Pallas kernels for 0% -> 0%
where the time goes in v4:
time: 38.1 us; the launch traced here: 37.8 us
  starting transfers between devices  25 us (66%)
  waiting for transfers between devices  6.34 us (17%)
  Pallas kernels  2.34 us (6%)
  local copies, waits for them, and re-layouts  2.19 us (6%)
  between operations  1.99 us (5%)
    ppermute x10, starting transfers between devices, collect(): return [block] + [lax.ppermute(block, AXES, pair) for pair in pairs]  13.6 us
    ppermute x10, starting transfers between devices, give_back(): lax.ppermute(x, AXES, p)  11.3 us
    ppermute x10, waiting for transfers between devices, give_back(): lax.ppermute(x, AXES, p)  4.15 us
    ppermute x10, waiting for transfers between devices, collect(): return [block] + [lax.ppermute(block, AXES, pair) for pair in pairs]  2.19 us
    unnamed x10, local copies, waits for them, and re-layouts  2.19 us
    pallas_call x1, Pallas kernels, local(): pl.pallas_call(functools.partial(final_kernel, a, b), out_shape=(jax.Shap...  0.93 us
    pallas_call x1, Pallas kernels, local(): pl.pallas_call(functools.partial(tile_kernel, a, b), out_shape=(jax.Shape...  0.76 us
  transfers between devices with their start and end apart: 20, of which 5 were waited for; matrix products, arithmetic and copies ran while one was open for 0% of the time, Pallas kernels for 0%

profile of v4, /device:TPU:0, one launch (start us, length us, event | category | flops | bytes accessed | tf_op | source)
XLA Modules:
  0.0 37.8 jit_solution(15079499121600536124)
XLA Ops:
  0.6 0.0 copy-start
  0.6 0.8 %copy-done = bf16[16,1152]{1,0:T(8,128)(2,1)S(1)} copy-done((bf16[16,1152]{1,0:T(8,128)(2,1)S(1)}, bf16[16,1152]{1,0:T(8,128)(2,1)}, u32[]{:S(2)}) %copy-start) | copy-done | bytes 36888
  1.4 0.0 copy-start.2
  1.4 0.8 %copy-done.2 = bf16[16,1152]{1,0:T(8,128)(2,1)S(1)} copy-done((bf16[16,1152]{1,0:T(8,128)(2,1)S(1)}, bf16[16,1152]{1,0:T(8,128)(2,1)}, u32[]{:S(2)}) %copy-start.2) | copy-done | bytes 36888
  2.2 0.0 copy-start.4
  2.2 0.7 %copy-done.4 = s32[16]{0:T(128)S(1)} copy-done((s32[16]{0:T(128)S(1)}, s32[16]{0:T(128)}, u32[]{:S(2)}) %copy-start.4) | copy-done | bytes 88
  2.8 0.7 %pack.1 = (bf16[16,1280]{1,0:T(8,128)(2,1)S(1)}, bf16[16,1280]{1,0:T(8,128)(2,1)S(1)}) custom-call(bf16[16,1152]{1,0:T(8,128)(2,1)S(1)} %copy-done, bf16[16,1152]{1,0:T(8,128)(2,1)S(1)} %copy-done.2, s32[16]{0:T(128)S(1)} %copy-done.4), custom_call_target="tpu_custom_call" | custom-call | tf_op jit(solution)/shard_map/pack/pallas_call | solution.py:176
  3.5 5.1 %collective-permute-start.2 = (bf16[16,1280]{1,0:T(8,128)(2,1)S(1)}, bf16[16,1280]{1,0:T(8,128)(2,1)S(1)}, u32[]{:S(2)}, u32[]{:S(2)}) collective-permute-start(bf16[16,1280]{1,0:T(8,128)(2,1)S(1)} %get-tuple-element.20.refs_0_), channel_id=1, source_target_pairs={{24,0},{25,1},{26,2},{27,3},{28,4},{29,5},{30,6},{31,7},{16,8},{17... | collective-permute-start | bytes 122888 | tf_op jit(solution)/shard_map/ppermute | solution.py:170
  8.6 0.0 collective-permute-start.1
  8.6 0.6 %collective-permute-start = (bf16[16,1280]{1,0:T(8,128)(2,1)S(1)}, bf16[16,1280]{1,0:T(8,128)(2,1)S(1)}, u32[]{:S(2)}, u32[]{:S(2)}) collective-permute-start(bf16[16,1280]{1,0:T(8,128)(2,1)S(1)} %get-tuple-element.20.refs_0_), channel_id=1, source_target_pairs={{8,0},{9,1},{10,2},{11,3},{12,4},{13,5},{14,6},{15,7},{0,8},{1,9},... | collective-permute-start | bytes 122888 | tf_op jit(solution)/shard_map/ppermute | solution.py:170
  9.2 1.3 %collective-permute-start.9 = (bf16[16,1280]{1,0:T(8,128)(2,1)S(1)}, bf16[16,1280]{1,0:T(8,128)(2,1)S(1)}, u32[]{:S(2)}, u32[]{:S(2)}) collective-permute-start(bf16[16,1280]{1,0:T(8,128)(2,1)S(1)} %get-tuple-element.21.refs_4_), channel_id=1, source_target_pairs={{7,0},{6,1},{5,2},{4,3},{3,4},{2,5},{1,6},{0,7},{15,8},{14,9},{13,... | collective-permute-start | bytes 122888 | tf_op jit(solution)/shard_map/ppermute | solution.py:170
  10.6 1.5 %collective-permute-start.8 = (bf16[16,1280]{1,0:T(8,128)(2,1)S(1)}, bf16[16,1280]{1,0:T(8,128)(2,1)S(1)}, u32[]{:S(2)}, u32[]{:S(2)}) collective-permute-start(bf16[16,1280]{1,0:T(8,128)(2,1)S(1)} %get-tuple-element.21.refs_4_), channel_id=1, source_target_pairs={{6,0},{7,1},{4,2},{5,3},{2,4},{3,5},{0,6},{1,7},{14,8},{15,9},{12,... | collective-permute-start | bytes 122888 | tf_op jit(solution)/shard_map/ppermute | solution.py:170
  12.1 0.0 collective-permute-done.2.refs_3_
  12.1 1.4 %collective-permute-start.7 = (bf16[16,1280]{1,0:T(8,128)(2,1)S(1)}, bf16[16,1280]{1,0:T(8,128)(2,1)S(1)}, u32[]{:S(2)}, u32[]{:S(2)}) collective-permute-start(bf16[16,1280]{1,0:T(8,128)(2,1)S(1)} %get-tuple-element.21.refs_4_), channel_id=1, source_target_pairs={{5,0},{4,1},{7,2},{6,3},{1,4},{0,5},{3,6},{2,7},{13,8},{12,9},{15,... | collective-permute-start | bytes 122888 | tf_op jit(solution)/shard_map/ppermute | solution.py:170
  13.5 0.0 collective-permute-done.1.refs_2_
  13.5 1.5 %collective-permute-start.6 = (bf16[16,1280]{1,0:T(8,128)(2,1)S(1)}, bf16[16,1280]{1,0:T(8,128)(2,1)S(1)}, u32[]{:S(2)}, u32[]{:S(2)}) collective-permute-start(bf16[16,1280]{1,0:T(8,128)(2,1)S(1)} %get-tuple-element.21.refs_4_), channel_id=1, source_target_pairs={{4,0},{5,1},{6,2},{7,3},{0,4},{1,5},{2,6},{3,7},{12,8},{13,9},{14,... | collective-permute-start | bytes 122888 | tf_op jit(solution)/shard_map/ppermute | solution.py:170
  15.0 0.0 collective-permute-done.refs_1_
  15.0 0.0 collective-permute-start.5
  15.0 0.0 collective-permute-done.9.refs_11_
  15.0 1.6 %collective-permute-start.4 = (bf16[16,1280]{1,0:T(8,128)(2,1)S(1)}, bf16[16,1280]{1,0:T(8,128)(2,1)S(1)}, u32[]{:S(2)}, u32[]{:S(2)}) collective-permute-start(bf16[16,1280]{1,0:T(8,128)(2,1)S(1)} %get-tuple-element.21.refs_4_), channel_id=1, source_target_pairs={{2,0},{3,1},{0,2},{1,3},{6,4},{7,5},{4,6},{5,7},{10,8},{11,9},{8,1... | collective-permute-start | bytes 122888 | tf_op jit(solution)/shard_map/ppermute | solution.py:170
  16.6 0.0 collective-permute-done.8.refs_10_
  16.6 0.5 %collective-permute-start.3 = (bf16[16,1280]{1,0:T(8,128)(2,1)S(1)}, bf16[16,1280]{1,0:T(8,128)(2,1)S(1)}, u32[]{:S(2)}, u32[]{:S(2)}) collective-permute-start(bf16[16,1280]{1,0:T(8,128)(2,1)S(1)} %get-tuple-element.21.refs_4_), channel_id=1, source_target_pairs={{1,0},{0,1},{3,2},{2,3},{5,4},{4,5},{7,6},{6,7},{9,8},{8,9},{11,10... | collective-permute-start | bytes 122888 | tf_op jit(solution)/shard_map/ppermute | solution.py:170
  18.4 0.0 collective-permute-done.7.refs_9_
  18.5 0.0 collective-permute-done.6.refs_8_
  18.5 0.3 collective-permute-done.5.refs_7_
  18.8 0.0 collective-permute-done.4.refs_6_
  18.8 1.9 %collective-permute-done.3.refs_5_ = bf16[16,1280]{1,0:T(8,128)(2,1)S(1)} collective-permute-done((bf16[16,1280]{1,0:T(8,128)(2,1)S(1)}, bf16[16,1280]{1,0:T(8,128)(2,1)S(1)}, u32[]{:S(2)}, u32[]{:S(2)}) %collective-permute-start.3) | collective-permute-done | bytes 40992 | tf_op jit(solution)/shard_map/ppermute | solution.py:170
  20.6 0.0 copy-start.1
  20.6 0.0 copy-start.3
  20.6 0.8 %tile.1 = (s16[16,1280]{1,0:T(8,128)(2,1)S(1)}, s16[16,1280]{1,0:T(8,128)(2,1)S(1)}, s16[16,1280]{1,0:T(8,128)(2,1)S(1)}, s16[16,1280]{1,0:T(8,128)(2,1)S(1)}, s...) custom-call(f32[1]{0:T(128)} %bitcast.3.scale_ref, ...), custom_call_target="tpu_custom_call" | custom-call | tf_op jit(solution)/shard_map/tile/pallas_call | solution.py:185
  21.4 0.4 %collective-permute-start.10 = (s16[16,1280]{1,0:T(8,128)(2,1)S(1)}, s16[16,1280]{1,0:T(8,128)(2,1)S(1)}, u32[]{:S(2)}, u32[]{:S(2)}) collective-permute-start(s16[16,1280]{1,0:T(8,128)(2,1)S(1)} %get-tuple-element.23), channel_id=1, source_target_pairs={{0,8},{1,9},{2,10},{3,11},{4,12},{5,13},{6,14},{7,15},{8,0},{9,1},... | collective-permute-start | bytes 122888 | tf_op jit(solution)/shard_map/ppermute | solution.py:174
  21.8 2.9 %collective-permute-start.11 = (s16[16,1280]{1,0:T(8,128)(2,1)S(1)}, s16[16,1280]{1,0:T(8,128)(2,1)S(1)}, u32[]{:S(2)}, u32[]{:S(2)}) collective-permute-start(s16[16,1280]{1,0:T(8,128)(2,1)S(1)} %get-tuple-element.24), channel_id=1, source_target_pairs={{0,16},{1,17},{2,18},{3,19},{4,20},{5,21},{6,22},{7,23},{8,24},{9,... | collective-permute-start | bytes 122888 | tf_op jit(solution)/shard_map/ppermute | solution.py:174
  24.7 1.1 %collective-permute-start.12 = (s16[16,1280]{1,0:T(8,128)(2,1)S(1)}, s16[16,1280]{1,0:T(8,128)(2,1)S(1)}, u32[]{:S(2)}, u32[]{:S(2)}) collective-permute-start(s16[16,1280]{1,0:T(8,128)(2,1)S(1)} %get-tuple-element.25), channel_id=1, source_target_pairs={{0,24},{1,25},{2,26},{3,27},{4,28},{5,29},{6,30},{7,31},{8,16},{9,... | collective-permute-start | bytes 122888 | tf_op jit(solution)/shard_map/ppermute | solution.py:174
  25.9 0.5 %collective-permute-start.13 = (s16[16,1280]{1,0:T(8,128)(2,1)S(1)}, s16[16,1280]{1,0:T(8,128)(2,1)S(1)}, u32[]{:S(2)}, u32[]{:S(2)}) collective-permute-start(s16[16,1280]{1,0:T(8,128)(2,1)S(1)} %get-tuple-element.27), channel_id=1, source_target_pairs={{0,1},{1,0},{2,3},{3,2},{4,5},{5,4},{6,7},{7,6},{8,9},{9,8},{10,11... | collective-permute-start | bytes 122888 | tf_op jit(solution)/shard_map/ppermute | solution.py:174
  26.4 0.0 collective-permute-start.14
  26.4 0.0 collective-permute-done.10.refs_1_
  26.4 1.6 %collective-permute-start.15 = (s16[16,1280]{1,0:T(8,128)(2,1)S(1)}, s16[16,1280]{1,0:T(8,128)(2,1)S(1)}, u32[]{:S(2)}, u32[]{:S(2)}) collective-permute-start(s16[16,1280]{1,0:T(8,128)(2,1)S(1)} %get-tuple-element.29), channel_id=1, source_target_pairs={{0,3},{1,2},{2,1},{3,0},{4,7},{5,6},{6,5},{7,4},{8,11},{9,10},{10,... | collective-permute-start | bytes 122888 | tf_op jit(solution)/shard_map/ppermute | solution.py:174
  28.0 0.0 collective-permute-done.11.refs_2_
  28.0 0.6 %collective-permute-start.16 = (s16[16,1280]{1,0:T(8,128)(2,1)S(1)}, s16[16,1280]{1,0:T(8,128)(2,1)S(1)}, u32[]{:S(2)}, u32[]{:S(2)}) collective-permute-start(s16[16,1280]{1,0:T(8,128)(2,1)S(1)} %get-tuple-element.30), channel_id=1, source_target_pairs={{0,4},{1,5},{2,6},{3,7},{4,0},{5,1},{6,2},{7,3},{8,12},{9,13},{10,... | collective-permute-start | bytes 122888 | tf_op jit(solution)/shard_map/ppermute | solution.py:174
  28.6 1.9 %collective-permute-done.12.refs_3_ = s16[16,1280]{1,0:T(8,128)(2,1)S(1)} collective-permute-done((s16[16,1280]{1,0:T(8,128)(2,1)S(1)}, s16[16,1280]{1,0:T(8,128)(2,1)S(1)}, u32[]{:S(2)}, u32[]{:S(2)}) %collective-permute-start.12) | collective-permute-done | bytes 40992 | tf_op jit(solution)/shard_map/ppermute | solution.py:174
  30.5 1.4 %collective-permute-start.17 = (s16[16,1280]{1,0:T(8,128)(2,1)S(1)}, s16[16,1280]{1,0:T(8,128)(2,1)S(1)}, u32[]{:S(2)}, u32[]{:S(2)}) collective-permute-start(s16[16,1280]{1,0:T(8,128)(2,1)S(1)} %get-tuple-element.31), channel_id=1, source_target_pairs={{0,5},{1,4},{2,7},{3,6},{4,1},{5,0},{6,3},{7,2},{8,13},{9,12},{10,... | collective-permute-start | bytes 122888 | tf_op jit(solution)/shard_map/ppermute | solution.py:174
  32.0 0.0 collective-permute-done.13.refs_5_
  32.0 0.0 collective-permute-start.18
  32.0 0.0 collective-permute-done.14.refs_6_
  32.0 2.7 %collective-permute-start.19 = (s16[16,1280]{1,0:T(8,128)(2,1)S(1)}, s16[16,1280]{1,0:T(8,128)(2,1)S(1)}, u32[]{:S(2)}, u32[]{:S(2)}) collective-permute-start(s16[16,1280]{1,0:T(8,128)(2,1)S(1)} %get-tuple-element.33), channel_id=1, source_target_pairs={{0,7},{1,6},{2,5},{3,4},{4,3},{5,2},{6,1},{7,0},{8,15},{9,14},{10,... | collective-permute-start | bytes 122888 | tf_op jit(solution)/shard_map/ppermute | solution.py:174
  34.7 0.0 collective-permute-done.15.refs_7_
  34.7 0.0 collective-permute-done.16.refs_8_
  34.7 0.8 %collective-permute-done.17.refs_9_ = s16[16,1280]{1,0:T(8,128)(2,1)S(1)} collective-permute-done((s16[16,1280]{1,0:T(8,128)(2,1)S(1)}, s16[16,1280]{1,0:T(8,128)(2,1)S(1)}, u32[]{:S(2)}, u32[]{:S(2)}) %collective-permute-start.17) | collective-permute-done | bytes 40992 | tf_op jit(solution)/shard_map/ppermute | solution.py:174
  35.4 0.0 collective-permute-done.18.refs_10_
  35.4 1.5 %collective-permute-done.19.refs_11_ = s16[16,1280]{1,0:T(8,128)(2,1)S(1)} collective-permute-done((s16[16,1280]{1,0:T(8,128)(2,1)S(1)}, s16[16,1280]{1,0:T(8,128)(2,1)S(1)}, u32[]{:S(2)}, u32[]{:S(2)}) %collective-permute-start.19) | collective-permute-done | bytes 40992 | tf_op jit(solution)/shard_map/ppermute | solution.py:174
  36.9 0.0 copy-done.1
  36.9 0.0 copy-done.3
  36.9 0.9 %final.1 = (f32[1,16]{1,0:T(1,128)}, f32[16,1152]{1,0:T(8,128)}, f32[16,1152]{1,0:T(8,128)}) custom-call(bf16[16,1152]{1,0:T(8,128)(2,1)S(1)} %copy-done.1, bf16[16,1152]{1,0:T(8,128)(2,1)S(1)} %copy-done.3, s16[16,1280]{1,0:T(8,128)(2,1)S(1)} %get-tuple-element.22.refs_0_, s16[16,1280]{1,0:T(8,128)(2,1)S(1)} %collective-permute-done.10.refs_1_, ...), custom_call_target="tpu_custom_call" | custom-call | tf_op jit(solution)/shard_map/final/pallas_call | solution.py:194
Async XLA Ops:
  0.6 0.8 %copy-start = (bf16[16,1152]{1,0:T(8,128)(2,1)S(1)}, bf16[16,1152]{1,0:T(8,128)(2,1)}, u32[]{:S(2)}) copy-start(bf16[16,1152]{1,0:T(8,128)(2,1)} %image_ref.3) | copy-start | bytes 110596
  1.4 0.8 %copy-start.2 = (bf16[16,1152]{1,0:T(8,128)(2,1)S(1)}, bf16[16,1152]{1,0:T(8,128)(2,1)}, u32[]{:S(2)}) copy-start(bf16[16,1152]{1,0:T(8,128)(2,1)} %text_ref.3) | copy-start | bytes 110596
  2.2 0.7 %copy-start.4 = (s32[16]{0:T(128)S(1)}, s32[16]{0:T(128)}, u32[]{:S(2)}) copy-start(s32[16]{0:T(128)} %class_ref.1) | copy-start | bytes 196
  3.5 8.6 %collective-permute-start.2 = (bf16[16,1280]{1,0:T(8,128)(2,1)S(1)}, bf16[16,1280]{1,0:T(8,128)(2,1)S(1)}, u32[]{:S(2)}, u32[]{:S(2)}) collective-permute-start(bf16[16,1280]{1,0:T(8,128)(2,1)S(1)} %get-tuple-element.20.refs_0_), channel_id=1, source_target_pairs={{24,0},{25,1},{26,2},{27,3},{28,4},{29,5},{30,6},{31,7},{16,8},{17... | collective-permute-start | bytes 122888 | tf_op jit(solution)/shard_map/ppermute | solution.py:170
  8.6 4.9 %collective-permute-start.1 = (bf16[16,1280]{1,0:T(8,128)(2,1)S(1)}, bf16[16,1280]{1,0:T(8,128)(2,1)S(1)}, u32[]{:S(2)}, u32[]{:S(2)}) collective-permute-start(bf16[16,1280]{1,0:T(8,128)(2,1)S(1)} %get-tuple-element.20.refs_0_), channel_id=1, source_target_pairs={{16,0},{17,1},{18,2},{19,3},{20,4},{21,5},{22,6},{23,7},{24,8},{25... | collective-permute-start | bytes 122888 | tf_op jit(solution)/shard_map/ppermute | solution.py:170
  8.6 6.4 %collective-permute-start = (bf16[16,1280]{1,0:T(8,128)(2,1)S(1)}, bf16[16,1280]{1,0:T(8,128)(2,1)S(1)}, u32[]{:S(2)}, u32[]{:S(2)}) collective-permute-start(bf16[16,1280]{1,0:T(8,128)(2,1)S(1)} %get-tuple-element.20.refs_0_), channel_id=1, source_target_pairs={{8,0},{9,1},{10,2},{11,3},{12,4},{13,5},{14,6},{15,7},{0,8},{1,9},... | collective-permute-start | bytes 122888 | tf_op jit(solution)/shard_map/ppermute | solution.py:170
  9.2 5.8 %collective-permute-start.9 = (bf16[16,1280]{1,0:T(8,128)(2,1)S(1)}, bf16[16,1280]{1,0:T(8,128)(2,1)S(1)}, u32[]{:S(2)}, u32[]{:S(2)}) collective-permute-start(bf16[16,1280]{1,0:T(8,128)(2,1)S(1)} %get-tuple-element.21.refs_4_), channel_id=1, source_target_pairs={{7,0},{6,1},{5,2},{4,3},{3,4},{2,5},{1,6},{0,7},{15,8},{14,9},{13,... | collective-permute-start | bytes 122888 | tf_op jit(solution)/shard_map/ppermute | solution.py:170
  10.6 6.1 %collective-permute-start.8 = (bf16[16,1280]{1,0:T(8,128)(2,1)S(1)}, bf16[16,1280]{1,0:T(8,128)(2,1)S(1)}, u32[]{:S(2)}, u32[]{:S(2)}) collective-permute-start(bf16[16,1280]{1,0:T(8,128)(2,1)S(1)} %get-tuple-element.21.refs_4_), channel_id=1, source_target_pairs={{6,0},{7,1},{4,2},{5,3},{2,4},{3,5},{0,6},{1,7},{14,8},{15,9},{12,... | collective-permute-start | bytes 122888 | tf_op jit(solution)/shard_map/ppermute | solution.py:170
  12.1 6.4 %collective-permute-start.7 = (bf16[16,1280]{1,0:T(8,128)(2,1)S(1)}, bf16[16,1280]{1,0:T(8,128)(2,1)S(1)}, u32[]{:S(2)}, u32[]{:S(2)}) collective-permute-start(bf16[16,1280]{1,0:T(8,128)(2,1)S(1)} %get-tuple-element.21.refs_4_), channel_id=1, source_target_pairs={{5,0},{4,1},{7,2},{6,3},{1,4},{0,5},{3,6},{2,7},{13,8},{12,9},{15,... | collective-permute-start | bytes 122888 | tf_op jit(solution)/shard_map/ppermute | solution.py:170
  13.5 4.9 %collective-permute-start.6 = (bf16[16,1280]{1,0:T(8,128)(2,1)S(1)}, bf16[16,1280]{1,0:T(8,128)(2,1)S(1)}, u32[]{:S(2)}, u32[]{:S(2)}) collective-permute-start(bf16[16,1280]{1,0:T(8,128)(2,1)S(1)} %get-tuple-element.21.refs_4_), channel_id=1, source_target_pairs={{4,0},{5,1},{6,2},{7,3},{0,4},{1,5},{2,6},{3,7},{12,8},{13,9},{14,... | collective-permute-start | bytes 122888 | tf_op jit(solution)/shard_map/ppermute | solution.py:170
  15.0 3.8 %collective-permute-start.5 = (bf16[16,1280]{1,0:T(8,128)(2,1)S(1)}, bf16[16,1280]{1,0:T(8,128)(2,1)S(1)}, u32[]{:S(2)}, u32[]{:S(2)}) collective-permute-start(bf16[16,1280]{1,0:T(8,128)(2,1)S(1)} %get-tuple-element.21.refs_4_), channel_id=1, source_target_pairs={{3,0},{2,1},{1,2},{0,3},{7,4},{6,5},{5,6},{4,7},{11,8},{10,9},{9,1... | collective-permute-start | bytes 122888 | tf_op jit(solution)/shard_map/ppermute | solution.py:170
  15.0 3.8 %collective-permute-start.4 = (bf16[16,1280]{1,0:T(8,128)(2,1)S(1)}, bf16[16,1280]{1,0:T(8,128)(2,1)S(1)}, u32[]{:S(2)}, u32[]{:S(2)}) collective-permute-start(bf16[16,1280]{1,0:T(8,128)(2,1)S(1)} %get-tuple-element.21.refs_4_), channel_id=1, source_target_pairs={{2,0},{3,1},{0,2},{1,3},{6,4},{7,5},{4,6},{5,7},{10,8},{11,9},{8,1... | collective-permute-start | bytes 122888 | tf_op jit(solution)/shard_map/ppermute | solution.py:170
  16.6 4.0 %collective-permute-start.3 = (bf16[16,1280]{1,0:T(8,128)(2,1)S(1)}, bf16[16,1280]{1,0:T(8,128)(2,1)S(1)}, u32[]{:S(2)}, u32[]{:S(2)}) collective-permute-start(bf16[16,1280]{1,0:T(8,128)(2,1)S(1)} %get-tuple-element.21.refs_4_), channel_id=1, source_target_pairs={{1,0},{0,1},{3,2},{2,3},{5,4},{4,5},{7,6},{6,7},{9,8},{8,9},{11,10... | collective-permute-start | bytes 122888 | tf_op jit(solution)/shard_map/ppermute | solution.py:170
  20.6 16.3 %copy-start.1 = (bf16[16,1152]{1,0:T(8,128)(2,1)S(1)}, bf16[16,1152]{1,0:T(8,128)(2,1)}, u32[]{:S(2)}) copy-start(bf16[16,1152]{1,0:T(8,128)(2,1)} %image_ref.3) | copy-start | bytes 110596
  20.6 16.3 %copy-start.3 = (bf16[16,1152]{1,0:T(8,128)(2,1)S(1)}, bf16[16,1152]{1,0:T(8,128)(2,1)}, u32[]{:S(2)}) copy-start(bf16[16,1152]{1,0:T(8,128)(2,1)} %text_ref.3) | copy-start | bytes 110596
  21.4 5.0 %collective-permute-start.10 = (s16[16,1280]{1,0:T(8,128)(2,1)S(1)}, s16[16,1280]{1,0:T(8,128)(2,1)S(1)}, u32[]{:S(2)}, u32[]{:S(2)}) collective-permute-start(s16[16,1280]{1,0:T(8,128)(2,1)S(1)} %get-tuple-element.23), channel_id=1, source_target_pairs={{0,8},{1,9},{2,10},{3,11},{4,12},{5,13},{6,14},{7,15},{8,0},{9,1},... | collective-permute-start | bytes 122888 | tf_op jit(solution)/shard_map/ppermute | solution.py:174
  21.8 6.2 %collective-permute-start.11 = (s16[16,1280]{1,0:T(8,128)(2,1)S(1)}, s16[16,1280]{1,0:T(8,128)(2,1)S(1)}, u32[]{:S(2)}, u32[]{:S(2)}) collective-permute-start(s16[16,1280]{1,0:T(8,128)(2,1)S(1)} %get-tuple-element.24), channel_id=1, source_target_pairs={{0,16},{1,17},{2,18},{3,19},{4,20},{5,21},{6,22},{7,23},{8,24},{9,... | collective-permute-start | bytes 122888 | tf_op jit(solution)/shard_map/ppermute | solution.py:174
  24.7 5.8 %collective-permute-start.12 = (s16[16,1280]{1,0:T(8,128)(2,1)S(1)}, s16[16,1280]{1,0:T(8,128)(2,1)S(1)}, u32[]{:S(2)}, u32[]{:S(2)}) collective-permute-start(s16[16,1280]{1,0:T(8,128)(2,1)S(1)} %get-tuple-element.25), channel_id=1, source_target_pairs={{0,24},{1,25},{2,26},{3,27},{4,28},{5,29},{6,30},{7,31},{8,16},{9,... | collective-permute-start | bytes 122888 | tf_op jit(solution)/shard_map/ppermute | solution.py:174
  25.9 6.1 %collective-permute-start.13 = (s16[16,1280]{1,0:T(8,128)(2,1)S(1)}, s16[16,1280]{1,0:T(8,128)(2,1)S(1)}, u32[]{:S(2)}, u32[]{:S(2)}) collective-permute-start(s16[16,1280]{1,0:T(8,128)(2,1)S(1)} %get-tuple-element.27), channel_id=1, source_target_pairs={{0,1},{1,0},{2,3},{3,2},{4,5},{5,4},{6,7},{7,6},{8,9},{9,8},{10,11... | collective-permute-start | bytes 122888 | tf_op jit(solution)/shard_map/ppermute | solution.py:174
  26.4 5.6 %collective-permute-start.14 = (s16[16,1280]{1,0:T(8,128)(2,1)S(1)}, s16[16,1280]{1,0:T(8,128)(2,1)S(1)}, u32[]{:S(2)}, u32[]{:S(2)}) collective-permute-start(s16[16,1280]{1,0:T(8,128)(2,1)S(1)} %get-tuple-element.28), channel_id=1, source_target_pairs={{0,2},{1,3},{2,0},{3,1},{4,6},{5,7},{6,4},{7,5},{8,10},{9,11},{10,... | collective-permute-start | bytes 122888 | tf_op jit(solution)/shard_map/ppermute | solution.py:174
  26.4 8.3 %collective-permute-start.15 = (s16[16,1280]{1,0:T(8,128)(2,1)S(1)}, s16[16,1280]{1,0:T(8,128)(2,1)S(1)}, u32[]{:S(2)}, u32[]{:S(2)}) collective-permute-start(s16[16,1280]{1,0:T(8,128)(2,1)S(1)} %get-tuple-element.29), channel_id=1, source_target_pairs={{0,3},{1,2},{2,1},{3,0},{4,7},{5,6},{6,5},{7,4},{8,11},{9,10},{10,... | collective-permute-start | bytes 122888 | tf_op jit(solution)/shard_map/ppermute | solution.py:174
  28.0 6.7 %collective-permute-start.16 = (s16[16,1280]{1,0:T(8,128)(2,1)S(1)}, s16[16,1280]{1,0:T(8,128)(2,1)S(1)}, u32[]{:S(2)}, u32[]{:S(2)}) collective-permute-start(s16[16,1280]{1,0:T(8,128)(2,1)S(1)} %get-tuple-element.30), channel_id=1, source_target_pairs={{0,4},{1,5},{2,6},{3,7},{4,0},{5,1},{6,2},{7,3},{8,12},{9,13},{10,... | collective-permute-start | bytes 122888 | tf_op jit(solution)/shard_map/ppermute | solution.py:174
  30.5 4.9 %collective-permute-start.17 = (s16[16,1280]{1,0:T(8,128)(2,1)S(1)}, s16[16,1280]{1,0:T(8,128)(2,1)S(1)}, u32[]{:S(2)}, u32[]{:S(2)}) collective-permute-start(s16[16,1280]{1,0:T(8,128)(2,1)S(1)} %get-tuple-element.31), channel_id=1, source_target_pairs={{0,5},{1,4},{2,7},{3,6},{4,1},{5,0},{6,3},{7,2},{8,13},{9,12},{10,... | collective-permute-start | bytes 122888 | tf_op jit(solution)/shard_map/ppermute | solution.py:174
  32.0 3.5 %collective-permute-start.18 = (s16[16,1280]{1,0:T(8,128)(2,1)S(1)}, s16[16,1280]{1,0:T(8,128)(2,1)S(1)}, u32[]{:S(2)}, u32[]{:S(2)}) collective-permute-start(s16[16,1280]{1,0:T(8,128)(2,1)S(1)} %get-tuple-element.32), channel_id=1, source_target_pairs={{0,6},{1,7},{2,4},{3,5},{4,2},{5,3},{6,0},{7,1},{8,14},{9,15},{10,... | collective-permute-start | bytes 122888 | tf_op jit(solution)/shard_map/ppermute | solution.py:174
  32.0 4.9 %collective-permute-start.19 = (s16[16,1280]{1,0:T(8,128)(2,1)S(1)}, s16[16,1280]{1,0:T(8,128)(2,1)S(1)}, u32[]{:S(2)}, u32[]{:S(2)}) collective-permute-start(s16[16,1280]{1,0:T(8,128)(2,1)S(1)} %get-tuple-element.33), channel_id=1, source_target_pairs={{0,7},{1,6},{2,5},{3,4},{4,3},{5,2},{6,1},{7,0},{8,15},{9,14},{10,... | collective-permute-start | bytes 122888 | tf_op jit(solution)/shard_map/ppermute | solution.py:174

commit v5 on v0

--- a/solution.py
+++ b/solution.py
@@ -1,7 +1,17 @@
+import functools
+import math
+
 import jax
 import jax.numpy as jnp
 from jax import lax
+from jax.experimental import pallas as pl
+from jax.experimental.pallas import tpu as pltpu
 from jax.sharding import PartitionSpec as P
+
+AXES = ("img", "txt")
+DIGITS = 4
+LANES = 128
+TOP = 32767.0
 
 
 def unit_rows(rows):
@@ -30,7 +40,7 @@
     return (coef, loss_part)
 
 
-def local(image_emb, text_emb, pair_class, scale, shift):
+def tile_plan(image_emb, text_emb, pair_class, scale, shift):
     image_unit, image_inv = unit_rows(image_emb)
     text_unit, text_inv = unit_rows(text_emb)
     own_rows = text_emb.shape[0]
@@ -64,7 +74,200 @@
     return (row_loss, grad_image, grad_text)
 
 
+def on_first_core():
+    return lax.rem(lax.axis_index("img"), 2) == 0
+
+
+def pack_kernel(image_ref, text_ref, got_image_ref, got_text_ref, class_ref, other_class_ref, out_ref):
+    rows, depth = image_ref.shape
+    first = on_first_core()
+    own = jnp.where(first, image_ref[...].astype(jnp.float32), text_ref[...].astype(jnp.float32))
+    got = got_image_ref[...].astype(jnp.float32) + got_text_ref[...].astype(jnp.float32)
+    row = lax.broadcasted_iota(jnp.int32, (2 * rows, LANES), 0)
+    lane = lax.broadcasted_iota(jnp.int32, (2 * rows, LANES), 1)
+    spread = jnp.zeros((2 * rows, LANES), jnp.int32)
+    for i in range(rows):
+        spread = jnp.where(row == i, jnp.where(first, class_ref[i], other_class_ref[i]), spread)
+        spread = jnp.where(row == rows + i, jnp.where(first, other_class_ref[i], class_ref[i]), spread)
+    digit = lax.shift_right_logical(spread, 8 * jnp.minimum(lane, DIGITS - 1)) & 255
+    digit = jnp.where(lane < DIGITS, digit, 0).astype(jnp.float32).astype(jnp.bfloat16)
+    out_ref[:rows, :depth] = unit_rows(jnp.where(first, own, got))[0].astype(jnp.bfloat16)
+    out_ref[rows:, :depth] = unit_rows(jnp.where(first, got, own))[0].astype(jnp.bfloat16)
+    out_ref[:, depth:] = digit
+
+
+def power_above(size):
+    return jnp.ceil(jnp.log2(jnp.maximum(size, 1e-30)) + 0.01)
+
+
+def code(values, power):
+    steps = jnp.clip(jnp.round(values * (TOP / jnp.exp2(power))), -TOP, TOP)
+    return steps.astype(jnp.int32).astype(jnp.int16)
+
+
+def decode(steps, power):
+    return steps.astype(jnp.int32).astype(jnp.float32) * (jnp.exp2(power) * (1.0 / TOP))
+
+
+def put_rows(outs, pull, extra):
+    blocks, (rows, width) = len(outs), outs[0].shape
+    depth = width - LANES
+    power = power_above(jnp.max(jnp.abs(pull), axis=1, keepdims=True))
+    steps = code(pull, power)
+    lane = lax.broadcasted_iota(jnp.int32, (blocks * rows, LANES), 1)
+    tail = jnp.where(lane == 0, power, 0.0)
+    if extra is not None:
+        loss_power = power_above(extra)
+        tail = jnp.where(lane == 1, loss_power, tail)
+        tail = jnp.where(lane == 2, jnp.round(extra * (TOP / jnp.exp2(loss_power))), tail)
+    tail = tail.astype(jnp.int32).astype(jnp.int16)
+    for k, out in enumerate(outs):
+        out[:, :depth] = steps[k * rows : (k + 1) * rows]
+        out[:, depth:] = tail[k * rows : (k + 1) * rows]
+
+
+def tile_kernel(count, scale_ref, shift_ref, *refs):
+    depth = refs[0].shape[1] - LANES
+    scale, shift = scale_ref[0], shift_ref[0]
+    lines = jnp.concatenate([ref[...] for ref in refs[:count]], axis=0)
+    columns = jnp.concatenate([ref[...] for ref in refs[count : 2 * count]], axis=0)
+    logits = (
+        scale
+        * lax.dot_general(
+            lines[:, :depth],
+            columns[:, :depth],
+            (((1,), (1,)), ((), ())),
+            preferred_element_type=jnp.float32,
+        )
+        + shift
+    )
+    pick = (
+        lax.broadcasted_iota(jnp.int32, (8, LANES), 0)
+        == lax.broadcasted_iota(jnp.int32, (8, LANES), 1)
+    )
+    column_digits = lax.dot_general(
+        pick.astype(jnp.bfloat16),
+        columns[:, depth:],
+        (((1,), (1,)), ((), ())),
+        preferred_element_type=jnp.float32,
+    )
+    line_digits = lines[:, depth:].astype(jnp.float32)
+    same = None
+    for k in range(DIGITS):
+        equal = line_digits[:, k : k + 1] == column_digits[k : k + 1, :]
+        same = equal if same is None else same & equal
+    sign = jnp.where(same, 1.0, -1.0).astype(jnp.float32)
+    margin = sign * logits
+    small = jnp.exp(-jnp.abs(margin))
+    over = 1.0 / (1.0 + small)
+    coef = -sign * jnp.where(margin >= 0, small * over, over) * scale
+    pull = jnp.dot(
+        coef.astype(jnp.bfloat16), columns[:, :depth], preferred_element_type=jnp.float32
+    )
+    loss = jnp.sum(jnp.log1p(small) - jnp.minimum(margin, 0.0), axis=1, keepdims=True)
+    put_rows(refs[2 * count :], pull, loss)
+
+
+def final_kernel(count, image_ref, text_ref, *refs):
+    mine, others = refs[:count], refs[count : 2 * count]
+    loss_ref, grad_image_ref, grad_text_ref = refs[2 * count :]
+    rows, depth = image_ref.shape
+    pairs = rows * 2 * count * count
+    first = on_first_core()
+    own_rows = pl.ds(pl.multiple_of(jnp.where(first, 0, rows), rows), rows)
+
+    def total(parts):
+        pull = jnp.zeros((rows, depth), jnp.float32)
+        loss = jnp.zeros((rows, 1), jnp.float32)
+        for part in parts:
+            tail = part[own_rows, depth:].astype(jnp.int32).astype(jnp.float32)
+            pull = pull + decode(part[own_rows, :depth], tail[:, 0:1])
+            loss = loss + tail[:, 2:3] * (jnp.exp2(tail[:, 1:2]) * (1.0 / TOP))
+        return pull, loss
+
+    (pull, loss), (other_pull, other_loss) = total(mine), total(others)
+    for source, side_pull, out in (
+        (image_ref, jnp.where(first, pull, other_pull), grad_image_ref),
+        (text_ref, jnp.where(first, other_pull, pull), grad_text_ref),
+    ):
+        unit, inverse = unit_rows(source[...])
+        out[...] = project_back(unit, inverse, side_pull)
+    loss = jnp.where(first, loss, other_loss)
+    row = lax.broadcasted_iota(jnp.int32, (rows, rows), 0)
+    column = lax.broadcasted_iota(jnp.int32, (rows, rows), 1)
+    across = jnp.where(row == column, loss / pairs, 0.0)
+    loss_ref[...] = jnp.sum(across, axis=0, keepdims=True)
+
+
+def chip_plan(image_emb, text_emb, pair_class, scale, shift, count):
+    rows, depth = image_emb.shape
+    lanes = lax.axis_size("txt")
+    n = lax.axis_size("img") * lanes
+    width = depth + LANES
+    vmem = pl.BlockSpec(memory_space=pltpu.VMEM)
+    smem = pl.BlockSpec(memory_space=pltpu.SMEM)
+    params = pltpu.CompilerParams(vmem_limit_bytes=32 << 20)
+
+    def core(i):
+        return i // lanes % 2
+
+    def partner(i, k):
+        chip = i // (2 * lanes) * lanes + i % lanes
+        chip ^= k if core(i) else k * count
+        return (chip // lanes * 2 + core(i)) * lanes + chip % lanes
+
+    def swap(x, senders=(0, 1)):
+        pairs = [(i, i ^ lanes) for i in range(n) if core(i) in senders]
+        return lax.ppermute(x, AXES, pairs)
+
+    def visit(blocks):
+        return [
+            lax.ppermute(x, AXES, [(i, partner(i, k)) for i in range(n)])
+            for k, x in zip(range(1, count), blocks)
+        ]
+
+    mine = pl.pallas_call(
+        pack_kernel,
+        out_shape=jax.ShapeDtypeStruct((2 * rows, width), jnp.bfloat16),
+        in_specs=[vmem] * 4 + [smem, smem],
+        out_specs=vmem,
+        name="pack",
+    )(image_emb, text_emb, swap(image_emb, (1,)), swap(text_emb, (0,)), pair_class, swap(pair_class))
+    lines = [mine] + visit([mine] * (count - 1))
+    columns = [swap(x) for x in lines]
+    parts = pl.pallas_call(
+        functools.partial(tile_kernel, count),
+        out_shape=(jax.ShapeDtypeStruct((2 * rows, width), jnp.int16),) * count,
+        in_specs=[smem, smem] + [vmem] * (2 * count),
+        out_specs=(vmem,) * count,
+        compiler_params=params,
+        name="tile",
+    )(scale[None], shift[None], *lines, *columns)
+    parts = [parts[0]] + visit(parts[1:])
+    loss, grad_image, grad_text = pl.pallas_call(
+        functools.partial(final_kernel, count),
+        out_shape=(
+            jax.ShapeDtypeStruct((1, rows), jnp.float32),
+            jax.ShapeDtypeStruct((rows, depth), jnp.float32),
+            jax.ShapeDtypeStruct((rows, depth), jnp.float32),
+        ),
+        in_specs=[vmem] * (2 + 2 * count),
+        out_specs=(vmem, vmem, vmem),
+        compiler_params=params,
+        name="final",
+    )(image_emb, text_emb, *parts, *[swap(x) for x in parts])
+    return (loss[0], grad_image, grad_text)
+
+
+def local(image_emb, text_emb, pair_class, scale, shift):
+    chips = lax.axis_size("img") * lax.axis_size("txt") // 2
+    count = math.isqrt(chips)
+    if count * count == chips and count & (count - 1) == 0:
+        return chip_plan(image_emb, text_emb, pair_class, scale, shift, count)
+    return tile_plan(image_emb, text_emb, pair_class, scale, shift)
+
+
 def solution(mesh):
-    in_specs = (P(("img", "txt"), None), P(("img", "txt"), None), P(("img", "txt")), P(), P())
-    out_specs = (P(("img", "txt")), P(("img", "txt"), None), P(("img", "txt"), None))
+    in_specs = (P(AXES, None), P(AXES, None), P(AXES), P(), P())
+    out_specs = (P(AXES), P(AXES, None), P(AXES, None))
     return jax.shard_map(local, mesh=mesh, in_specs=in_specs, out_specs=out_specs, check_vma=False)

time: 142 us -> 33.9 us (0.24)
  waiting for transfers between devices: 59.9 us -> 10.8 us
  blocking collectives: 47.1 us -> 0 us
  starting transfers between devices: 0.08 us -> 15.4 us
  between operations: 17.3 us -> 2.03 us
  other arithmetic: 9.42 us -> 0 us
  Pallas kernels: 0 us -> 3.22 us
  matrix products: 2.79 us -> 0 us
  local copies, waits for them, and re-layouts: 4.28 us -> 2.11 us
    reduce_scatter x2 -> x0, waiting for transfers between devices: 59.8 us -> none  [the longest x1 58.9 us: local(): lax.psum_scatter(lax.dot_general(coef, rows_half, (((0,), (0,)), ((), ())...]
    all_gather x2 -> x0, blocking collectives: 24.2 us -> none  [the longest x1 19.5 us: local(): lax.all_gather(text_half, 'img', axis=0, tiled=True)]
    unnamed x3 -> x0, blocking collectives: 22.9 us -> none
    ppermute x0 -> x17, starting transfers between devices: none -> 15.4 us  [the longest x6 10.1 us: visit(): lax.ppermute(x, AXES, [(i, partner(i, k)) for i in range(n)])]
    ppermute x0 -> x17, waiting for transfers between devices: none -> 10.8 us  [the longest x6 8.25 us: visit(): lax.ppermute(x, AXES, [(i, partner(i, k)) for i in range(n)])]
    reduce_sum x4 -> x0, other arithmetic: 3.93 us -> none  [the longest x2 2.15 us: project_back(): inner = jnp.sum(unit * pull, axis=1, keepdims=True)]
    pallas_call x0 -> x3, Pallas kernels: none -> 3.22 us  [the longest x1 1.59 us: chip_plan(): pl.pallas_call(pack_kernel, out_shape=jax.ShapeDtypeStruct((2 * rows, wid...]
    mul x2 -> x0, other arithmetic: 3.2 us -> none  [project_back(): return (pull - unit * inner) * inverse]
  transfers between devices with their start and end apart: 2 -> 17, of which waited for: 2 -> 6; matrix products, arithmetic and copies ran while one was open for 3% -> 0% of each run, Pallas kernels for 0% -> 0%
where the time goes in v5:
time: 33.9 us; the launch traced here: 33.6 us
  starting transfers between devices  15.4 us (45%)
  waiting for transfers between devices  10.8 us (32%)
  Pallas kernels  3.22 us (9%)
  local copies, waits for them, and re-layouts  2.11 us (6%)
  between operations  2.03 us (6%)
    ppermute x6, starting transfers between devices, visit(): lax.ppermute(x, AXES, [(i, partner(i, k)) for i in range(n)])  10.1 us
    ppermute x6, waiting for transfers between devices, visit(): lax.ppermute(x, AXES, [(i, partner(i, k)) for i in range(n)])  8.25 us
    ppermute x11, starting transfers between devices, swap(): return lax.ppermute(x, AXES, pairs)  5.38 us
    ppermute x11, waiting for transfers between devices, swap(): return lax.ppermute(x, AXES, pairs)  2.52 us
    unnamed x12, local copies, waits for them, and re-layouts  2.11 us
    pallas_call x1, Pallas kernels, chip_plan(): pl.pallas_call(pack_kernel, out_shape=jax.ShapeDtypeStruct((2 * rows, wid...  1.59 us
    pallas_call x1, Pallas kernels, chip_plan(): pl.pallas_call(functools.partial(final_kernel, count), out_shape=(jax.Sha...  0.91 us
    pallas_call x1, Pallas kernels, chip_plan(): pl.pallas_call(functools.partial(tile_kernel, count), out_shape=(jax.Shap...  0.72 us
  transfers between devices with their start and end apart: 17, of which 6 were waited for; matrix products, arithmetic and copies ran while one was open for 0% of the time, Pallas kernels for 0%

profile of v5, /device:TPU:0, one launch (start us, length us, event | category | flops | bytes accessed | tf_op | source)
XLA Modules:
  0.0 33.6 jit_solution(16966159477243122443)
XLA Ops:
  0.6 1.3 %collective-permute-start = (bf16[16,1152]{1,0:T(8,128)(2,1)}, bf16[16,1152]{1,0:T(8,128)(2,1)S(1)}, u32[]{:S(2)}, u32[]{:S(2)}) collective-permute-start(bf16[16,1152]{1,0:T(8,128)(2,1)} %image_ref.3), channel_id=1, source_target_pairs={{2,0},{3,1},{6,4},{7,5},{10,8},{11,9},{14,12},{15,13},{18,16},{19,... | collective-permute-start | bytes 110600 | tf_op jit(solution)/shard_map/ppermute | solution.py:221
  1.9 3.0 %collective-permute-start.1 = (bf16[16,1152]{1,0:T(8,128)(2,1)}, bf16[16,1152]{1,0:T(8,128)(2,1)S(1)}, u32[]{:S(2)}, u32[]{:S(2)}) collective-permute-start(bf16[16,1152]{1,0:T(8,128)(2,1)} %text_ref.3), channel_id=1, source_target_pairs={{0,2},{1,3},{4,6},{5,7},{8,10},{9,11},{12,14},{13,15},{16,18},{17,... | collective-permute-start | bytes 110600 | tf_op jit(solution)/shard_map/ppermute | solution.py:221
  5.0 0.1 collective-permute-start.2
  5.1 1.2 %collective-permute-done.2.other_class_ref = s32[16]{0:T(128)S(1)} collective-permute-done((s32[16]{0:T(128)}, s32[16]{0:T(128)S(1)}, u32[]{:S(2)}, u32[]{:S(2)}) %collective-permute-start.2) | collective-permute-done | bytes 96 | tf_op jit(solution)/shard_map/ppermute | solution.py:221
  6.3 0.0 copy-start.5
  6.3 0.0 collective-permute-done.got_image_ref
  6.3 0.0 copy-start.3
  6.3 0.0 collective-permute-done.1.got_text_ref
  6.3 0.5 %copy-done.5 = s32[16]{0:T(128)} copy-done((s32[16]{0:T(128)}, s32[16]{0:T(128)S(1)}, u32[]{:S(2)}) %copy-start.5) | copy-done | bytes 88
  6.8 0.1 copy-done.3
  6.9 0.0 copy-start.4
  6.9 0.6 %copy-done.4 = bf16[16,1152]{1,0:T(8,128)(2,1)} copy-done((bf16[16,1152]{1,0:T(8,128)(2,1)}, bf16[16,1152]{1,0:T(8,128)(2,1)S(1)}, u32[]{:S(2)}) %copy-start.4) | copy-done | bytes 36888
  7.5 1.6 %pack.1.refs_0_ = bf16[32,1280]{1,0:T(8,128)(2,1)} custom-call(bf16[16,1152]{1,0:T(8,128)(2,1)} %image_ref.3, bf16[16,1152]{1,0:T(8,128)(2,1)} %text_ref.3, bf16[16,1152]{1,0:T(8,128)(2,1)} %copy-done.3, bf16[16,1152]{1,0:T(8,128)(2,1)} %copy-done.4, s32[16]{0:T(128)} %class_ref.1, s32[16]{0:T(128)} %copy-done.5), custom_call_target="tpu_custom_call" | custom-call | tf_op jit(solution)/shard_map/pack/pallas_call | solution.py:229
  9.1 5.0 %collective-permute-start.5 = (bf16[32,1280]{1,0:T(8,128)(2,1)}, bf16[32,1280]{1,0:T(8,128)(2,1)S(1)}, u32[]{:S(2)}, u32[]{:S(2)}) collective-permute-start(bf16[32,1280]{1,0:T(8,128)(2,1)} %pack.1.refs_0_), channel_id=1, source_target_pairs={{0,24},{1,25},{2,7},{3,6},{4,28},{5,29},{6,3},{7,2},{8,16},{9,17},... | collective-permute-start | bytes 245768 | tf_op jit(solution)/shard_map/ppermute | solution.py:225
  14.2 0.0 collective-permute-start.4
  14.2 0.6 %collective-permute-start.3 = (bf16[32,1280]{1,0:T(8,128)(2,1)}, bf16[32,1280]{1,0:T(8,128)(2,1)S(1)}, u32[]{:S(2)}, u32[]{:S(2)}) collective-permute-start(bf16[32,1280]{1,0:T(8,128)(2,1)} %pack.1.refs_0_), channel_id=1, source_target_pairs={{0,8},{1,9},{2,3},{3,2},{4,12},{5,13},{6,7},{7,6},{8,0},{9,1},{10,... | collective-permute-start | bytes 245768 | tf_op jit(solution)/shard_map/ppermute | solution.py:225
  14.7 0.0 collective-permute-start.6
  14.7 2.2 %collective-permute-done.5.refs_3_ = bf16[32,1280]{1,0:T(8,128)(2,1)S(1)} collective-permute-done((bf16[32,1280]{1,0:T(8,128)(2,1)}, bf16[32,1280]{1,0:T(8,128)(2,1)S(1)}, u32[]{:S(2)}, u32[]{:S(2)}) %collective-permute-start.5) | collective-permute-done | bytes 81952 | tf_op jit(solution)/shard_map/ppermute | solution.py:225
  16.9 0.0 collective-permute-start.9
  16.9 2.8 %collective-permute-done.4.refs_2_ = bf16[32,1280]{1,0:T(8,128)(2,1)S(1)} collective-permute-done((bf16[32,1280]{1,0:T(8,128)(2,1)}, bf16[32,1280]{1,0:T(8,128)(2,1)S(1)}, u32[]{:S(2)}, u32[]{:S(2)}) %collective-permute-start.4) | collective-permute-done | bytes 81952 | tf_op jit(solution)/shard_map/ppermute | solution.py:225
  19.7 0.0 collective-permute-start.8
  19.7 0.0 collective-permute-done.3.refs_1_
  19.7 0.5 %collective-permute-start.7 = (bf16[32,1280]{1,0:T(8,128)(2,1)S(1)}, bf16[32,1280]{1,0:T(8,128)(2,1)S(1)}, u32[]{:S(2)}, u32[]{:S(2)}) collective-permute-start(bf16[32,1280]{1,0:T(8,128)(2,1)S(1)} %collective-permute-done.3.refs_1_), channel_id=1, source_target_pairs={{0,2},{1,3},{2,0},{3,1},{4,6},{5,7},{6,4},{7,5},{8,10},{9,11},{10,... | collective-permute-start | bytes 245768 | tf_op jit(solution)/shard_map/ppermute | solution.py:221
  21.5 0.0 collective-permute-done.6.refs_4_
  21.5 0.0 collective-permute-done.9.refs_7_
  21.6 0.0 collective-permute-done.8.refs_6_
  21.6 0.0 collective-permute-done.7.refs_5_
  21.6 0.0 copy-start
  21.6 0.9 %copy-done = bf16[32,1280]{1,0:T(8,128)(2,1)S(1)} copy-done((bf16[32,1280]{1,0:T(8,128)(2,1)S(1)}, bf16[32,1280]{1,0:T(8,128)(2,1)}, u32[]{:S(2)}) %copy-start) | copy-done | bytes 81944
  22.5 0.0 copy-start.1
  22.5 0.0 copy-start.2
  22.5 0.7 %tile.1 = (s16[32,1280]{1,0:T(8,128)(2,1)S(1)}, s16[32,1280]{1,0:T(8,128)(2,1)S(1)}, s16[32,1280]{1,0:T(8,128)(2,1)S(1)}, s16[32,1280]{1,0:T(8,128)(2,1)S(1)}) custom-call(f32[1]{0:T(128)} %bitcast.3.scale_ref, f32[1]{0:T(128)} %bitcast.4.shift_ref, bf16[32,1280]{1,0:T(8,128)(2,1)S(1)} %copy-done, bf16[32,1280]{1,0:T(8,128)(2,1)S(1)} %collective-permute-done.3.refs_1_, ...), custom_call_target="tpu_custom_call" | custom-call | tf_op jit(solution)/shard_map/tile/pallas_call | solution.py:238
  23.2 0.4 %collective-permute-start.10 = (s16[32,1280]{1,0:T(8,128)(2,1)S(1)}, s16[32,1280]{1,0:T(8,128)(2,1)S(1)}, u32[]{:S(2)}, u32[]{:S(2)}) collective-permute-start(s16[32,1280]{1,0:T(8,128)(2,1)S(1)} %get-tuple-element.11), channel_id=1, source_target_pairs={{0,8},{1,9},{2,3},{3,2},{4,12},{5,13},{6,7},{7,6},{8,0},{9,1},{10,... | collective-permute-start | bytes 245768 | tf_op jit(solution)/shard_map/ppermute | solution.py:225
  23.6 1.5 %collective-permute-start.11 = (s16[32,1280]{1,0:T(8,128)(2,1)S(1)}, s16[32,1280]{1,0:T(8,128)(2,1)S(1)}, u32[]{:S(2)}, u32[]{:S(2)}) collective-permute-start(s16[32,1280]{1,0:T(8,128)(2,1)S(1)} %get-tuple-element.12), channel_id=1, source_target_pairs={{0,16},{1,17},{2,6},{3,7},{4,20},{5,21},{6,2},{7,3},{8,24},{9,25},... | collective-permute-start | bytes 245768 | tf_op jit(solution)/shard_map/ppermute | solution.py:225
  25.1 2.6 %collective-permute-start.12 = (s16[32,1280]{1,0:T(8,128)(2,1)S(1)}, s16[32,1280]{1,0:T(8,128)(2,1)S(1)}, u32[]{:S(2)}, u32[]{:S(2)}) collective-permute-start(s16[32,1280]{1,0:T(8,128)(2,1)S(1)} %get-tuple-element.13), channel_id=1, source_target_pairs={{0,24},{1,25},{2,7},{3,6},{4,28},{5,29},{6,3},{7,2},{8,16},{9,17},... | collective-permute-start | bytes 245768 | tf_op jit(solution)/shard_map/ppermute | solution.py:225
  27.7 0.0 collective-permute-start.13
  27.7 0.0 collective-permute-done.10.refs_1_
  27.7 0.5 %collective-permute-start.14 = (s16[32,1280]{1,0:T(8,128)(2,1)S(1)}, s16[32,1280]{1,0:T(8,128)(2,1)S(1)}, u32[]{:S(2)}, u32[]{:S(2)}) collective-permute-start(s16[32,1280]{1,0:T(8,128)(2,1)S(1)} %collective-permute-done.10.refs_1_), channel_id=1, source_target_pairs={{0,2},{1,3},{2,0},{3,1},{4,6},{5,7},{6,4},{7,5},{8,10},{9,11},{10,... | collective-permute-start | bytes 245768 | tf_op jit(solution)/shard_map/ppermute | solution.py:221
  28.2 0.8 %collective-permute-done.11.refs_2_ = s16[32,1280]{1,0:T(8,128)(2,1)S(1)} collective-permute-done((s16[32,1280]{1,0:T(8,128)(2,1)S(1)}, s16[32,1280]{1,0:T(8,128)(2,1)S(1)}, u32[]{:S(2)}, u32[]{:S(2)}) %collective-permute-start.11) | collective-permute-done | bytes 81952 | tf_op jit(solution)/shard_map/ppermute | solution.py:225
  29.0 0.0 collective-permute-start.15
  29.0 2.4 %collective-permute-done.12.refs_3_ = s16[32,1280]{1,0:T(8,128)(2,1)S(1)} collective-permute-done((s16[32,1280]{1,0:T(8,128)(2,1)S(1)}, s16[32,1280]{1,0:T(8,128)(2,1)S(1)}, u32[]{:S(2)}, u32[]{:S(2)}) %collective-permute-start.12) | collective-permute-done | bytes 81952 | tf_op jit(solution)/shard_map/ppermute | solution.py:225
  31.4 0.0 collective-permute-start.16
  31.4 0.0 collective-permute-done.13.refs_4_
  31.4 0.0 collective-permute-done.14.refs_5_
  31.4 0.0 collective-permute-done.15.refs_6_
  31.4 1.3 %collective-permute-done.16.refs_7_ = s16[32,1280]{1,0:T(8,128)(2,1)S(1)} collective-permute-done((s16[32,1280]{1,0:T(8,128)(2,1)S(1)}, s16[32,1280]{1,0:T(8,128)(2,1)S(1)}, u32[]{:S(2)}, u32[]{:S(2)}) %collective-permute-start.16) | collective-permute-done | bytes 81952 | tf_op jit(solution)/shard_map/ppermute | solution.py:221
  32.7 0.0 copy-done.1
  32.7 0.0 copy-done.2
  32.7 0.9 %final.1 = (f32[1,16]{1,0:T(1,128)}, f32[16,1152]{1,0:T(8,128)}, f32[16,1152]{1,0:T(8,128)}) custom-call(bf16[16,1152]{1,0:T(8,128)(2,1)S(1)} %copy-done.1, bf16[16,1152]{1,0:T(8,128)(2,1)S(1)} %copy-done.2, s16[32,1280]{1,0:T(8,128)(2,1)S(1)} %get-tuple-element.10.refs_0_, s16[32,1280]{1,0:T(8,128)(2,1)S(1)} %collective-permute-done.10.refs_1_, ...), custom_call_target="tpu_custom_call" | custom-call | tf_op jit(solution)/shard_map/final/pallas_call | solution.py:247
Async XLA Ops:
  0.6 5.7 %collective-permute-start = (bf16[16,1152]{1,0:T(8,128)(2,1)}, bf16[16,1152]{1,0:T(8,128)(2,1)S(1)}, u32[]{:S(2)}, u32[]{:S(2)}) collective-permute-start(bf16[16,1152]{1,0:T(8,128)(2,1)} %image_ref.3), channel_id=1, source_target_pairs={{2,0},{3,1},{6,4},{7,5},{10,8},{11,9},{14,12},{15,13},{18,16},{19,... | collective-permute-start | bytes 110600 | tf_op jit(solution)/shard_map/ppermute | solution.py:221
  1.9 4.4 %collective-permute-start.1 = (bf16[16,1152]{1,0:T(8,128)(2,1)}, bf16[16,1152]{1,0:T(8,128)(2,1)S(1)}, u32[]{:S(2)}, u32[]{:S(2)}) collective-permute-start(bf16[16,1152]{1,0:T(8,128)(2,1)} %text_ref.3), channel_id=1, source_target_pairs={{0,2},{1,3},{4,6},{5,7},{8,10},{9,11},{12,14},{13,15},{16,18},{17,... | collective-permute-start | bytes 110600 | tf_op jit(solution)/shard_map/ppermute | solution.py:221
  5.0 1.3 %collective-permute-start.2 = (s32[16]{0:T(128)}, s32[16]{0:T(128)S(1)}, u32[]{:S(2)}, u32[]{:S(2)}) collective-permute-start(s32[16]{0:T(128)} %class_ref.1), channel_id=1, source_target_pairs={{0,2},{1,3},{2,0},{3,1},{4,6},{5,7},{6,4},{7,5},{8,10},{9,11},{10,... | collective-permute-start | bytes 200 | tf_op jit(solution)/shard_map/ppermute | solution.py:221
  6.3 0.5 %copy-start.5 = (s32[16]{0:T(128)}, s32[16]{0:T(128)S(1)}, u32[]{:S(2)}) copy-start(s32[16]{0:T(128)S(1)} %collective-permute-done.2.other_class_ref) | copy-start | bytes 196
  6.3 0.6 %copy-start.3 = (bf16[16,1152]{1,0:T(8,128)(2,1)}, bf16[16,1152]{1,0:T(8,128)(2,1)S(1)}, u32[]{:S(2)}) copy-start(bf16[16,1152]{1,0:T(8,128)(2,1)S(1)} %collective-permute-done.got_image_ref) | copy-start | bytes 110596
  6.9 0.6 %copy-start.4 = (bf16[16,1152]{1,0:T(8,128)(2,1)}, bf16[16,1152]{1,0:T(8,128)(2,1)S(1)}, u32[]{:S(2)}) copy-start(bf16[16,1152]{1,0:T(8,128)(2,1)S(1)} %collective-permute-done.1.got_text_ref) | copy-start | bytes 110596
  9.1 7.8 %collective-permute-start.5 = (bf16[32,1280]{1,0:T(8,128)(2,1)}, bf16[32,1280]{1,0:T(8,128)(2,1)S(1)}, u32[]{:S(2)}, u32[]{:S(2)}) collective-permute-start(bf16[32,1280]{1,0:T(8,128)(2,1)} %pack.1.refs_0_), channel_id=1, source_target_pairs={{0,24},{1,25},{2,7},{3,6},{4,28},{5,29},{6,3},{7,2},{8,16},{9,17},... | collective-permute-start | bytes 245768 | tf_op jit(solution)/shard_map/ppermute | solution.py:225
  14.2 5.6 %collective-permute-start.4 = (bf16[32,1280]{1,0:T(8,128)(2,1)}, bf16[32,1280]{1,0:T(8,128)(2,1)S(1)}, u32[]{:S(2)}, u32[]{:S(2)}) collective-permute-start(bf16[32,1280]{1,0:T(8,128)(2,1)} %pack.1.refs_0_), channel_id=1, source_target_pairs={{0,16},{1,17},{2,6},{3,7},{4,20},{5,21},{6,2},{7,3},{8,24},{9,25},... | collective-permute-start | bytes 245768 | tf_op jit(solution)/shard_map/ppermute | solution.py:225
  14.2 5.6 %collective-permute-start.3 = (bf16[32,1280]{1,0:T(8,128)(2,1)}, bf16[32,1280]{1,0:T(8,128)(2,1)S(1)}, u32[]{:S(2)}, u32[]{:S(2)}) collective-permute-start(bf16[32,1280]{1,0:T(8,128)(2,1)} %pack.1.refs_0_), channel_id=1, source_target_pairs={{0,8},{1,9},{2,3},{3,2},{4,12},{5,13},{6,7},{7,6},{8,0},{9,1},{10,... | collective-permute-start | bytes 245768 | tf_op jit(solution)/shard_map/ppermute | solution.py:225
  14.7 6.8 %collective-permute-start.6 = (bf16[32,1280]{1,0:T(8,128)(2,1)}, bf16[32,1280]{1,0:T(8,128)(2,1)S(1)}, u32[]{:S(2)}, u32[]{:S(2)}) collective-permute-start(bf16[32,1280]{1,0:T(8,128)(2,1)} %pack.1.refs_0_), channel_id=1, source_target_pairs={{0,2},{1,3},{2,0},{3,1},{4,6},{5,7},{6,4},{7,5},{8,10},{9,11},{10,... | collective-permute-start | bytes 245768 | tf_op jit(solution)/shard_map/ppermute | solution.py:221
  16.9 4.6 %collective-permute-start.9 = (bf16[32,1280]{1,0:T(8,128)(2,1)S(1)}, bf16[32,1280]{1,0:T(8,128)(2,1)S(1)}, u32[]{:S(2)}, u32[]{:S(2)}) collective-permute-start(bf16[32,1280]{1,0:T(8,128)(2,1)S(1)} %collective-permute-done.5.refs_3_), channel_id=1, source_target_pairs={{0,2},{1,3},{2,0},{3,1},{4,6},{5,7},{6,4},{7,5},{8,10},{9,11},{10,... | collective-permute-start | bytes 245768 | tf_op jit(solution)/shard_map/ppermute | solution.py:221
  19.7 1.8 %collective-permute-start.8 = (bf16[32,1280]{1,0:T(8,128)(2,1)S(1)}, bf16[32,1280]{1,0:T(8,128)(2,1)S(1)}, u32[]{:S(2)}, u32[]{:S(2)}) collective-permute-start(bf16[32,1280]{1,0:T(8,128)(2,1)S(1)} %collective-permute-done.4.refs_2_), channel_id=1, source_target_pairs={{0,2},{1,3},{2,0},{3,1},{4,6},{5,7},{6,4},{7,5},{8,10},{9,11},{10,... | collective-permute-start | bytes 245768 | tf_op jit(solution)/shard_map/ppermute | solution.py:221
  19.7 1.8 %collective-permute-start.7 = (bf16[32,1280]{1,0:T(8,128)(2,1)S(1)}, bf16[32,1280]{1,0:T(8,128)(2,1)S(1)}, u32[]{:S(2)}, u32[]{:S(2)}) collective-permute-start(bf16[32,1280]{1,0:T(8,128)(2,1)S(1)} %collective-permute-done.3.refs_1_), channel_id=1, source_target_pairs={{0,2},{1,3},{2,0},{3,1},{4,6},{5,7},{6,4},{7,5},{8,10},{9,11},{10,... | collective-permute-start | bytes 245768 | tf_op jit(solution)/shard_map/ppermute | solution.py:221
  21.6 0.9 %copy-start = (bf16[32,1280]{1,0:T(8,128)(2,1)S(1)}, bf16[32,1280]{1,0:T(8,128)(2,1)}, u32[]{:S(2)}) copy-start(bf16[32,1280]{1,0:T(8,128)(2,1)} %pack.1.refs_0_) | copy-start | bytes 245764
  22.5 10.2 %copy-start.1 = (bf16[16,1152]{1,0:T(8,128)(2,1)S(1)}, bf16[16,1152]{1,0:T(8,128)(2,1)}, u32[]{:S(2)}) copy-start(bf16[16,1152]{1,0:T(8,128)(2,1)} %image_ref.3) | copy-start | bytes 110596
  22.5 10.2 %copy-start.2 = (bf16[16,1152]{1,0:T(8,128)(2,1)S(1)}, bf16[16,1152]{1,0:T(8,128)(2,1)}, u32[]{:S(2)}) copy-start(bf16[16,1152]{1,0:T(8,128)(2,1)} %text_ref.3) | copy-start | bytes 110596
  23.2 4.5 %collective-permute-start.10 = (s16[32,1280]{1,0:T(8,128)(2,1)S(1)}, s16[32,1280]{1,0:T(8,128)(2,1)S(1)}, u32[]{:S(2)}, u32[]{:S(2)}) collective-permute-start(s16[32,1280]{1,0:T(8,128)(2,1)S(1)} %get-tuple-element.11), channel_id=1, source_target_pairs={{0,8},{1,9},{2,3},{3,2},{4,12},{5,13},{6,7},{7,6},{8,0},{9,1},{10,... | collective-permute-start | bytes 245768 | tf_op jit(solution)/shard_map/ppermute | solution.py:225
  23.6 5.3 %collective-permute-start.11 = (s16[32,1280]{1,0:T(8,128)(2,1)S(1)}, s16[32,1280]{1,0:T(8,128)(2,1)S(1)}, u32[]{:S(2)}, u32[]{:S(2)}) collective-permute-start(s16[32,1280]{1,0:T(8,128)(2,1)S(1)} %get-tuple-element.12), channel_id=1, source_target_pairs={{0,16},{1,17},{2,6},{3,7},{4,20},{5,21},{6,2},{7,3},{8,24},{9,25},... | collective-permute-start | bytes 245768 | tf_op jit(solution)/shard_map/ppermute | solution.py:225
  25.1 6.3 %collective-permute-start.12 = (s16[32,1280]{1,0:T(8,128)(2,1)S(1)}, s16[32,1280]{1,0:T(8,128)(2,1)S(1)}, u32[]{:S(2)}, u32[]{:S(2)}) collective-permute-start(s16[32,1280]{1,0:T(8,128)(2,1)S(1)} %get-tuple-element.13), channel_id=1, source_target_pairs={{0,24},{1,25},{2,7},{3,6},{4,28},{5,29},{6,3},{7,2},{8,16},{9,17},... | collective-permute-start | bytes 245768 | tf_op jit(solution)/shard_map/ppermute | solution.py:225
  27.7 3.7 %collective-permute-start.13 = (s16[32,1280]{1,0:T(8,128)(2,1)S(1)}, s16[32,1280]{1,0:T(8,128)(2,1)S(1)}, u32[]{:S(2)}, u32[]{:S(2)}) collective-permute-start(s16[32,1280]{1,0:T(8,128)(2,1)S(1)} %get-tuple-element.10.refs_0_), channel_id=1, source_target_pairs={{0,2},{1,3},{2,0},{3,1},{4,6},{5,7},{6,4},{7,5},{8,10},{9,11},{10,... | collective-permute-start | bytes 245768 | tf_op jit(solution)/shard_map/ppermute | solution.py:221
  27.7 3.7 %collective-permute-start.14 = (s16[32,1280]{1,0:T(8,128)(2,1)S(1)}, s16[32,1280]{1,0:T(8,128)(2,1)S(1)}, u32[]{:S(2)}, u32[]{:S(2)}) collective-permute-start(s16[32,1280]{1,0:T(8,128)(2,1)S(1)} %collective-permute-done.10.refs_1_), channel_id=1, source_target_pairs={{0,2},{1,3},{2,0},{3,1},{4,6},{5,7},{6,4},{7,5},{8,10},{9,11},{10,... | collective-permute-start | bytes 245768 | tf_op jit(solution)/shard_map/ppermute | solution.py:221
  29.0 2.5 %collective-permute-start.15 = (s16[32,1280]{1,0:T(8,128)(2,1)S(1)}, s16[32,1280]{1,0:T(8,128)(2,1)S(1)}, u32[]{:S(2)}, u32[]{:S(2)}) collective-permute-start(s16[32,1280]{1,0:T(8,128)(2,1)S(1)} %collective-permute-done.11.refs_2_), channel_id=1, source_target_pairs={{0,2},{1,3},{2,0},{3,1},{4,6},{5,7},{6,4},{7,5},{8,10},{9,11},{10,... | collective-permute-start | bytes 245768 | tf_op jit(solution)/shard_map/ppermute | solution.py:221
  31.4 1.3 %collective-permute-start.16 = (s16[32,1280]{1,0:T(8,128)(2,1)S(1)}, s16[32,1280]{1,0:T(8,128)(2,1)S(1)}, u32[]{:S(2)}, u32[]{:S(2)}) collective-permute-start(s16[32,1280]{1,0:T(8,128)(2,1)S(1)} %collective-permute-done.12.refs_3_), channel_id=1, source_target_pairs={{0,2},{1,3},{2,0},{3,1},{4,6},{5,7},{6,4},{7,5},{8,10},{9,11},{10,... | collective-permute-start | bytes 245768 | tf_op jit(solution)/shard_map/ppermute | solution.py:221

commit v6 on v5

--- a/solution.py
+++ b/solution.py
@@ -78,22 +78,31 @@
     return lax.rem(lax.axis_index("img"), 2) == 0
 
 
-def pack_kernel(image_ref, text_ref, got_image_ref, got_text_ref, class_ref, other_class_ref, out_ref):
+def pack_kernel(image_ref, text_ref, class_ref, out_ref):
     rows, depth = image_ref.shape
-    first = on_first_core()
-    own = jnp.where(first, image_ref[...].astype(jnp.float32), text_ref[...].astype(jnp.float32))
-    got = got_image_ref[...].astype(jnp.float32) + got_text_ref[...].astype(jnp.float32)
-    row = lax.broadcasted_iota(jnp.int32, (2 * rows, LANES), 0)
-    lane = lax.broadcasted_iota(jnp.int32, (2 * rows, LANES), 1)
-    spread = jnp.zeros((2 * rows, LANES), jnp.int32)
+    row = lax.broadcasted_iota(jnp.int32, (rows, LANES), 0)
+    lane = lax.broadcasted_iota(jnp.int32, (rows, LANES), 1)
+    spread = jnp.zeros((rows, LANES), jnp.int32)
     for i in range(rows):
-        spread = jnp.where(row == i, jnp.where(first, class_ref[i], other_class_ref[i]), spread)
-        spread = jnp.where(row == rows + i, jnp.where(first, other_class_ref[i], class_ref[i]), spread)
+        spread = jnp.where(row == i, class_ref[i], spread)
     digit = lax.shift_right_logical(spread, 8 * jnp.minimum(lane, DIGITS - 1)) & 255
     digit = jnp.where(lane < DIGITS, digit, 0).astype(jnp.float32).astype(jnp.bfloat16)
-    out_ref[:rows, :depth] = unit_rows(jnp.where(first, own, got))[0].astype(jnp.bfloat16)
-    out_ref[rows:, :depth] = unit_rows(jnp.where(first, got, own))[0].astype(jnp.bfloat16)
-    out_ref[:, depth:] = digit
+    for start, source in ((0, image_ref), (rows, text_ref)):
+        out_ref[start : start + rows, :depth] = unit_rows(source[...])[0].astype(jnp.bfloat16)
+        out_ref[start : start + rows, depth:] = digit
+
+
+def join_kernel(scale_ref, shift_ref, own_ref, got_ref, lines_ref, columns_ref, pair_ref):
+    first = on_first_core()
+    rows = own_ref.shape[0] // 2
+    own, got = own_ref[...].astype(jnp.float32), got_ref[...].astype(jnp.float32)
+    low, high = jnp.where(first, own, got), jnp.where(first, got, own)
+    images = jnp.concatenate([low[:rows], high[:rows]], axis=0)
+    texts = jnp.concatenate([low[rows:], high[rows:]], axis=0)
+    lines_ref[...] = jnp.where(first, images, texts).astype(jnp.bfloat16)
+    columns_ref[...] = jnp.where(first, texts, images).astype(jnp.bfloat16)
+    row = lax.broadcasted_iota(jnp.int32, pair_ref.shape, 0)
+    pair_ref[...] = jnp.where(row == 0, scale_ref[0], shift_ref[0])
 
 
 def power_above(size):
@@ -126,9 +135,9 @@
         out[:, depth:] = tail[k * rows : (k + 1) * rows]
 
 
-def tile_kernel(count, scale_ref, shift_ref, *refs):
+def tile_kernel(count, pair_ref, *refs):
     depth = refs[0].shape[1] - LANES
-    scale, shift = scale_ref[0], shift_ref[0]
+    scale, shift = pair_ref[0:1, 0:1], pair_ref[1:2, 0:1]
     lines = jnp.concatenate([ref[...] for ref in refs[:count]], axis=0)
     columns = jnp.concatenate([ref[...] for ref in refs[count : 2 * count]], axis=0)
     logits = (
@@ -216,34 +225,38 @@
         chip ^= k if core(i) else k * count
         return (chip // lanes * 2 + core(i)) * lanes + chip % lanes
 
-    def swap(x, senders=(0, 1)):
-        pairs = [(i, i ^ lanes) for i in range(n) if core(i) in senders]
-        return lax.ppermute(x, AXES, pairs)
-
-    def visit(blocks):
-        return [
-            lax.ppermute(x, AXES, [(i, partner(i, k)) for i in range(n)])
-            for k, x in zip(range(1, count), blocks)
-        ]
-
-    mine = pl.pallas_call(
+    def swap(x):
+        return lax.ppermute(x, AXES, [(i, i ^ lanes) for i in range(n)])
+
+    def visit(x, k):
+        return lax.ppermute(x, AXES, [(i, partner(i, k)) for i in range(n)])
+
+    block = jax.ShapeDtypeStruct((2 * rows, width), jnp.bfloat16)
+    own = pl.pallas_call(
         pack_kernel,
-        out_shape=jax.ShapeDtypeStruct((2 * rows, width), jnp.bfloat16),
-        in_specs=[vmem] * 4 + [smem, smem],
+        out_shape=block,
+        in_specs=[vmem, vmem, smem],
         out_specs=vmem,
         name="pack",
-    )(image_emb, text_emb, swap(image_emb, (1,)), swap(text_emb, (0,)), pair_class, swap(pair_class))
-    lines = [mine] + visit([mine] * (count - 1))
-    columns = [swap(x) for x in lines]
+    )(image_emb, text_emb, pair_class)
+    lines, columns, pair = pl.pallas_call(
+        join_kernel,
+        out_shape=(block, block, jax.ShapeDtypeStruct((8, LANES), jnp.float32)),
+        in_specs=[smem, smem, vmem, vmem],
+        out_specs=(vmem, vmem, vmem),
+        compiler_params=params,
+        name="join",
+    )(scale[None], shift[None], own, swap(own))
+    got = [visit(lines, k) for k in range(1, count)]
     parts = pl.pallas_call(
         functools.partial(tile_kernel, count),
         out_shape=(jax.ShapeDtypeStruct((2 * rows, width), jnp.int16),) * count,
-        in_specs=[smem, smem] + [vmem] * (2 * count),
+        in_specs=[vmem] * (1 + 2 * count),
         out_specs=(vmem,) * count,
         compiler_params=params,
         name="tile",
-    )(scale[None], shift[None], *lines, *columns)
-    parts = [parts[0]] + visit(parts[1:])
+    )(pair, *got[::-1], lines, *[swap(x) for x in got[::-1]], columns)
+    parts = [visit(x, k) for x, k in zip(parts, range(count - 1, 0, -1))] + [parts[-1]]
     loss, grad_image, grad_text = pl.pallas_call(
         functools.partial(final_kernel, count),
         out_shape=(

time: 33.9 us -> 29.2 us (0.86)
  starting transfers between devices: 15.4 us -> 10.8 us
  local copies, waits for them, and re-layouts: 2.11 us -> 0.89 us
  waiting for transfers between devices: 10.8 us -> 12 us
    ppermute x17 -> x14, starting transfers between devices: 15.4 us -> 10.8 us  [the longest x6 9.86 us: visit(): return lax.ppermute(x, AXES, [(i, partner(i, k)) for i in range(n)])]
    ppermute x17 -> x14, waiting for transfers between devices: 10.8 us -> 12 us  [the longest x6 9.82 us: visit(): return lax.ppermute(x, AXES, [(i, partner(i, k)) for i in range(n)])]
    unnamed x12 -> x6, local copies, waits for them, and re-layouts: 2.11 us -> 0.89 us
    pallas_call x1 -> x2, Pallas kernels: 1.59 us -> 1.6 us  [the longest x1 1.54 us: chip_plan(): pl.pallas_call(pack_kernel, out_shape=block, in_specs=[vmem, vmem, smem],...]
  transfers between devices with their start and end apart: 17 -> 14, of which waited for: 6 -> 7; matrix products, arithmetic and copies ran while one was open for 0% -> 0% of each run, Pallas kernels for 0% -> 0%
where the time goes in v6:
time: 29.2 us; the launch traced here: 29 us
  waiting for transfers between devices  12 us (41%)
  starting transfers between devices  10.8 us (37%)
  Pallas kernels  3.24 us (11%)
  between operations  1.99 us (7%)
  local copies, waits for them, and re-layouts  0.89 us (3%)
    ppermute x6, starting transfers between devices, visit(): return lax.ppermute(x, AXES, [(i, partner(i, k)) for i in range(n)])  9.86 us
    ppermute x6, waiting for transfers between devices, visit(): return lax.ppermute(x, AXES, [(i, partner(i, k)) for i in range(n)])  9.82 us
    ppermute x8, waiting for transfers between devices, swap(): return lax.ppermute(x, AXES, [(i, i ^ lanes) for i in range(n)])  2.19 us
    pallas_call x1, Pallas kernels, chip_plan(): pl.pallas_call(pack_kernel, out_shape=block, in_specs=[vmem, vmem, smem],...  1.54 us
    ppermute x8, starting transfers between devices, swap(): return lax.ppermute(x, AXES, [(i, i ^ lanes) for i in range(n)])  0.98 us
    pallas_call x1, Pallas kernels, chip_plan(): pl.pallas_call(functools.partial(final_kernel, count), out_shape=(jax.Sha...  0.91 us
    unnamed x6, local copies, waits for them, and re-layouts  0.89 us
    pallas_call x1, Pallas kernels, chip_plan(): pl.pallas_call(functools.partial(tile_kernel, count), out_shape=(jax.Shap...  0.74 us
  transfers between devices with their start and end apart: 14, of which 7 were waited for; matrix products, arithmetic and copies ran while one was open for 0% of the time, Pallas kernels for 0%

profile of v6, /device:TPU:0, one launch (start us, length us, event | category | flops | bytes accessed | tf_op | source)
XLA Modules:
  0.0 29.0 jit_solution(431076710173690449)
XLA Ops:
  0.6 1.5 %pack.1.own_ref = bf16[32,1280]{1,0:T(8,128)(2,1)} custom-call(bf16[16,1152]{1,0:T(8,128)(2,1)} %image_ref.3, bf16[16,1152]{1,0:T(8,128)(2,1)} %text_ref.3, s32[16]{0:T(128)} %class_ref.1), custom_call_target="tpu_custom_call" | custom-call | tf_op jit(solution)/shard_map/pack/pallas_call | solution.py:235
  2.2 0.5 %collective-permute-start = (bf16[32,1280]{1,0:T(8,128)(2,1)}, bf16[32,1280]{1,0:T(8,128)(2,1)S(1)}, u32[]{:S(2)}, u32[]{:S(2)}) collective-permute-start(bf16[32,1280]{1,0:T(8,128)(2,1)} %pack.1.own_ref), channel_id=1, source_target_pairs={{0,2},{1,3},{2,0},{3,1},{4,6},{5,7},{6,4},{7,5},{8,10},{9,11},{10,... | collective-permute-start | bytes 245768 | tf_op jit(solution)/shard_map/ppermute | solution.py:229
  3.9 0.0 collective-permute-done.got_ref
  3.9 0.0 copy-start
  3.9 0.9 %copy-done = bf16[32,1280]{1,0:T(8,128)(2,1)S(1)} copy-done((bf16[32,1280]{1,0:T(8,128)(2,1)S(1)}, bf16[32,1280]{1,0:T(8,128)(2,1)}, u32[]{:S(2)}) %copy-start) | copy-done | bytes 81944
  4.8 0.1 join.1
  4.9 2.8 %collective-permute-start.3 = (bf16[32,1280]{1,0:T(8,128)(2,1)S(1)}, bf16[32,1280]{1,0:T(8,128)(2,1)S(1)}, u32[]{:S(2)}, u32[]{:S(2)}) collective-permute-start(bf16[32,1280]{1,0:T(8,128)(2,1)S(1)} %get-tuple-element.14.refs_3_), channel_id=1, source_target_pairs={{0,8},{1,9},{2,3},{3,2},{4,12},{5,13},{6,7},{7,6},{8,0},{9,1},{10,... | collective-permute-start | bytes 245768 | tf_op jit(solution)/shard_map/ppermute | solution.py:232
  7.7 2.6 %collective-permute-start.2 = (bf16[32,1280]{1,0:T(8,128)(2,1)S(1)}, bf16[32,1280]{1,0:T(8,128)(2,1)S(1)}, u32[]{:S(2)}, u32[]{:S(2)}) collective-permute-start(bf16[32,1280]{1,0:T(8,128)(2,1)S(1)} %get-tuple-element.14.refs_3_), channel_id=1, source_target_pairs={{0,16},{1,17},{2,6},{3,7},{4,20},{5,21},{6,2},{7,3},{8,24},{9,25},... | collective-permute-start | bytes 245768 | tf_op jit(solution)/shard_map/ppermute | solution.py:232
  10.3 0.0 collective-permute-start.1
  10.3 0.0 collective-permute-done.3.refs_2_
  10.3 0.0 collective-permute-start.6
  10.3 3.6 %collective-permute-done.2.refs_1_ = bf16[32,1280]{1,0:T(8,128)(2,1)S(1)} collective-permute-done((bf16[32,1280]{1,0:T(8,128)(2,1)S(1)}, bf16[32,1280]{1,0:T(8,128)(2,1)S(1)}, u32[]{:S(2)}, u32[]{:S(2)}) %collective-permute-start.2) | collective-permute-done | bytes 81952 | tf_op jit(solution)/shard_map/ppermute | solution.py:232
  13.9 0.0 collective-permute-start.5
  13.9 2.6 %collective-permute-done.1.refs_0_ = bf16[32,1280]{1,0:T(8,128)(2,1)S(1)} collective-permute-done((bf16[32,1280]{1,0:T(8,128)(2,1)S(1)}, bf16[32,1280]{1,0:T(8,128)(2,1)S(1)}, u32[]{:S(2)}, u32[]{:S(2)}) %collective-permute-start.1) | collective-permute-done | bytes 81952 | tf_op jit(solution)/shard_map/ppermute | solution.py:232
  16.5 0.0 collective-permute-start.4
  16.5 0.0 collective-permute-done.6.refs_6_
  16.5 0.0 collective-permute-done.5.refs_5_
  16.5 1.3 %collective-permute-done.4.refs_4_ = bf16[32,1280]{1,0:T(8,128)(2,1)S(1)} collective-permute-done((bf16[32,1280]{1,0:T(8,128)(2,1)S(1)}, bf16[32,1280]{1,0:T(8,128)(2,1)S(1)}, u32[]{:S(2)}, u32[]{:S(2)}) %collective-permute-start.4) | collective-permute-done | bytes 81952 | tf_op jit(solution)/shard_map/ppermute | solution.py:229
  17.8 0.0 copy-start.1
  17.8 0.0 copy-start.2
  17.8 0.7 %tile.1 = (s16[32,1280]{1,0:T(8,128)(2,1)S(1)}, s16[32,1280]{1,0:T(8,128)(2,1)S(1)}, s16[32,1280]{1,0:T(8,128)(2,1)S(1)}, s16[32,1280]{1,0:T(8,128)(2,1)S(1)}) custom-call(f32[8,128]{1,0:T(8,128)S(1)} %get-tuple-element.13.pair_ref, bf16[32,1280]{1,0:T(8,128)(2,1)S(1)} %collective-permute-done.1.refs_0_, ...), custom_call_target="tpu_custom_call" | custom-call | tf_op jit(solution)/shard_map/tile/pallas_call | solution.py:251
  18.6 1.0 %collective-permute-start.7 = (s16[32,1280]{1,0:T(8,128)(2,1)S(1)}, s16[32,1280]{1,0:T(8,128)(2,1)S(1)}, u32[]{:S(2)}, u32[]{:S(2)}) collective-permute-start(s16[32,1280]{1,0:T(8,128)(2,1)S(1)} %get-tuple-element.16), channel_id=1, source_target_pairs={{0,24},{1,25},{2,7},{3,6},{4,28},{5,29},{6,3},{7,2},{8,16},{9,17},... | collective-permute-start | bytes 245768 | tf_op jit(solution)/shard_map/ppermute | solution.py:232
  19.6 0.0 collective-permute-start.8
  19.6 3.4 %collective-permute-start.9 = (s16[32,1280]{1,0:T(8,128)(2,1)S(1)}, s16[32,1280]{1,0:T(8,128)(2,1)S(1)}, u32[]{:S(2)}, u32[]{:S(2)}) collective-permute-start(s16[32,1280]{1,0:T(8,128)(2,1)S(1)} %get-tuple-element.18), channel_id=1, source_target_pairs={{0,8},{1,9},{2,3},{3,2},{4,12},{5,13},{6,7},{7,6},{8,0},{9,1},{10,... | collective-permute-start | bytes 245768 | tf_op jit(solution)/shard_map/ppermute | solution.py:232
  23.0 0.0 collective-permute-start.13
  23.0 2.0 %collective-permute-done.7.refs_0_ = s16[32,1280]{1,0:T(8,128)(2,1)S(1)} collective-permute-done((s16[32,1280]{1,0:T(8,128)(2,1)S(1)}, s16[32,1280]{1,0:T(8,128)(2,1)S(1)}, u32[]{:S(2)}, u32[]{:S(2)}) %collective-permute-start.7) | collective-permute-done | bytes 81952 | tf_op jit(solution)/shard_map/ppermute | solution.py:232
  25.0 0.0 collective-permute-start.10
  25.0 1.6 %collective-permute-done.8.refs_1_ = s16[32,1280]{1,0:T(8,128)(2,1)S(1)} collective-permute-done((s16[32,1280]{1,0:T(8,128)(2,1)S(1)}, s16[32,1280]{1,0:T(8,128)(2,1)S(1)}, u32[]{:S(2)}, u32[]{:S(2)}) %collective-permute-start.8) | collective-permute-done | bytes 81952 | tf_op jit(solution)/shard_map/ppermute | solution.py:232
  26.6 0.0 collective-permute-start.11
  26.6 0.0 collective-permute-done.9.refs_2_
  26.6 0.5 %collective-permute-start.12 = (s16[32,1280]{1,0:T(8,128)(2,1)S(1)}, s16[32,1280]{1,0:T(8,128)(2,1)S(1)}, u32[]{:S(2)}, u32[]{:S(2)}) collective-permute-start(s16[32,1280]{1,0:T(8,128)(2,1)S(1)} %collective-permute-done.9.refs_2_), channel_id=1, source_target_pairs={{0,2},{1,3},{2,0},{3,1},{4,6},{5,7},{6,4},{7,5},{8,10},{9,11},{10,... | collective-permute-start | bytes 245768 | tf_op jit(solution)/shard_map/ppermute | solution.py:229
  27.1 0.0 collective-permute-done.13.refs_7_
  27.1 0.0 collective-permute-done.10.refs_4_
  27.1 0.8 %collective-permute-done.11.refs_5_ = s16[32,1280]{1,0:T(8,128)(2,1)S(1)} collective-permute-done((s16[32,1280]{1,0:T(8,128)(2,1)S(1)}, s16[32,1280]{1,0:T(8,128)(2,1)S(1)}, u32[]{:S(2)}, u32[]{:S(2)}) %collective-permute-start.11) | collective-permute-done | bytes 81952 | tf_op jit(solution)/shard_map/ppermute | solution.py:229
  27.9 0.2 collective-permute-done.12.refs_6_
  28.1 0.0 copy-done.1
  28.1 0.0 copy-done.2
  28.1 0.9 %final.1 = (f32[1,16]{1,0:T(1,128)}, f32[16,1152]{1,0:T(8,128)}, f32[16,1152]{1,0:T(8,128)}) custom-call(bf16[16,1152]{1,0:T(8,128)(2,1)S(1)} %copy-done.1, bf16[16,1152]{1,0:T(8,128)(2,1)S(1)} %copy-done.2, s16[32,1280]{1,0:T(8,128)(2,1)S(1)} %collective-permute-done.7.refs_0_, s16[32,1280]{1,0:T(8,128)(2,1)S(1)} %collective-permute-done.8.refs_1_, ...), custom_call_target="tpu_custom_call" | custom-call | tf_op jit(solution)/shard_map/final/pallas_call | solution.py:260
Async XLA Ops:
  2.2 1.8 %collective-permute-start = (bf16[32,1280]{1,0:T(8,128)(2,1)}, bf16[32,1280]{1,0:T(8,128)(2,1)S(1)}, u32[]{:S(2)}, u32[]{:S(2)}) collective-permute-start(bf16[32,1280]{1,0:T(8,128)(2,1)} %pack.1.own_ref), channel_id=1, source_target_pairs={{0,2},{1,3},{2,0},{3,1},{4,6},{5,7},{6,4},{7,5},{8,10},{9,11},{10,... | collective-permute-start | bytes 245768 | tf_op jit(solution)/shard_map/ppermute | solution.py:229
  3.9 0.9 %copy-start = (bf16[32,1280]{1,0:T(8,128)(2,1)S(1)}, bf16[32,1280]{1,0:T(8,128)(2,1)}, u32[]{:S(2)}) copy-start(bf16[32,1280]{1,0:T(8,128)(2,1)} %pack.1.own_ref) | copy-start | bytes 245764
  4.9 5.4 %collective-permute-start.3 = (bf16[32,1280]{1,0:T(8,128)(2,1)S(1)}, bf16[32,1280]{1,0:T(8,128)(2,1)S(1)}, u32[]{:S(2)}, u32[]{:S(2)}) collective-permute-start(bf16[32,1280]{1,0:T(8,128)(2,1)S(1)} %get-tuple-element.14.refs_3_), channel_id=1, source_target_pairs={{0,8},{1,9},{2,3},{3,2},{4,12},{5,13},{6,7},{7,6},{8,0},{9,1},{10,... | collective-permute-start | bytes 245768 | tf_op jit(solution)/shard_map/ppermute | solution.py:232
  7.7 6.2 %collective-permute-start.2 = (bf16[32,1280]{1,0:T(8,128)(2,1)S(1)}, bf16[32,1280]{1,0:T(8,128)(2,1)S(1)}, u32[]{:S(2)}, u32[]{:S(2)}) collective-permute-start(bf16[32,1280]{1,0:T(8,128)(2,1)S(1)} %get-tuple-element.14.refs_3_), channel_id=1, source_target_pairs={{0,16},{1,17},{2,6},{3,7},{4,20},{5,21},{6,2},{7,3},{8,24},{9,25},... | collective-permute-start | bytes 245768 | tf_op jit(solution)/shard_map/ppermute | solution.py:232
  10.3 6.2 %collective-permute-start.1 = (bf16[32,1280]{1,0:T(8,128)(2,1)S(1)}, bf16[32,1280]{1,0:T(8,128)(2,1)S(1)}, u32[]{:S(2)}, u32[]{:S(2)}) collective-permute-start(bf16[32,1280]{1,0:T(8,128)(2,1)S(1)} %get-tuple-element.14.refs_3_), channel_id=1, source_target_pairs={{0,24},{1,25},{2,7},{3,6},{4,28},{5,29},{6,3},{7,2},{8,16},{9,17},... | collective-permute-start | bytes 245768 | tf_op jit(solution)/shard_map/ppermute | solution.py:232
  10.3 6.2 %collective-permute-start.6 = (bf16[32,1280]{1,0:T(8,128)(2,1)S(1)}, bf16[32,1280]{1,0:T(8,128)(2,1)S(1)}, u32[]{:S(2)}, u32[]{:S(2)}) collective-permute-start(bf16[32,1280]{1,0:T(8,128)(2,1)S(1)} %collective-permute-done.3.refs_2_), channel_id=1, source_target_pairs={{0,2},{1,3},{2,0},{3,1},{4,6},{5,7},{6,4},{7,5},{8,10},{9,11},{10,... | collective-permute-start | bytes 245768 | tf_op jit(solution)/shard_map/ppermute | solution.py:229
  13.9 2.6 %collective-permute-start.5 = (bf16[32,1280]{1,0:T(8,128)(2,1)S(1)}, bf16[32,1280]{1,0:T(8,128)(2,1)S(1)}, u32[]{:S(2)}, u32[]{:S(2)}) collective-permute-start(bf16[32,1280]{1,0:T(8,128)(2,1)S(1)} %collective-permute-done.2.refs_1_), channel_id=1, source_target_pairs={{0,2},{1,3},{2,0},{3,1},{4,6},{5,7},{6,4},{7,5},{8,10},{9,11},{10,... | collective-permute-start | bytes 245768 | tf_op jit(solution)/shard_map/ppermute | solution.py:229
  16.5 1.3 %collective-permute-start.4 = (bf16[32,1280]{1,0:T(8,128)(2,1)S(1)}, bf16[32,1280]{1,0:T(8,128)(2,1)S(1)}, u32[]{:S(2)}, u32[]{:S(2)}) collective-permute-start(bf16[32,1280]{1,0:T(8,128)(2,1)S(1)} %collective-permute-done.1.refs_0_), channel_id=1, source_target_pairs={{0,2},{1,3},{2,0},{3,1},{4,6},{5,7},{6,4},{7,5},{8,10},{9,11},{10,... | collective-permute-start | bytes 245768 | tf_op jit(solution)/shard_map/ppermute | solution.py:229
  17.8 10.2 %copy-start.1 = (bf16[16,1152]{1,0:T(8,128)(2,1)S(1)}, bf16[16,1152]{1,0:T(8,128)(2,1)}, u32[]{:S(2)}) copy-start(bf16[16,1152]{1,0:T(8,128)(2,1)} %image_ref.3) | copy-start | bytes 110596
  17.8 10.2 %copy-start.2 = (bf16[16,1152]{1,0:T(8,128)(2,1)S(1)}, bf16[16,1152]{1,0:T(8,128)(2,1)}, u32[]{:S(2)}) copy-start(bf16[16,1152]{1,0:T(8,128)(2,1)} %text_ref.3) | copy-start | bytes 110596
  18.6 6.4 %collective-permute-start.7 = (s16[32,1280]{1,0:T(8,128)(2,1)S(1)}, s16[32,1280]{1,0:T(8,128)(2,1)S(1)}, u32[]{:S(2)}, u32[]{:S(2)}) collective-permute-start(s16[32,1280]{1,0:T(8,128)(2,1)S(1)} %get-tuple-element.16), channel_id=1, source_target_pairs={{0,24},{1,25},{2,7},{3,6},{4,28},{5,29},{6,3},{7,2},{8,16},{9,17},... | collective-permute-start | bytes 245768 | tf_op jit(solution)/shard_map/ppermute | solution.py:232
  19.6 7.0 %collective-permute-start.8 = (s16[32,1280]{1,0:T(8,128)(2,1)S(1)}, s16[32,1280]{1,0:T(8,128)(2,1)S(1)}, u32[]{:S(2)}, u32[]{:S(2)}) collective-permute-start(s16[32,1280]{1,0:T(8,128)(2,1)S(1)} %get-tuple-element.17), channel_id=1, source_target_pairs={{0,16},{1,17},{2,6},{3,7},{4,20},{5,21},{6,2},{7,3},{8,24},{9,25},... | collective-permute-start | bytes 245768 | tf_op jit(solution)/shard_map/ppermute | solution.py:232
  19.6 7.0 %collective-permute-start.9 = (s16[32,1280]{1,0:T(8,128)(2,1)S(1)}, s16[32,1280]{1,0:T(8,128)(2,1)S(1)}, u32[]{:S(2)}, u32[]{:S(2)}) collective-permute-start(s16[32,1280]{1,0:T(8,128)(2,1)S(1)} %get-tuple-element.18), channel_id=1, source_target_pairs={{0,8},{1,9},{2,3},{3,2},{4,12},{5,13},{6,7},{7,6},{8,0},{9,1},{10,... | collective-permute-start | bytes 245768 | tf_op jit(solution)/shard_map/ppermute | solution.py:232
  23.0 4.1 %collective-permute-start.13 = (s16[32,1280]{1,0:T(8,128)(2,1)S(1)}, s16[32,1280]{1,0:T(8,128)(2,1)S(1)}, u32[]{:S(2)}, u32[]{:S(2)}) collective-permute-start(s16[32,1280]{1,0:T(8,128)(2,1)S(1)} %get-tuple-element.19.refs_3_), channel_id=1, source_target_pairs={{0,2},{1,3},{2,0},{3,1},{4,6},{5,7},{6,4},{7,5},{8,10},{9,11},{10,... | collective-permute-start | bytes 245768 | tf_op jit(solution)/shard_map/ppermute | solution.py:229
  25.0 2.2 %collective-permute-start.10 = (s16[32,1280]{1,0:T(8,128)(2,1)S(1)}, s16[32,1280]{1,0:T(8,128)(2,1)S(1)}, u32[]{:S(2)}, u32[]{:S(2)}) collective-permute-start(s16[32,1280]{1,0:T(8,128)(2,1)S(1)} %collective-permute-done.7.refs_0_), channel_id=1, source_target_pairs={{0,2},{1,3},{2,0},{3,1},{4,6},{5,7},{6,4},{7,5},{8,10},{9,11},{10,... | collective-permute-start | bytes 245768 | tf_op jit(solution)/shard_map/ppermute | solution.py:229
  26.6 1.3 %collective-permute-start.11 = (s16[32,1280]{1,0:T(8,128)(2,1)S(1)}, s16[32,1280]{1,0:T(8,128)(2,1)S(1)}, u32[]{:S(2)}, u32[]{:S(2)}) collective-permute-start(s16[32,1280]{1,0:T(8,128)(2,1)S(1)} %collective-permute-done.8.refs_1_), channel_id=1, source_target_pairs={{0,2},{1,3},{2,0},{3,1},{4,6},{5,7},{6,4},{7,5},{8,10},{9,11},{10,... | collective-permute-start | bytes 245768 | tf_op jit(solution)/shard_map/ppermute | solution.py:229
  26.6 1.4 %collective-permute-start.12 = (s16[32,1280]{1,0:T(8,128)(2,1)S(1)}, s16[32,1280]{1,0:T(8,128)(2,1)S(1)}, u32[]{:S(2)}, u32[]{:S(2)}) collective-permute-start(s16[32,1280]{1,0:T(8,128)(2,1)S(1)} %collective-permute-done.9.refs_2_), channel_id=1, source_target_pairs={{0,2},{1,3},{2,0},{3,1},{4,6},{5,7},{6,4},{7,5},{8,10},{9,11},{10,... | collective-permute-start | bytes 245768 | tf_op jit(solution)/shard_map/ppermute | solution.py:229

commit v7 on v4

--- a/solution.py
+++ b/solution.py
@@ -24,23 +24,35 @@
     return (pull - unit * inner) * inverse
 
 
-def class_digits(class_ref, rows):
+def pack_kernel(image_ref, text_ref, class_ref, image_out, text_out):
+    rows, depth = image_ref.shape
     row = lax.broadcasted_iota(jnp.int32, (rows, LANES), 0)
     lane = lax.broadcasted_iota(jnp.int32, (rows, LANES), 1)
     spread = jnp.zeros((rows, LANES), jnp.int32)
     for i in range(rows):
         spread = jnp.where(row == i, class_ref[i], spread)
     digit = lax.shift_right_logical(spread, 8 * jnp.minimum(lane, DIGITS - 1)) & 255
-    return jnp.where(lane < DIGITS, digit, 0).astype(jnp.float32).astype(jnp.bfloat16)
-
-
-def pack_kernel(image_ref, text_ref, class_ref, image_out, text_out):
-    rows, depth = image_ref.shape
-    digits = class_digits(class_ref, rows)
+    digit = jnp.where(lane < DIGITS, digit, 0).astype(jnp.float32).astype(jnp.bfloat16)
     for source, out in ((image_ref, image_out), (text_ref, text_out)):
-        half = unit_rows(source[...])[0].astype(jnp.bfloat16)
-        out[:, :depth] = half
-        out[:, depth:] = digits
+        out[:, :depth] = unit_rows(source[...])[0].astype(jnp.bfloat16)
+        out[:, depth:] = digit
+
+
+def put_blocks(out_ref, refs):
+    start = 0
+    for ref in refs:
+        out_ref[start : start + ref.shape[0], :] = ref[...]
+        start += ref.shape[0]
+
+
+def join_kernel(*refs):
+    put_blocks(refs[-1], refs[:-1])
+
+
+def join_with_pair_kernel(scale_ref, shift_ref, *refs):
+    put_blocks(refs[-2], refs[:-2])
+    row = lax.broadcasted_iota(jnp.int32, refs[-1].shape, 0)
+    refs[-1][...] = jnp.where(row == 0, scale_ref[0], shift_ref[0])
 
 
 def power_above(size):
@@ -73,18 +85,13 @@
         out[:, depth:] = tail[k * rows : (k + 1) * rows]
 
 
-def tile_kernel(a, b, scale_ref, shift_ref, *refs):
-    image_refs, text_refs = refs[:a], refs[a : a + b]
-    image_outs, text_outs = refs[a + b : 2 * a + b], refs[2 * a + b :]
-    depth = image_refs[0].shape[1] - LANES
-    scale, shift = scale_ref[0], shift_ref[0]
-    image = jnp.concatenate([ref[...] for ref in image_refs], axis=0)
-    text = jnp.concatenate([ref[...] for ref in text_refs], axis=0)
+def partial_pull(lines, columns, scale, shift):
+    depth = lines.shape[1] - LANES
     logits = (
         scale
         * lax.dot_general(
-            image[:, :depth],
-            text[:, :depth],
+            lines[:, :depth],
+            columns[:, :depth],
             (((1,), (1,)), ((), ())),
             preferred_element_type=jnp.float32,
         )
@@ -94,38 +101,47 @@
         lax.broadcasted_iota(jnp.int32, (8, LANES), 0)
         == lax.broadcasted_iota(jnp.int32, (8, LANES), 1)
     )
-    text_digits = lax.dot_general(
+    column_digits = lax.dot_general(
         pick.astype(jnp.bfloat16),
-        text[:, depth:],
+        columns[:, depth:],
         (((1,), (1,)), ((), ())),
         preferred_element_type=jnp.float32,
     )
-    image_digits = image[:, depth:].astype(jnp.float32)
+    line_digits = lines[:, depth:].astype(jnp.float32)
     same = None
     for k in range(DIGITS):
-        equal = image_digits[:, k : k + 1] == text_digits[k : k + 1, :]
+        equal = line_digits[:, k : k + 1] == column_digits[k : k + 1, :]
         same = equal if same is None else same & equal
     sign = jnp.where(same, 1.0, -1.0).astype(jnp.float32)
     margin = sign * logits
     small = jnp.exp(-jnp.abs(margin))
     over = 1.0 / (1.0 + small)
     coef = -sign * jnp.where(margin >= 0, small * over, over) * scale
-    image_pull = jnp.dot(
-        coef.astype(jnp.bfloat16), text[:, :depth], preferred_element_type=jnp.float32
-    )
-    text_pull = jnp.dot(
-        coef.T.astype(jnp.bfloat16), image[:, :depth], preferred_element_type=jnp.float32
+    pull = jnp.dot(
+        coef.astype(jnp.bfloat16), columns[:, :depth], preferred_element_type=jnp.float32
     )
     loss = jnp.sum(jnp.log1p(small) - jnp.minimum(margin, 0.0), axis=1, keepdims=True)
-    put_rows(image_outs, image_pull, loss)
-    put_rows(text_outs, text_pull, None)
+    return pull, loss
+
+
+def tile_kernel(a, pair_ref, images_ref, texts_ref, other_images_ref, other_texts_ref, *outs):
+    scale, shift = pair_ref[0:1, 0:1], pair_ref[1:2, 0:1]
+    images, texts = images_ref[...], texts_ref[...]
+    pull, loss = partial_pull(
+        images, jnp.concatenate([texts, other_texts_ref[...]], axis=0), scale, shift
+    )
+    put_rows(outs[:a][::-1], pull, loss)
+    pull, _ = partial_pull(
+        texts, jnp.concatenate([images, other_images_ref[...]], axis=0), scale, shift
+    )
+    put_rows(outs[a:][::-1], pull, None)
 
 
 def final_kernel(a, b, image_ref, text_ref, *refs):
     image_parts, text_parts = refs[:a], refs[a : a + b]
     loss_ref, grad_image_ref, grad_text_ref = refs[a + b :]
     rows, depth = image_ref.shape
-    pairs = rows * a * b
+    pairs = 2 * rows * a * b
     for source, parts, out in (
         (image_ref, image_parts, grad_image_ref),
         (text_ref, text_parts, grad_text_ref),
@@ -151,46 +167,79 @@
 
 def local(image_emb, text_emb, pair_class, scale, shift):
     rows, depth = image_emb.shape
-    n = lax.axis_size("img") * lax.axis_size("txt")
-    b = min(d for d in range(1, n + 1) if n % d == 0 and d * d >= n)
-    a = n // b
     width = depth + LANES
+    lanes = lax.axis_size("txt")
+    n = lax.axis_size("img") * lanes
+    chips = n // 2
+    b = min(d for d in range(1, chips + 1) if chips % d == 0 and d * d >= chips)
+    a = chips // b
     vmem = pl.BlockSpec(memory_space=pltpu.VMEM)
     smem = pl.BlockSpec(memory_space=pltpu.SMEM)
     params = pltpu.CompilerParams(vmem_limit_bytes=32 << 20)
 
+    def split(i):
+        return i // (2 * lanes) * lanes + i % lanes, i // lanes % 2
+
+    def place(chip, core):
+        return (chip // lanes * 2 + core) * lanes + chip % lanes
+
     def along_a(i, k):
-        return partner(i // b, k, a) * b + i % b
+        chip, core = split(i)
+        return place(partner(chip // b, k, a) * b + chip % b, core)
 
     def along_b(i, k):
-        return i // b * b + partner(i % b, k, b)
-
-    def collect(block, size, along):
-        pairs = [[(along(i, k), i) for i in range(n)] for k in range(1, size)]
-        return [block] + [lax.ppermute(block, AXES, pair) for pair in pairs]
-
-    def give_back(blocks, along):
-        pairs = [[(i, along(i, k)) for i in range(n)] for k in range(len(blocks))]
-        return blocks[:1] + [lax.ppermute(x, AXES, p) for x, p in zip(blocks[1:], pairs[1:])]
-
+        chip, core = split(i)
+        return place(chip // b * b + partner(chip % b, k, b), core)
+
+    def move(x, pairs):
+        return lax.ppermute(x, AXES, pairs)
+
+    def collect(x, size, along):
+        return [x] + [move(x, [(along(i, k), i) for i in range(n)]) for k in range(1, size)]
+
+    def give_back(parts, along):
+        steps = range(len(parts) - 1, 0, -1)
+        return [move(x, [(i, along(i, k)) for i in range(n)]) for x, k in zip(parts, steps)] + [parts[-1]]
+
+    def swap(x):
+        return move(x, [(i, place(split(i)[0], 1 - split(i)[1])) for i in range(n)])
+
+    block = jax.ShapeDtypeStruct((rows, width), jnp.bfloat16)
     image_rows, text_rows = pl.pallas_call(
         pack_kernel,
-        out_shape=(jax.ShapeDtypeStruct((rows, width), jnp.bfloat16),) * 2,
+        out_shape=(block, block),
         in_specs=[vmem, vmem, smem],
         out_specs=(vmem, vmem),
-        compiler_params=params,
         name="pack",
     )(image_emb, text_emb, pair_class)
-    images, texts = collect(image_rows, a, along_a), collect(text_rows, b, along_b)
+    images = pl.pallas_call(
+        join_kernel,
+        out_shape=jax.ShapeDtypeStruct((a * rows, width), jnp.bfloat16),
+        in_specs=[vmem] * a,
+        out_specs=vmem,
+        compiler_params=params,
+        name="join_images",
+    )(*collect(image_rows, a, along_a))
+    texts, pair = pl.pallas_call(
+        join_with_pair_kernel,
+        out_shape=(
+            jax.ShapeDtypeStruct((b * rows, width), jnp.bfloat16),
+            jax.ShapeDtypeStruct((8, LANES), jnp.float32),
+        ),
+        in_specs=[smem, smem] + [vmem] * b,
+        out_specs=(vmem, vmem),
+        compiler_params=params,
+        name="join_texts",
+    )(scale[None], shift[None], *collect(text_rows, b, along_b))
     parts = pl.pallas_call(
-        functools.partial(tile_kernel, a, b),
+        functools.partial(tile_kernel, a),
         out_shape=(jax.ShapeDtypeStruct((rows, width), jnp.int16),) * (a + b),
-        in_specs=[smem, smem] + [vmem] * (a + b),
+        in_specs=[vmem] * 5,
         out_specs=(vmem,) * (a + b),
         compiler_params=params,
         name="tile",
-    )(scale[None], shift[None], *images, *texts)
-    parts = give_back(list(parts[:a]), along_a) + give_back(list(parts[a:]), along_b)
+    )(pair, images, texts, swap(images), swap(texts))
+    parts = give_back(parts[:a], along_a) + give_back(parts[a:], along_b)
     loss, grad_image, grad_text = pl.pallas_call(
         functools.partial(final_kernel, a, b),
         out_shape=(

time: 38.1 us -> 29.1 us (0.76)
  starting transfers between devices: 25 us -> 17.2 us
  local copies, waits for them, and re-layouts: 2.19 us -> 0.79 us
  Pallas kernels: 2.34 us -> 3.43 us
  waiting for transfers between devices: 6.34 us -> 5.4 us
    ppermute x20 -> x14, starting transfers between devices: 25 us -> 17.2 us  [move(): return lax.ppermute(x, AXES, pairs)]
    unnamed x10 -> x8, local copies, waits for them, and re-layouts: 2.19 us -> 0.79 us
    pallas_call x2 -> x4, Pallas kernels: 1.42 us -> 2.53 us  [the longest x1 1.54 us: local(): pl.pallas_call(pack_kernel, out_shape=(block, block), in_specs=[vmem, vme...]
    ppermute x20 -> x14, waiting for transfers between devices: 6.34 us -> 5.4 us  [move(): return lax.ppermute(x, AXES, pairs)]
  transfers between devices with their start and end apart: 20 -> 14, of which waited for: 5 -> 7; matrix products, arithmetic and copies ran while one was open for 0% -> 0% of each run, Pallas kernels for 0% -> 0%
where the time goes in v7:
time: 29.1 us; the launch traced here: 28.9 us
  starting transfers between devices  17.2 us (59%)
  waiting for transfers between devices  5.4 us (19%)
  Pallas kernels  3.43 us (12%)
  between operations  2.02 us (7%)
  local copies, waits for them, and re-layouts  0.79 us (3%)
    ppermute x14, starting transfers between devices, move(): return lax.ppermute(x, AXES, pairs)  17.2 us
    ppermute x14, waiting for transfers between devices, move(): return lax.ppermute(x, AXES, pairs)  5.4 us
    pallas_call x1, Pallas kernels, local(): pl.pallas_call(pack_kernel, out_shape=(block, block), in_specs=[vmem, vme...  1.54 us
    pallas_call x1, Pallas kernels, local(): pl.pallas_call(functools.partial(tile_kernel, a), out_shape=(jax.ShapeDty...  0.96 us
    pallas_call x1, Pallas kernels, local(): pl.pallas_call(functools.partial(final_kernel, a, b), out_shape=(jax.Shap...  0.91 us
    unnamed x8, local copies, waits for them, and re-layouts  0.79 us
  transfers between devices with their start and end apart: 14, of which 7 were waited for; matrix products, arithmetic and copies ran while one was open for 0% of the time, Pallas kernels for 0%

profile of v7, /device:TPU:0, one launch (start us, length us, event | category | flops | bytes accessed | tf_op | source)
XLA Modules:
  0.0 28.9 jit_solution(6941676423894564444)
XLA Ops:
  0.6 1.5 %pack.1 = (bf16[16,1280]{1,0:T(8,128)(2,1)}, bf16[16,1280]{1,0:T(8,128)(2,1)}) custom-call(bf16[16,1152]{1,0:T(8,128)(2,1)} %image_ref.3, bf16[16,1152]{1,0:T(8,128)(2,1)} %text_ref.3, s32[16]{0:T(128)} %class_ref.1), custom_call_target="tpu_custom_call" | custom-call | tf_op jit(solution)/shard_map/pack/pallas_call | solution.py:208
  2.2 5.0 %collective-permute-start.5 = (bf16[16,1280]{1,0:T(8,128)(2,1)}, bf16[16,1280]{1,0:T(8,128)(2,1)S(1)}, u32[]{:S(2)}, u32[]{:S(2)}) collective-permute-start(bf16[16,1280]{1,0:T(8,128)(2,1)} %get-tuple-element.20.refs_0_), channel_id=1, source_target_pairs={{24,0},{25,1},{26,2},{27,3},{28,4},{29,5},{30,6},{31,7},{16,8},{17... | collective-permute-start | bytes 122888 | tf_op jit(solution)/shard_map/ppermute | solution.py:195
  7.2 0.0 collective-permute-start.4
  7.2 0.6 %collective-permute-start.3 = (bf16[16,1280]{1,0:T(8,128)(2,1)}, bf16[16,1280]{1,0:T(8,128)(2,1)S(1)}, u32[]{:S(2)}, u32[]{:S(2)}) collective-permute-start(bf16[16,1280]{1,0:T(8,128)(2,1)} %get-tuple-element.20.refs_0_), channel_id=1, source_target_pairs={{8,0},{9,1},{10,2},{11,3},{12,4},{13,5},{14,6},{15,7},{0,8},{1,9},... | collective-permute-start | bytes 122888 | tf_op jit(solution)/shard_map/ppermute | solution.py:195
  7.8 2.7 %collective-permute-start.2 = (bf16[16,1280]{1,0:T(8,128)(2,1)}, bf16[16,1280]{1,0:T(8,128)(2,1)S(1)}, u32[]{:S(2)}, u32[]{:S(2)}) collective-permute-start(bf16[16,1280]{1,0:T(8,128)(2,1)} %get-tuple-element.18.refs_0_), channel_id=1, source_target_pairs={{5,0},{4,1},{7,2},{6,3},{1,4},{0,5},{3,6},{2,7},{13,8},{12,9},{15,... | collective-permute-start | bytes 122888 | tf_op jit(solution)/shard_map/ppermute | solution.py:195
  10.5 0.5 %collective-permute-start.1 = (bf16[16,1280]{1,0:T(8,128)(2,1)}, bf16[16,1280]{1,0:T(8,128)(2,1)S(1)}, u32[]{:S(2)}, u32[]{:S(2)}) collective-permute-start(bf16[16,1280]{1,0:T(8,128)(2,1)} %get-tuple-element.18.refs_0_), channel_id=1, source_target_pairs={{4,0},{5,1},{6,2},{7,3},{0,4},{1,5},{2,6},{3,7},{12,8},{13,9},{14,... | collective-permute-start | bytes 122888 | tf_op jit(solution)/shard_map/ppermute | solution.py:195
  11.0 0.0 collective-permute-done.5.refs_3_
  11.0 0.3 %collective-permute-start = (bf16[16,1280]{1,0:T(8,128)(2,1)}, bf16[16,1280]{1,0:T(8,128)(2,1)S(1)}, u32[]{:S(2)}, u32[]{:S(2)}) collective-permute-start(bf16[16,1280]{1,0:T(8,128)(2,1)} %get-tuple-element.18.refs_0_), channel_id=1, source_target_pairs={{1,0},{0,1},{3,2},{2,3},{5,4},{4,5},{7,6},{6,7},{9,8},{8,9},{11,10... | collective-permute-start | bytes 122888 | tf_op jit(solution)/shard_map/ppermute | solution.py:195
  12.6 0.0 copy-start.2
  12.6 0.0 collective-permute-done.4.refs_2_
  12.6 0.0 collective-permute-done.3.refs_1_
  12.6 0.0 copy-start.3
  12.7 0.8 %copy-done.3 = bf16[16,1280]{1,0:T(8,128)(2,1)S(1)} copy-done((bf16[16,1280]{1,0:T(8,128)(2,1)S(1)}, bf16[16,1280]{1,0:T(8,128)(2,1)}, u32[]{:S(2)}) %copy-start.3) | copy-done | bytes 40984
  13.4 0.1 collective-permute-start.6
  13.5 0.0 collective-permute-done.2.refs_3_
  13.5 1.1 %collective-permute-done.1.refs_2_ = bf16[16,1280]{1,0:T(8,128)(2,1)S(1)} collective-permute-done((bf16[16,1280]{1,0:T(8,128)(2,1)}, bf16[16,1280]{1,0:T(8,128)(2,1)S(1)}, u32[]{:S(2)}, u32[]{:S(2)}) %collective-permute-start.1) | collective-permute-done | bytes 40992 | tf_op jit(solution)/shard_map/ppermute | solution.py:195
  14.7 0.5 %collective-permute-done.refs_1_ = bf16[16,1280]{1,0:T(8,128)(2,1)S(1)} collective-permute-done((bf16[16,1280]{1,0:T(8,128)(2,1)}, bf16[16,1280]{1,0:T(8,128)(2,1)S(1)}, u32[]{:S(2)}, u32[]{:S(2)}) %collective-permute-start) | collective-permute-done | bytes 40992 | tf_op jit(solution)/shard_map/ppermute | solution.py:195
  15.2 0.0 copy-done.2
  15.2 0.1 collective-permute-start.7
  15.3 0.0 collective-permute-done.6.other_images_ref
  15.3 1.4 %collective-permute-done.7.other_texts_ref = bf16[64,1280]{1,0:T(8,128)(2,1)S(1)} collective-permute-done((bf16[64,1280]{1,0:T(8,128)(2,1)S(1)}, bf16[64,1280]{1,0:T(8,128)(2,1)S(1)}, u32[]{:S(2)}, u32[]{:S(2)}) %collective-permute-start.7) | collective-permute-done | bytes 163872 | tf_op jit(solution)/shard_map/ppermute | solution.py:195
  16.7 0.0 copy-start
  16.7 0.0 copy-start.1
  16.7 1.0 %tile.1 = (s16[16,1280]{1,0:T(8,128)(2,1)S(1)}, s16[16,1280]{1,0:T(8,128)(2,1)S(1)}, s16[16,1280]{1,0:T(8,128)(2,1)S(1)}, s16[16,1280]{1,0:T(8,128)(2,1)S(1)}, s...) custom-call(f32[8,128]{1,0:T(8,128)S(1)} %get-tuple-element.19.pair_, ...), custom_call_target="tpu_custom_call" | custom-call | tf_op jit(solution)/shard_map/tile/pallas_call | solution.py:234
  17.7 3.7 %collective-permute-start.8 = (s16[16,1280]{1,0:T(8,128)(2,1)S(1)}, s16[16,1280]{1,0:T(8,128)(2,1)S(1)}, u32[]{:S(2)}, u32[]{:S(2)}) collective-permute-start(s16[16,1280]{1,0:T(8,128)(2,1)S(1)} %get-tuple-element.22), channel_id=1, source_target_pairs={{0,24},{1,25},{2,26},{3,27},{4,28},{5,29},{6,30},{7,31},{8,16},{9,... | collective-permute-start | bytes 122888 | tf_op jit(solution)/shard_map/ppermute | solution.py:195
  21.3 0.0 collective-permute-start.9
  21.3 0.8 %collective-permute-start.10 = (s16[16,1280]{1,0:T(8,128)(2,1)S(1)}, s16[16,1280]{1,0:T(8,128)(2,1)S(1)}, u32[]{:S(2)}, u32[]{:S(2)}) collective-permute-start(s16[16,1280]{1,0:T(8,128)(2,1)S(1)} %get-tuple-element.24), channel_id=1, source_target_pairs={{0,8},{1,9},{2,10},{3,11},{4,12},{5,13},{6,14},{7,15},{8,0},{9,1},... | collective-permute-start | bytes 122888 | tf_op jit(solution)/shard_map/ppermute | solution.py:195
  22.1 1.4 %collective-permute-start.11 = (s16[16,1280]{1,0:T(8,128)(2,1)S(1)}, s16[16,1280]{1,0:T(8,128)(2,1)S(1)}, u32[]{:S(2)}, u32[]{:S(2)}) collective-permute-start(s16[16,1280]{1,0:T(8,128)(2,1)S(1)} %get-tuple-element.26), channel_id=1, source_target_pairs={{0,5},{1,4},{2,7},{3,6},{4,1},{5,0},{6,3},{7,2},{8,13},{9,12},{10,... | collective-permute-start | bytes 122888 | tf_op jit(solution)/shard_map/ppermute | solution.py:195
  23.5 0.4 %collective-permute-start.12 = (s16[16,1280]{1,0:T(8,128)(2,1)S(1)}, s16[16,1280]{1,0:T(8,128)(2,1)S(1)}, u32[]{:S(2)}, u32[]{:S(2)}) collective-permute-start(s16[16,1280]{1,0:T(8,128)(2,1)S(1)} %get-tuple-element.27), channel_id=1, source_target_pairs={{0,4},{1,5},{2,6},{3,7},{4,0},{5,1},{6,2},{7,3},{8,12},{9,13},{10,... | collective-permute-start | bytes 122888 | tf_op jit(solution)/shard_map/ppermute | solution.py:195
  23.9 0.0 collective-permute-done.8.refs_0_
  23.9 1.7 %collective-permute-start.13 = (s16[16,1280]{1,0:T(8,128)(2,1)S(1)}, s16[16,1280]{1,0:T(8,128)(2,1)S(1)}, u32[]{:S(2)}, u32[]{:S(2)}) collective-permute-start(s16[16,1280]{1,0:T(8,128)(2,1)S(1)} %get-tuple-element.28), channel_id=1, source_target_pairs={{0,1},{1,0},{2,3},{3,2},{4,5},{5,4},{6,7},{7,6},{8,9},{9,8},{10,11... | collective-permute-start | bytes 122888 | tf_op jit(solution)/shard_map/ppermute | solution.py:195
  25.6 0.6 %collective-permute-done.9.refs_1_ = s16[16,1280]{1,0:T(8,128)(2,1)S(1)} collective-permute-done((s16[16,1280]{1,0:T(8,128)(2,1)S(1)}, s16[16,1280]{1,0:T(8,128)(2,1)S(1)}, u32[]{:S(2)}, u32[]{:S(2)}) %collective-permute-start.9) | collective-permute-done | bytes 40992 | tf_op jit(solution)/shard_map/ppermute | solution.py:195
  26.2 0.0 collective-permute-done.10.refs_2_
  26.2 0.9 %collective-permute-done.11.refs_4_ = s16[16,1280]{1,0:T(8,128)(2,1)S(1)} collective-permute-done((s16[16,1280]{1,0:T(8,128)(2,1)S(1)}, s16[16,1280]{1,0:T(8,128)(2,1)S(1)}, u32[]{:S(2)}, u32[]{:S(2)}) %collective-permute-start.11) | collective-permute-done | bytes 40992 | tf_op jit(solution)/shard_map/ppermute | solution.py:195
  27.1 0.4 %collective-permute-done.12.refs_5_ = s16[16,1280]{1,0:T(8,128)(2,1)S(1)} collective-permute-done((s16[16,1280]{1,0:T(8,128)(2,1)S(1)}, s16[16,1280]{1,0:T(8,128)(2,1)S(1)}, u32[]{:S(2)}, u32[]{:S(2)}) %collective-permute-start.12) | collective-permute-done | bytes 40992 | tf_op jit(solution)/shard_map/ppermute | solution.py:195
  27.6 0.4 %collective-permute-done.13.refs_6_ = s16[16,1280]{1,0:T(8,128)(2,1)S(1)} collective-permute-done((s16[16,1280]{1,0:T(8,128)(2,1)S(1)}, s16[16,1280]{1,0:T(8,128)(2,1)S(1)}, u32[]{:S(2)}, u32[]{:S(2)}) %collective-permute-start.13) | collective-permute-done | bytes 40992 | tf_op jit(solution)/shard_map/ppermute | solution.py:195
  27.9 0.0 copy-done
  28.0 0.0 copy-done.1
  28.0 0.9 %final.1 = (f32[1,16]{1,0:T(1,128)}, f32[16,1152]{1,0:T(8,128)}, f32[16,1152]{1,0:T(8,128)}) custom-call(bf16[16,1152]{1,0:T(8,128)(2,1)S(1)} %copy-done, bf16[16,1152]{1,0:T(8,128)(2,1)S(1)} %copy-done.1, s16[16,1280]{1,0:T(8,128)(2,1)S(1)} %collective-permute-done.8.refs_0_, s16[16,1280]{1,0:T(8,128)(2,1)S(1)} %collective-permute-done.9.refs_1_, ...), custom_call_target="tpu_custom_call" | custom-call | tf_op jit(solution)/shard_map/final/pallas_call | solution.py:243
  (2 shorter events, 0.0 us)
Async XLA Ops:
  2.2 8.8 %collective-permute-start.5 = (bf16[16,1280]{1,0:T(8,128)(2,1)}, bf16[16,1280]{1,0:T(8,128)(2,1)S(1)}, u32[]{:S(2)}, u32[]{:S(2)}) collective-permute-start(bf16[16,1280]{1,0:T(8,128)(2,1)} %get-tuple-element.20.refs_0_), channel_id=1, source_target_pairs={{24,0},{25,1},{26,2},{27,3},{28,4},{29,5},{30,6},{31,7},{16,8},{17... | collective-permute-start | bytes 122888 | tf_op jit(solution)/shard_map/ppermute | solution.py:195
  7.2 5.4 %collective-permute-start.4 = (bf16[16,1280]{1,0:T(8,128)(2,1)}, bf16[16,1280]{1,0:T(8,128)(2,1)S(1)}, u32[]{:S(2)}, u32[]{:S(2)}) collective-permute-start(bf16[16,1280]{1,0:T(8,128)(2,1)} %get-tuple-element.20.refs_0_), channel_id=1, source_target_pairs={{16,0},{17,1},{18,2},{19,3},{20,4},{21,5},{22,6},{23,7},{24,8},{25... | collective-permute-start | bytes 122888 | tf_op jit(solution)/shard_map/ppermute | solution.py:195
  7.2 5.4 %collective-permute-start.3 = (bf16[16,1280]{1,0:T(8,128)(2,1)}, bf16[16,1280]{1,0:T(8,128)(2,1)S(1)}, u32[]{:S(2)}, u32[]{:S(2)}) collective-permute-start(bf16[16,1280]{1,0:T(8,128)(2,1)} %get-tuple-element.20.refs_0_), channel_id=1, source_target_pairs={{8,0},{9,1},{10,2},{11,3},{12,4},{13,5},{14,6},{15,7},{0,8},{1,9},... | collective-permute-start | bytes 122888 | tf_op jit(solution)/shard_map/ppermute | solution.py:195
  7.8 5.7 %collective-permute-start.2 = (bf16[16,1280]{1,0:T(8,128)(2,1)}, bf16[16,1280]{1,0:T(8,128)(2,1)S(1)}, u32[]{:S(2)}, u32[]{:S(2)}) collective-permute-start(bf16[16,1280]{1,0:T(8,128)(2,1)} %get-tuple-element.18.refs_0_), channel_id=1, source_target_pairs={{5,0},{4,1},{7,2},{6,3},{1,4},{0,5},{3,6},{2,7},{13,8},{12,9},{15,... | collective-permute-start | bytes 122888 | tf_op jit(solution)/shard_map/ppermute | solution.py:195
  10.5 4.2 %collective-permute-start.1 = (bf16[16,1280]{1,0:T(8,128)(2,1)}, bf16[16,1280]{1,0:T(8,128)(2,1)S(1)}, u32[]{:S(2)}, u32[]{:S(2)}) collective-permute-start(bf16[16,1280]{1,0:T(8,128)(2,1)} %get-tuple-element.18.refs_0_), channel_id=1, source_target_pairs={{4,0},{5,1},{6,2},{7,3},{0,4},{1,5},{2,6},{3,7},{12,8},{13,9},{14,... | collective-permute-start | bytes 122888 | tf_op jit(solution)/shard_map/ppermute | solution.py:195
  11.0 4.2 %collective-permute-start = (bf16[16,1280]{1,0:T(8,128)(2,1)}, bf16[16,1280]{1,0:T(8,128)(2,1)S(1)}, u32[]{:S(2)}, u32[]{:S(2)}) collective-permute-start(bf16[16,1280]{1,0:T(8,128)(2,1)} %get-tuple-element.18.refs_0_), channel_id=1, source_target_pairs={{1,0},{0,1},{3,2},{2,3},{5,4},{4,5},{7,6},{6,7},{9,8},{8,9},{11,10... | collective-permute-start | bytes 122888 | tf_op jit(solution)/shard_map/ppermute | solution.py:195
  12.6 2.6 %copy-start.2 = (bf16[16,1280]{1,0:T(8,128)(2,1)S(1)}, bf16[16,1280]{1,0:T(8,128)(2,1)}, u32[]{:S(2)}) copy-start(bf16[16,1280]{1,0:T(8,128)(2,1)} %get-tuple-element.18.refs_0_) | copy-start | bytes 122884
  12.6 0.8 %copy-start.3 = (bf16[16,1280]{1,0:T(8,128)(2,1)S(1)}, bf16[16,1280]{1,0:T(8,128)(2,1)}, u32[]{:S(2)}) copy-start(bf16[16,1280]{1,0:T(8,128)(2,1)} %get-tuple-element.20.refs_0_) | copy-start | bytes 122884
  13.4 1.9 %collective-permute-start.6 = (bf16[64,1280]{1,0:T(8,128)(2,1)S(1)}, bf16[64,1280]{1,0:T(8,128)(2,1)S(1)}, u32[]{:S(2)}, u32[]{:S(2)}) collective-permute-start(bf16[64,1280]{1,0:T(8,128)(2,1)S(1)} %join_images.1.images_ref), channel_id=1, source_target_pairs={{0,2},{1,3},{2,0},{3,1},{4,6},{5,7},{6,4},{7,5},{8,10},{9,11},{10,... | collective-permute-start | bytes 491528 | tf_op jit(solution)/shard_map/ppermute | solution.py:195
  15.2 1.5 %collective-permute-start.7 = (bf16[64,1280]{1,0:T(8,128)(2,1)S(1)}, bf16[64,1280]{1,0:T(8,128)(2,1)S(1)}, u32[]{:S(2)}, u32[]{:S(2)}) collective-permute-start(bf16[64,1280]{1,0:T(8,128)(2,1)S(1)} %get-tuple-element.21.texts_ref), channel_id=1, source_target_pairs={{0,2},{1,3},{2,0},{3,1},{4,6},{5,7},{6,4},{7,5},{8,10},{9,11},{10,... | collective-permute-start | bytes 491528 | tf_op jit(solution)/shard_map/ppermute | solution.py:195
  16.7 11.3 %copy-start = (bf16[16,1152]{1,0:T(8,128)(2,1)S(1)}, bf16[16,1152]{1,0:T(8,128)(2,1)}, u32[]{:S(2)}) copy-start(bf16[16,1152]{1,0:T(8,128)(2,1)} %image_ref.3) | copy-start | bytes 110596
  16.7 11.3 %copy-start.1 = (bf16[16,1152]{1,0:T(8,128)(2,1)S(1)}, bf16[16,1152]{1,0:T(8,128)(2,1)}, u32[]{:S(2)}) copy-start(bf16[16,1152]{1,0:T(8,128)(2,1)} %text_ref.3) | copy-start | bytes 110596
  17.7 6.3 %collective-permute-start.8 = (s16[16,1280]{1,0:T(8,128)(2,1)S(1)}, s16[16,1280]{1,0:T(8,128)(2,1)S(1)}, u32[]{:S(2)}, u32[]{:S(2)}) collective-permute-start(s16[16,1280]{1,0:T(8,128)(2,1)S(1)} %get-tuple-element.22), channel_id=1, source_target_pairs={{0,24},{1,25},{2,26},{3,27},{4,28},{5,29},{6,30},{7,31},{8,16},{9,... | collective-permute-start | bytes 122888 | tf_op jit(solution)/shard_map/ppermute | solution.py:195
  21.3 4.9 %collective-permute-start.9 = (s16[16,1280]{1,0:T(8,128)(2,1)S(1)}, s16[16,1280]{1,0:T(8,128)(2,1)S(1)}, u32[]{:S(2)}, u32[]{:S(2)}) collective-permute-start(s16[16,1280]{1,0:T(8,128)(2,1)S(1)} %get-tuple-element.23), channel_id=1, source_target_pairs={{0,16},{1,17},{2,18},{3,19},{4,20},{5,21},{6,22},{7,23},{8,24},{9,... | collective-permute-start | bytes 122888 | tf_op jit(solution)/shard_map/ppermute | solution.py:195
  21.3 4.9 %collective-permute-start.10 = (s16[16,1280]{1,0:T(8,128)(2,1)S(1)}, s16[16,1280]{1,0:T(8,128)(2,1)S(1)}, u32[]{:S(2)}, u32[]{:S(2)}) collective-permute-start(s16[16,1280]{1,0:T(8,128)(2,1)S(1)} %get-tuple-element.24), channel_id=1, source_target_pairs={{0,8},{1,9},{2,10},{3,11},{4,12},{5,13},{6,14},{7,15},{8,0},{9,1},... | collective-permute-start | bytes 122888 | tf_op jit(solution)/shard_map/ppermute | solution.py:195
  22.1 5.0 %collective-permute-start.11 = (s16[16,1280]{1,0:T(8,128)(2,1)S(1)}, s16[16,1280]{1,0:T(8,128)(2,1)S(1)}, u32[]{:S(2)}, u32[]{:S(2)}) collective-permute-start(s16[16,1280]{1,0:T(8,128)(2,1)S(1)} %get-tuple-element.26), channel_id=1, source_target_pairs={{0,5},{1,4},{2,7},{3,6},{4,1},{5,0},{6,3},{7,2},{8,13},{9,12},{10,... | collective-permute-start | bytes 122888 | tf_op jit(solution)/shard_map/ppermute | solution.py:195
  23.5 4.0 %collective-permute-start.12 = (s16[16,1280]{1,0:T(8,128)(2,1)S(1)}, s16[16,1280]{1,0:T(8,128)(2,1)S(1)}, u32[]{:S(2)}, u32[]{:S(2)}) collective-permute-start(s16[16,1280]{1,0:T(8,128)(2,1)S(1)} %get-tuple-element.27), channel_id=1, source_target_pairs={{0,4},{1,5},{2,6},{3,7},{4,0},{5,1},{6,2},{7,3},{8,12},{9,13},{10,... | collective-permute-start | bytes 122888 | tf_op jit(solution)/shard_map/ppermute | solution.py:195
  23.9 4.0 %collective-permute-start.13 = (s16[16,1280]{1,0:T(8,128)(2,1)S(1)}, s16[16,1280]{1,0:T(8,128)(2,1)S(1)}, u32[]{:S(2)}, u32[]{:S(2)}) collective-permute-start(s16[16,1280]{1,0:T(8,128)(2,1)S(1)} %get-tuple-element.28), channel_id=1, source_target_pairs={{0,1},{1,0},{2,3},{3,2},{4,5},{5,4},{6,7},{7,6},{8,9},{9,8},{10,11... | collective-permute-start | bytes 122888 | tf_op jit(solution)/shard_map/ppermute | solution.py:195

commit v8 on v7

v8 whole, which is shorter than its diff:
```python
import functools

import jax
import jax.numpy as jnp
from jax import lax
from jax.experimental import pallas as pl
from jax.experimental.pallas import tpu as pltpu
from jax.sharding import PartitionSpec as P

AXES = ("img", "txt")
DIGITS = 4
LANES = 128
TOP = 32767.0


def unit_rows(rows):
    wide = rows.astype(jnp.float32)
    inverse = 1.0 / jnp.sqrt(jnp.sum(wide * wide, axis=1, keepdims=True) + 1e-06)
    return (wide * inverse, inverse)


def project_back(unit, inverse, pull):
    inner = jnp.sum(unit * pull, axis=1, keepdims=True)
    return (pull - unit * inner) * inverse


def pack_kernel(rows_ref, class_ref, out_ref):
    rows, depth = rows_ref.shape
    row = lax.broadcasted_iota(jnp.int32, (rows, LANES), 0)
    lane = lax.broadcasted_iota(jnp.int32, (rows, LANES), 1)
    spread = jnp.zeros((rows, LANES), jnp.int32)
    for i in range(rows):
        spread = jnp.where(row == i, class_ref[i], spread)
    digit = lax.shift_right_logical(spread, 8 * jnp.minimum(lane, DIGITS - 1)) & 255
    digit = jnp.where(lane < DIGITS, digit, 0).astype(jnp.float32).astype(jnp.bfloat16)
    out_ref[:, :depth] = unit_rows(rows_ref[...])[0].astype(jnp.bfloat16)
    out_ref[:, depth:] = digit


def put_blocks(out_ref, refs):
    start = 0
    for ref in refs:
        out_ref[start : start + ref.shape[0], :] = ref[...]
        start += ref.shape[0]


def join_kernel(*refs):
    put_blocks(refs[-1], refs[:-1])


def join_with_pair_kernel(scale_ref, shift_ref, *refs):
    put_blocks(refs[-2], refs[:-2])
    row = lax.broadcasted_iota(jnp.int32, refs[-1].shape, 0)
    refs[-1][...] = jnp.where(row == 0, scale_ref[0], shift_ref[0])


def power_above(size):
    return jnp.ceil(jnp.log2(jnp.maximum(size, 1e-30)) + 0.01)


def code(values, power):
    steps = jnp.clip(jnp.round(values * (TOP / jnp.exp2(power))), -TOP, TOP)
    return steps.astype(jnp.int32).astype(jnp.int16)


def decode(steps, power):
    return steps.astype(jnp.int32).astype(jnp.float32) * (jnp.exp2(power) * (1.0 / TOP))


def put_rows(outs, pull, loss):
    blocks, (rows, width) = len(outs), outs[0].shape
    depth = width - LANES
    power = power_above(jnp.max(jnp.abs(pull), axis=1, keepdims=True))
    steps = code(pull, power)
    lane = lax.broadcasted_iota(jnp.int32, (blocks * rows, LANES), 1)
    loss_power = power_above(loss)
    tail = jnp.where(lane == 0, power, 0.0)
    tail = jnp.where(lane == 1, loss_power, tail)
    tail = jnp.where(lane == 2, jnp.round(loss * (TOP / jnp.exp2(loss_power))), tail)
    tail = tail.astype(jnp.int32).astype(jnp.int16)
    for k, out in enumerate(outs):
        out[:, :depth] = steps[k * rows : (k + 1) * rows]
        out[:, depth:] = tail[k * rows : (k + 1) * rows]


def partial_pull(lines, columns, scale, shift):
    depth = lines.shape[1] - LANES
    logits = (
        scale
        * lax.dot_general(
            lines[:, :depth],
            columns[:, :depth],
            (((1,), (1,)), ((), ())),
            preferred_element_type=jnp.float32,
        )
        + shift
    )
    pick = (
        lax.broadcasted_iota(jnp.int32, (8, LANES), 0)
        == lax.broadcasted_iota(jnp.int32, (8, LANES), 1)
    )
    column_digits = lax.dot_general(
        pick.astype(jnp.bfloat16),
        columns[:, depth:],
        (((1,), (1,)), ((), ())),
        preferred_element_type=jnp.float32,
    )
    line_digits = lines[:, depth:].astype(jnp.float32)
    same = None
    for k in range(DIGITS):
        equal = line_digits[:, k : k + 1] == column_digits[k : k + 1, :]
        same = equal if same is None else same & equal
    sign = jnp.where(same, 1.0, -1.0).astype(jnp.float32)
    margin = sign * logits
    small = jnp.exp(-jnp.abs(margin))
    over = 1.0 / (1.0 + small)
    coef = -sign * jnp.where(margin >= 0, small * over, over) * scale
    pull = jnp.dot(
        coef.astype(jnp.bfloat16), columns[:, :depth], preferred_element_type=jnp.float32
    )
    loss = jnp.sum(jnp.log1p(small) - jnp.minimum(margin, 0.0), axis=1, keepdims=True)
    return pull, loss


def tile_kernel(count, pair_ref, images_ref, texts_ref, other_images_ref, other_texts_ref, *outs):
    scale, shift = pair_ref[0:1, 0:1], pair_ref[1:2, 0:1]
    images, texts = images_ref[...], texts_ref[...]
    pull, loss = partial_pull(
        images, jnp.concatenate([texts, other_texts_ref[...]], axis=0), scale, shift
    )
    put_rows(outs[:count], pull, loss)
    pull, loss = partial_pull(
        texts, jnp.concatenate([images, other_images_ref[...]], axis=0), scale, shift
    )
    put_rows(outs[count:], pull, loss)


def total(parts, rows, depth):
    pull = jnp.zeros((rows, depth), jnp.float32)
    loss = jnp.zeros((rows, 1), jnp.float32)
    for part in parts:
        tail = part[:, depth:].astype(jnp.int32).astype(jnp.float32)
        pull = pull + decode(part[:, :depth], tail[:, 0:1])
        loss = loss + tail[:, 2:3] * (jnp.exp2(tail[:, 1:2]) * (1.0 / TOP))
    return pull, loss


def add_kernel(count, *refs):
    rows, width = refs[0].shape
    pull, loss = total(refs[:count], rows, width - LANES)
    put_rows(refs[count:], pull, loss)


def final_kernel(count, pairs, image_ref, text_ref, *refs):
    image_parts, text_parts = refs[:count], refs[count:-3]
    loss_ref, grad_image_ref, grad_text_ref = refs[-3:]
    rows, depth = image_ref.shape
    for source, parts, out in (
        (image_ref, image_parts, grad_image_ref),
        (text_ref, text_parts, grad_text_ref),
    ):
        unit, inverse = unit_rows(source[...])
        pull, loss = total(parts, rows, depth)
        out[...] = project_back(unit, inverse, pull)
        if out is grad_image_ref:
            row = lax.broadcasted_iota(jnp.int32, (rows, rows), 0)
            column = lax.broadcasted_iota(jnp.int32, (rows, rows), 1)
            across = jnp.where(row == column, loss / pairs, 0.0)
            loss_ref[...] = jnp.sum(across, axis=0, keepdims=True)


def steps_of(size):
    steps, left = [], size
    while left > 1:
        factor = min(d for d in range(2, left + 1) if left % d == 0)
        left //= factor
        steps.append((factor, left))
    return steps


def local(image_emb, text_emb, pair_class, scale, shift):
    rows, depth = image_emb.shape
    width = depth + LANES
    lanes = lax.axis_size("txt")
    n = lax.axis_size("img") * lanes
    chips = n // 2
    b = min(d for d in range(1, chips + 1) if chips % d == 0 and d * d >= chips)
    a = chips // b
    vmem = pl.BlockSpec(memory_space=pltpu.VMEM)
    smem = pl.BlockSpec(memory_space=pltpu.SMEM)
    params = pltpu.CompilerParams(vmem_limit_bytes=32 << 20)

    def call(kernel, shapes, operands, scalars, name):
        return pl.pallas_call(
            kernel,
            out_shape=shapes,
            in_specs=[smem] * scalars + [vmem] * (len(operands) - scalars),
            out_specs=jax.tree.map(lambda _: vmem, shapes),
            compiler_params=params,
            name=name,
        )(*operands)

    def coded(count, dtype=jnp.int16):
        return jax.ShapeDtypeStruct((count, width), dtype)

    def split(i):
        return i // (2 * lanes) * lanes + i % lanes, i // lanes % 2

    def place(chip, core):
        return (chip // lanes * 2 + core) * lanes + chip % lanes

    def turn(i, k, factor, stride):
        chip, core = split(i)
        digit = chip // stride % factor
        return place(chip + ((digit + k) % factor - digit) * stride, core)

    def move(x, pairs):
        return lax.ppermute(x, AXES, pairs)

    def collect(x, steps, name, extra=()):
        for factor, stride in steps:
            blocks = [x] + [
                move(x, [(turn(i, k, factor, stride), i) for i in range(n)])
                for k in range(1, factor)
            ]
            shape = coded(factor * x.shape[0], jnp.bfloat16)
            if extra and (factor, stride) == steps[-1]:
                pair = jax.ShapeDtypeStruct((8, LANES), jnp.float32)
                return call(join_with_pair_kernel, (shape, pair), [*extra, *blocks], 2, name)
            x = call(join_kernel, shape, blocks, 0, name)
        return x

    def give_back(parts, steps, name):
        for index, (factor, stride) in enumerate(steps):
            parts = [parts[0]] + [
                move(parts[k], [(i, turn(i, k, factor, stride)) for i in range(n)])
                for k in range(1, factor)
            ]
            if index + 1 < len(steps):
                count = steps[index + 1][0]
                shapes = (coded(parts[0].shape[0] // count),) * count
                parts = call(functools.partial(add_kernel, factor), shapes, parts, 0, name)
        return list(parts)

    def swap(x):
        return move(x, [(i, place(split(i)[0], 1 - split(i)[1])) for i in range(n)])

    along_a = [(factor, stride * b) for factor, stride in steps_of(a)]
    along_b = steps_of(b)
    sides = [
        pl.pallas_call(
            pack_kernel,
            out_shape=coded(rows, jnp.bfloat16),
            in_specs=[vmem, smem],
            out_specs=vmem,
            compiler_params=params,
            name=name,
        )(x, pair_class)
        for x, name in ((image_emb, "pack_images"), (text_emb, "pack_texts"))
    ]
    images = collect(sides[0], along_a, "join_images")
    texts, pair = collect(sides[1], along_b, "join_texts", (scale[None], shift[None]))
    back_a, back_b = along_a[::-1], along_b[::-1]
    count = back_a[0][0]
    shapes = (coded(a * rows // count),) * count + (coded(b * rows // back_b[0][0]),) * back_b[0][0]
    parts = call(
        functools.partial(tile_kernel, count),
        shapes,
        [pair, images, texts, swap(images), swap(texts)],
        0,
        "tile",
    )
    image_parts = give_back(parts[:count], back_a, "add_images")
    text_parts = give_back(parts[count:], back_b, "add_texts")
    loss, grad_image, grad_text = call(
        functools.partial(final_kernel, len(image_parts), n * rows),
        (
            jax.ShapeDtypeStruct((1, rows), jnp.float32),
            jax.ShapeDtypeStruct((rows, depth), jnp.float32),
            jax.ShapeDtypeStruct((rows, depth), jnp.float32),
        ),
        [image_emb, text_emb, *image_parts, *text_parts],
        0,
        "final",
    )
    return (loss[0], grad_image, grad_text)


def solution(mesh):
    in_specs = (P(AXES, None), P(AXES, None), P(AXES), P(), P())
    out_specs = (P(AXES), P(AXES, None), P(AXES, None))
    return jax.shard_map(local, mesh=mesh, in_specs=in_specs, out_specs=out_specs, check_vma=False)
```

time: 29.1 us -> 31.2 us (1.072)
  waiting for transfers between devices: 5.4 us -> 8.53 us
  starting transfers between devices: 17.2 us -> 15.4 us
  local copies, waits for them, and re-layouts: 0.79 us -> 1.43 us
    ppermute x14 -> x10, waiting for transfers between devices: 5.4 us -> 8.53 us  [move(): return lax.ppermute(x, AXES, pairs)]
    ppermute x14 -> x10, starting transfers between devices: 17.2 us -> 15.4 us  [move(): return lax.ppermute(x, AXES, pairs)]
    unnamed x8, local copies, waits for them, and re-layouts: 0.79 us -> 1.43 us
    pallas_call x5 -> x10, Pallas kernels: 3.43 us -> 3.6 us  [the longest x8 2.32 us: call(): pl.pallas_call(kernel, out_shape=shapes, in_specs=[smem] * scalars + [vme...]
  transfers between devices with their start and end apart: 14 -> 10, of which waited for: 7 -> 6; matrix products, arithmetic and copies ran while one was open for 0% -> 0% of each run, Pallas kernels for 0% -> 4%
where the time goes in v8:
time: 31.2 us; the launch traced here: 31 us
  starting transfers between devices  15.4 us (49%)
  waiting for transfers between devices  8.53 us (27%)
  Pallas kernels  3.6 us (12%)
  between operations  2.04 us (7%)
  local copies, waits for them, and re-layouts  1.43 us (5%)
    ppermute x10, starting transfers between devices, move(): return lax.ppermute(x, AXES, pairs)  15.4 us
    ppermute x10, waiting for transfers between devices, move(): return lax.ppermute(x, AXES, pairs)  8.53 us
    pallas_call x8, Pallas kernels, call(): pl.pallas_call(kernel, out_shape=shapes, in_specs=[smem] * scalars + [vme...  2.32 us
    unnamed x8, local copies, waits for them, and re-layouts  1.43 us
    pallas_call x2, Pallas kernels, local(): pl.pallas_call(pack_kernel, out_shape=coded(rows, jnp.bfloat16), in_specs...  1.28 us
  transfers between devices with their start and end apart: 10, of which 6 were waited for; matrix products, arithmetic and copies ran while one was open for 0% of the time, Pallas kernels for 4%

profile of v8, /device:TPU:0, one launch (start us, length us, event | category | flops | bytes accessed | tf_op | source)
XLA Modules:
  0.0 31.0 jit_solution(3490692217975155654)
XLA Ops:
  0.6 0.0 copy-start
  0.6 0.0 copy-start.1
  0.7 0.8 %copy-done.1 = bf16[16,1152]{1,0:T(8,128)(2,1)S(1)} copy-done((bf16[16,1152]{1,0:T(8,128)(2,1)S(1)}, bf16[16,1152]{1,0:T(8,128)(2,1)}, u32[]{:S(2)}) %copy-start.1) | copy-done | bytes 36888
  1.4 0.0 copy-start.3
  1.4 0.7 %copy-done.3 = s32[16]{0:T(128)S(1)} copy-done((s32[16]{0:T(128)S(1)}, s32[16]{0:T(128)}, u32[]{:S(2)}) %copy-start.3) | copy-done | bytes 88
  2.1 0.6 %pack_texts.1.refs_0_ = bf16[16,1280]{1,0:T(8,128)(2,1)S(1)} custom-call(bf16[16,1152]{1,0:T(8,128)(2,1)S(1)} %copy-done.1, s32[16]{0:T(128)S(1)} %copy-done.3), custom_call_target="tpu_custom_call" | custom-call | tf_op jit(solution)/shard_map/pack_texts/pallas_call | solution.py:251
  2.7 3.0 %collective-permute-start = (bf16[16,1280]{1,0:T(8,128)(2,1)S(1)}, bf16[16,1280]{1,0:T(8,128)(2,1)S(1)}, u32[]{:S(2)}, u32[]{:S(2)}) collective-permute-start(bf16[16,1280]{1,0:T(8,128)(2,1)S(1)} %pack_texts.1.refs_0_), channel_id=1, source_target_pairs={{4,0},{5,1},{6,2},{7,3},{0,4},{1,5},{2,6},{3,7},{12,8},{13,9},{14,... | collective-permute-start | bytes 122888 | tf_op jit(solution)/shard_map/ppermute | solution.py:218
  5.7 0.0 copy-done
  5.7 0.6 %pack_images.1.refs_0_ = bf16[16,1280]{1,0:T(8,128)(2,1)S(1)} custom-call(bf16[16,1152]{1,0:T(8,128)(2,1)S(1)} %copy-done, s32[16]{0:T(128)S(1)} %copy-done.3), custom_call_target="tpu_custom_call" | custom-call | tf_op jit(solution)/shard_map/pack_images/pallas_call | solution.py:251
  6.4 2.7 %collective-permute-start.2 = (bf16[16,1280]{1,0:T(8,128)(2,1)S(1)}, bf16[16,1280]{1,0:T(8,128)(2,1)S(1)}, u32[]{:S(2)}, u32[]{:S(2)}) collective-permute-start(bf16[16,1280]{1,0:T(8,128)(2,1)S(1)} %pack_images.1.refs_0_), channel_id=1, source_target_pairs={{16,0},{17,1},{18,2},{19,3},{20,4},{21,5},{22,6},{23,7},{24,8},{25... | collective-permute-start | bytes 122888 | tf_op jit(solution)/shard_map/ppermute | solution.py:218
  9.0 0.0 collective-permute-done.refs_1_
  9.0 1.6 %collective-permute-start.1 = (bf16[32,1280]{1,0:T(8,128)(2,1)S(1)}, bf16[32,1280]{1,0:T(8,128)(2,1)S(1)}, u32[]{:S(2)}, u32[]{:S(2)}) collective-permute-start(bf16[32,1280]{1,0:T(8,128)(2,1)S(1)} %join_texts.2.refs_0_), channel_id=1, source_target_pairs={{1,0},{0,1},{3,2},{2,3},{5,4},{4,5},{7,6},{6,7},{9,8},{8,9},{11,10... | collective-permute-start | bytes 245768 | tf_op jit(solution)/shard_map/ppermute | solution.py:218
  10.6 0.8 %collective-permute-done.2.refs_1_ = bf16[16,1280]{1,0:T(8,128)(2,1)S(1)} collective-permute-done((bf16[16,1280]{1,0:T(8,128)(2,1)S(1)}, bf16[16,1280]{1,0:T(8,128)(2,1)S(1)}, u32[]{:S(2)}, u32[]{:S(2)}) %collective-permute-start.2) | collective-permute-done | bytes 40992 | tf_op jit(solution)/shard_map/ppermute | solution.py:218
  11.4 1.5 %collective-permute-start.3 = (bf16[32,1280]{1,0:T(8,128)(2,1)S(1)}, bf16[32,1280]{1,0:T(8,128)(2,1)S(1)}, u32[]{:S(2)}, u32[]{:S(2)}) collective-permute-start(bf16[32,1280]{1,0:T(8,128)(2,1)S(1)} %join_images.2.refs_0_), channel_id=1, source_target_pairs={{8,0},{9,1},{10,2},{11,3},{12,4},{13,5},{14,6},{15,7},{0,8},{1,9},... | collective-permute-start | bytes 245768 | tf_op jit(solution)/shard_map/ppermute | solution.py:218
  14.2 0.0 collective-permute-done.1.refs_1_
  14.3 0.1 collective-permute-start.5
  14.3 1.5 %collective-permute-done.3.refs_1_ = bf16[32,1280]{1,0:T(8,128)(2,1)S(1)} collective-permute-done((bf16[32,1280]{1,0:T(8,128)(2,1)S(1)}, bf16[32,1280]{1,0:T(8,128)(2,1)S(1)}, u32[]{:S(2)}, u32[]{:S(2)}) %collective-permute-start.3) | collective-permute-done | bytes 81952 | tf_op jit(solution)/shard_map/ppermute | solution.py:218
  15.8 0.1 collective-permute-start.4
  15.9 0.0 collective-permute-done.5.other_texts_ref
  15.9 1.4 %collective-permute-done.4.other_images_ref = bf16[64,1280]{1,0:T(8,128)(2,1)S(1)} collective-permute-done((bf16[64,1280]{1,0:T(8,128)(2,1)S(1)}, bf16[64,1280]{1,0:T(8,128)(2,1)S(1)}, u32[]{:S(2)}, u32[]{:S(2)}) %collective-permute-start.4) | collective-permute-done | bytes 163872 | tf_op jit(solution)/shard_map/ppermute | solution.py:218
  17.3 1.0 %tile.1 = (s16[32,1280]{1,0:T(8,128)(2,1)S(1)}, s16[32,1280]{1,0:T(8,128)(2,1)S(1)}, s16[32,1280]{1,0:T(8,128)(2,1)S(1)}, s16[32,1280]{1,0:T(8,128)(2,1)S(1)}) custom-call(f32[8,128]{1,0:T(8,128)S(1)} %get-tuple-element.16.pair_ref, bf16[64,1280]{1,0:T(8,128)(2,1)S(1)} %join_images.3.images_ref, bf16[64,1280]{1,0:T(8,128)(2,1)S(1)} %get-tuple-element.17.texts_ref, ...), custom_call_target="tpu_custom_call" | custom-call | tf_op jit(solution)/shard_map/tile/pallas_call | solution.py:194
  18.3 1.6 %collective-permute-start.6 = (s16[32,1280]{1,0:T(8,128)(2,1)S(1)}, s16[32,1280]{1,0:T(8,128)(2,1)S(1)}, u32[]{:S(2)}, u32[]{:S(2)}) collective-permute-start(s16[32,1280]{1,0:T(8,128)(2,1)S(1)} %get-tuple-element.19), channel_id=1, source_target_pairs={{0,8},{1,9},{2,10},{3,11},{4,12},{5,13},{6,14},{7,15},{8,0},{9,1},... | collective-permute-start | bytes 245768 | tf_op jit(solution)/shard_map/ppermute | solution.py:218
  19.9 1.5 %collective-permute-start.8 = (s16[32,1280]{1,0:T(8,128)(2,1)S(1)}, s16[32,1280]{1,0:T(8,128)(2,1)S(1)}, u32[]{:S(2)}, u32[]{:S(2)}) collective-permute-start(s16[32,1280]{1,0:T(8,128)(2,1)S(1)} %get-tuple-element.23), channel_id=1, source_target_pairs={{0,1},{1,0},{2,3},{3,2},{4,5},{5,4},{6,7},{7,6},{8,9},{9,8},{10,11... | collective-permute-start | bytes 245768 | tf_op jit(solution)/shard_map/ppermute | solution.py:218
  21.4 1.4 %collective-permute-done.6.refs_1_ = s16[32,1280]{1,0:T(8,128)(2,1)S(1)} collective-permute-done((s16[32,1280]{1,0:T(8,128)(2,1)S(1)}, s16[32,1280]{1,0:T(8,128)(2,1)S(1)}, u32[]{:S(2)}, u32[]{:S(2)}) %collective-permute-start.6) | collective-permute-done | bytes 81952 | tf_op jit(solution)/shard_map/ppermute | solution.py:218
  22.8 0.2 add_images.1
  23.0 2.8 %collective-permute-start.7 = (s16[16,1280]{1,0:T(8,128)(2,1)S(1)}, s16[16,1280]{1,0:T(8,128)(2,1)S(1)}, u32[]{:S(2)}, u32[]{:S(2)}) collective-permute-start(s16[16,1280]{1,0:T(8,128)(2,1)S(1)} %get-tuple-element.21), channel_id=1, source_target_pairs={{0,16},{1,17},{2,18},{3,19},{4,20},{5,21},{6,22},{7,23},{8,24},{9,... | collective-permute-start | bytes 122888 | tf_op jit(solution)/shard_map/ppermute | solution.py:218
  25.8 0.0 collective-permute-done.8.refs_1_
  25.8 0.0 copy-start.2
  25.8 0.2 add_texts.1
  26.1 0.6 %collective-permute-start.9 = (s16[16,1280]{1,0:T(8,128)(2,1)S(1)}, s16[16,1280]{1,0:T(8,128)(2,1)S(1)}, u32[]{:S(2)}, u32[]{:S(2)}) collective-permute-start(s16[16,1280]{1,0:T(8,128)(2,1)S(1)} %get-tuple-element.25), channel_id=1, source_target_pairs={{0,4},{1,5},{2,6},{3,7},{4,0},{5,1},{6,2},{7,3},{8,12},{9,13},{10,... | collective-permute-start | bytes 122888 | tf_op jit(solution)/shard_map/ppermute | solution.py:218
  26.7 1.4 %collective-permute-done.7.refs_1_ = s16[16,1280]{1,0:T(8,128)(2,1)S(1)} collective-permute-done((s16[16,1280]{1,0:T(8,128)(2,1)S(1)}, s16[16,1280]{1,0:T(8,128)(2,1)S(1)}, u32[]{:S(2)}, u32[]{:S(2)}) %collective-permute-start.7) | collective-permute-done | bytes 40992 | tf_op jit(solution)/shard_map/ppermute | solution.py:218
  28.1 2.1 %collective-permute-done.9.refs_3_ = s16[16,1280]{1,0:T(8,128)(2,1)S(1)} collective-permute-done((s16[16,1280]{1,0:T(8,128)(2,1)S(1)}, s16[16,1280]{1,0:T(8,128)(2,1)S(1)}, u32[]{:S(2)}, u32[]{:S(2)}) %collective-permute-start.9) | collective-permute-done | bytes 40992 | tf_op jit(solution)/shard_map/ppermute | solution.py:218
  30.1 0.0 copy-done.2
  30.1 0.9 %final.1 = (f32[1,16]{1,0:T(1,128)}, f32[16,1152]{1,0:T(8,128)}, f32[16,1152]{1,0:T(8,128)}) custom-call(bf16[16,1152]{1,0:T(8,128)(2,1)S(1)} %copy-done, bf16[16,1152]{1,0:T(8,128)(2,1)S(1)} %copy-done.2, s16[16,1280]{1,0:T(8,128)(2,1)S(1)} %get-tuple-element.20.refs_0_, s16[16,1280]{1,0:T(8,128)(2,1)S(1)} %collective-permute-done.7.refs_1_, ...), custom_call_target="tpu_custom_call" | custom-call | tf_op jit(solution)/shard_map/final/pallas_call | solution.py:194
  (4 shorter events, 0.0 us)
Async XLA Ops:
  0.6 5.1 %copy-start = (bf16[16,1152]{1,0:T(8,128)(2,1)S(1)}, bf16[16,1152]{1,0:T(8,128)(2,1)}, u32[]{:S(2)}) copy-start(bf16[16,1152]{1,0:T(8,128)(2,1)} %image_ref.1) | copy-start | bytes 110596
  0.6 0.8 %copy-start.1 = (bf16[16,1152]{1,0:T(8,128)(2,1)S(1)}, bf16[16,1152]{1,0:T(8,128)(2,1)}, u32[]{:S(2)}) copy-start(bf16[16,1152]{1,0:T(8,128)(2,1)} %text_ref.1) | copy-start | bytes 110596
  1.4 0.7 %copy-start.3 = (s32[16]{0:T(128)S(1)}, s32[16]{0:T(128)}, u32[]{:S(2)}) copy-start(s32[16]{0:T(128)} %class_ref.3) | copy-start | bytes 196
  2.7 6.3 %collective-permute-start = (bf16[16,1280]{1,0:T(8,128)(2,1)S(1)}, bf16[16,1280]{1,0:T(8,128)(2,1)S(1)}, u32[]{:S(2)}, u32[]{:S(2)}) collective-permute-start(bf16[16,1280]{1,0:T(8,128)(2,1)S(1)} %pack_texts.1.refs_0_), channel_id=1, source_target_pairs={{4,0},{5,1},{6,2},{7,3},{0,4},{1,5},{2,6},{3,7},{12,8},{13,9},{14,... | collective-permute-start | bytes 122888 | tf_op jit(solution)/shard_map/ppermute | solution.py:218
  6.4 5.0 %collective-permute-start.2 = (bf16[16,1280]{1,0:T(8,128)(2,1)S(1)}, bf16[16,1280]{1,0:T(8,128)(2,1)S(1)}, u32[]{:S(2)}, u32[]{:S(2)}) collective-permute-start(bf16[16,1280]{1,0:T(8,128)(2,1)S(1)} %pack_images.1.refs_0_), channel_id=1, source_target_pairs={{16,0},{17,1},{18,2},{19,3},{20,4},{21,5},{22,6},{23,7},{24,8},{25... | collective-permute-start | bytes 122888 | tf_op jit(solution)/shard_map/ppermute | solution.py:218
  9.0 5.2 %collective-permute-start.1 = (bf16[32,1280]{1,0:T(8,128)(2,1)S(1)}, bf16[32,1280]{1,0:T(8,128)(2,1)S(1)}, u32[]{:S(2)}, u32[]{:S(2)}) collective-permute-start(bf16[32,1280]{1,0:T(8,128)(2,1)S(1)} %join_texts.2.refs_0_), channel_id=1, source_target_pairs={{1,0},{0,1},{3,2},{2,3},{5,4},{4,5},{7,6},{6,7},{9,8},{8,9},{11,10... | collective-permute-start | bytes 245768 | tf_op jit(solution)/shard_map/ppermute | solution.py:218
  11.4 4.4 %collective-permute-start.3 = (bf16[32,1280]{1,0:T(8,128)(2,1)S(1)}, bf16[32,1280]{1,0:T(8,128)(2,1)S(1)}, u32[]{:S(2)}, u32[]{:S(2)}) collective-permute-start(bf16[32,1280]{1,0:T(8,128)(2,1)S(1)} %join_images.2.refs_0_), channel_id=1, source_target_pairs={{8,0},{9,1},{10,2},{11,3},{12,4},{13,5},{14,6},{15,7},{0,8},{1,9},... | collective-permute-start | bytes 245768 | tf_op jit(solution)/shard_map/ppermute | solution.py:218
  14.3 1.7 %collective-permute-start.5 = (bf16[64,1280]{1,0:T(8,128)(2,1)S(1)}, bf16[64,1280]{1,0:T(8,128)(2,1)S(1)}, u32[]{:S(2)}, u32[]{:S(2)}) collective-permute-start(bf16[64,1280]{1,0:T(8,128)(2,1)S(1)} %get-tuple-element.17.texts_ref), channel_id=1, source_target_pairs={{0,2},{1,3},{2,0},{3,1},{4,6},{5,7},{6,4},{7,5},{8,10},{9,11},{10,... | collective-permute-start | bytes 491528 | tf_op jit(solution)/shard_map/ppermute | solution.py:218
  15.8 1.5 %collective-permute-start.4 = (bf16[64,1280]{1,0:T(8,128)(2,1)S(1)}, bf16[64,1280]{1,0:T(8,128)(2,1)S(1)}, u32[]{:S(2)}, u32[]{:S(2)}) collective-permute-start(bf16[64,1280]{1,0:T(8,128)(2,1)S(1)} %join_images.3.images_ref), channel_id=1, source_target_pairs={{0,2},{1,3},{2,0},{3,1},{4,6},{5,7},{6,4},{7,5},{8,10},{9,11},{10,... | collective-permute-start | bytes 491528 | tf_op jit(solution)/shard_map/ppermute | solution.py:218
  18.3 4.6 %collective-permute-start.6 = (s16[32,1280]{1,0:T(8,128)(2,1)S(1)}, s16[32,1280]{1,0:T(8,128)(2,1)S(1)}, u32[]{:S(2)}, u32[]{:S(2)}) collective-permute-start(s16[32,1280]{1,0:T(8,128)(2,1)S(1)} %get-tuple-element.19), channel_id=1, source_target_pairs={{0,8},{1,9},{2,10},{3,11},{4,12},{5,13},{6,14},{7,15},{8,0},{9,1},... | collective-permute-start | bytes 245768 | tf_op jit(solution)/shard_map/ppermute | solution.py:218
  19.9 6.0 %collective-permute-start.8 = (s16[32,1280]{1,0:T(8,128)(2,1)S(1)}, s16[32,1280]{1,0:T(8,128)(2,1)S(1)}, u32[]{:S(2)}, u32[]{:S(2)}) collective-permute-start(s16[32,1280]{1,0:T(8,128)(2,1)S(1)} %get-tuple-element.23), channel_id=1, source_target_pairs={{0,1},{1,0},{2,3},{3,2},{4,5},{5,4},{6,7},{7,6},{8,9},{9,8},{10,11... | collective-permute-start | bytes 245768 | tf_op jit(solution)/shard_map/ppermute | solution.py:218
  23.0 5.0 %collective-permute-start.7 = (s16[16,1280]{1,0:T(8,128)(2,1)S(1)}, s16[16,1280]{1,0:T(8,128)(2,1)S(1)}, u32[]{:S(2)}, u32[]{:S(2)}) collective-permute-start(s16[16,1280]{1,0:T(8,128)(2,1)S(1)} %get-tuple-element.21), channel_id=1, source_target_pairs={{0,16},{1,17},{2,18},{3,19},{4,20},{5,21},{6,22},{7,23},{8,24},{9,... | collective-permute-start | bytes 122888 | tf_op jit(solution)/shard_map/ppermute | solution.py:218
  25.8 4.3 %copy-start.2 = (bf16[16,1152]{1,0:T(8,128)(2,1)S(1)}, bf16[16,1152]{1,0:T(8,128)(2,1)}, u32[]{:S(2)}) copy-start(bf16[16,1152]{1,0:T(8,128)(2,1)} %text_ref.1) | copy-start | bytes 110596
  26.1 4.1 %collective-permute-start.9 = (s16[16,1280]{1,0:T(8,128)(2,1)S(1)}, s16[16,1280]{1,0:T(8,128)(2,1)S(1)}, u32[]{:S(2)}, u32[]{:S(2)}) collective-permute-start(s16[16,1280]{1,0:T(8,128)(2,1)S(1)} %get-tuple-element.25), channel_id=1, source_target_pairs={{0,4},{1,5},{2,6},{3,7},{4,0},{5,1},{6,2},{7,3},{8,12},{9,13},{10,... | collective-permute-start | bytes 122888 | tf_op jit(solution)/shard_map/ppermute | solution.py:218

commit v9 on v6

v9 whole, which is shorter than its diff:
```python
import functools

import jax
import jax.numpy as jnp
from jax import lax
from jax.experimental import pallas as pl
from jax.experimental.pallas import tpu as pltpu
from jax.sharding import PartitionSpec as P

AXES = ("img", "txt")
DIGITS = 4
LANES = 128
TOP = 32767.0


def unit_rows(rows):
    wide = rows.astype(jnp.float32)
    inverse = 1.0 / jnp.sqrt(jnp.sum(wide * wide, axis=1, keepdims=True) + 1e-06)
    return (wide * inverse, inverse)


def project_back(unit, inverse, pull):
    inner = jnp.sum(unit * pull, axis=1, keepdims=True)
    return (pull - unit * inner) * inverse


def tile_terms(rows_half, row_class, cols_half, col_class, scale, shift):
    logits = (
        scale
        * lax.dot_general(
            rows_half, cols_half, (((1,), (1,)), ((), ())), preferred_element_type=jnp.float32
        )
        + shift
    )
    sign = jnp.where(row_class[:, None] == col_class[None, :], 1.0, -1.0).astype(jnp.float32)
    margin = sign * logits
    loss_part = -jnp.sum(jax.nn.log_sigmoid(margin), axis=1)
    coef = (-sign * jax.nn.sigmoid(-margin) * scale).astype(jnp.bfloat16)
    return (coef, loss_part)


def tile_plan(image_emb, text_emb, pair_class, scale, shift):
    image_unit, image_inv = unit_rows(image_emb)
    text_unit, text_inv = unit_rows(text_emb)
    own_rows = text_emb.shape[0]
    pairs = own_rows * lax.axis_size("img") * lax.axis_size("txt")
    text_half = text_unit.astype(jnp.bfloat16)
    rows_half, row_class = (
        lax.all_gather(image_unit.astype(jnp.bfloat16), "txt", axis=0, tiled=True),
        lax.all_gather(pair_class, "txt", axis=0, tiled=True),
    )
    cols_half, col_class = (
        lax.all_gather(text_half, "img", axis=0, tiled=True),
        lax.all_gather(pair_class, "img", axis=0, tiled=True),
    )
    coef, loss_part = tile_terms(rows_half, row_class, cols_half, col_class, scale, shift)
    image_pull = jnp.dot(coef, cols_half, preferred_element_type=jnp.float32)
    text_pull = lax.psum_scatter(
        lax.dot_general(
            coef, rows_half, (((0,), (0,)), ((), ())), preferred_element_type=jnp.float32
        ),
        "img",
        scatter_dimension=0,
        tiled=True,
    )
    image_sum, loss_sum = (
        lax.psum_scatter(image_pull, "txt", scatter_dimension=0, tiled=True),
        lax.psum_scatter(loss_part, "txt", scatter_dimension=0, tiled=True),
    )
    row_loss = loss_sum / pairs
    grad_image = project_back(image_unit, image_inv, image_sum)
    grad_text = project_back(text_unit, text_inv, text_pull)
    return (row_loss, grad_image, grad_text)


def on_first_core():
    return lax.rem(lax.axis_index("img"), 2) == 0


def class_digits(class_ref):
    rows = class_ref.shape[0]
    across = jnp.broadcast_to(class_ref[...][None, :], (rows, rows))
    row = lax.broadcasted_iota(jnp.int32, (rows, rows), 0)
    column = lax.broadcasted_iota(jnp.int32, (rows, rows), 1)
    lane = lax.broadcasted_iota(jnp.int32, (rows, LANES), 1)
    digits = jnp.zeros((rows, LANES), jnp.float32)
    for k in range(DIGITS):
        byte = (lax.shift_right_logical(across, 8 * k) & 255).astype(jnp.float32)
        down = jnp.sum(jnp.where(row == column, byte, 0.0), axis=1, keepdims=True)
        digits = jnp.where(lane == k, down, digits)
    return digits.astype(jnp.bfloat16)


def pack_kernel(image_ref, text_ref, class_ref, out_ref):
    rows, depth = image_ref.shape
    digits = class_digits(class_ref)
    for start, source in ((0, image_ref), (rows, text_ref)):
        out_ref[start : start + rows, :depth] = unit_rows(source[...])[0].astype(jnp.bfloat16)
        out_ref[start : start + rows, depth:] = digits


def join_kernel(scale_ref, shift_ref, own_ref, got_ref, mine_ref, other_ref, again_ref, pair_ref):
    first = on_first_core()
    rows = own_ref.shape[0] // 2
    own, got = own_ref[...].astype(jnp.float32), got_ref[...].astype(jnp.float32)
    low, high = jnp.where(first, own, got), jnp.where(first, got, own)
    images = jnp.concatenate([low[:rows], high[:rows]], axis=0)
    texts = jnp.concatenate([low[rows:], high[rows:]], axis=0)
    mine = jnp.where(first, images, texts).astype(jnp.bfloat16)
    mine_ref[...] = mine
    again_ref[...] = mine
    other_ref[...] = jnp.where(first, texts, images).astype(jnp.bfloat16)
    row = lax.broadcasted_iota(jnp.int32, pair_ref.shape, 0)
    pair_ref[...] = jnp.where(row == 0, scale_ref[0], shift_ref[0])


def gather_kernel(*refs):
    rows = refs[0].shape[0]
    for k, ref in enumerate(refs[:-1]):
        refs[-1][k * rows : (k + 1) * rows, :] = ref[...]


def power_above(size):
    return jnp.ceil(jnp.log2(jnp.maximum(size, 1e-30)) + 0.01)


def code(values, power):
    steps = jnp.clip(jnp.round(values * (TOP / jnp.exp2(power))), -TOP, TOP)
    return steps.astype(jnp.int32).astype(jnp.int16)


def decode(steps, power):
    return steps.astype(jnp.int32).astype(jnp.float32) * (jnp.exp2(power) * (1.0 / TOP))


def put_rows(outs, pull, loss):
    blocks, (rows, width) = len(outs), outs[0].shape
    depth = width - LANES
    power = power_above(jnp.max(jnp.abs(pull), axis=1, keepdims=True))
    steps = code(pull, power)
    lane = lax.broadcasted_iota(jnp.int32, (blocks * rows, LANES), 1)
    loss_power = power_above(loss)
    tail = jnp.where(lane == 0, power, 0.0)
    tail = jnp.where(lane == 1, loss_power, tail)
    tail = jnp.where(lane == 2, jnp.round(loss * (TOP / jnp.exp2(loss_power))), tail)
    tail = tail.astype(jnp.int32).astype(jnp.int16)
    for k, out in enumerate(outs):
        out[:, :depth] = steps[k * rows : (k + 1) * rows]
        out[:, depth:] = tail[k * rows : (k + 1) * rows]


def partial_pull(lines, columns, scale, shift):
    depth = lines.shape[1] - LANES
    logits = (
        scale
        * lax.dot_general(
            lines[:, :depth],
            columns[:, :depth],
            (((1,), (1,)), ((), ())),
            preferred_element_type=jnp.float32,
        )
        + shift
    )
    pick = (
        lax.broadcasted_iota(jnp.int32, (8, LANES), 0)
        == lax.broadcasted_iota(jnp.int32, (8, LANES), 1)
    )
    column_digits = lax.dot_general(
        pick.astype(jnp.bfloat16),
        columns[:, depth:],
        (((1,), (1,)), ((), ())),
        preferred_element_type=jnp.float32,
    )
    line_digits = lines[:, depth:].astype(jnp.float32)
    same = None
    for k in range(DIGITS):
        equal = line_digits[:, k : k + 1] == column_digits[k : k + 1, :]
        same = equal if same is None else same & equal
    sign = jnp.where(same, 1.0, -1.0).astype(jnp.float32)
    margin = sign * logits
    small = jnp.exp(-jnp.abs(margin))
    over = 1.0 / (1.0 + small)
    coef = -sign * jnp.where(margin >= 0, small * over, over) * scale
    pull = jnp.dot(
        coef.astype(jnp.bfloat16), columns[:, :depth], preferred_element_type=jnp.float32
    )
    loss = jnp.sum(jnp.log1p(small) - jnp.minimum(margin, 0.0), axis=1, keepdims=True)
    return pull, loss


def tile_kernel(pair_ref, mine_ref, other_ref, got_ref, swapped_ref, *outs):
    rows = mine_ref.shape[0]
    scale, shift = pair_ref[0:1, 0:1], pair_ref[1:2, 0:1]
    got = [got_ref[k * rows : (k + 1) * rows, :] for k in range(3)]
    swapped = [swapped_ref[k * rows : (k + 1) * rows, :] for k in range(3)]
    mine_side = jnp.concatenate([mine_ref[...], got[0], swapped[1], got[2]], axis=0)
    other_side = jnp.concatenate([other_ref[...], swapped[0], got[1], swapped[2]], axis=0)
    lines = jnp.concatenate([got[0], got[2], mine_ref[...]], axis=0)
    put_rows([outs[0], outs[2], outs[3]], *partial_pull(lines, other_side, scale, shift))
    put_rows([outs[1]], *partial_pull(got[1], mine_side, scale, shift))


def total(parts, rows, depth):
    pull = jnp.zeros((rows, depth), jnp.float32)
    loss = jnp.zeros((rows, 1), jnp.float32)
    for part in parts:
        tail = part[:, depth:].astype(jnp.int32).astype(jnp.float32)
        pull = pull + decode(part[:, :depth], tail[:, 0:1])
        loss = loss + tail[:, 2:3] * (jnp.exp2(tail[:, 1:2]) * (1.0 / TOP))
    return pull, loss


def place_of(first, rows):
    own = pl.multiple_of(jnp.where(first, 0, rows), rows)
    return pl.ds(own, rows), pl.ds(pl.multiple_of(rows - own, rows), rows)


def add_kernel(own_ref, back_0, back_1, back_2, keep_ref, loss_ref, give_ref):
    rows, depth = keep_ref.shape[1:]
    own, other = place_of(on_first_core(), rows)
    for side, parts in enumerate(((own_ref, back_0, back_2), (back_1,))):
        keep_ref[side], loss = total([part[own, :] for part in parts], rows, depth)
        loss_ref[side] = jnp.broadcast_to(loss, loss_ref.shape[1:])
        pull, loss = total([part[other, :] for part in parts], rows, depth)
        put_rows([give_ref.at[side * rows : (side + 1) * rows, :]], pull, loss)


def final_kernel(pairs, image_ref, text_ref, keep_ref, kept_loss_ref, got_ref, loss_ref, grad_image_ref, grad_text_ref):
    first = on_first_core()
    rows, depth = image_ref.shape
    pulls, losses = [], []
    for side in (0, 1):
        pull, loss = total([got_ref[(1 - side) * rows : (2 - side) * rows, :]], rows, depth)
        pulls.append(keep_ref[side] + pull)
        losses.append(kept_loss_ref[side][:, 0:1] + loss)
    for source, pull, out in (
        (image_ref, jnp.where(first, pulls[0], pulls[1]), grad_image_ref),
        (text_ref, jnp.where(first, pulls[1], pulls[0]), grad_text_ref),
    ):
        unit, inverse = unit_rows(source[...])
        out[...] = project_back(unit, inverse, pull)
    row = lax.broadcasted_iota(jnp.int32, (rows, rows), 0)
    column = lax.broadcasted_iota(jnp.int32, (rows, rows), 1)
    loss = jnp.where(first, losses[0], losses[1])
    across = jnp.where(row == column, loss / pairs, 0.0)
    loss_ref[...] = jnp.sum(across, axis=0, keepdims=True)


def chip_plan(image_emb, text_emb, pair_class, scale, shift):
    rows, depth = image_emb.shape
    width = depth + LANES
    lanes = lax.axis_size("txt")
    n = lax.axis_size("img") * lanes
    vmem = pl.BlockSpec(memory_space=pltpu.VMEM)
    smem = pl.BlockSpec(memory_space=pltpu.SMEM)

    def call(kernel, shapes, operands, name, scalars=0):
        return pl.pallas_call(
            kernel,
            out_shape=shapes,
            in_specs=[smem] * scalars + [vmem] * (len(operands) - scalars),
            out_specs=jax.tree.map(lambda _: vmem, shapes),
            compiler_params=pltpu.CompilerParams(vmem_limit_bytes=32 << 20),
            name=name,
        )(*operands)

    def block(count, dtype=jnp.bfloat16):
        return jax.ShapeDtypeStruct((count * rows, width), dtype)

    def wide(*shape):
        return jax.ShapeDtypeStruct(shape, jnp.float32)

    def core(i):
        return i // lanes % 2

    def visit(x, masks):
        pairs = []
        for i in range(n):
            chip = (i // (2 * lanes) * lanes + i % lanes) ^ masks[core(i)]
            pairs.append((i, (chip // lanes * 2 + core(i)) * lanes + chip % lanes))
        return lax.ppermute(x, AXES, pairs)

    def swap(x):
        return lax.ppermute(x, AXES, [(i, i ^ lanes) for i in range(n)])

    visits = ((12, 3), (2, 8), (4, 1))
    own = call(pack_kernel, block(2), [image_emb, text_emb, pair_class], "pack")
    mine, other, again, pair = call(
        join_kernel,
        (block(2), block(2), block(2), wide(8, LANES)),
        [scale[None], shift[None], own, swap(own)],
        "join",
        2,
    )
    got = [visit(x, masks) for x, masks in zip((mine, other, again), visits)]
    got = call(gather_kernel, block(6), got, "gather")
    parts = call(
        tile_kernel, (block(2, jnp.int16),) * 4, [pair, mine, other, got, swap(got)], "tile"
    )
    back = [visit(x, masks) for x, masks in zip(parts, visits)]
    keep, kept_loss, give = call(
        add_kernel,
        (wide(2, rows, depth), wide(2, rows, LANES), block(2, jnp.int16)),
        [parts[3], *back],
        "add",
    )
    loss, grad_image, grad_text = call(
        functools.partial(final_kernel, n * rows),
        (wide(1, rows), wide(rows, depth), wide(rows, depth)),
        [image_emb, text_emb, keep, kept_loss, swap(give)],
        "final",
    )
    return (loss[0], grad_image, grad_text)


def local(image_emb, text_emb, pair_class, scale, shift):
    if lax.axis_size("img") * lax.axis_size("txt") == 2 * 4 * 4 and lax.axis_size("txt") in (1, 2, 4):
        return chip_plan(image_emb, text_emb, pair_class, scale, shift)
    return tile_plan(image_emb, text_emb, pair_class, scale, shift)


def solution(mesh):
    in_specs = (P(AXES, None), P(AXES, None), P(AXES), P(), P())
    out_specs = (P(AXES), P(AXES, None), P(AXES, None))
    return jax.shard_map(local, mesh=mesh, in_specs=in_specs, out_specs=out_specs, check_vma=False)
```

time: 29.2 us -> 28.9 us (0.990)
  waiting for transfers between devices: 12 us -> 9.81 us
  starting transfers between devices: 10.8 us -> 12.3 us
  local copies, waits for them, and re-layouts: 0.89 us -> 2.19 us
  Pallas kernels: 3.24 us -> 2.29 us
    ppermute x6, waiting for transfers between devices: 9.82 us -> 7.4 us  [visit(): return lax.ppermute(x, AXES, pairs)]
    unnamed x6 -> x10, local copies, waits for them, and re-layouts: 0.89 us -> 2.19 us
    ppermute x6, starting transfers between devices: 9.86 us -> 11.1 us  [visit(): return lax.ppermute(x, AXES, pairs)]
    pallas_call x4 -> x6, Pallas kernels: 3.24 us -> 2.29 us  [call(): pl.pallas_call(kernel, out_shape=shapes, in_specs=[smem] * scalars + [vme...]
    ppermute x8 -> x3, starting transfers between devices: 0.98 us -> 1.2 us  [swap(): return lax.ppermute(x, AXES, [(i, i ^ lanes) for i in range(n)])]
    ppermute x8 -> x3, waiting for transfers between devices: 2.19 us -> 2.41 us  [swap(): return lax.ppermute(x, AXES, [(i, i ^ lanes) for i in range(n)])]
  transfers between devices with their start and end apart: 14 -> 9, of which waited for: 7 -> 7; matrix products, arithmetic and copies ran while one was open for 0% -> 0% of each run, Pallas kernels for 0% -> 0%
where the time goes in v9:
time: 28.9 us; the launch traced here: 28.6 us
  starting transfers between devices  12.3 us (43%)
  waiting for transfers between devices  9.81 us (34%)
  Pallas kernels  2.29 us (8%)
  local copies, waits for them, and re-layouts  2.19 us (8%)
  between operations  2 us (7%)
    ppermute x6, starting transfers between devices, visit(): return lax.ppermute(x, AXES, pairs)  11.1 us
    ppermute x6, waiting for transfers between devices, visit(): return lax.ppermute(x, AXES, pairs)  7.4 us
    ppermute x3, waiting for transfers between devices, swap(): return lax.ppermute(x, AXES, [(i, i ^ lanes) for i in range(n)])  2.41 us
    pallas_call x6, Pallas kernels, call(): pl.pallas_call(kernel, out_shape=shapes, in_specs=[smem] * scalars + [vme...  2.29 us
    unnamed x10, local copies, waits for them, and re-layouts  2.19 us
    ppermute x3, starting transfers between devices, swap(): return lax.ppermute(x, AXES, [(i, i ^ lanes) for i in range(n)])  1.2 us
  transfers between devices with their start and end apart: 9, of which 7 were waited for; matrix products, arithmetic and copies ran while one was open for 0% of the time, Pallas kernels for 0%

profile of v9, /device:TPU:0, one launch (start us, length us, event | category | flops | bytes accessed | tf_op | source)
XLA Modules:
  0.0 28.6 jit_solution(12676215885192713705)
XLA Ops:
  0.6 0.0 copy-start
  0.6 0.8 %copy-done = bf16[16,1152]{1,0:T(8,128)(2,1)S(1)} copy-done((bf16[16,1152]{1,0:T(8,128)(2,1)S(1)}, bf16[16,1152]{1,0:T(8,128)(2,1)}, u32[]{:S(2)}) %copy-start) | copy-done | bytes 36888
  1.4 0.0 copy-start.2
  1.4 0.8 %copy-done.2 = bf16[16,1152]{1,0:T(8,128)(2,1)S(1)} copy-done((bf16[16,1152]{1,0:T(8,128)(2,1)S(1)}, bf16[16,1152]{1,0:T(8,128)(2,1)}, u32[]{:S(2)}) %copy-start.2) | copy-done | bytes 36888
  2.2 0.0 copy-start.4
  2.2 0.7 %copy-done.4 = s32[16]{0:T(128)S(1)} copy-done((s32[16]{0:T(128)S(1)}, s32[16]{0:T(128)}, u32[]{:S(2)}) %copy-start.4) | copy-done | bytes 88
  2.8 0.1 pack.1.own_ref
  2.9 0.5 %collective-permute-start = (bf16[32,1280]{1,0:T(8,128)(2,1)S(1)}, bf16[32,1280]{1,0:T(8,128)(2,1)S(1)}, u32[]{:S(2)}, u32[]{:S(2)}) collective-permute-start(bf16[32,1280]{1,0:T(8,128)(2,1)S(1)} %pack.1.own_ref), channel_id=1, source_target_pairs={{0,2},{1,3},{2,0},{3,1},{4,6},{5,7},{6,4},{7,5},{8,10},{9,11},{10,... | collective-permute-start | bytes 245768 | tf_op jit(solution)/shard_map/ppermute | solution.py:284
  4.8 0.0 collective-permute-done.got_ref
  4.8 0.1 join.1
  4.8 2.6 %collective-permute-start.3 = (bf16[32,1280]{1,0:T(8,128)(2,1)S(1)}, bf16[32,1280]{1,0:T(8,128)(2,1)S(1)}, u32[]{:S(2)}, u32[]{:S(2)}) collective-permute-start(bf16[32,1280]{1,0:T(8,128)(2,1)S(1)} %get-tuple-element.20), channel_id=1, source_target_pairs={{0,8},{1,9},{2,3},{3,2},{4,12},{5,13},{6,7},{7,6},{8,0},{9,1},{10,... | collective-permute-start | bytes 245768 | tf_op jit(solution)/shard_map/ppermute | solution.py:281
  7.5 2.5 %collective-permute-start.1 = (bf16[32,1280]{1,0:T(8,128)(2,1)S(1)}, bf16[32,1280]{1,0:T(8,128)(2,1)S(1)}, u32[]{:S(2)}, u32[]{:S(2)}) collective-permute-start(bf16[32,1280]{1,0:T(8,128)(2,1)S(1)} %get-tuple-element.18.mine_ref), channel_id=1, source_target_pairs={{0,24},{1,25},{2,7},{3,6},{4,28},{5,29},{6,3},{7,2},{8,16},{9,17},... | collective-permute-start | bytes 245768 | tf_op jit(solution)/shard_map/ppermute | solution.py:281
  10.0 1.5 %collective-permute-start.2 = (bf16[32,1280]{1,0:T(8,128)(2,1)S(1)}, bf16[32,1280]{1,0:T(8,128)(2,1)S(1)}, u32[]{:S(2)}, u32[]{:S(2)}) collective-permute-start(bf16[32,1280]{1,0:T(8,128)(2,1)S(1)} %get-tuple-element.19.other_ref), channel_id=1, source_target_pairs={{0,4},{1,5},{2,18},{3,19},{4,0},{5,1},{6,22},{7,23},{8,12},{9,13},... | collective-permute-start | bytes 245768 | tf_op jit(solution)/shard_map/ppermute | solution.py:281
  11.5 0.0 collective-permute-done.3.refs_2_
  11.5 2.9 %collective-permute-done.1.refs_0_ = bf16[32,1280]{1,0:T(8,128)(2,1)S(1)} collective-permute-done((bf16[32,1280]{1,0:T(8,128)(2,1)S(1)}, bf16[32,1280]{1,0:T(8,128)(2,1)S(1)}, u32[]{:S(2)}, u32[]{:S(2)}) %collective-permute-start.1) | collective-permute-done | bytes 81952 | tf_op jit(solution)/shard_map/ppermute | solution.py:281
  14.3 0.1 collective-permute-done.2.refs_1_
  14.4 0.6 %collective-permute-start.4 = (bf16[96,1280]{1,0:T(8,128)(2,1)S(1)}, bf16[96,1280]{1,0:T(8,128)(2,1)S(1)}, u32[]{:S(2)}, u32[]{:S(2)}) collective-permute-start(bf16[96,1280]{1,0:T(8,128)(2,1)S(1)} %gather.1.got_ref), channel_id=1, source_target_pairs={{0,2},{1,3},{2,0},{3,1},{4,6},{5,7},{6,4},{7,5},{8,10},{9,11},{10,... | collective-permute-start | bytes 737288 | tf_op jit(solution)/shard_map/ppermute | solution.py:284
  15.0 1.1 %collective-permute-done.4.swapped_ref = bf16[96,1280]{1,0:T(8,128)(2,1)S(1)} collective-permute-done((bf16[96,1280]{1,0:T(8,128)(2,1)S(1)}, bf16[96,1280]{1,0:T(8,128)(2,1)S(1)}, u32[]{:S(2)}, u32[]{:S(2)}) %collective-permute-start.4) | collective-permute-done | bytes 245792 | tf_op jit(solution)/shard_map/ppermute | solution.py:284
  16.2 0.9 %tile.1 = (s16[32,1280]{1,0:T(8,128)(2,1)S(1)}, s16[32,1280]{1,0:T(8,128)(2,1)S(1)}, s16[32,1280]{1,0:T(8,128)(2,1)S(1)}, s16[32,1280]{1,0:T(8,128)(2,1)S(1)}) custom-call(f32[8,128]{1,0:T(8,128)S(1)} %get-tuple-element.17.pair_ref, bf16[32,1280]{1,0:T(8,128)(2,1)S(1)} %get-tuple-element.18.mine_ref, bf16[32,1280]{1,0:T(8,128)(2,1)S(1)} %get-tuple-element.19.other_ref, ...), custom_call_target="tpu_custom_call" | custom-call | tf_op jit(solution)/shard_map/tile/pallas_call | solution.py:258
  17.1 3.0 %collective-permute-start.5 = (s16[32,1280]{1,0:T(8,128)(2,1)S(1)}, s16[32,1280]{1,0:T(8,128)(2,1)S(1)}, u32[]{:S(2)}, u32[]{:S(2)}) collective-permute-start(s16[32,1280]{1,0:T(8,128)(2,1)S(1)} %get-tuple-element.22), channel_id=1, source_target_pairs={{0,24},{1,25},{2,7},{3,6},{4,28},{5,29},{6,3},{7,2},{8,16},{9,17},... | collective-permute-start | bytes 245768 | tf_op jit(solution)/shard_map/ppermute | solution.py:281
  20.1 1.5 %collective-permute-start.6 = (s16[32,1280]{1,0:T(8,128)(2,1)S(1)}, s16[32,1280]{1,0:T(8,128)(2,1)S(1)}, u32[]{:S(2)}, u32[]{:S(2)}) collective-permute-start(s16[32,1280]{1,0:T(8,128)(2,1)S(1)} %get-tuple-element.23), channel_id=1, source_target_pairs={{0,4},{1,5},{2,18},{3,19},{4,0},{5,1},{6,22},{7,23},{8,12},{9,13},... | collective-permute-start | bytes 245768 | tf_op jit(solution)/shard_map/ppermute | solution.py:281
  21.6 0.0 collective-permute-start.7
  21.6 1.9 %collective-permute-done.5.back_0 = s16[32,1280]{1,0:T(8,128)(2,1)S(1)} collective-permute-done((s16[32,1280]{1,0:T(8,128)(2,1)S(1)}, s16[32,1280]{1,0:T(8,128)(2,1)S(1)}, u32[]{:S(2)}, u32[]{:S(2)}) %collective-permute-start.5) | collective-permute-done | bytes 81952 | tf_op jit(solution)/shard_map/ppermute | solution.py:281
  23.5 1.1 %collective-permute-done.6.back_1 = s16[32,1280]{1,0:T(8,128)(2,1)S(1)} collective-permute-done((s16[32,1280]{1,0:T(8,128)(2,1)S(1)}, s16[32,1280]{1,0:T(8,128)(2,1)S(1)}, u32[]{:S(2)}, u32[]{:S(2)}) %collective-permute-start.6) | collective-permute-done | bytes 81952 | tf_op jit(solution)/shard_map/ppermute | solution.py:281
  24.6 1.5 %collective-permute-done.7.back_2 = s16[32,1280]{1,0:T(8,128)(2,1)S(1)} collective-permute-done((s16[32,1280]{1,0:T(8,128)(2,1)S(1)}, s16[32,1280]{1,0:T(8,128)(2,1)S(1)}, u32[]{:S(2)}, u32[]{:S(2)}) %collective-permute-start.7) | collective-permute-done | bytes 81952 | tf_op jit(solution)/shard_map/ppermute | solution.py:281
  26.1 0.0 copy-start.1
  26.1 0.0 copy-start.3
  26.1 0.2 add.1
  26.3 0.1 collective-permute-start.8
  26.4 1.3 %collective-permute-done.8.got_ref = s16[32,1280]{1,0:T(8,128)(2,1)S(1)} collective-permute-done((s16[32,1280]{1,0:T(8,128)(2,1)S(1)}, s16[32,1280]{1,0:T(8,128)(2,1)S(1)}, u32[]{:S(2)}, u32[]{:S(2)}) %collective-permute-start.8) | collective-permute-done | bytes 81952 | tf_op jit(solution)/shard_map/ppermute | solution.py:284
  27.7 0.0 copy-done.1
  27.7 0.0 copy-done.3
  27.7 0.9 %final.1 = (f32[1,16]{1,0:T(1,128)}, f32[16,1152]{1,0:T(8,128)}, f32[16,1152]{1,0:T(8,128)}) custom-call(bf16[16,1152]{1,0:T(8,128)(2,1)S(1)} %copy-done.1, bf16[16,1152]{1,0:T(8,128)(2,1)S(1)} %copy-done.3, f32[2,16,1152]{2,1,0:T(8,128)S(1)} %get-tuple-element.25.keep_ref, f32[2,16,128]{2,1,0:T(8,128)S(1)} %get-tuple-element.26.kept_loss_ref, ...), custom_call_target="tpu_custom_call" | custom-call | tf_op jit(solution)/shard_map/final/pallas_call | solution.py:258
  (1 shorter events, 0.0 us)
Async XLA Ops:
  0.6 0.8 %copy-start = (bf16[16,1152]{1,0:T(8,128)(2,1)S(1)}, bf16[16,1152]{1,0:T(8,128)(2,1)}, u32[]{:S(2)}) copy-start(bf16[16,1152]{1,0:T(8,128)(2,1)} %image_ref.3) | copy-start | bytes 110596
  1.4 0.8 %copy-start.2 = (bf16[16,1152]{1,0:T(8,128)(2,1)S(1)}, bf16[16,1152]{1,0:T(8,128)(2,1)}, u32[]{:S(2)}) copy-start(bf16[16,1152]{1,0:T(8,128)(2,1)} %text_ref.3) | copy-start | bytes 110596
  2.2 0.7 %copy-start.4 = (s32[16]{0:T(128)S(1)}, s32[16]{0:T(128)}, u32[]{:S(2)}) copy-start(s32[16]{0:T(128)} %class_ref.1) | copy-start | bytes 196
  2.9 1.8 %collective-permute-start = (bf16[32,1280]{1,0:T(8,128)(2,1)S(1)}, bf16[32,1280]{1,0:T(8,128)(2,1)S(1)}, u32[]{:S(2)}, u32[]{:S(2)}) collective-permute-start(bf16[32,1280]{1,0:T(8,128)(2,1)S(1)} %pack.1.own_ref), channel_id=1, source_target_pairs={{0,2},{1,3},{2,0},{3,1},{4,6},{5,7},{6,4},{7,5},{8,10},{9,11},{10,... | collective-permute-start | bytes 245768 | tf_op jit(solution)/shard_map/ppermute | solution.py:284
  4.8 6.6 %collective-permute-start.3 = (bf16[32,1280]{1,0:T(8,128)(2,1)S(1)}, bf16[32,1280]{1,0:T(8,128)(2,1)S(1)}, u32[]{:S(2)}, u32[]{:S(2)}) collective-permute-start(bf16[32,1280]{1,0:T(8,128)(2,1)S(1)} %get-tuple-element.20), channel_id=1, source_target_pairs={{0,8},{1,9},{2,3},{3,2},{4,12},{5,13},{6,7},{7,6},{8,0},{9,1},{10,... | collective-permute-start | bytes 245768 | tf_op jit(solution)/shard_map/ppermute | solution.py:281
  7.5 6.8 %collective-permute-start.1 = (bf16[32,1280]{1,0:T(8,128)(2,1)S(1)}, bf16[32,1280]{1,0:T(8,128)(2,1)S(1)}, u32[]{:S(2)}, u32[]{:S(2)}) collective-permute-start(bf16[32,1280]{1,0:T(8,128)(2,1)S(1)} %get-tuple-element.18.mine_ref), channel_id=1, source_target_pairs={{0,24},{1,25},{2,7},{3,6},{4,28},{5,29},{6,3},{7,2},{8,16},{9,17},... | collective-permute-start | bytes 245768 | tf_op jit(solution)/shard_map/ppermute | solution.py:281
  10.0 4.4 %collective-permute-start.2 = (bf16[32,1280]{1,0:T(8,128)(2,1)S(1)}, bf16[32,1280]{1,0:T(8,128)(2,1)S(1)}, u32[]{:S(2)}, u32[]{:S(2)}) collective-permute-start(bf16[32,1280]{1,0:T(8,128)(2,1)S(1)} %get-tuple-element.19.other_ref), channel_id=1, source_target_pairs={{0,4},{1,5},{2,18},{3,19},{4,0},{5,1},{6,22},{7,23},{8,12},{9,13},... | collective-permute-start | bytes 245768 | tf_op jit(solution)/shard_map/ppermute | solution.py:281
  14.4 1.7 %collective-permute-start.4 = (bf16[96,1280]{1,0:T(8,128)(2,1)S(1)}, bf16[96,1280]{1,0:T(8,128)(2,1)S(1)}, u32[]{:S(2)}, u32[]{:S(2)}) collective-permute-start(bf16[96,1280]{1,0:T(8,128)(2,1)S(1)} %gather.1.got_ref), channel_id=1, source_target_pairs={{0,2},{1,3},{2,0},{3,1},{4,6},{5,7},{6,4},{7,5},{8,10},{9,11},{10,... | collective-permute-start | bytes 737288 | tf_op jit(solution)/shard_map/ppermute | solution.py:284
  17.1 6.4 %collective-permute-start.5 = (s16[32,1280]{1,0:T(8,128)(2,1)S(1)}, s16[32,1280]{1,0:T(8,128)(2,1)S(1)}, u32[]{:S(2)}, u32[]{:S(2)}) collective-permute-start(s16[32,1280]{1,0:T(8,128)(2,1)S(1)} %get-tuple-element.22), channel_id=1, source_target_pairs={{0,24},{1,25},{2,7},{3,6},{4,28},{5,29},{6,3},{7,2},{8,16},{9,17},... | collective-permute-start | bytes 245768 | tf_op jit(solution)/shard_map/ppermute | solution.py:281
  20.1 4.4 %collective-permute-start.6 = (s16[32,1280]{1,0:T(8,128)(2,1)S(1)}, s16[32,1280]{1,0:T(8,128)(2,1)S(1)}, u32[]{:S(2)}, u32[]{:S(2)}) collective-permute-start(s16[32,1280]{1,0:T(8,128)(2,1)S(1)} %get-tuple-element.23), channel_id=1, source_target_pairs={{0,4},{1,5},{2,18},{3,19},{4,0},{5,1},{6,22},{7,23},{8,12},{9,13},... | collective-permute-start | bytes 245768 | tf_op jit(solution)/shard_map/ppermute | solution.py:281
  21.6 4.5 %collective-permute-start.7 = (s16[32,1280]{1,0:T(8,128)(2,1)S(1)}, s16[32,1280]{1,0:T(8,128)(2,1)S(1)}, u32[]{:S(2)}, u32[]{:S(2)}) collective-permute-start(s16[32,1280]{1,0:T(8,128)(2,1)S(1)} %get-tuple-element.24), channel_id=1, source_target_pairs={{0,8},{1,9},{2,3},{3,2},{4,12},{5,13},{6,7},{7,6},{8,0},{9,1},{10,... | collective-permute-start | bytes 245768 | tf_op jit(solution)/shard_map/ppermute | solution.py:281
  26.1 1.6 %copy-start.1 = (bf16[16,1152]{1,0:T(8,128)(2,1)S(1)}, bf16[16,1152]{1,0:T(8,128)(2,1)}, u32[]{:S(2)}) copy-start(bf16[16,1152]{1,0:T(8,128)(2,1)} %image_ref.3) | copy-start | bytes 110596
  26.1 1.6 %copy-start.3 = (bf16[16,1152]{1,0:T(8,128)(2,1)S(1)}, bf16[16,1152]{1,0:T(8,128)(2,1)}, u32[]{:S(2)}) copy-start(bf16[16,1152]{1,0:T(8,128)(2,1)} %text_ref.3) | copy-start | bytes 110596
  26.3 1.3 %collective-permute-start.8 = (s16[32,1280]{1,0:T(8,128)(2,1)S(1)}, s16[32,1280]{1,0:T(8,128)(2,1)S(1)}, u32[]{:S(2)}, u32[]{:S(2)}) collective-permute-start(s16[32,1280]{1,0:T(8,128)(2,1)S(1)} %get-tuple-element.27), channel_id=1, source_target_pairs={{0,2},{1,3},{2,0},{3,1},{4,6},{5,7},{6,4},{7,5},{8,10},{9,11},{10,... | collective-permute-start | bytes 245768 | tf_op jit(solution)/shard_map/ppermute | solution.py:284

commit v10 on v7

--- a/solution.py
+++ b/solution.py
@@ -24,18 +24,24 @@
     return (pull - unit * inner) * inverse
 
 
-def pack_kernel(image_ref, text_ref, class_ref, image_out, text_out):
-    rows, depth = image_ref.shape
-    row = lax.broadcasted_iota(jnp.int32, (rows, LANES), 0)
+def class_digits(class_ref):
+    rows = class_ref.shape[0]
+    across = jnp.broadcast_to(class_ref[...][None, :], (rows, rows))
+    row = lax.broadcasted_iota(jnp.int32, (rows, rows), 0)
+    column = lax.broadcasted_iota(jnp.int32, (rows, rows), 1)
     lane = lax.broadcasted_iota(jnp.int32, (rows, LANES), 1)
-    spread = jnp.zeros((rows, LANES), jnp.int32)
-    for i in range(rows):
-        spread = jnp.where(row == i, class_ref[i], spread)
-    digit = lax.shift_right_logical(spread, 8 * jnp.minimum(lane, DIGITS - 1)) & 255
-    digit = jnp.where(lane < DIGITS, digit, 0).astype(jnp.float32).astype(jnp.bfloat16)
-    for source, out in ((image_ref, image_out), (text_ref, text_out)):
-        out[:, :depth] = unit_rows(source[...])[0].astype(jnp.bfloat16)
-        out[:, depth:] = digit
+    digits = jnp.zeros((rows, LANES), jnp.float32)
+    for k in range(DIGITS):
+        byte = (lax.shift_right_logical(across, 8 * k) & 255).astype(jnp.float32)
+        down = jnp.sum(jnp.where(row == column, byte, 0.0), axis=1, keepdims=True)
+        digits = jnp.where(lane == k, down, digits)
+    return digits.astype(jnp.bfloat16)
+
+
+def pack_kernel(rows_ref, class_ref, out_ref):
+    depth = rows_ref.shape[1]
+    out_ref[:, :depth] = unit_rows(rows_ref[...])[0].astype(jnp.bfloat16)
+    out_ref[:, depth:] = class_digits(class_ref)
 
 
 def put_blocks(out_ref, refs):
@@ -68,17 +74,16 @@
     return steps.astype(jnp.int32).astype(jnp.float32) * (jnp.exp2(power) * (1.0 / TOP))
 
 
-def put_rows(outs, pull, extra):
+def put_rows(outs, pull, loss):
     blocks, (rows, width) = len(outs), outs[0].shape
     depth = width - LANES
     power = power_above(jnp.max(jnp.abs(pull), axis=1, keepdims=True))
     steps = code(pull, power)
     lane = lax.broadcasted_iota(jnp.int32, (blocks * rows, LANES), 1)
+    loss_power = power_above(loss)
     tail = jnp.where(lane == 0, power, 0.0)
-    if extra is not None:
-        loss_power = power_above(extra)
-        tail = jnp.where(lane == 1, loss_power, tail)
-        tail = jnp.where(lane == 2, jnp.round(extra * (TOP / jnp.exp2(loss_power))), tail)
+    tail = jnp.where(lane == 1, loss_power, tail)
+    tail = jnp.where(lane == 2, jnp.round(loss * (TOP / jnp.exp2(loss_power))), tail)
     tail = tail.astype(jnp.int32).astype(jnp.int16)
     for k, out in enumerate(outs):
         out[:, :depth] = steps[k * rows : (k + 1) * rows]
@@ -124,17 +129,11 @@
     return pull, loss
 
 
-def tile_kernel(a, pair_ref, images_ref, texts_ref, other_images_ref, other_texts_ref, *outs):
+def lines_kernel(pair_ref, lines_ref, columns_ref, other_columns_ref, out_ref):
     scale, shift = pair_ref[0:1, 0:1], pair_ref[1:2, 0:1]
-    images, texts = images_ref[...], texts_ref[...]
-    pull, loss = partial_pull(
-        images, jnp.concatenate([texts, other_texts_ref[...]], axis=0), scale, shift
-    )
-    put_rows(outs[:a][::-1], pull, loss)
-    pull, _ = partial_pull(
-        texts, jnp.concatenate([images, other_images_ref[...]], axis=0), scale, shift
-    )
-    put_rows(outs[a:][::-1], pull, None)
+    columns = jnp.concatenate([columns_ref[...], other_columns_ref[...]], axis=0)
+    pull, loss = partial_pull(lines_ref[...], columns, scale, shift)
+    put_rows([out_ref], pull, loss)
 
 
 def final_kernel(a, b, image_ref, text_ref, *refs):
@@ -194,64 +193,83 @@
     def move(x, pairs):
         return lax.ppermute(x, AXES, pairs)
 
-    def collect(x, size, along):
-        return [x] + [move(x, [(along(i, k), i) for i in range(n)]) for k in range(1, size)]
-
-    def give_back(parts, along):
-        steps = range(len(parts) - 1, 0, -1)
-        return [move(x, [(i, along(i, k)) for i in range(n)]) for x, k in zip(parts, steps)] + [parts[-1]]
+    def call(kernel, shapes, operands, name, scalars=0, after=()):
+        def body(*refs):
+            kernel(*refs[len(after) :])
+
+        return pl.pallas_call(
+            body,
+            out_shape=shapes,
+            in_specs=[pl.BlockSpec(memory_space=pl.ANY)] * len(after)
+            + [smem] * scalars
+            + [vmem] * (len(operands) - scalars),
+            out_specs=jax.tree.map(lambda _: vmem, shapes),
+            compiler_params=params,
+            name=name,
+        )(*after, *operands)
+
+    def block(count, dtype=jnp.bfloat16):
+        return jax.ShapeDtypeStruct((count * rows, width), dtype)
+
+    def wide(*shape):
+        return jax.ShapeDtypeStruct(shape, jnp.float32)
+
+    def fetch(x, k, along):
+        return move(x, [(along(i, k), i) for i in range(n)])
+
+    def give(x, k, along):
+        return move(x, [(i, along(i, k)) for i in range(n)])
 
     def swap(x):
         return move(x, [(i, place(split(i)[0], 1 - split(i)[1])) for i in range(n)])
 
-    block = jax.ShapeDtypeStruct((rows, width), jnp.bfloat16)
-    image_rows, text_rows = pl.pallas_call(
-        pack_kernel,
-        out_shape=(block, block),
-        in_specs=[vmem, vmem, smem],
-        out_specs=(vmem, vmem),
-        name="pack",
-    )(image_emb, text_emb, pair_class)
-    images = pl.pallas_call(
-        join_kernel,
-        out_shape=jax.ShapeDtypeStruct((a * rows, width), jnp.bfloat16),
-        in_specs=[vmem] * a,
-        out_specs=vmem,
-        compiler_params=params,
-        name="join_images",
-    )(*collect(image_rows, a, along_a))
-    texts, pair = pl.pallas_call(
+    far_a, far_b = range(a - 1, 0, -1), range(b - 1, 0, -1)
+    own_texts = call(pack_kernel, block(1), [text_emb, pair_class], "pack_texts")
+    own_images = call(
+        pack_kernel, block(1), [image_emb, pair_class], "pack_images", after=[own_texts]
+    )
+    texts = [own_texts] + [fetch(own_texts, k, along_b) for k in far_b]
+    got_texts = dict(zip([0, *far_b], texts))
+    images = [own_images] + [fetch(own_images, k, along_a) for k in far_a]
+    texts, pair = call(
         join_with_pair_kernel,
-        out_shape=(
-            jax.ShapeDtypeStruct((b * rows, width), jnp.bfloat16),
-            jax.ShapeDtypeStruct((8, LANES), jnp.float32),
-        ),
-        in_specs=[smem, smem] + [vmem] * b,
-        out_specs=(vmem, vmem),
-        compiler_params=params,
-        name="join_texts",
-    )(scale[None], shift[None], *collect(text_rows, b, along_b))
-    parts = pl.pallas_call(
-        functools.partial(tile_kernel, a),
-        out_shape=(jax.ShapeDtypeStruct((rows, width), jnp.int16),) * (a + b),
-        in_specs=[vmem] * 5,
-        out_specs=(vmem,) * (a + b),
-        compiler_params=params,
-        name="tile",
-    )(pair, images, texts, swap(images), swap(texts))
-    parts = give_back(parts[:a], along_a) + give_back(parts[a:], along_b)
-    loss, grad_image, grad_text = pl.pallas_call(
+        (block(b), wide(8, LANES)),
+        [scale[None], shift[None], *texts[::-1]],
+        "join_texts",
+        2,
+        after=images[2:0:-1],
+    )
+    other_texts = swap(texts)
+    image_parts = [
+        call(
+            lines_kernel,
+            block(1, jnp.int16),
+            [pair, x, texts, other_texts],
+            "image_lines",
+        )
+        for x in images
+    ]
+    given = [give(x, k, along_a) for x, k in zip(image_parts[1:], far_a)]
+    images = call(join_kernel, block(a), images, "join_images", after=image_parts[1:-1])
+    other_images = swap(images)
+    text_parts = []
+    for position, k in enumerate([*far_b, 0]):
+        after = given[position - 1 : position] if position else []
+        part = call(
+            lines_kernel,
+            block(1, jnp.int16),
+            [pair, got_texts[k], images, other_images],
+            "text_lines",
+            after=after,
+        )
+        text_parts.append(give(part, k, along_b) if k else part)
+    image_parts = [image_parts[0]] + given
+    loss, grad_image, grad_text = call(
         functools.partial(final_kernel, a, b),
-        out_shape=(
-            jax.ShapeDtypeStruct((1, rows), jnp.float32),
-            jax.ShapeDtypeStruct((rows, depth), jnp.float32),
-            jax.ShapeDtypeStruct((rows, depth), jnp.float32),
-        ),
-        in_specs=[vmem] * (2 + a + b),
-        out_specs=(vmem, vmem, vmem),
-        compiler_params=params,
-        name="final",
-    )(image_emb, text_emb, *parts)
+        (wide(1, rows), wide(rows, depth), wide(rows, depth)),
+        [image_emb, text_emb, *image_parts, *text_parts],
+        "final",
+    )
     return (loss[0], grad_image, grad_text)
 
 

time: 29.1 us -> 33.5 us (1.15)
  Pallas kernels: 3.43 us -> 5.68 us
  local copies, waits for them, and re-layouts: 0.79 us -> 2.09 us
  starting transfers between devices: 17.2 us -> 17.8 us
    pallas_call x5 -> x13, Pallas kernels: 3.43 us -> 5.68 us  [call(): pl.pallas_call(body, out_shape=shapes, in_specs=[pl.BlockSpec(memory_spac...]
    unnamed x8 -> x10, local copies, waits for them, and re-layouts: 0.79 us -> 2.09 us
    ppermute x14, starting transfers between devices: 17.2 us -> 17.8 us  [move(): return lax.ppermute(x, AXES, pairs)]
  transfers between devices with their start and end apart: 14 -> 14, of which waited for: 7 -> 8; matrix products, arithmetic and copies ran while one was open for 0% -> 0% of each run, Pallas kernels for 0% -> 14%
where the time goes in v10:
time: 33.5 us; the launch traced here: 33.2 us
  starting transfers between devices  17.8 us (53%)
  Pallas kernels  5.68 us (17%)
  waiting for transfers between devices  5.56 us (17%)
  local copies, waits for them, and re-layouts  2.09 us (6%)
  between operations  2.08 us (6%)
    ppermute x14, starting transfers between devices, move(): return lax.ppermute(x, AXES, pairs)  17.8 us
    pallas_call x13, Pallas kernels, call(): pl.pallas_call(body, out_shape=shapes, in_specs=[pl.BlockSpec(memory_spac...  5.68 us
    ppermute x14, waiting for transfers between devices, move(): return lax.ppermute(x, AXES, pairs)  5.56 us
    unnamed x10, local copies, waits for them, and re-layouts  2.09 us
  transfers between devices with their start and end apart: 14, of which 8 were waited for; matrix products, arithmetic and copies ran while one was open for 0% of the time, Pallas kernels for 14%

profile of v10, /device:TPU:0, one launch (start us, length us, event | category | flops | bytes accessed | tf_op | source)
XLA Modules:
  0.0 33.2 jit_solution(18098503202700106995)
XLA Ops:
  0.6 0.0 copy-start
  0.6 0.8 %copy-done = bf16[16,1152]{1,0:T(8,128)(2,1)S(1)} copy-done((bf16[16,1152]{1,0:T(8,128)(2,1)S(1)}, bf16[16,1152]{1,0:T(8,128)(2,1)}, u32[]{:S(2)}) %copy-start) | copy-done | bytes 36888
  1.4 0.0 copy-start.3
  1.4 0.7 %copy-done.3 = s32[16]{0:T(128)S(1)} copy-done((s32[16]{0:T(128)S(1)}, s32[16]{0:T(128)}, u32[]{:S(2)}) %copy-start.3) | copy-done | bytes 88
  2.1 0.0 copy-start.2
  2.1 0.0 copy-start.4
  2.1 0.1 pack_texts.1.refs_0_.refs_7_.refs_2_
  2.2 0.7 %copy-done.2 = bf16[16,1152]{1,0:T(8,128)(2,1)S(1)} copy-done((bf16[16,1152]{1,0:T(8,128)(2,1)S(1)}, bf16[16,1152]{1,0:T(8,128)(2,1)}, u32[]{:S(2)}) %copy-start.2) | copy-done | bytes 36888
  2.8 0.0 copy-done.4
  2.8 0.1 pack_images.1.refs_1_.refs_2_
  2.9 5.1 %collective-permute-start.1 = (bf16[16,1280]{1,0:T(8,128)(2,1)S(1)}, bf16[16,1280]{1,0:T(8,128)(2,1)S(1)}, u32[]{:S(2)}, u32[]{:S(2)}) collective-permute-start(bf16[16,1280]{1,0:T(8,128)(2,1)S(1)} %pack_images.1.refs_1_.refs_2_), channel_id=1, source_target_pairs={{24,0},{25,1},{26,2},{27,3},{28,4},{29,5},{30,6},{31,7},{16,8},{17... | collective-permute-start | bytes 122888 | tf_op jit(solution)/shard_map/ppermute | solution.py:194
  8.1 0.0 collective-permute-start
  8.1 2.4 %collective-permute-start.4 = (bf16[16,1280]{1,0:T(8,128)(2,1)S(1)}, bf16[16,1280]{1,0:T(8,128)(2,1)S(1)}, u32[]{:S(2)}, u32[]{:S(2)}) collective-permute-start(bf16[16,1280]{1,0:T(8,128)(2,1)S(1)} %pack_texts.1.refs_0_.refs_7_.refs_2_), channel_id=1, source_target_pairs={{5,0},{4,1},{7,2},{6,3},{1,4},{0,5},{3,6},{2,7},{13,8},{12,9},{15,... | collective-permute-start | bytes 122888 | tf_op jit(solution)/shard_map/ppermute | solution.py:194
  10.5 0.5 %collective-permute-start.3 = (bf16[16,1280]{1,0:T(8,128)(2,1)S(1)}, bf16[16,1280]{1,0:T(8,128)(2,1)S(1)}, u32[]{:S(2)}, u32[]{:S(2)}) collective-permute-start(bf16[16,1280]{1,0:T(8,128)(2,1)S(1)} %pack_texts.1.refs_0_.refs_7_.refs_2_), channel_id=1, source_target_pairs={{4,0},{5,1},{6,2},{7,3},{0,4},{1,5},{2,6},{3,7},{12,8},{13,9},{14,... | collective-permute-start | bytes 122888 | tf_op jit(solution)/shard_map/ppermute | solution.py:194
  11.0 0.5 %collective-permute-start.2 = (bf16[16,1280]{1,0:T(8,128)(2,1)S(1)}, bf16[16,1280]{1,0:T(8,128)(2,1)S(1)}, u32[]{:S(2)}, u32[]{:S(2)}) collective-permute-start(bf16[16,1280]{1,0:T(8,128)(2,1)S(1)} %pack_texts.1.refs_0_.refs_7_.refs_2_), channel_id=1, source_target_pairs={{1,0},{0,1},{3,2},{2,3},{5,4},{4,5},{7,6},{6,7},{9,8},{8,9},{11,10... | collective-permute-start | bytes 122888 | tf_op jit(solution)/shard_map/ppermute | solution.py:194
  12.8 0.0 collective-permute-done.1.refs_1_.refs_3_
  12.9 0.1 collective-permute-done.refs_0_.refs_1_.refs_4_
  13.0 0.3 %collective-permute-done.4.refs_6_.refs_1_ = bf16[16,1280]{1,0:T(8,128)(2,1)S(1)} collective-permute-done((bf16[16,1280]{1,0:T(8,128)(2,1)S(1)}, bf16[16,1280]{1,0:T(8,128)(2,1)S(1)}, u32[]{:S(2)}, u32[]{:S(2)}) %collective-permute-start.4) | collective-permute-done | bytes 40992 | tf_op jit(solution)/shard_map/ppermute | solution.py:194
  13.3 1.2 %collective-permute-done.3.refs_5_.refs_2_ = bf16[16,1280]{1,0:T(8,128)(2,1)S(1)} collective-permute-done((bf16[16,1280]{1,0:T(8,128)(2,1)S(1)}, bf16[16,1280]{1,0:T(8,128)(2,1)S(1)}, u32[]{:S(2)}, u32[]{:S(2)}) %collective-permute-start.3) | collective-permute-done | bytes 40992 | tf_op jit(solution)/shard_map/ppermute | solution.py:194
  14.5 0.5 %collective-permute-done.2.refs_4_.refs_2_ = bf16[16,1280]{1,0:T(8,128)(2,1)S(1)} collective-permute-done((bf16[16,1280]{1,0:T(8,128)(2,1)S(1)}, bf16[16,1280]{1,0:T(8,128)(2,1)S(1)}, u32[]{:S(2)}, u32[]{:S(2)}) %collective-permute-start.2) | collective-permute-done | bytes 40992 | tf_op jit(solution)/shard_map/ppermute | solution.py:194
  15.1 0.1 collective-permute-start.5
  15.1 0.8 %collective-permute-start.8 = (bf16[16,1280]{1,0:T(8,128)(2,1)S(1)}, bf16[16,1280]{1,0:T(8,128)(2,1)S(1)}, u32[]{:S(2)}, u32[]{:S(2)}) collective-permute-start(bf16[16,1280]{1,0:T(8,128)(2,1)S(1)} %pack_images.1.refs_1_.refs_2_), channel_id=1, source_target_pairs={{8,0},{9,1},{10,2},{11,3},{12,4},{13,5},{14,6},{15,7},{0,8},{1,9},... | collective-permute-start | bytes 122888 | tf_op jit(solution)/shard_map/ppermute | solution.py:194
  16.0 0.5 %collective-permute-done.5.refs_3_ = bf16[64,1280]{1,0:T(8,128)(2,1)S(1)} collective-permute-done((bf16[64,1280]{1,0:T(8,128)(2,1)S(1)}, bf16[64,1280]{1,0:T(8,128)(2,1)S(1)}, u32[]{:S(2)}, u32[]{:S(2)}) %collective-permute-start.5) | collective-permute-done | bytes 163872 | tf_op jit(solution)/shard_map/ppermute | solution.py:194
  16.5 0.6 %image_lines.6.refs_1_ = s16[16,1280]{1,0:T(8,128)(2,1)S(1)} custom-call(f32[8,128]{1,0:T(8,128)S(1)} %get-tuple-element.8.refs_0_.refs_1_, bf16[16,1280]{1,0:T(8,128)(2,1)S(1)} %collective-permute-done.refs_0_.refs_1_.refs_4_, bf16[64,1280]{1,0:T(8,128)(2,1)S(1)} %get-tuple-element.9.refs_2_, bf16[64,1280]{1,0:T(8,128)(2,1)S(1)} %collective-permute-done.5.refs_3_), custom_call_target="tpu_custom_call" | custom-call | tf_op jit(solution)/shard_map/image_lines/pallas_call | solution.py:200
  17.1 0.6 %image_lines.5.refs_0_ = s16[16,1280]{1,0:T(8,128)(2,1)S(1)} custom-call(f32[8,128]{1,0:T(8,128)S(1)} %get-tuple-element.8.refs_0_.refs_1_, bf16[16,1280]{1,0:T(8,128)(2,1)S(1)} %collective-permute-done.1.refs_1_.refs_3_, bf16[64,1280]{1,0:T(8,128)(2,1)S(1)} %get-tuple-element.9.refs_2_, bf16[64,1280]{1,0:T(8,128)(2,1)S(1)} %collective-permute-done.5.refs_3_), custom_call_target="tpu_custom_call" | custom-call | tf_op jit(solution)/shard_map/image_lines/pallas_call | solution.py:200
  17.7 1.5 %collective-permute-done.8.refs_1_.refs_5_ = bf16[16,1280]{1,0:T(8,128)(2,1)S(1)} collective-permute-done((bf16[16,1280]{1,0:T(8,128)(2,1)S(1)}, bf16[16,1280]{1,0:T(8,128)(2,1)S(1)}, u32[]{:S(2)}, u32[]{:S(2)}) %collective-permute-start.8) | collective-permute-done | bytes 40992 | tf_op jit(solution)/shard_map/ppermute | solution.py:194
  19.2 0.1 collective-permute-start.10
  19.3 2.6 %collective-permute-start.6 = (s16[16,1280]{1,0:T(8,128)(2,1)S(1)}, s16[16,1280]{1,0:T(8,128)(2,1)S(1)}, u32[]{:S(2)}, u32[]{:S(2)}) collective-permute-start(s16[16,1280]{1,0:T(8,128)(2,1)S(1)} %image_lines.5.refs_0_), channel_id=1, source_target_pairs={{0,24},{1,25},{2,26},{3,27},{4,28},{5,29},{6,30},{7,31},{8,16},{9,... | collective-permute-start | bytes 122888 | tf_op jit(solution)/shard_map/ppermute | solution.py:194
  21.9 0.5 %collective-permute-start.7 = (s16[16,1280]{1,0:T(8,128)(2,1)S(1)}, s16[16,1280]{1,0:T(8,128)(2,1)S(1)}, u32[]{:S(2)}, u32[]{:S(2)}) collective-permute-start(s16[16,1280]{1,0:T(8,128)(2,1)S(1)} %image_lines.6.refs_1_), channel_id=1, source_target_pairs={{0,16},{1,17},{2,18},{3,19},{4,20},{5,21},{6,22},{7,23},{8,24},{9,... | collective-permute-start | bytes 122888 | tf_op jit(solution)/shard_map/ppermute | solution.py:194
  22.4 0.6 %image_lines.7 = s16[16,1280]{1,0:T(8,128)(2,1)S(1)} custom-call(f32[8,128]{1,0:T(8,128)S(1)} %get-tuple-element.8.refs_0_.refs_1_, bf16[16,1280]{1,0:T(8,128)(2,1)S(1)} %collective-permute-done.8.refs_1_.refs_5_, bf16[64,1280]{1,0:T(8,128)(2,1)S(1)} %get-tuple-element.9.refs_2_, bf16[64,1280]{1,0:T(8,128)(2,1)S(1)} %collective-permute-done.5.refs_3_), custom_call_target="tpu_custom_call" | custom-call | tf_op jit(solution)/shard_map/image_lines/pallas_call | solution.py:200
  22.9 1.5 %collective-permute-start.9 = (s16[16,1280]{1,0:T(8,128)(2,1)S(1)}, s16[16,1280]{1,0:T(8,128)(2,1)S(1)}, u32[]{:S(2)}, u32[]{:S(2)}) collective-permute-start(s16[16,1280]{1,0:T(8,128)(2,1)S(1)} %image_lines.7), channel_id=1, source_target_pairs={{0,8},{1,9},{2,10},{3,11},{4,12},{5,13},{6,14},{7,15},{8,0},{9,1},... | collective-permute-start | bytes 122888 | tf_op jit(solution)/shard_map/ppermute | solution.py:194
  24.4 0.0 collective-permute-done.10.refs_3_.refs_4_
  24.4 0.6 %text_lines.4 = s16[16,1280]{1,0:T(8,128)(2,1)S(1)} custom-call(f32[8,128]{1,0:T(8,128)S(1)} %get-tuple-element.8.refs_0_.refs_1_, bf16[16,1280]{1,0:T(8,128)(2,1)S(1)} %collective-permute-done.4.refs_6_.refs_1_, bf16[64,1280]{1,0:T(8,128)(2,1)S(1)} %join_images.1.refs_2_.refs_3_, bf16[64,1280]{1,0:T(8,128)(2,1)S(1)} %collective-permute-done.10.refs_3_.refs_4_), custom_call_target="tpu_custom_call" | custom-call | tf_op jit(solution)/shard_map/text_lines/pallas_call | solution.py:200
  25.0 1.5 %collective-permute-start.11 = (s16[16,1280]{1,0:T(8,128)(2,1)S(1)}, s16[16,1280]{1,0:T(8,128)(2,1)S(1)}, u32[]{:S(2)}, u32[]{:S(2)}) collective-permute-start(s16[16,1280]{1,0:T(8,128)(2,1)S(1)} %text_lines.4), channel_id=1, source_target_pairs={{0,5},{1,4},{2,7},{3,6},{4,1},{5,0},{6,3},{7,2},{8,13},{9,12},{10,... | collective-permute-start | bytes 122888 | tf_op jit(solution)/shard_map/ppermute | solution.py:194
  26.5 0.0 collective-permute-done.6.refs_0_.refs_3_
  26.5 0.6 %text_lines.5 = s16[16,1280]{1,0:T(8,128)(2,1)S(1)} custom-call(s16[16,1280]{1,0:T(8,128)(2,1)S(1)} %collective-permute-done.6.refs_0_.refs_3_, f32[8,128]{1,0:T(8,128)S(1)} %get-tuple-element.8.refs_0_.refs_1_, bf16[16,1280]{1,0:T(8,128)(2,1)S(1)} %collective-permute-done.3.refs_5_.refs_2_, bf16[64,1280]{1,0:T(8,128)(2,1)S(1)} %join_images.1.refs_2_.refs_3_, ...), custom_call_target="tpu_custom_call" | custom-call | tf_op jit(solution)/shard_map/text_lines/pallas_call | solution.py:200
  27.0 0.6 %collective-permute-start.12 = (s16[16,1280]{1,0:T(8,128)(2,1)S(1)}, s16[16,1280]{1,0:T(8,128)(2,1)S(1)}, u32[]{:S(2)}, u32[]{:S(2)}) collective-permute-start(s16[16,1280]{1,0:T(8,128)(2,1)S(1)} %text_lines.5), channel_id=1, source_target_pairs={{0,4},{1,5},{2,6},{3,7},{4,0},{5,1},{6,2},{7,3},{8,12},{9,13},{10,... | collective-permute-start | bytes 122888 | tf_op jit(solution)/shard_map/ppermute | solution.py:194
  27.6 0.0 collective-permute-done.7.refs_0_.refs_4_
  27.7 0.6 %text_lines.6 = s16[16,1280]{1,0:T(8,128)(2,1)S(1)} custom-call(s16[16,1280]{1,0:T(8,128)(2,1)S(1)} %collective-permute-done.7.refs_0_.refs_4_, f32[8,128]{1,0:T(8,128)S(1)} %get-tuple-element.8.refs_0_.refs_1_, bf16[16,1280]{1,0:T(8,128)(2,1)S(1)} %collective-permute-done.2.refs_4_.refs_2_, bf16[64,1280]{1,0:T(8,128)(2,1)S(1)} %join_images.1.refs_2_.refs_3_, ...), custom_call_target="tpu_custom_call" | custom-call | tf_op jit(solution)/shard_map/text_lines/pallas_call | solution.py:200
  28.2 1.6 %collective-permute-start.13 = (s16[16,1280]{1,0:T(8,128)(2,1)S(1)}, s16[16,1280]{1,0:T(8,128)(2,1)S(1)}, u32[]{:S(2)}, u32[]{:S(2)}) collective-permute-start(s16[16,1280]{1,0:T(8,128)(2,1)S(1)} %text_lines.6), channel_id=1, source_target_pairs={{0,1},{1,0},{2,3},{3,2},{4,5},{5,4},{6,7},{7,6},{8,9},{9,8},{10,11... | collective-permute-start | bytes 122888 | tf_op jit(solution)/shard_map/ppermute | solution.py:194
  29.8 0.6 %image_lines.4.refs_2_ = s16[16,1280]{1,0:T(8,128)(2,1)S(1)} custom-call(f32[8,128]{1,0:T(8,128)S(1)} %get-tuple-element.8.refs_0_.refs_1_, bf16[16,1280]{1,0:T(8,128)(2,1)S(1)} %pack_images.1.refs_1_.refs_2_, bf16[64,1280]{1,0:T(8,128)(2,1)S(1)} %get-tuple-element.9.refs_2_, bf16[64,1280]{1,0:T(8,128)(2,1)S(1)} %collective-permute-done.5.refs_3_), custom_call_target="tpu_custom_call" | custom-call | tf_op jit(solution)/shard_map/image_lines/pallas_call | solution.py:200
  30.4 0.0 copy-start.1
  30.4 0.0 collective-permute-done.9.refs_0_.refs_5_
  30.4 0.6 %text_lines.7.refs_9_ = s16[16,1280]{1,0:T(8,128)(2,1)S(1)} custom-call(s16[16,1280]{1,0:T(8,128)(2,1)S(1)} %collective-permute-done.9.refs_0_.refs_5_, f32[8,128]{1,0:T(8,128)S(1)} %get-tuple-element.8.refs_0_.refs_1_, bf16[16,1280]{1,0:T(8,128)(2,1)S(1)} %pack_texts.1.refs_0_.refs_7_.refs_2_, bf16[64,1280]{1,0:T(8,128)(2,1)S(1)} %join_images.1.refs_2_.refs_3_, ...), custom_call_target="tpu_custom_call" | custom-call | tf_op jit(solution)/shard_map/text_lines/pallas_call | solution.py:200
  31.0 0.0 collective-permute-done.11.refs_6_
  31.0 0.1 collective-permute-done.12.refs_7_
  31.1 1.2 %collective-permute-done.13.refs_8_ = s16[16,1280]{1,0:T(8,128)(2,1)S(1)} collective-permute-done((s16[16,1280]{1,0:T(8,128)(2,1)S(1)}, s16[16,1280]{1,0:T(8,128)(2,1)S(1)}, u32[]{:S(2)}, u32[]{:S(2)}) %collective-permute-start.13) | collective-permute-done | bytes 40992 | tf_op jit(solution)/shard_map/ppermute | solution.py:194
  32.3 0.0 copy-done.1
  32.3 0.9 %final.1 = (f32[1,16]{1,0:T(1,128)}, f32[16,1152]{1,0:T(8,128)}, f32[16,1152]{1,0:T(8,128)}) custom-call(bf16[16,1152]{1,0:T(8,128)(2,1)S(1)} %copy-done.2, bf16[16,1152]{1,0:T(8,128)(2,1)S(1)} %copy-done.1, s16[16,1280]{1,0:T(8,128)(2,1)S(1)} %image_lines.4.refs_2_, s16[16,1280]{1,0:T(8,128)(2,1)S(1)} %collective-permute-done.6.refs_0_.refs_3_, ...), custom_call_target="tpu_custom_call" | custom-call | tf_op jit(solution)/shard_map/final/pallas_call | solution.py:200
  (2 shorter events, 0.0 us)
Async XLA Ops:
  0.6 0.8 %copy-start = (bf16[16,1152]{1,0:T(8,128)(2,1)S(1)}, bf16[16,1152]{1,0:T(8,128)(2,1)}, u32[]{:S(2)}) copy-start(bf16[16,1152]{1,0:T(8,128)(2,1)} %refs_1_.5) | copy-start | bytes 110596
  1.4 0.7 %copy-start.3 = (s32[16]{0:T(128)S(1)}, s32[16]{0:T(128)}, u32[]{:S(2)}) copy-start(s32[16]{0:T(128)} %refs_2_.1) | copy-start | bytes 196
  2.1 0.8 %copy-start.2 = (bf16[16,1152]{1,0:T(8,128)(2,1)S(1)}, bf16[16,1152]{1,0:T(8,128)(2,1)}, u32[]{:S(2)}) copy-start(bf16[16,1152]{1,0:T(8,128)(2,1)} %refs_0_.3) | copy-start | bytes 110596
  2.1 0.8 %copy-start.4 = (s32[16]{0:T(128)S(1)}, s32[16]{0:T(128)}, u32[]{:S(2)}) copy-start(s32[16]{0:T(128)} %refs_2_.1) | copy-start | bytes 196
  2.9 9.9 %collective-permute-start.1 = (bf16[16,1280]{1,0:T(8,128)(2,1)S(1)}, bf16[16,1280]{1,0:T(8,128)(2,1)S(1)}, u32[]{:S(2)}, u32[]{:S(2)}) collective-permute-start(bf16[16,1280]{1,0:T(8,128)(2,1)S(1)} %pack_images.1.refs_1_.refs_2_), channel_id=1, source_target_pairs={{24,0},{25,1},{26,2},{27,3},{28,4},{29,5},{30,6},{31,7},{16,8},{17... | collective-permute-start | bytes 122888 | tf_op jit(solution)/shard_map/ppermute | solution.py:194
  8.1 4.9 %collective-permute-start = (bf16[16,1280]{1,0:T(8,128)(2,1)S(1)}, bf16[16,1280]{1,0:T(8,128)(2,1)S(1)}, u32[]{:S(2)}, u32[]{:S(2)}) collective-permute-start(bf16[16,1280]{1,0:T(8,128)(2,1)S(1)} %pack_images.1.refs_1_.refs_2_), channel_id=1, source_target_pairs={{16,0},{17,1},{18,2},{19,3},{20,4},{21,5},{22,6},{23,7},{24,8},{25... | collective-permute-start | bytes 122888 | tf_op jit(solution)/shard_map/ppermute | solution.py:194
  8.1 5.2 %collective-permute-start.4 = (bf16[16,1280]{1,0:T(8,128)(2,1)S(1)}, bf16[16,1280]{1,0:T(8,128)(2,1)S(1)}, u32[]{:S(2)}, u32[]{:S(2)}) collective-permute-start(bf16[16,1280]{1,0:T(8,128)(2,1)S(1)} %pack_texts.1.refs_0_.refs_7_.refs_2_), channel_id=1, source_target_pairs={{5,0},{4,1},{7,2},{6,3},{1,4},{0,5},{3,6},{2,7},{13,8},{12,9},{15,... | collective-permute-start | bytes 122888 | tf_op jit(solution)/shard_map/ppermute | solution.py:194
  10.5 4.0 %collective-permute-start.3 = (bf16[16,1280]{1,0:T(8,128)(2,1)S(1)}, bf16[16,1280]{1,0:T(8,128)(2,1)S(1)}, u32[]{:S(2)}, u32[]{:S(2)}) collective-permute-start(bf16[16,1280]{1,0:T(8,128)(2,1)S(1)} %pack_texts.1.refs_0_.refs_7_.refs_2_), channel_id=1, source_target_pairs={{4,0},{5,1},{6,2},{7,3},{0,4},{1,5},{2,6},{3,7},{12,8},{13,9},{14,... | collective-permute-start | bytes 122888 | tf_op jit(solution)/shard_map/ppermute | solution.py:194
  11.0 4.0 %collective-permute-start.2 = (bf16[16,1280]{1,0:T(8,128)(2,1)S(1)}, bf16[16,1280]{1,0:T(8,128)(2,1)S(1)}, u32[]{:S(2)}, u32[]{:S(2)}) collective-permute-start(bf16[16,1280]{1,0:T(8,128)(2,1)S(1)} %pack_texts.1.refs_0_.refs_7_.refs_2_), channel_id=1, source_target_pairs={{1,0},{0,1},{3,2},{2,3},{5,4},{4,5},{7,6},{6,7},{9,8},{8,9},{11,10... | collective-permute-start | bytes 122888 | tf_op jit(solution)/shard_map/ppermute | solution.py:194
  15.1 1.5 %collective-permute-start.5 = (bf16[64,1280]{1,0:T(8,128)(2,1)S(1)}, bf16[64,1280]{1,0:T(8,128)(2,1)S(1)}, u32[]{:S(2)}, u32[]{:S(2)}) collective-permute-start(bf16[64,1280]{1,0:T(8,128)(2,1)S(1)} %get-tuple-element.9.refs_2_), channel_id=1, source_target_pairs={{0,2},{1,3},{2,0},{3,1},{4,6},{5,7},{6,4},{7,5},{8,10},{9,11},{10,... | collective-permute-start | bytes 491528 | tf_op jit(solution)/shard_map/ppermute | solution.py:194
  15.1 4.1 %collective-permute-start.8 = (bf16[16,1280]{1,0:T(8,128)(2,1)S(1)}, bf16[16,1280]{1,0:T(8,128)(2,1)S(1)}, u32[]{:S(2)}, u32[]{:S(2)}) collective-permute-start(bf16[16,1280]{1,0:T(8,128)(2,1)S(1)} %pack_images.1.refs_1_.refs_2_), channel_id=1, source_target_pairs={{8,0},{9,1},{10,2},{11,3},{12,4},{13,5},{14,6},{15,7},{0,8},{1,9},... | collective-permute-start | bytes 122888 | tf_op jit(solution)/shard_map/ppermute | solution.py:194
  19.2 5.2 %collective-permute-start.10 = (bf16[64,1280]{1,0:T(8,128)(2,1)S(1)}, bf16[64,1280]{1,0:T(8,128)(2,1)S(1)}, u32[]{:S(2)}, u32[]{:S(2)}) collective-permute-start(bf16[64,1280]{1,0:T(8,128)(2,1)S(1)} %join_images.1.refs_2_.refs_3_), channel_id=1, source_target_pairs={{0,2},{1,3},{2,0},{3,1},{4,6},{5,7},{6,4},{7,5},{8,10},{9,11},{10,... | collective-permute-start | bytes 491528 | tf_op jit(solution)/shard_map/ppermute | solution.py:194
  19.3 7.2 %collective-permute-start.6 = (s16[16,1280]{1,0:T(8,128)(2,1)S(1)}, s16[16,1280]{1,0:T(8,128)(2,1)S(1)}, u32[]{:S(2)}, u32[]{:S(2)}) collective-permute-start(s16[16,1280]{1,0:T(8,128)(2,1)S(1)} %image_lines.5.refs_0_), channel_id=1, source_target_pairs={{0,24},{1,25},{2,26},{3,27},{4,28},{5,29},{6,30},{7,31},{8,16},{9,... | collective-permute-start | bytes 122888 | tf_op jit(solution)/shard_map/ppermute | solution.py:194
  21.9 5.7 %collective-permute-start.7 = (s16[16,1280]{1,0:T(8,128)(2,1)S(1)}, s16[16,1280]{1,0:T(8,128)(2,1)S(1)}, u32[]{:S(2)}, u32[]{:S(2)}) collective-permute-start(s16[16,1280]{1,0:T(8,128)(2,1)S(1)} %image_lines.6.refs_1_), channel_id=1, source_target_pairs={{0,16},{1,17},{2,18},{3,19},{4,20},{5,21},{6,22},{7,23},{8,24},{9,... | collective-permute-start | bytes 122888 | tf_op jit(solution)/shard_map/ppermute | solution.py:194
  22.9 7.5 %collective-permute-start.9 = (s16[16,1280]{1,0:T(8,128)(2,1)S(1)}, s16[16,1280]{1,0:T(8,128)(2,1)S(1)}, u32[]{:S(2)}, u32[]{:S(2)}) collective-permute-start(s16[16,1280]{1,0:T(8,128)(2,1)S(1)} %image_lines.7), channel_id=1, source_target_pairs={{0,8},{1,9},{2,10},{3,11},{4,12},{5,13},{6,14},{7,15},{8,0},{9,1},... | collective-permute-start | bytes 122888 | tf_op jit(solution)/shard_map/ppermute | solution.py:194
  25.0 6.0 %collective-permute-start.11 = (s16[16,1280]{1,0:T(8,128)(2,1)S(1)}, s16[16,1280]{1,0:T(8,128)(2,1)S(1)}, u32[]{:S(2)}, u32[]{:S(2)}) collective-permute-start(s16[16,1280]{1,0:T(8,128)(2,1)S(1)} %text_lines.4), channel_id=1, source_target_pairs={{0,5},{1,4},{2,7},{3,6},{4,1},{5,0},{6,3},{7,2},{8,13},{9,12},{10,... | collective-permute-start | bytes 122888 | tf_op jit(solution)/shard_map/ppermute | solution.py:194
  27.0 4.1 %collective-permute-start.12 = (s16[16,1280]{1,0:T(8,128)(2,1)S(1)}, s16[16,1280]{1,0:T(8,128)(2,1)S(1)}, u32[]{:S(2)}, u32[]{:S(2)}) collective-permute-start(s16[16,1280]{1,0:T(8,128)(2,1)S(1)} %text_lines.5), channel_id=1, source_target_pairs={{0,4},{1,5},{2,6},{3,7},{4,0},{5,1},{6,2},{7,3},{8,12},{9,13},{10,... | collective-permute-start | bytes 122888 | tf_op jit(solution)/shard_map/ppermute | solution.py:194
  28.2 4.1 %collective-permute-start.13 = (s16[16,1280]{1,0:T(8,128)(2,1)S(1)}, s16[16,1280]{1,0:T(8,128)(2,1)S(1)}, u32[]{:S(2)}, u32[]{:S(2)}) collective-permute-start(s16[16,1280]{1,0:T(8,128)(2,1)S(1)} %text_lines.6), channel_id=1, source_target_pairs={{0,1},{1,0},{2,3},{3,2},{4,5},{5,4},{6,7},{7,6},{8,9},{9,8},{10,11... | collective-permute-start | bytes 122888 | tf_op jit(solution)/shard_map/ppermute | solution.py:194
  30.4 1.9 %copy-start.1 = (bf16[16,1152]{1,0:T(8,128)(2,1)S(1)}, bf16[16,1152]{1,0:T(8,128)(2,1)}, u32[]{:S(2)}) copy-start(bf16[16,1152]{1,0:T(8,128)(2,1)} %refs_1_.5) | copy-start | bytes 110596

commit v11 on v9

--- a/solution.py
+++ b/solution.py
@@ -91,15 +91,18 @@
     return digits.astype(jnp.bfloat16)
 
 
-def pack_kernel(image_ref, text_ref, class_ref, out_ref):
+def digits_kernel(class_ref, digits_ref):
+    digits_ref[...] = class_digits(class_ref)
+
+
+def pack_kernel(image_ref, text_ref, digits_ref, out_ref):
     rows, depth = image_ref.shape
-    digits = class_digits(class_ref)
     for start, source in ((0, image_ref), (rows, text_ref)):
         out_ref[start : start + rows, :depth] = unit_rows(source[...])[0].astype(jnp.bfloat16)
-        out_ref[start : start + rows, depth:] = digits
-
-
-def join_kernel(scale_ref, shift_ref, own_ref, got_ref, mine_ref, other_ref, again_ref, pair_ref):
+        out_ref[start : start + rows, depth:] = digits_ref[...]
+
+
+def join_kernel(scale_ref, shift_ref, own_ref, got_ref, *refs):
     first = on_first_core()
     rows = own_ref.shape[0] // 2
     own, got = own_ref[...].astype(jnp.float32), got_ref[...].astype(jnp.float32)
@@ -107,9 +110,10 @@
     images = jnp.concatenate([low[:rows], high[:rows]], axis=0)
     texts = jnp.concatenate([low[rows:], high[rows:]], axis=0)
     mine = jnp.where(first, images, texts).astype(jnp.bfloat16)
-    mine_ref[...] = mine
-    again_ref[...] = mine
-    other_ref[...] = jnp.where(first, texts, images).astype(jnp.bfloat16)
+    other = jnp.where(first, texts, images).astype(jnp.bfloat16)
+    for ref, block in zip(refs[:-1], (mine, other, mine, mine, other)):
+        ref[...] = block
+    pair_ref = refs[-1]
     row = lax.broadcasted_iota(jnp.int32, pair_ref.shape, 0)
     pair_ref[...] = jnp.where(row == 0, scale_ref[0], shift_ref[0])
 
@@ -254,9 +258,10 @@
     vmem = pl.BlockSpec(memory_space=pltpu.VMEM)
     smem = pl.BlockSpec(memory_space=pltpu.SMEM)
 
-    def call(kernel, shapes, operands, name, scalars=0):
+    def call(kernel, shapes, operands, name, scalars=0, cost=None):
         return pl.pallas_call(
             kernel,
+            cost_estimate=cost,
             out_shape=shapes,
             in_specs=[smem] * scalars + [vmem] * (len(operands) - scalars),
             out_specs=jax.tree.map(lambda _: vmem, shapes),
@@ -284,15 +289,18 @@
         return lax.ppermute(x, AXES, [(i, i ^ lanes) for i in range(n)])
 
     visits = ((12, 3), (2, 8), (4, 1))
-    own = call(pack_kernel, block(2), [image_emb, text_emb, pair_class], "pack")
-    mine, other, again, pair = call(
+    digits = call(
+        digits_kernel, jax.ShapeDtypeStruct((rows, LANES), jnp.bfloat16), [pair_class], "digits", cost=pl.CostEstimate(flops=10**9, bytes_accessed=10**7, transcendentals=0)
+    )
+    own = call(pack_kernel, block(2), [image_emb, text_emb, digits], "pack")
+    *sent, mine, other, pair = call(
         join_kernel,
-        (block(2), block(2), block(2), wide(8, LANES)),
+        (block(2),) * 5 + (wide(8, LANES),),
         [scale[None], shift[None], own, swap(own)],
         "join",
         2,
     )
-    got = [visit(x, masks) for x, masks in zip((mine, other, again), visits)]
+    got = [visit(x, masks) for x, masks in zip(sent, visits)]
     got = call(gather_kernel, block(6), got, "gather")
     parts = call(
         tile_kernel, (block(2, jnp.int16),) * 4, [pair, mine, other, got, swap(got)], "tile"

time: 28.9 us -> 27.5 us (0.952)
  waiting for transfers between devices: 9.81 us -> 12.6 us
  starting transfers between devices: 12.3 us -> 9.62 us
  local copies, waits for them, and re-layouts: 2.19 us -> 0.67 us
    ppermute x6, waiting for transfers between devices: 7.4 us -> 9.83 us  [visit(): return lax.ppermute(x, AXES, pairs)]
    ppermute x6, starting transfers between devices: 11.1 us -> 8.96 us  [visit(): return lax.ppermute(x, AXES, pairs)]
    unnamed x10 -> x6, local copies, waits for them, and re-layouts: 2.19 us -> 0.67 us
    ppermute x3, starting transfers between devices: 1.2 us -> 0.66 us  [swap(): return lax.ppermute(x, AXES, [(i, i ^ lanes) for i in range(n)])]
    ppermute x3, waiting for transfers between devices: 2.41 us -> 2.77 us  [swap(): return lax.ppermute(x, AXES, [(i, i ^ lanes) for i in range(n)])]
    pallas_call x6 -> x7, Pallas kernels: 2.29 us -> 2.38 us  [call(): pl.pallas_call(kernel, cost_estimate=cost, out_shape=shapes, in_specs=[sm...]
where the time goes in v11:
time: 27.5 us; the launch traced here: 27.3 us
  waiting for transfers between devices  12.6 us (46%)
  starting transfers between devices  9.62 us (35%)
  Pallas kernels  2.38 us (9%)
  between operations  2.03 us (7%)
  local copies, waits for them, and re-layouts  0.67 us (2%)
    ppermute x6, waiting for transfers between devices, visit(): return lax.ppermute(x, AXES, pairs)  9.83 us
    ppermute x6, starting transfers between devices, visit(): return lax.ppermute(x, AXES, pairs)  8.96 us
    ppermute x3, waiting for transfers between devices, swap(): return lax.ppermute(x, AXES, [(i, i ^ lanes) for i in range(n)])  2.77 us
    pallas_call x7, Pallas kernels, call(): pl.pallas_call(kernel, cost_estimate=cost, out_shape=shapes, in_specs=[sm...  2.38 us
    unnamed x6, local copies, waits for them, and re-layouts  0.67 us
    ppermute x3, starting transfers between devices, swap(): return lax.ppermute(x, AXES, [(i, i ^ lanes) for i in range(n)])  0.66 us
  transfers between devices with their start and end apart: 9, of which 7 were waited for; matrix products, arithmetic and copies ran while one was open for 0% of the time, Pallas kernels for 0%

profile of v11, /device:TPU:0, one launch (start us, length us, event | category | flops | bytes accessed | tf_op | source)
XLA Modules:
  0.0 27.3 jit_solution(2907982522823635845)
XLA Ops:
  0.6 0.0 copy-start.1
  0.6 0.0 copy-start
  0.7 0.0 copy-start.2
  0.7 0.7 %copy-done.2 = s32[16]{0:T(128)S(1)} copy-done((s32[16]{0:T(128)S(1)}, s32[16]{0:T(128)}, u32[]{:S(2)}) %copy-start.2) | copy-done | bytes 88
  1.3 0.1 digits.1.digits_ref
  1.4 0.0 copy-done.1
  1.4 0.0 copy-done
  1.4 0.1 pack.1.own_ref
  1.5 0.5 %collective-permute-start = (bf16[32,1280]{1,0:T(8,128)(2,1)S(1)}, bf16[32,1280]{1,0:T(8,128)(2,1)S(1)}, u32[]{:S(2)}, u32[]{:S(2)}) collective-permute-start(bf16[32,1280]{1,0:T(8,128)(2,1)S(1)} %pack.1.own_ref), channel_id=1, source_target_pairs={{0,2},{1,3},{2,0},{3,1},{4,6},{5,7},{6,4},{7,5},{8,10},{9,11},{10,... | collective-permute-start | bytes 245768 | tf_op jit(solution)/shard_map/ppermute | solution.py:289
  3.4 0.0 collective-permute-done.got_ref
  3.4 0.1 join.1
  3.5 4.7 %collective-permute-start.1 = (bf16[32,1280]{1,0:T(8,128)(2,1)S(1)}, bf16[32,1280]{1,0:T(8,128)(2,1)S(1)}, u32[]{:S(2)}, u32[]{:S(2)}) collective-permute-start(bf16[32,1280]{1,0:T(8,128)(2,1)S(1)} %get-tuple-element.22), channel_id=1, source_target_pairs={{0,24},{1,25},{2,7},{3,6},{4,28},{5,29},{6,3},{7,2},{8,16},{9,17},... | collective-permute-start | bytes 245768 | tf_op jit(solution)/shard_map/ppermute | solution.py:286
  8.1 1.5 %collective-permute-start.2 = (bf16[32,1280]{1,0:T(8,128)(2,1)S(1)}, bf16[32,1280]{1,0:T(8,128)(2,1)S(1)}, u32[]{:S(2)}, u32[]{:S(2)}) collective-permute-start(bf16[32,1280]{1,0:T(8,128)(2,1)S(1)} %get-tuple-element.23), channel_id=1, source_target_pairs={{0,4},{1,5},{2,18},{3,19},{4,0},{5,1},{6,22},{7,23},{8,12},{9,13},... | collective-permute-start | bytes 245768 | tf_op jit(solution)/shard_map/ppermute | solution.py:286
  9.6 0.0 collective-permute-start.3
  9.6 1.0 %collective-permute-done.1.refs_0_ = bf16[32,1280]{1,0:T(8,128)(2,1)S(1)} collective-permute-done((bf16[32,1280]{1,0:T(8,128)(2,1)S(1)}, bf16[32,1280]{1,0:T(8,128)(2,1)S(1)}, u32[]{:S(2)}, u32[]{:S(2)}) %collective-permute-start.1) | collective-permute-done | bytes 81952 | tf_op jit(solution)/shard_map/ppermute | solution.py:286
  10.6 1.9 %collective-permute-done.2.refs_1_ = bf16[32,1280]{1,0:T(8,128)(2,1)S(1)} collective-permute-done((bf16[32,1280]{1,0:T(8,128)(2,1)S(1)}, bf16[32,1280]{1,0:T(8,128)(2,1)S(1)}, u32[]{:S(2)}, u32[]{:S(2)}) %collective-permute-start.2) | collective-permute-done | bytes 81952 | tf_op jit(solution)/shard_map/ppermute | solution.py:286
  12.6 1.5 %collective-permute-done.3.refs_2_ = bf16[32,1280]{1,0:T(8,128)(2,1)S(1)} collective-permute-done((bf16[32,1280]{1,0:T(8,128)(2,1)S(1)}, bf16[32,1280]{1,0:T(8,128)(2,1)S(1)}, u32[]{:S(2)}, u32[]{:S(2)}) %collective-permute-start.3) | collective-permute-done | bytes 81952 | tf_op jit(solution)/shard_map/ppermute | solution.py:286
  14.1 0.1 collective-permute-start.4
  14.2 1.5 %collective-permute-done.4.swapped_ref = bf16[96,1280]{1,0:T(8,128)(2,1)S(1)} collective-permute-done((bf16[96,1280]{1,0:T(8,128)(2,1)S(1)}, bf16[96,1280]{1,0:T(8,128)(2,1)S(1)}, u32[]{:S(2)}, u32[]{:S(2)}) %collective-permute-start.4) | collective-permute-done | bytes 245792 | tf_op jit(solution)/shard_map/ppermute | solution.py:289
  15.7 0.9 %tile.1 = (s16[32,1280]{1,0:T(8,128)(2,1)S(1)}, s16[32,1280]{1,0:T(8,128)(2,1)S(1)}, s16[32,1280]{1,0:T(8,128)(2,1)S(1)}, s16[32,1280]{1,0:T(8,128)(2,1)S(1)}) custom-call(f32[8,128]{1,0:T(8,128)S(1)} %get-tuple-element.19.pair_ref, bf16[32,1280]{1,0:T(8,128)(2,1)S(1)} %get-tuple-element.20.mine_ref, bf16[32,1280]{1,0:T(8,128)(2,1)S(1)} %get-tuple-element.21.other_ref, ...), custom_call_target="tpu_custom_call" | custom-call | tf_op jit(solution)/shard_map/tile/pallas_call | solution.py:262
  16.6 1.6 %collective-permute-start.5 = (s16[32,1280]{1,0:T(8,128)(2,1)S(1)}, s16[32,1280]{1,0:T(8,128)(2,1)S(1)}, u32[]{:S(2)}, u32[]{:S(2)}) collective-permute-start(s16[32,1280]{1,0:T(8,128)(2,1)S(1)} %get-tuple-element.26), channel_id=1, source_target_pairs={{0,24},{1,25},{2,7},{3,6},{4,28},{5,29},{6,3},{7,2},{8,16},{9,17},... | collective-permute-start | bytes 245768 | tf_op jit(solution)/shard_map/ppermute | solution.py:286
  18.2 1.2 %collective-permute-start.6 = (s16[32,1280]{1,0:T(8,128)(2,1)S(1)}, s16[32,1280]{1,0:T(8,128)(2,1)S(1)}, u32[]{:S(2)}, u32[]{:S(2)}) collective-permute-start(s16[32,1280]{1,0:T(8,128)(2,1)S(1)} %get-tuple-element.27), channel_id=1, source_target_pairs={{0,4},{1,5},{2,18},{3,19},{4,0},{5,1},{6,22},{7,23},{8,12},{9,13},... | collective-permute-start | bytes 245768 | tf_op jit(solution)/shard_map/ppermute | solution.py:286
  19.4 0.0 collective-permute-start.7
  19.4 3.8 %collective-permute-done.5.back_0 = s16[32,1280]{1,0:T(8,128)(2,1)S(1)} collective-permute-done((s16[32,1280]{1,0:T(8,128)(2,1)S(1)}, s16[32,1280]{1,0:T(8,128)(2,1)S(1)}, u32[]{:S(2)}, u32[]{:S(2)}) %collective-permute-start.5) | collective-permute-done | bytes 81952 | tf_op jit(solution)/shard_map/ppermute | solution.py:286
  23.2 0.0 collective-permute-done.6.back_1
  23.2 1.6 %collective-permute-done.7.back_2 = s16[32,1280]{1,0:T(8,128)(2,1)S(1)} collective-permute-done((s16[32,1280]{1,0:T(8,128)(2,1)S(1)}, s16[32,1280]{1,0:T(8,128)(2,1)S(1)}, u32[]{:S(2)}, u32[]{:S(2)}) %collective-permute-start.7) | collective-permute-done | bytes 81952 | tf_op jit(solution)/shard_map/ppermute | solution.py:286
  24.8 0.2 add.1
  25.0 0.1 collective-permute-start.8
  25.1 1.3 %collective-permute-done.8.got_ref = s16[32,1280]{1,0:T(8,128)(2,1)S(1)} collective-permute-done((s16[32,1280]{1,0:T(8,128)(2,1)S(1)}, s16[32,1280]{1,0:T(8,128)(2,1)S(1)}, u32[]{:S(2)}, u32[]{:S(2)}) %collective-permute-start.8) | collective-permute-done | bytes 81952 | tf_op jit(solution)/shard_map/ppermute | solution.py:289
  26.4 0.9 %final.1 = (f32[1,16]{1,0:T(1,128)}, f32[16,1152]{1,0:T(8,128)}, f32[16,1152]{1,0:T(8,128)}) custom-call(bf16[16,1152]{1,0:T(8,128)(2,1)S(1)} %copy-done, bf16[16,1152]{1,0:T(8,128)(2,1)S(1)} %copy-done.1, f32[2,16,1152]{2,1,0:T(8,128)S(1)} %get-tuple-element.29.keep_ref, f32[2,16,128]{2,1,0:T(8,128)S(1)} %get-tuple-element.30.kept_loss_ref, ...), custom_call_target="tpu_custom_call" | custom-call | tf_op jit(solution)/shard_map/final/pallas_call | solution.py:262
  (1 shorter events, 0.0 us)
Async XLA Ops:
  0.6 0.8 %copy-start.1 = (bf16[16,1152]{1,0:T(8,128)(2,1)S(1)}, bf16[16,1152]{1,0:T(8,128)(2,1)}, u32[]{:S(2)}) copy-start(bf16[16,1152]{1,0:T(8,128)(2,1)} %text_ref.3) | copy-start | bytes 110596
  0.6 0.8 %copy-start = (bf16[16,1152]{1,0:T(8,128)(2,1)S(1)}, bf16[16,1152]{1,0:T(8,128)(2,1)}, u32[]{:S(2)}) copy-start(bf16[16,1152]{1,0:T(8,128)(2,1)} %image_ref.3) | copy-start | bytes 110596
  0.7 0.7 %copy-start.2 = (s32[16]{0:T(128)S(1)}, s32[16]{0:T(128)}, u32[]{:S(2)}) copy-start(s32[16]{0:T(128)} %class_ref.1) | copy-start | bytes 196
  1.5 1.8 %collective-permute-start = (bf16[32,1280]{1,0:T(8,128)(2,1)S(1)}, bf16[32,1280]{1,0:T(8,128)(2,1)S(1)}, u32[]{:S(2)}, u32[]{:S(2)}) collective-permute-start(bf16[32,1280]{1,0:T(8,128)(2,1)S(1)} %pack.1.own_ref), channel_id=1, source_target_pairs={{0,2},{1,3},{2,0},{3,1},{4,6},{5,7},{6,4},{7,5},{8,10},{9,11},{10,... | collective-permute-start | bytes 245768 | tf_op jit(solution)/shard_map/ppermute | solution.py:289
  3.5 7.2 %collective-permute-start.1 = (bf16[32,1280]{1,0:T(8,128)(2,1)S(1)}, bf16[32,1280]{1,0:T(8,128)(2,1)S(1)}, u32[]{:S(2)}, u32[]{:S(2)}) collective-permute-start(bf16[32,1280]{1,0:T(8,128)(2,1)S(1)} %get-tuple-element.22), channel_id=1, source_target_pairs={{0,24},{1,25},{2,7},{3,6},{4,28},{5,29},{6,3},{7,2},{8,16},{9,17},... | collective-permute-start | bytes 245768 | tf_op jit(solution)/shard_map/ppermute | solution.py:286
  8.1 4.4 %collective-permute-start.2 = (bf16[32,1280]{1,0:T(8,128)(2,1)S(1)}, bf16[32,1280]{1,0:T(8,128)(2,1)S(1)}, u32[]{:S(2)}, u32[]{:S(2)}) collective-permute-start(bf16[32,1280]{1,0:T(8,128)(2,1)S(1)} %get-tuple-element.23), channel_id=1, source_target_pairs={{0,4},{1,5},{2,18},{3,19},{4,0},{5,1},{6,22},{7,23},{8,12},{9,13},... | collective-permute-start | bytes 245768 | tf_op jit(solution)/shard_map/ppermute | solution.py:286
  9.6 4.4 %collective-permute-start.3 = (bf16[32,1280]{1,0:T(8,128)(2,1)S(1)}, bf16[32,1280]{1,0:T(8,128)(2,1)S(1)}, u32[]{:S(2)}, u32[]{:S(2)}) collective-permute-start(bf16[32,1280]{1,0:T(8,128)(2,1)S(1)} %get-tuple-element.24), channel_id=1, source_target_pairs={{0,8},{1,9},{2,3},{3,2},{4,12},{5,13},{6,7},{7,6},{8,0},{9,1},{10,... | collective-permute-start | bytes 245768 | tf_op jit(solution)/shard_map/ppermute | solution.py:286
  14.1 1.6 %collective-permute-start.4 = (bf16[96,1280]{1,0:T(8,128)(2,1)S(1)}, bf16[96,1280]{1,0:T(8,128)(2,1)S(1)}, u32[]{:S(2)}, u32[]{:S(2)}) collective-permute-start(bf16[96,1280]{1,0:T(8,128)(2,1)S(1)} %gather.1.got_ref), channel_id=1, source_target_pairs={{0,2},{1,3},{2,0},{3,1},{4,6},{5,7},{6,4},{7,5},{8,10},{9,11},{10,... | collective-permute-start | bytes 737288 | tf_op jit(solution)/shard_map/ppermute | solution.py:289
  16.6 6.6 %collective-permute-start.5 = (s16[32,1280]{1,0:T(8,128)(2,1)S(1)}, s16[32,1280]{1,0:T(8,128)(2,1)S(1)}, u32[]{:S(2)}, u32[]{:S(2)}) collective-permute-start(s16[32,1280]{1,0:T(8,128)(2,1)S(1)} %get-tuple-element.26), channel_id=1, source_target_pairs={{0,24},{1,25},{2,7},{3,6},{4,28},{5,29},{6,3},{7,2},{8,16},{9,17},... | collective-permute-start | bytes 245768 | tf_op jit(solution)/shard_map/ppermute | solution.py:286
  18.2 5.0 %collective-permute-start.6 = (s16[32,1280]{1,0:T(8,128)(2,1)S(1)}, s16[32,1280]{1,0:T(8,128)(2,1)S(1)}, u32[]{:S(2)}, u32[]{:S(2)}) collective-permute-start(s16[32,1280]{1,0:T(8,128)(2,1)S(1)} %get-tuple-element.27), channel_id=1, source_target_pairs={{0,4},{1,5},{2,18},{3,19},{4,0},{5,1},{6,22},{7,23},{8,12},{9,13},... | collective-permute-start | bytes 245768 | tf_op jit(solution)/shard_map/ppermute | solution.py:286
  19.4 5.4 %collective-permute-start.7 = (s16[32,1280]{1,0:T(8,128)(2,1)S(1)}, s16[32,1280]{1,0:T(8,128)(2,1)S(1)}, u32[]{:S(2)}, u32[]{:S(2)}) collective-permute-start(s16[32,1280]{1,0:T(8,128)(2,1)S(1)} %get-tuple-element.28), channel_id=1, source_target_pairs={{0,8},{1,9},{2,3},{3,2},{4,12},{5,13},{6,7},{7,6},{8,0},{9,1},{10,... | collective-permute-start | bytes 245768 | tf_op jit(solution)/shard_map/ppermute | solution.py:286
  25.0 1.3 %collective-permute-start.8 = (s16[32,1280]{1,0:T(8,128)(2,1)S(1)}, s16[32,1280]{1,0:T(8,128)(2,1)S(1)}, u32[]{:S(2)}, u32[]{:S(2)}) collective-permute-start(s16[32,1280]{1,0:T(8,128)(2,1)S(1)} %get-tuple-element.31), channel_id=1, source_target_pairs={{0,2},{1,3},{2,0},{3,1},{4,6},{5,7},{6,4},{7,5},{8,10},{9,11},{10,... | collective-permute-start | bytes 245768 | tf_op jit(solution)/shard_map/ppermute | solution.py:289

commit v12 on v11

--- a/solution.py
+++ b/solution.py
@@ -128,9 +128,12 @@
     return jnp.ceil(jnp.log2(jnp.maximum(size, 1e-30)) + 0.01)
 
 
+def nearest(values):
+    return jnp.floor(values + 0.5).astype(jnp.int32)
+
+
 def code(values, power):
-    steps = jnp.clip(jnp.round(values * (TOP / jnp.exp2(power))), -TOP, TOP)
-    return steps.astype(jnp.int32).astype(jnp.int16)
+    return nearest(values * (TOP / jnp.exp2(power))).astype(jnp.int16)
 
 
 def decode(steps, power):
@@ -146,8 +149,8 @@
     loss_power = power_above(loss)
     tail = jnp.where(lane == 0, power, 0.0)
     tail = jnp.where(lane == 1, loss_power, tail)
-    tail = jnp.where(lane == 2, jnp.round(loss * (TOP / jnp.exp2(loss_power))), tail)
-    tail = tail.astype(jnp.int32).astype(jnp.int16)
+    tail = jnp.where(lane == 2, loss * (TOP / jnp.exp2(loss_power)), tail)
+    tail = nearest(tail).astype(jnp.int16)
     for k, out in enumerate(outs):
         out[:, :depth] = steps[k * rows : (k + 1) * rows]
         out[:, depth:] = tail[k * rows : (k + 1) * rows]
@@ -199,8 +202,17 @@
     swapped = [swapped_ref[k * rows : (k + 1) * rows, :] for k in range(3)]
     mine_side = jnp.concatenate([mine_ref[...], got[0], swapped[1], got[2]], axis=0)
     other_side = jnp.concatenate([other_ref[...], swapped[0], got[1], swapped[2]], axis=0)
-    lines = jnp.concatenate([got[0], got[2], mine_ref[...]], axis=0)
-    put_rows([outs[0], outs[2], outs[3]], *partial_pull(lines, other_side, scale, shift))
+    lines = jnp.concatenate([got[0], mine_ref[...], got[2]], axis=0)
+    pull, loss = partial_pull(lines, other_side, scale, shift)
+    put_rows([outs[0], outs[4]], pull[: 2 * rows], loss[: 2 * rows])
+    half = rows // 2
+    first = on_first_core()
+    last = []
+    for part in (pull, loss):
+        low, high = part[2 * rows : 2 * rows + half], part[2 * rows + half :]
+        last.append((jnp.where(first, low, high), jnp.where(first, high, low)))
+    for out, part, part_loss in zip(outs[2:4], *last):
+        put_rows([out], part, part_loss)
     put_rows([outs[1]], *partial_pull(got[1], mine_side, scale, shift))
 
 
@@ -219,14 +231,22 @@
     return pl.ds(own, rows), pl.ds(pl.multiple_of(rows - own, rows), rows)
 
 
-def add_kernel(own_ref, back_0, back_1, back_2, keep_ref, loss_ref, give_ref):
+def add_kernel(own_ref, back_0, back_1, keep_ref, loss_ref, give_ref):
     rows, depth = keep_ref.shape[1:]
     own, other = place_of(on_first_core(), rows)
-    for side, parts in enumerate(((own_ref, back_0, back_2), (back_1,))):
+    for side, parts in enumerate(((own_ref, back_0), (back_1,))):
         keep_ref[side], loss = total([part[own, :] for part in parts], rows, depth)
         loss_ref[side] = jnp.broadcast_to(loss, loss_ref.shape[1:])
         pull, loss = total([part[other, :] for part in parts], rows, depth)
         put_rows([give_ref.at[side * rows : (side + 1) * rows, :]], pull, loss)
+
+
+def more_kernel(keep_ref, kept_loss_ref, same_ref, cross_ref, sum_ref, sum_loss_ref):
+    rows, depth = keep_ref.shape[1:]
+    for side, ref in enumerate((same_ref, cross_ref)):
+        pull, loss = total([ref[...]], rows, depth)
+        sum_ref[side] = keep_ref[side] + pull
+        sum_loss_ref[side] = kept_loss_ref[side] + loss
 
 
 def final_kernel(pairs, image_ref, text_ref, keep_ref, kept_loss_ref, got_ref, loss_ref, grad_image_ref, grad_text_ref):
@@ -278,11 +298,11 @@
     def core(i):
         return i // lanes % 2
 
-    def visit(x, masks):
+    def visit(x, masks, cross=0):
         pairs = []
         for i in range(n):
             chip = (i // (2 * lanes) * lanes + i % lanes) ^ masks[core(i)]
-            pairs.append((i, (chip // lanes * 2 + core(i)) * lanes + chip % lanes))
+            pairs.append((i, (chip // lanes * 2 + (core(i) ^ cross)) * lanes + chip % lanes))
         return lax.ppermute(x, AXES, pairs)
 
     def swap(x):
@@ -302,15 +322,24 @@
     )
     got = [visit(x, masks) for x, masks in zip(sent, visits)]
     got = call(gather_kernel, block(6), got, "gather")
+    one, two = block(1, jnp.int16), block(2, jnp.int16)
     parts = call(
-        tile_kernel, (block(2, jnp.int16),) * 4, [pair, mine, other, got, swap(got)], "tile"
+        tile_kernel, (two, two, one, one, two), [pair, mine, other, got, swap(got)], "tile"
     )
     back = [visit(x, masks) for x, masks in zip(parts, visits)]
+    cross = visit(parts[3], visits[2], 1)
     keep, kept_loss, give = call(
         add_kernel,
-        (wide(2, rows, depth), wide(2, rows, LANES), block(2, jnp.int16)),
-        [parts[3], *back],
+        (wide(2, rows, depth), wide(2, rows, LANES), two),
+        [parts[4], *back[:2]],
         "add",
+    )
+    keep, kept_loss = call(
+        more_kernel,
+        (wide(2, rows, depth), wide(2, rows, LANES)),
+        [keep, kept_loss, back[2], cross],
+        "more",
+        cost=pl.CostEstimate(flops=10**9, bytes_accessed=10**7, transcendentals=0),
     )
     loss, grad_image, grad_text = call(
         functools.partial(final_kernel, n * rows),

time: 27.5 us -> 26.2 us (0.953)
  waiting for transfers between devices: 12.6 us -> 9.3 us
  starting transfers between devices: 9.62 us -> 11.5 us
    ppermute x6 -> x7, waiting for transfers between devices: 9.83 us -> 7.25 us  [visit(): return lax.ppermute(x, AXES, pairs)]
    ppermute x6 -> x7, starting transfers between devices: 8.96 us -> 10.1 us  [visit(): return lax.ppermute(x, AXES, pairs)]
    ppermute x3, waiting for transfers between devices: 2.77 us -> 2.06 us  [swap(): return lax.ppermute(x, AXES, [(i, i ^ lanes) for i in range(n)])]
    ppermute x3, starting transfers between devices: 0.66 us -> 1.34 us  [swap(): return lax.ppermute(x, AXES, [(i, i ^ lanes) for i in range(n)])]
    pallas_call x7 -> x8, Pallas kernels: 2.38 us -> 2.59 us  [call(): pl.pallas_call(kernel, cost_estimate=cost, out_shape=shapes, in_specs=[sm...]
  transfers between devices with their start and end apart: 9 -> 10, of which waited for: 7 -> 7; matrix products, arithmetic and copies ran while one was open for 0% -> 0% of each run, Pallas kernels for 0% -> 1%
where the time goes in v12:
time: 26.2 us; the launch traced here: 26.1 us
  starting transfers between devices  11.5 us (44%)
  waiting for transfers between devices  9.3 us (35%)
  Pallas kernels  2.59 us (10%)
  between operations  2.02 us (8%)
  local copies, waits for them, and re-layouts  0.67 us (3%)
    ppermute x7, starting transfers between devices, visit(): return lax.ppermute(x, AXES, pairs)  10.1 us
    ppermute x7, waiting for transfers between devices, visit(): return lax.ppermute(x, AXES, pairs)  7.25 us
    pallas_call x8, Pallas kernels, call(): pl.pallas_call(kernel, cost_estimate=cost, out_shape=shapes, in_specs=[sm...  2.59 us
    ppermute x3, waiting for transfers between devices, swap(): return lax.ppermute(x, AXES, [(i, i ^ lanes) for i in range(n)])  2.06 us
    ppermute x3, starting transfers between devices, swap(): return lax.ppermute(x, AXES, [(i, i ^ lanes) for i in range(n)])  1.34 us
    unnamed x6, local copies, waits for them, and re-layouts  0.67 us
  transfers between devices with their start and end apart: 10, of which 7 were waited for; matrix products, arithmetic and copies ran while one was open for 0% of the time, Pallas kernels for 1%

profile of v12, /device:TPU:0, one launch (start us, length us, event | category | flops | bytes accessed | tf_op | source)
XLA Modules:
  0.0 26.1 jit_solution(1479166701814456534)
XLA Ops:
  0.6 0.0 copy-start.1
  0.6 0.0 copy-start
  0.7 0.0 copy-start.2
  0.7 0.7 %copy-done.2 = s32[16]{0:T(128)S(1)} copy-done((s32[16]{0:T(128)S(1)}, s32[16]{0:T(128)}, u32[]{:S(2)}) %copy-start.2) | copy-done | bytes 88
  1.3 0.1 digits.1.digits_ref
  1.4 0.0 copy-done.1
  1.4 0.0 copy-done
  1.4 0.1 pack.1.own_ref
  1.5 0.5 %collective-permute-start = (bf16[32,1280]{1,0:T(8,128)(2,1)S(1)}, bf16[32,1280]{1,0:T(8,128)(2,1)S(1)}, u32[]{:S(2)}, u32[]{:S(2)}) collective-permute-start(bf16[32,1280]{1,0:T(8,128)(2,1)S(1)} %pack.1.own_ref), channel_id=1, source_target_pairs={{0,2},{1,3},{2,0},{3,1},{4,6},{5,7},{6,4},{7,5},{8,10},{9,11},{10,... | collective-permute-start | bytes 245768 | tf_op jit(solution)/shard_map/ppermute | solution.py:309
  3.4 0.0 collective-permute-done.got_ref
  3.4 0.1 join.1
  3.5 4.7 %collective-permute-start.1 = (bf16[32,1280]{1,0:T(8,128)(2,1)S(1)}, bf16[32,1280]{1,0:T(8,128)(2,1)S(1)}, u32[]{:S(2)}, u32[]{:S(2)}) collective-permute-start(bf16[32,1280]{1,0:T(8,128)(2,1)S(1)} %get-tuple-element.25), channel_id=1, source_target_pairs={{0,24},{1,25},{2,7},{3,6},{4,28},{5,29},{6,3},{7,2},{8,16},{9,17},... | collective-permute-start | bytes 245768 | tf_op jit(solution)/shard_map/ppermute | solution.py:306
  8.1 1.5 %collective-permute-start.2 = (bf16[32,1280]{1,0:T(8,128)(2,1)S(1)}, bf16[32,1280]{1,0:T(8,128)(2,1)S(1)}, u32[]{:S(2)}, u32[]{:S(2)}) collective-permute-start(bf16[32,1280]{1,0:T(8,128)(2,1)S(1)} %get-tuple-element.26), channel_id=1, source_target_pairs={{0,4},{1,5},{2,18},{3,19},{4,0},{5,1},{6,22},{7,23},{8,12},{9,13},... | collective-permute-start | bytes 245768 | tf_op jit(solution)/shard_map/ppermute | solution.py:306
  9.6 0.0 collective-permute-start.3
  9.6 1.0 %collective-permute-done.1.refs_0_ = bf16[32,1280]{1,0:T(8,128)(2,1)S(1)} collective-permute-done((bf16[32,1280]{1,0:T(8,128)(2,1)S(1)}, bf16[32,1280]{1,0:T(8,128)(2,1)S(1)}, u32[]{:S(2)}, u32[]{:S(2)}) %collective-permute-start.1) | collective-permute-done | bytes 81952 | tf_op jit(solution)/shard_map/ppermute | solution.py:306
  10.6 1.9 %collective-permute-done.2.refs_1_ = bf16[32,1280]{1,0:T(8,128)(2,1)S(1)} collective-permute-done((bf16[32,1280]{1,0:T(8,128)(2,1)S(1)}, bf16[32,1280]{1,0:T(8,128)(2,1)S(1)}, u32[]{:S(2)}, u32[]{:S(2)}) %collective-permute-start.2) | collective-permute-done | bytes 81952 | tf_op jit(solution)/shard_map/ppermute | solution.py:306
  12.6 1.5 %collective-permute-done.3.refs_2_ = bf16[32,1280]{1,0:T(8,128)(2,1)S(1)} collective-permute-done((bf16[32,1280]{1,0:T(8,128)(2,1)S(1)}, bf16[32,1280]{1,0:T(8,128)(2,1)S(1)}, u32[]{:S(2)}, u32[]{:S(2)}) %collective-permute-start.3) | collective-permute-done | bytes 81952 | tf_op jit(solution)/shard_map/ppermute | solution.py:306
  14.1 0.1 collective-permute-start.4
  14.2 1.5 %collective-permute-done.4.swapped_ref = bf16[96,1280]{1,0:T(8,128)(2,1)S(1)} collective-permute-done((bf16[96,1280]{1,0:T(8,128)(2,1)S(1)}, bf16[96,1280]{1,0:T(8,128)(2,1)S(1)}, u32[]{:S(2)}, u32[]{:S(2)}) %collective-permute-start.4) | collective-permute-done | bytes 245792 | tf_op jit(solution)/shard_map/ppermute | solution.py:309
  15.7 1.0 %tile.1 = (s16[32,1280]{1,0:T(8,128)(2,1)S(1)}, s16[32,1280]{1,0:T(8,128)(2,1)S(1)}, s16[16,1280]{1,0:T(8,128)(2,1)S(1)}, s16[16,1280]{1,0:T(8,128)(2,1)S(1)}, s16[32,1280]{1,0:T(8,128)(2,1)S(1)}) custom-call(f32[8,128]{1,0:T(8,128)S(1)} %get-tuple-element.22.pair_ref, bf16[32,1280]{1,0:T(8,128)(2,1)S(1)} %get-tuple-element.23.mine_ref, ...), custom_call_target="tpu_custom_call" | custom-call | tf_op jit(solution)/shard_map/tile/pallas_call | solution.py:282
  16.7 1.6 %collective-permute-start.5 = (s16[32,1280]{1,0:T(8,128)(2,1)S(1)}, s16[32,1280]{1,0:T(8,128)(2,1)S(1)}, u32[]{:S(2)}, u32[]{:S(2)}) collective-permute-start(s16[32,1280]{1,0:T(8,128)(2,1)S(1)} %get-tuple-element.29), channel_id=1, source_target_pairs={{0,24},{1,25},{2,7},{3,6},{4,28},{5,29},{6,3},{7,2},{8,16},{9,17},... | collective-permute-start | bytes 245768 | tf_op jit(solution)/shard_map/ppermute | solution.py:306
  18.3 1.2 %collective-permute-start.6 = (s16[32,1280]{1,0:T(8,128)(2,1)S(1)}, s16[32,1280]{1,0:T(8,128)(2,1)S(1)}, u32[]{:S(2)}, u32[]{:S(2)}) collective-permute-start(s16[32,1280]{1,0:T(8,128)(2,1)S(1)} %get-tuple-element.30), channel_id=1, source_target_pairs={{0,4},{1,5},{2,18},{3,19},{4,0},{5,1},{6,22},{7,23},{8,12},{9,13},... | collective-permute-start | bytes 245768 | tf_op jit(solution)/shard_map/ppermute | solution.py:306
  19.5 0.0 collective-permute-start.7
  19.5 1.2 %collective-permute-start.8 = (s16[16,1280]{1,0:T(8,128)(2,1)S(1)}, s16[16,1280]{1,0:T(8,128)(2,1)S(1)}, u32[]{:S(2)}, u32[]{:S(2)}) collective-permute-start(s16[16,1280]{1,0:T(8,128)(2,1)S(1)} %get-tuple-element.34), channel_id=1, source_target_pairs={{0,10},{1,11},{2,1},{3,0},{4,14},{5,15},{6,5},{7,4},{8,2},{9,3},{1... | collective-permute-start | bytes 122888 | tf_op jit(solution)/shard_map/ppermute | solution.py:306
  20.6 2.6 %collective-permute-done.5.back_0 = s16[32,1280]{1,0:T(8,128)(2,1)S(1)} collective-permute-done((s16[32,1280]{1,0:T(8,128)(2,1)S(1)}, s16[32,1280]{1,0:T(8,128)(2,1)S(1)}, u32[]{:S(2)}, u32[]{:S(2)}) %collective-permute-start.5) | collective-permute-done | bytes 81952 | tf_op jit(solution)/shard_map/ppermute | solution.py:306
  23.2 0.0 collective-permute-done.6.back_1
  23.2 0.2 add.1
  23.5 0.7 %collective-permute-start.9 = (s16[32,1280]{1,0:T(8,128)(2,1)S(1)}, s16[32,1280]{1,0:T(8,128)(2,1)S(1)}, u32[]{:S(2)}, u32[]{:S(2)}) collective-permute-start(s16[32,1280]{1,0:T(8,128)(2,1)S(1)} %get-tuple-element.37), channel_id=1, source_target_pairs={{0,2},{1,3},{2,0},{3,1},{4,6},{5,7},{6,4},{7,5},{8,10},{9,11},{10,... | collective-permute-start | bytes 245768 | tf_op jit(solution)/shard_map/ppermute | solution.py:309
  24.2 0.2 collective-permute-done.7.same_ref
  24.4 0.0 collective-permute-done.8.cross_ref
  24.4 0.1 more.1
  24.6 0.6 %collective-permute-done.9.got_ref = s16[32,1280]{1,0:T(8,128)(2,1)S(1)} collective-permute-done((s16[32,1280]{1,0:T(8,128)(2,1)S(1)}, s16[32,1280]{1,0:T(8,128)(2,1)S(1)}, u32[]{:S(2)}, u32[]{:S(2)}) %collective-permute-start.9) | collective-permute-done | bytes 81952 | tf_op jit(solution)/shard_map/ppermute | solution.py:309
  25.1 0.9 %final.1 = (f32[1,16]{1,0:T(1,128)}, f32[16,1152]{1,0:T(8,128)}, f32[16,1152]{1,0:T(8,128)}) custom-call(bf16[16,1152]{1,0:T(8,128)(2,1)S(1)} %copy-done, bf16[16,1152]{1,0:T(8,128)(2,1)S(1)} %copy-done.1, f32[2,16,1152]{2,1,0:T(8,128)S(1)} %get-tuple-element.35.keep_ref, f32[2,16,128]{2,1,0:T(8,128)S(1)} %get-tuple-element.36.kept_loss_ref, ...), custom_call_target="tpu_custom_call" | custom-call | tf_op jit(solution)/shard_map/final/pallas_call | solution.py:282
  (1 shorter events, 0.0 us)
Async XLA Ops:
  0.6 0.8 %copy-start.1 = (bf16[16,1152]{1,0:T(8,128)(2,1)S(1)}, bf16[16,1152]{1,0:T(8,128)(2,1)}, u32[]{:S(2)}) copy-start(bf16[16,1152]{1,0:T(8,128)(2,1)} %text_ref.3) | copy-start | bytes 110596
  0.6 0.8 %copy-start = (bf16[16,1152]{1,0:T(8,128)(2,1)S(1)}, bf16[16,1152]{1,0:T(8,128)(2,1)}, u32[]{:S(2)}) copy-start(bf16[16,1152]{1,0:T(8,128)(2,1)} %image_ref.3) | copy-start | bytes 110596
  0.7 0.7 %copy-start.2 = (s32[16]{0:T(128)S(1)}, s32[16]{0:T(128)}, u32[]{:S(2)}) copy-start(s32[16]{0:T(128)} %class_ref.1) | copy-start | bytes 196
  1.5 1.8 %collective-permute-start = (bf16[32,1280]{1,0:T(8,128)(2,1)S(1)}, bf16[32,1280]{1,0:T(8,128)(2,1)S(1)}, u32[]{:S(2)}, u32[]{:S(2)}) collective-permute-start(bf16[32,1280]{1,0:T(8,128)(2,1)S(1)} %pack.1.own_ref), channel_id=1, source_target_pairs={{0,2},{1,3},{2,0},{3,1},{4,6},{5,7},{6,4},{7,5},{8,10},{9,11},{10,... | collective-permute-start | bytes 245768 | tf_op jit(solution)/shard_map/ppermute | solution.py:309
  3.5 7.2 %collective-permute-start.1 = (bf16[32,1280]{1,0:T(8,128)(2,1)S(1)}, bf16[32,1280]{1,0:T(8,128)(2,1)S(1)}, u32[]{:S(2)}, u32[]{:S(2)}) collective-permute-start(bf16[32,1280]{1,0:T(8,128)(2,1)S(1)} %get-tuple-element.25), channel_id=1, source_target_pairs={{0,24},{1,25},{2,7},{3,6},{4,28},{5,29},{6,3},{7,2},{8,16},{9,17},... | collective-permute-start | bytes 245768 | tf_op jit(solution)/shard_map/ppermute | solution.py:306
  8.1 4.4 %collective-permute-start.2 = (bf16[32,1280]{1,0:T(8,128)(2,1)S(1)}, bf16[32,1280]{1,0:T(8,128)(2,1)S(1)}, u32[]{:S(2)}, u32[]{:S(2)}) collective-permute-start(bf16[32,1280]{1,0:T(8,128)(2,1)S(1)} %get-tuple-element.26), channel_id=1, source_target_pairs={{0,4},{1,5},{2,18},{3,19},{4,0},{5,1},{6,22},{7,23},{8,12},{9,13},... | collective-permute-start | bytes 245768 | tf_op jit(solution)/shard_map/ppermute | solution.py:306
  9.6 4.4 %collective-permute-start.3 = (bf16[32,1280]{1,0:T(8,128)(2,1)S(1)}, bf16[32,1280]{1,0:T(8,128)(2,1)S(1)}, u32[]{:S(2)}, u32[]{:S(2)}) collective-permute-start(bf16[32,1280]{1,0:T(8,128)(2,1)S(1)} %get-tuple-element.27), channel_id=1, source_target_pairs={{0,8},{1,9},{2,3},{3,2},{4,12},{5,13},{6,7},{7,6},{8,0},{9,1},{10,... | collective-permute-start | bytes 245768 | tf_op jit(solution)/shard_map/ppermute | solution.py:306
  14.1 1.6 %collective-permute-start.4 = (bf16[96,1280]{1,0:T(8,128)(2,1)S(1)}, bf16[96,1280]{1,0:T(8,128)(2,1)S(1)}, u32[]{:S(2)}, u32[]{:S(2)}) collective-permute-start(bf16[96,1280]{1,0:T(8,128)(2,1)S(1)} %gather.1.got_ref), channel_id=1, source_target_pairs={{0,2},{1,3},{2,0},{3,1},{4,6},{5,7},{6,4},{7,5},{8,10},{9,11},{10,... | collective-permute-start | bytes 737288 | tf_op jit(solution)/shard_map/ppermute | solution.py:309
  16.7 6.6 %collective-permute-start.5 = (s16[32,1280]{1,0:T(8,128)(2,1)S(1)}, s16[32,1280]{1,0:T(8,128)(2,1)S(1)}, u32[]{:S(2)}, u32[]{:S(2)}) collective-permute-start(s16[32,1280]{1,0:T(8,128)(2,1)S(1)} %get-tuple-element.29), channel_id=1, source_target_pairs={{0,24},{1,25},{2,7},{3,6},{4,28},{5,29},{6,3},{7,2},{8,16},{9,17},... | collective-permute-start | bytes 245768 | tf_op jit(solution)/shard_map/ppermute | solution.py:306
  18.3 5.0 %collective-permute-start.6 = (s16[32,1280]{1,0:T(8,128)(2,1)S(1)}, s16[32,1280]{1,0:T(8,128)(2,1)S(1)}, u32[]{:S(2)}, u32[]{:S(2)}) collective-permute-start(s16[32,1280]{1,0:T(8,128)(2,1)S(1)} %get-tuple-element.30), channel_id=1, source_target_pairs={{0,4},{1,5},{2,18},{3,19},{4,0},{5,1},{6,22},{7,23},{8,12},{9,13},... | collective-permute-start | bytes 245768 | tf_op jit(solution)/shard_map/ppermute | solution.py:306
  19.5 5.0 %collective-permute-start.7 = (s16[16,1280]{1,0:T(8,128)(2,1)S(1)}, s16[16,1280]{1,0:T(8,128)(2,1)S(1)}, u32[]{:S(2)}, u32[]{:S(2)}) collective-permute-start(s16[16,1280]{1,0:T(8,128)(2,1)S(1)} %get-tuple-element.33), channel_id=1, source_target_pairs={{0,8},{1,9},{2,3},{3,2},{4,12},{5,13},{6,7},{7,6},{8,0},{9,1},{10,... | collective-permute-start | bytes 122888 | tf_op jit(solution)/shard_map/ppermute | solution.py:306
  19.5 5.0 %collective-permute-start.8 = (s16[16,1280]{1,0:T(8,128)(2,1)S(1)}, s16[16,1280]{1,0:T(8,128)(2,1)S(1)}, u32[]{:S(2)}, u32[]{:S(2)}) collective-permute-start(s16[16,1280]{1,0:T(8,128)(2,1)S(1)} %get-tuple-element.34), channel_id=1, source_target_pairs={{0,10},{1,11},{2,1},{3,0},{4,14},{5,15},{6,5},{7,4},{8,2},{9,3},{1... | collective-permute-start | bytes 122888 | tf_op jit(solution)/shard_map/ppermute | solution.py:306
  23.5 1.7 %collective-permute-start.9 = (s16[32,1280]{1,0:T(8,128)(2,1)S(1)}, s16[32,1280]{1,0:T(8,128)(2,1)S(1)}, u32[]{:S(2)}, u32[]{:S(2)}) collective-permute-start(s16[32,1280]{1,0:T(8,128)(2,1)S(1)} %get-tuple-element.37), channel_id=1, source_target_pairs={{0,2},{1,3},{2,0},{3,1},{4,6},{5,7},{6,4},{7,5},{8,10},{9,11},{10,... | collective-permute-start | bytes 245768 | tf_op jit(solution)/shard_map/ppermute | solution.py:309

commit v13 on v12

--- a/solution.py
+++ b/solution.py
@@ -102,7 +102,7 @@
         out_ref[start : start + rows, depth:] = digits_ref[...]
 
 
-def join_kernel(scale_ref, shift_ref, own_ref, got_ref, *refs):
+def join_kernel(own_ref, got_ref, *refs):
     first = on_first_core()
     rows = own_ref.shape[0] // 2
     own, got = own_ref[...].astype(jnp.float32), got_ref[...].astype(jnp.float32)
@@ -111,17 +111,20 @@
     texts = jnp.concatenate([low[rows:], high[rows:]], axis=0)
     mine = jnp.where(first, images, texts).astype(jnp.bfloat16)
     other = jnp.where(first, texts, images).astype(jnp.bfloat16)
-    for ref, block in zip(refs[:-1], (mine, other, mine, mine, other)):
+    for ref, block in zip(refs, (mine, other, mine, mine, mine, other)):
         ref[...] = block
-    pair_ref = refs[-1]
+
+
+def put_pair(upper_ref, lower_ref, out_ref):
+    rows = upper_ref.shape[0]
+    out_ref[:rows, :] = upper_ref[...]
+    out_ref[rows:, :] = lower_ref[...]
+
+
+def far_kernel(scale_ref, shift_ref, upper_ref, lower_ref, out_ref, pair_ref):
+    put_pair(upper_ref, lower_ref, out_ref)
     row = lax.broadcasted_iota(jnp.int32, pair_ref.shape, 0)
     pair_ref[...] = jnp.where(row == 0, scale_ref[0], shift_ref[0])
-
-
-def gather_kernel(*refs):
-    rows = refs[0].shape[0]
-    for k, ref in enumerate(refs[:-1]):
-        refs[-1][k * rows : (k + 1) * rows, :] = ref[...]
 
 
 def power_above(size):
@@ -195,11 +198,11 @@
     return pull, loss
 
 
-def tile_kernel(pair_ref, mine_ref, other_ref, got_ref, swapped_ref, *outs):
+def tile_kernel(pair_ref, mine_ref, other_ref, far_ref, swapped_ref, near_ref, *outs):
     rows = mine_ref.shape[0]
     scale, shift = pair_ref[0:1, 0:1], pair_ref[1:2, 0:1]
-    got = [got_ref[k * rows : (k + 1) * rows, :] for k in range(3)]
-    swapped = [swapped_ref[k * rows : (k + 1) * rows, :] for k in range(3)]
+    got = [far_ref[:rows, :], far_ref[rows:, :], near_ref[:rows, :]]
+    swapped = [swapped_ref[:rows, :], swapped_ref[rows:, :], near_ref[rows:, :]]
     mine_side = jnp.concatenate([mine_ref[...], got[0], swapped[1], got[2]], axis=0)
     other_side = jnp.concatenate([other_ref[...], swapped[0], got[1], swapped[2]], axis=0)
     lines = jnp.concatenate([got[0], mine_ref[...], got[2]], axis=0)
@@ -241,28 +244,33 @@
         put_rows([give_ref.at[side * rows : (side + 1) * rows, :]], pull, loss)
 
 
-def more_kernel(keep_ref, kept_loss_ref, same_ref, cross_ref, sum_ref, sum_loss_ref):
+def more_kernel(keep_ref, kept_loss_ref, same_ref, cross_ref, image_ref, text_ref, sum_ref, sum_loss_ref, *units):
     rows, depth = keep_ref.shape[1:]
     for side, ref in enumerate((same_ref, cross_ref)):
         pull, loss = total([ref[...]], rows, depth)
         sum_ref[side] = keep_ref[side] + pull
         sum_loss_ref[side] = kept_loss_ref[side] + loss
-
-
-def final_kernel(pairs, image_ref, text_ref, keep_ref, kept_loss_ref, got_ref, loss_ref, grad_image_ref, grad_text_ref):
+    for side, ref in enumerate((image_ref, text_ref)):
+        unit, inverse = unit_rows(ref[...])
+        units[0][side] = unit
+        units[1][side] = jnp.broadcast_to(inverse, units[1].shape[1:])
+
+
+def final_kernel(pairs, keep_ref, kept_loss_ref, unit_ref, inverse_ref, got_ref, loss_ref, grad_image_ref, grad_text_ref):
     first = on_first_core()
-    rows, depth = image_ref.shape
+    rows, depth = keep_ref.shape[1:]
     pulls, losses = [], []
     for side in (0, 1):
         pull, loss = total([got_ref[(1 - side) * rows : (2 - side) * rows, :]], rows, depth)
         pulls.append(keep_ref[side] + pull)
         losses.append(kept_loss_ref[side][:, 0:1] + loss)
-    for source, pull, out in (
-        (image_ref, jnp.where(first, pulls[0], pulls[1]), grad_image_ref),
-        (text_ref, jnp.where(first, pulls[1], pulls[0]), grad_text_ref),
+    for side, (pull, out) in enumerate(
+        (
+            (jnp.where(first, pulls[0], pulls[1]), grad_image_ref),
+            (jnp.where(first, pulls[1], pulls[0]), grad_text_ref),
+        )
     ):
-        unit, inverse = unit_rows(source[...])
-        out[...] = project_back(unit, inverse, pull)
+        out[...] = project_back(unit_ref[side], inverse_ref[side][:, 0:1], pull)
     row = lax.broadcasted_iota(jnp.int32, (rows, rows), 0)
     column = lax.broadcasted_iota(jnp.int32, (rows, rows), 1)
     loss = jnp.where(first, losses[0], losses[1])
@@ -308,43 +316,52 @@
     def swap(x):
         return lax.ppermute(x, AXES, [(i, i ^ lanes) for i in range(n)])
 
-    visits = ((12, 3), (2, 8), (4, 1))
+    visits = ((12, 3), (2, 8), (4, 1), (4, 1))
+    crosses = (0, 0, 0, 1)
+    late = pl.CostEstimate(flops=10**9, bytes_accessed=10**7, transcendentals=0)
     digits = call(
-        digits_kernel, jax.ShapeDtypeStruct((rows, LANES), jnp.bfloat16), [pair_class], "digits", cost=pl.CostEstimate(flops=10**9, bytes_accessed=10**7, transcendentals=0)
+        digits_kernel,
+        jax.ShapeDtypeStruct((rows, LANES), jnp.bfloat16),
+        [pair_class],
+        "digits",
+        cost=late,
     )
     own = call(pack_kernel, block(2), [image_emb, text_emb, digits], "pack")
-    *sent, mine, other, pair = call(
-        join_kernel,
-        (block(2),) * 5 + (wide(8, LANES),),
-        [scale[None], shift[None], own, swap(own)],
-        "join",
+    *sent, mine, other = call(join_kernel, (block(2),) * 6, [own, swap(own)], "join")
+    got = [visit(*three) for three in zip(sent, visits, crosses)]
+    far, pair = call(
+        far_kernel,
+        (block(4), wide(8, LANES)),
+        [scale[None], shift[None], *got[:2]],
+        "far",
         2,
     )
-    got = [visit(x, masks) for x, masks in zip(sent, visits)]
-    got = call(gather_kernel, block(6), got, "gather")
+    near = call(put_pair, block(4), got[2:], "near", cost=late)
     one, two = block(1, jnp.int16), block(2, jnp.int16)
     parts = call(
-        tile_kernel, (two, two, one, one, two), [pair, mine, other, got, swap(got)], "tile"
-    )
-    back = [visit(x, masks) for x, masks in zip(parts, visits)]
-    cross = visit(parts[3], visits[2], 1)
+        tile_kernel,
+        (two, two, one, one, two),
+        [pair, mine, other, far, swap(far), near],
+        "tile",
+    )
+    back = [visit(*three) for three in zip(parts, visits, crosses)]
     keep, kept_loss, give = call(
         add_kernel,
         (wide(2, rows, depth), wide(2, rows, LANES), two),
         [parts[4], *back[:2]],
         "add",
     )
-    keep, kept_loss = call(
+    sums = call(
         more_kernel,
-        (wide(2, rows, depth), wide(2, rows, LANES)),
-        [keep, kept_loss, back[2], cross],
+        (wide(2, rows, depth), wide(2, rows, LANES)) * 2,
+        [keep, kept_loss, *back[2:], image_emb, text_emb],
         "more",
-        cost=pl.CostEstimate(flops=10**9, bytes_accessed=10**7, transcendentals=0),
+        cost=late,
     )
     loss, grad_image, grad_text = call(
         functools.partial(final_kernel, n * rows),
         (wide(1, rows), wide(rows, depth), wide(rows, depth)),
-        [image_emb, text_emb, keep, kept_loss, swap(give)],
+        [*sums, swap(give)],
         "final",
     )
     return (loss[0], grad_image, grad_text)

time: 26.2 us -> 25.5 us (0.973)
  waiting for transfers between devices: 9.3 us -> 6.21 us
  starting transfers between devices: 11.5 us -> 13.8 us
    ppermute x7 -> x8, waiting for transfers between devices: 7.25 us -> 4.76 us  [visit(): return lax.ppermute(x, AXES, pairs)]
    ppermute x7 -> x8, starting transfers between devices: 10.1 us -> 12.6 us  [visit(): return lax.ppermute(x, AXES, pairs)]
    ppermute x3, waiting for transfers between devices: 2.06 us -> 1.45 us  [swap(): return lax.ppermute(x, AXES, [(i, i ^ lanes) for i in range(n)])]
    pallas_call x8 -> x9, Pallas kernels: 2.59 us -> 2.59 us  [call(): pl.pallas_call(kernel, cost_estimate=cost, out_shape=shapes, in_specs=[sm...]
  transfers between devices with their start and end apart: 10 -> 11, of which waited for: 7 -> 7; matrix products, arithmetic and copies ran while one was open for 0% -> 0% of each run, Pallas kernels for 1% -> 2%
where the time goes in v13:
time: 25.5 us; the launch traced here: 25.3 us
  starting transfers between devices  13.8 us (54%)
  waiting for transfers between devices  6.21 us (24%)
  Pallas kernels  2.59 us (10%)
  between operations  2.02 us (8%)
  local copies, waits for them, and re-layouts  0.67 us (3%)
    ppermute x8, starting transfers between devices, visit(): return lax.ppermute(x, AXES, pairs)  12.6 us
    ppermute x8, waiting for transfers between devices, visit(): return lax.ppermute(x, AXES, pairs)  4.76 us
    pallas_call x9, Pallas kernels, call(): pl.pallas_call(kernel, cost_estimate=cost, out_shape=shapes, in_specs=[sm...  2.59 us
    ppermute x3, waiting for transfers between devices, swap(): return lax.ppermute(x, AXES, [(i, i ^ lanes) for i in range(n)])  1.45 us
    ppermute x3, starting transfers between devices, swap(): return lax.ppermute(x, AXES, [(i, i ^ lanes) for i in range(n)])  1.23 us
    unnamed x6, local copies, waits for them, and re-layouts  0.67 us
  transfers between devices with their start and end apart: 11, of which 7 were waited for; matrix products, arithmetic and copies ran while one was open for 0% of the time, Pallas kernels for 2%

profile of v13, /device:TPU:0, one launch (start us, length us, event | category | flops | bytes accessed | tf_op | source)
XLA Modules:
  0.0 25.3 jit_solution(12302473703991453470)
XLA Ops:
  0.6 0.0 copy-start.1
  0.6 0.0 copy-start
  0.7 0.0 copy-start.2
  0.7 0.7 %copy-done.2 = s32[16]{0:T(128)S(1)} copy-done((s32[16]{0:T(128)S(1)}, s32[16]{0:T(128)}, u32[]{:S(2)}) %copy-start.2) | copy-done | bytes 88
  1.3 0.1 digits.1.digits_ref
  1.4 0.0 copy-done.1
  1.4 0.0 copy-done
  1.4 0.1 pack.1.own_ref
  1.5 0.5 %collective-permute-start = (bf16[32,1280]{1,0:T(8,128)(2,1)S(1)}, bf16[32,1280]{1,0:T(8,128)(2,1)S(1)}, u32[]{:S(2)}, u32[]{:S(2)}) collective-permute-start(bf16[32,1280]{1,0:T(8,128)(2,1)S(1)} %pack.1.own_ref), channel_id=1, source_target_pairs={{0,2},{1,3},{2,0},{3,1},{4,6},{5,7},{6,4},{7,5},{8,10},{9,11},{10,... | collective-permute-start | bytes 245768 | tf_op jit(solution)/shard_map/ppermute | solution.py:317
  2.1 0.9 %collective-permute-done.got_ref = bf16[32,1280]{1,0:T(8,128)(2,1)S(1)} collective-permute-done((bf16[32,1280]{1,0:T(8,128)(2,1)S(1)}, bf16[32,1280]{1,0:T(8,128)(2,1)S(1)}, u32[]{:S(2)}, u32[]{:S(2)}) %collective-permute-start) | collective-permute-done | bytes 81952 | tf_op jit(solution)/shard_map/ppermute | solution.py:317
  3.0 0.1 join.1
  3.1 5.0 %collective-permute-start.1 = (bf16[32,1280]{1,0:T(8,128)(2,1)S(1)}, bf16[32,1280]{1,0:T(8,128)(2,1)S(1)}, u32[]{:S(2)}, u32[]{:S(2)}) collective-permute-start(bf16[32,1280]{1,0:T(8,128)(2,1)S(1)} %get-tuple-element.26), channel_id=1, source_target_pairs={{0,24},{1,25},{2,7},{3,6},{4,28},{5,29},{6,3},{7,2},{8,16},{9,17},... | collective-permute-start | bytes 245768 | tf_op jit(solution)/shard_map/ppermute | solution.py:314
  8.1 1.5 %collective-permute-start.2 = (bf16[32,1280]{1,0:T(8,128)(2,1)S(1)}, bf16[32,1280]{1,0:T(8,128)(2,1)S(1)}, u32[]{:S(2)}, u32[]{:S(2)}) collective-permute-start(bf16[32,1280]{1,0:T(8,128)(2,1)S(1)} %get-tuple-element.27), channel_id=1, source_target_pairs={{0,4},{1,5},{2,18},{3,19},{4,0},{5,1},{6,22},{7,23},{8,12},{9,13},... | collective-permute-start | bytes 245768 | tf_op jit(solution)/shard_map/ppermute | solution.py:314
  9.6 0.0 collective-permute-start.4
  9.6 0.9 %collective-permute-start.5 = (bf16[32,1280]{1,0:T(8,128)(2,1)S(1)}, bf16[32,1280]{1,0:T(8,128)(2,1)S(1)}, u32[]{:S(2)}, u32[]{:S(2)}) collective-permute-start(bf16[32,1280]{1,0:T(8,128)(2,1)S(1)} %get-tuple-element.33), channel_id=1, source_target_pairs={{0,10},{1,11},{2,1},{3,0},{4,14},{5,15},{6,5},{7,4},{8,2},{9,3},{1... | collective-permute-start | bytes 245768 | tf_op jit(solution)/shard_map/ppermute | solution.py:314
  11.8 0.0 collective-permute-done.1.upper_ref
  11.8 0.7 %collective-permute-done.2.lower_ref = bf16[32,1280]{1,0:T(8,128)(2,1)S(1)} collective-permute-done((bf16[32,1280]{1,0:T(8,128)(2,1)S(1)}, bf16[32,1280]{1,0:T(8,128)(2,1)S(1)}, u32[]{:S(2)}, u32[]{:S(2)}) %collective-permute-start.2) | collective-permute-done | bytes 81952 | tf_op jit(solution)/shard_map/ppermute | solution.py:314
  12.5 0.1 collective-permute-start.3
  12.6 1.4 %collective-permute-done.4.upper_ref = bf16[32,1280]{1,0:T(8,128)(2,1)S(1)} collective-permute-done((bf16[32,1280]{1,0:T(8,128)(2,1)S(1)}, bf16[32,1280]{1,0:T(8,128)(2,1)S(1)}, u32[]{:S(2)}, u32[]{:S(2)}) %collective-permute-start.4) | collective-permute-done | bytes 81952 | tf_op jit(solution)/shard_map/ppermute | solution.py:314
  14.0 0.0 collective-permute-done.5.lower_ref
  14.0 0.0 collective-permute-done.3.swapped_ref
  14.0 1.0 %tile.1 = (s16[32,1280]{1,0:T(8,128)(2,1)S(1)}, s16[32,1280]{1,0:T(8,128)(2,1)S(1)}, s16[16,1280]{1,0:T(8,128)(2,1)S(1)}, s16[16,1280]{1,0:T(8,128)(2,1)S(1)}, s16[32,1280]{1,0:T(8,128)(2,1)S(1)}) custom-call(f32[8,128]{1,0:T(8,128)S(1)} %get-tuple-element.28.pair_ref, bf16[32,1280]{1,0:T(8,128)(2,1)S(1)} %get-tuple-element.29.mine_ref, ...), custom_call_target="tpu_custom_call" | custom-call | tf_op jit(solution)/shard_map/tile/pallas_call | solution.py:290
  15.1 3.1 %collective-permute-start.6 = (s16[32,1280]{1,0:T(8,128)(2,1)S(1)}, s16[32,1280]{1,0:T(8,128)(2,1)S(1)}, u32[]{:S(2)}, u32[]{:S(2)}) collective-permute-start(s16[32,1280]{1,0:T(8,128)(2,1)S(1)} %get-tuple-element.35), channel_id=1, source_target_pairs={{0,24},{1,25},{2,7},{3,6},{4,28},{5,29},{6,3},{7,2},{8,16},{9,17},... | collective-permute-start | bytes 245768 | tf_op jit(solution)/shard_map/ppermute | solution.py:314
  18.1 0.9 %collective-permute-start.7 = (s16[32,1280]{1,0:T(8,128)(2,1)S(1)}, s16[32,1280]{1,0:T(8,128)(2,1)S(1)}, u32[]{:S(2)}, u32[]{:S(2)}) collective-permute-start(s16[32,1280]{1,0:T(8,128)(2,1)S(1)} %get-tuple-element.36), channel_id=1, source_target_pairs={{0,4},{1,5},{2,18},{3,19},{4,0},{5,1},{6,22},{7,23},{8,12},{9,13},... | collective-permute-start | bytes 245768 | tf_op jit(solution)/shard_map/ppermute | solution.py:314
  19.0 0.0 collective-permute-start.8
  19.0 1.2 %collective-permute-start.9 = (s16[16,1280]{1,0:T(8,128)(2,1)S(1)}, s16[16,1280]{1,0:T(8,128)(2,1)S(1)}, u32[]{:S(2)}, u32[]{:S(2)}) collective-permute-start(s16[16,1280]{1,0:T(8,128)(2,1)S(1)} %get-tuple-element.40), channel_id=1, source_target_pairs={{0,10},{1,11},{2,1},{3,0},{4,14},{5,15},{6,5},{7,4},{8,2},{9,3},{1... | collective-permute-start | bytes 122888 | tf_op jit(solution)/shard_map/ppermute | solution.py:314
  20.2 2.1 %collective-permute-done.6.back_0 = s16[32,1280]{1,0:T(8,128)(2,1)S(1)} collective-permute-done((s16[32,1280]{1,0:T(8,128)(2,1)S(1)}, s16[32,1280]{1,0:T(8,128)(2,1)S(1)}, u32[]{:S(2)}, u32[]{:S(2)}) %collective-permute-start.6) | collective-permute-done | bytes 81952 | tf_op jit(solution)/shard_map/ppermute | solution.py:314
  22.2 0.4 %collective-permute-done.7.back_1 = s16[32,1280]{1,0:T(8,128)(2,1)S(1)} collective-permute-done((s16[32,1280]{1,0:T(8,128)(2,1)S(1)}, s16[32,1280]{1,0:T(8,128)(2,1)S(1)}, u32[]{:S(2)}, u32[]{:S(2)}) %collective-permute-start.7) | collective-permute-done | bytes 81952 | tf_op jit(solution)/shard_map/ppermute | solution.py:314
  22.6 0.2 add.1
  22.8 0.6 %collective-permute-start.10 = (s16[32,1280]{1,0:T(8,128)(2,1)S(1)}, s16[32,1280]{1,0:T(8,128)(2,1)S(1)}, u32[]{:S(2)}, u32[]{:S(2)}) collective-permute-start(s16[32,1280]{1,0:T(8,128)(2,1)S(1)} %get-tuple-element.45), channel_id=1, source_target_pairs={{0,2},{1,3},{2,0},{3,1},{4,6},{5,7},{6,4},{7,5},{8,10},{9,11},{10,... | collective-permute-start | bytes 245768 | tf_op jit(solution)/shard_map/ppermute | solution.py:317
  23.5 0.2 collective-permute-done.8.same_ref
  23.7 0.0 collective-permute-done.9.cross_ref
  23.7 0.2 more.1
  23.9 0.5 %collective-permute-done.10.got_ref = s16[32,1280]{1,0:T(8,128)(2,1)S(1)} collective-permute-done((s16[32,1280]{1,0:T(8,128)(2,1)S(1)}, s16[32,1280]{1,0:T(8,128)(2,1)S(1)}, u32[]{:S(2)}, u32[]{:S(2)}) %collective-permute-start.10) | collective-permute-done | bytes 81952 | tf_op jit(solution)/shard_map/ppermute | solution.py:317
  24.4 0.9 %final.1 = (f32[1,16]{1,0:T(1,128)}, f32[16,1152]{1,0:T(8,128)}, f32[16,1152]{1,0:T(8,128)}) custom-call(f32[2,16,1152]{2,1,0:T(8,128)S(1)} %get-tuple-element.41.keep_ref, f32[2,16,128]{2,1,0:T(8,128)S(1)} %get-tuple-element.42.kept_loss_ref, f32[2,16,1152]{2,1,0:T(8,128)S(1)} %get-tuple-element.43.unit_ref, ...), custom_call_target="tpu_custom_call" | custom-call | tf_op jit(solution)/shard_map/final/pallas_call | solution.py:290
  (2 shorter events, 0.0 us)
Async XLA Ops:
  0.6 0.8 %copy-start.1 = (bf16[16,1152]{1,0:T(8,128)(2,1)S(1)}, bf16[16,1152]{1,0:T(8,128)(2,1)}, u32[]{:S(2)}) copy-start(bf16[16,1152]{1,0:T(8,128)(2,1)} %text_ref.3) | copy-start | bytes 110596
  0.6 0.8 %copy-start = (bf16[16,1152]{1,0:T(8,128)(2,1)S(1)}, bf16[16,1152]{1,0:T(8,128)(2,1)}, u32[]{:S(2)}) copy-start(bf16[16,1152]{1,0:T(8,128)(2,1)} %image_ref.3) | copy-start | bytes 110596
  0.7 0.7 %copy-start.2 = (s32[16]{0:T(128)S(1)}, s32[16]{0:T(128)}, u32[]{:S(2)}) copy-start(s32[16]{0:T(128)} %class_ref.1) | copy-start | bytes 196
  1.5 1.4 %collective-permute-start = (bf16[32,1280]{1,0:T(8,128)(2,1)S(1)}, bf16[32,1280]{1,0:T(8,128)(2,1)S(1)}, u32[]{:S(2)}, u32[]{:S(2)}) collective-permute-start(bf16[32,1280]{1,0:T(8,128)(2,1)S(1)} %pack.1.own_ref), channel_id=1, source_target_pairs={{0,2},{1,3},{2,0},{3,1},{4,6},{5,7},{6,4},{7,5},{8,10},{9,11},{10,... | collective-permute-start | bytes 245768 | tf_op jit(solution)/shard_map/ppermute | solution.py:317
  3.1 8.8 %collective-permute-start.1 = (bf16[32,1280]{1,0:T(8,128)(2,1)S(1)}, bf16[32,1280]{1,0:T(8,128)(2,1)S(1)}, u32[]{:S(2)}, u32[]{:S(2)}) collective-permute-start(bf16[32,1280]{1,0:T(8,128)(2,1)S(1)} %get-tuple-element.26), channel_id=1, source_target_pairs={{0,24},{1,25},{2,7},{3,6},{4,28},{5,29},{6,3},{7,2},{8,16},{9,17},... | collective-permute-start | bytes 245768 | tf_op jit(solution)/shard_map/ppermute | solution.py:314
  8.1 4.4 %collective-permute-start.2 = (bf16[32,1280]{1,0:T(8,128)(2,1)S(1)}, bf16[32,1280]{1,0:T(8,128)(2,1)S(1)}, u32[]{:S(2)}, u32[]{:S(2)}) collective-permute-start(bf16[32,1280]{1,0:T(8,128)(2,1)S(1)} %get-tuple-element.27), channel_id=1, source_target_pairs={{0,4},{1,5},{2,18},{3,19},{4,0},{5,1},{6,22},{7,23},{8,12},{9,13},... | collective-permute-start | bytes 245768 | tf_op jit(solution)/shard_map/ppermute | solution.py:314
  9.6 4.4 %collective-permute-start.4 = (bf16[32,1280]{1,0:T(8,128)(2,1)S(1)}, bf16[32,1280]{1,0:T(8,128)(2,1)S(1)}, u32[]{:S(2)}, u32[]{:S(2)}) collective-permute-start(bf16[32,1280]{1,0:T(8,128)(2,1)S(1)} %get-tuple-element.32), channel_id=1, source_target_pairs={{0,8},{1,9},{2,3},{3,2},{4,12},{5,13},{6,7},{7,6},{8,0},{9,1},{10,... | collective-permute-start | bytes 245768 | tf_op jit(solution)/shard_map/ppermute | solution.py:314
  9.6 4.4 %collective-permute-start.5 = (bf16[32,1280]{1,0:T(8,128)(2,1)S(1)}, bf16[32,1280]{1,0:T(8,128)(2,1)S(1)}, u32[]{:S(2)}, u32[]{:S(2)}) collective-permute-start(bf16[32,1280]{1,0:T(8,128)(2,1)S(1)} %get-tuple-element.33), channel_id=1, source_target_pairs={{0,10},{1,11},{2,1},{3,0},{4,14},{5,15},{6,5},{7,4},{8,2},{9,3},{1... | collective-permute-start | bytes 245768 | tf_op jit(solution)/shard_map/ppermute | solution.py:314
  12.5 1.5 %collective-permute-start.3 = (bf16[64,1280]{1,0:T(8,128)(2,1)S(1)}, bf16[64,1280]{1,0:T(8,128)(2,1)S(1)}, u32[]{:S(2)}, u32[]{:S(2)}) collective-permute-start(bf16[64,1280]{1,0:T(8,128)(2,1)S(1)} %get-tuple-element.31.far_ref), channel_id=1, source_target_pairs={{0,2},{1,3},{2,0},{3,1},{4,6},{5,7},{6,4},{7,5},{8,10},{9,11},{10,... | collective-permute-start | bytes 491528 | tf_op jit(solution)/shard_map/ppermute | solution.py:317
  15.1 7.2 %collective-permute-start.6 = (s16[32,1280]{1,0:T(8,128)(2,1)S(1)}, s16[32,1280]{1,0:T(8,128)(2,1)S(1)}, u32[]{:S(2)}, u32[]{:S(2)}) collective-permute-start(s16[32,1280]{1,0:T(8,128)(2,1)S(1)} %get-tuple-element.35), channel_id=1, source_target_pairs={{0,24},{1,25},{2,7},{3,6},{4,28},{5,29},{6,3},{7,2},{8,16},{9,17},... | collective-permute-start | bytes 245768 | tf_op jit(solution)/shard_map/ppermute | solution.py:314
  18.1 4.4 %collective-permute-start.7 = (s16[32,1280]{1,0:T(8,128)(2,1)S(1)}, s16[32,1280]{1,0:T(8,128)(2,1)S(1)}, u32[]{:S(2)}, u32[]{:S(2)}) collective-permute-start(s16[32,1280]{1,0:T(8,128)(2,1)S(1)} %get-tuple-element.36), channel_id=1, source_target_pairs={{0,4},{1,5},{2,18},{3,19},{4,0},{5,1},{6,22},{7,23},{8,12},{9,13},... | collective-permute-start | bytes 245768 | tf_op jit(solution)/shard_map/ppermute | solution.py:314
  19.0 4.7 %collective-permute-start.8 = (s16[16,1280]{1,0:T(8,128)(2,1)S(1)}, s16[16,1280]{1,0:T(8,128)(2,1)S(1)}, u32[]{:S(2)}, u32[]{:S(2)}) collective-permute-start(s16[16,1280]{1,0:T(8,128)(2,1)S(1)} %get-tuple-element.39), channel_id=1, source_target_pairs={{0,8},{1,9},{2,3},{3,2},{4,12},{5,13},{6,7},{7,6},{8,0},{9,1},{10,... | collective-permute-start | bytes 122888 | tf_op jit(solution)/shard_map/ppermute | solution.py:314
  19.0 4.7 %collective-permute-start.9 = (s16[16,1280]{1,0:T(8,128)(2,1)S(1)}, s16[16,1280]{1,0:T(8,128)(2,1)S(1)}, u32[]{:S(2)}, u32[]{:S(2)}) collective-permute-start(s16[16,1280]{1,0:T(8,128)(2,1)S(1)} %get-tuple-element.40), channel_id=1, source_target_pairs={{0,10},{1,11},{2,1},{3,0},{4,14},{5,15},{6,5},{7,4},{8,2},{9,3},{1... | collective-permute-start | bytes 122888 | tf_op jit(solution)/shard_map/ppermute | solution.py:314
  22.8 1.6 %collective-permute-start.10 = (s16[32,1280]{1,0:T(8,128)(2,1)S(1)}, s16[32,1280]{1,0:T(8,128)(2,1)S(1)}, u32[]{:S(2)}, u32[]{:S(2)}) collective-permute-start(s16[32,1280]{1,0:T(8,128)(2,1)S(1)} %get-tuple-element.45), channel_id=1, source_target_pairs={{0,2},{1,3},{2,0},{3,1},{4,6},{5,7},{6,4},{7,5},{8,10},{9,11},{10,... | collective-permute-start | bytes 245768 | tf_op jit(solution)/shard_map/ppermute | solution.py:317

commit v14 on v13

--- a/solution.py
+++ b/solution.py
@@ -159,7 +159,7 @@
         out[:, depth:] = tail[k * rows : (k + 1) * rows]
 
 
-def partial_pull(lines, columns, scale, shift):
+def tile_terms_of(lines, columns, scale, shift):
     depth = lines.shape[1] - LANES
     logits = (
         scale
@@ -191,32 +191,36 @@
     small = jnp.exp(-jnp.abs(margin))
     over = 1.0 / (1.0 + small)
     coef = -sign * jnp.where(margin >= 0, small * over, over) * scale
+    return jnp.log1p(small) - jnp.minimum(margin, 0.0), coef
+
+
+def pulls_of(loss, coef, columns):
+    depth = columns.shape[1] - LANES
     pull = jnp.dot(
         coef.astype(jnp.bfloat16), columns[:, :depth], preferred_element_type=jnp.float32
     )
-    loss = jnp.sum(jnp.log1p(small) - jnp.minimum(margin, 0.0), axis=1, keepdims=True)
-    return pull, loss
+    return pull, jnp.sum(loss, axis=1, keepdims=True)
 
 
 def tile_kernel(pair_ref, mine_ref, other_ref, far_ref, swapped_ref, near_ref, *outs):
     rows = mine_ref.shape[0]
     scale, shift = pair_ref[0:1, 0:1], pair_ref[1:2, 0:1]
-    got = [far_ref[:rows, :], far_ref[rows:, :], near_ref[:rows, :]]
-    swapped = [swapped_ref[:rows, :], swapped_ref[rows:, :], near_ref[rows:, :]]
-    mine_side = jnp.concatenate([mine_ref[...], got[0], swapped[1], got[2]], axis=0)
-    other_side = jnp.concatenate([other_ref[...], swapped[0], got[1], swapped[2]], axis=0)
-    lines = jnp.concatenate([got[0], mine_ref[...], got[2]], axis=0)
-    pull, loss = partial_pull(lines, other_side, scale, shift)
-    put_rows([outs[0], outs[4]], pull[: 2 * rows], loss[: 2 * rows])
+    lines = jnp.concatenate(
+        [far_ref[:rows, :], near_ref[:rows, :], mine_ref[...], swapped_ref[rows:, :]], axis=0
+    )
+    columns = jnp.concatenate(
+        [far_ref[rows:, :], swapped_ref[:rows, :], near_ref[rows:, :], other_ref[...]], axis=0
+    )
+    loss, coef = tile_terms_of(lines, columns, scale, shift)
+    put_rows([outs[0], outs[1], outs[4]], *pulls_of(loss[: 3 * rows], coef[: 3 * rows], columns))
+    first = on_first_core()
     half = rows // 2
-    first = on_first_core()
-    last = []
-    for part in (pull, loss):
-        low, high = part[2 * rows : 2 * rows + half], part[2 * rows + half :]
-        last.append((jnp.where(first, low, high), jnp.where(first, high, low)))
-    for out, part, part_loss in zip(outs[2:4], *last):
-        put_rows([out], part, part_loss)
-    put_rows([outs[1]], *partial_pull(got[1], mine_side, scale, shift))
+    halves = []
+    for part in pulls_of(loss.T[:rows], coef.T[:rows], lines):
+        low, high = part[:half], part[half:]
+        halves.append((jnp.where(first, low, high), jnp.where(first, high, low)))
+    for out, pull, part_loss in zip(outs[2:4], *halves):
+        put_rows([out], pull, part_loss)
 
 
 def total(parts, rows, depth):
@@ -235,35 +239,34 @@
 
 
 def add_kernel(own_ref, back_0, back_1, keep_ref, loss_ref, give_ref):
-    rows, depth = keep_ref.shape[1:]
+    rows, depth = keep_ref.shape
     own, other = place_of(on_first_core(), rows)
-    for side, parts in enumerate(((own_ref, back_0), (back_1,))):
-        keep_ref[side], loss = total([part[own, :] for part in parts], rows, depth)
-        loss_ref[side] = jnp.broadcast_to(loss, loss_ref.shape[1:])
-        pull, loss = total([part[other, :] for part in parts], rows, depth)
-        put_rows([give_ref.at[side * rows : (side + 1) * rows, :]], pull, loss)
+    parts = (own_ref, back_0, back_1)
+    pull, loss = total([part[other, :] for part in parts], rows, depth)
+    put_rows([give_ref], pull, loss)
+    keep_ref[...], loss = total([part[own, :] for part in parts], rows, depth)
+    loss_ref[...] = jnp.broadcast_to(loss, loss_ref.shape)
 
 
 def more_kernel(keep_ref, kept_loss_ref, same_ref, cross_ref, image_ref, text_ref, sum_ref, sum_loss_ref, *units):
-    rows, depth = keep_ref.shape[1:]
-    for side, ref in enumerate((same_ref, cross_ref)):
-        pull, loss = total([ref[...]], rows, depth)
-        sum_ref[side] = keep_ref[side] + pull
-        sum_loss_ref[side] = kept_loss_ref[side] + loss
+    rows, depth = keep_ref.shape
+    pull, loss = total([cross_ref], rows, depth)
+    sum_ref[0] = keep_ref[...] + pull
+    sum_loss_ref[0] = kept_loss_ref[...] + loss
+    sum_ref[1], loss = total([same_ref], rows, depth)
+    sum_loss_ref[1] = jnp.broadcast_to(loss, sum_loss_ref.shape[1:])
     for side, ref in enumerate((image_ref, text_ref)):
         unit, inverse = unit_rows(ref[...])
         units[0][side] = unit
         units[1][side] = jnp.broadcast_to(inverse, units[1].shape[1:])
 
 
-def final_kernel(pairs, keep_ref, kept_loss_ref, unit_ref, inverse_ref, got_ref, loss_ref, grad_image_ref, grad_text_ref):
+def final_kernel(pairs, sum_ref, sum_loss_ref, unit_ref, inverse_ref, got_ref, loss_ref, grad_image_ref, grad_text_ref):
     first = on_first_core()
-    rows, depth = keep_ref.shape[1:]
-    pulls, losses = [], []
-    for side in (0, 1):
-        pull, loss = total([got_ref[(1 - side) * rows : (2 - side) * rows, :]], rows, depth)
-        pulls.append(keep_ref[side] + pull)
-        losses.append(kept_loss_ref[side][:, 0:1] + loss)
+    rows, depth = sum_ref.shape[1:]
+    pull, loss = total([got_ref], rows, depth)
+    pulls = (sum_ref[0], sum_ref[1] + pull)
+    losses = (sum_loss_ref[0][:, 0:1], sum_loss_ref[1][:, 0:1] + loss)
     for side, (pull, out) in enumerate(
         (
             (jnp.where(first, pulls[0], pulls[1]), grad_image_ref),
@@ -306,7 +309,7 @@
     def core(i):
         return i // lanes % 2
 
-    def visit(x, masks, cross=0):
+    def visit(x, masks, cross):
         pairs = []
         for i in range(n):
             chip = (i // (2 * lanes) * lanes + i % lanes) ^ masks[core(i)]
@@ -316,8 +319,8 @@
     def swap(x):
         return lax.ppermute(x, AXES, [(i, i ^ lanes) for i in range(n)])
 
-    visits = ((12, 3), (2, 8), (4, 1), (4, 1))
-    crosses = (0, 0, 0, 1)
+    out_visits = (((12, 3), 0), ((2, 8), 0), ((4, 1), 0), ((4, 1), 1))
+    back_visits = (((12, 3), 0), ((4, 1), 0), ((2, 8), 0), ((2, 8), 1))
     late = pl.CostEstimate(flops=10**9, bytes_accessed=10**7, transcendentals=0)
     digits = call(
         digits_kernel,
@@ -328,7 +331,7 @@
     )
     own = call(pack_kernel, block(2), [image_emb, text_emb, digits], "pack")
     *sent, mine, other = call(join_kernel, (block(2),) * 6, [own, swap(own)], "join")
-    got = [visit(*three) for three in zip(sent, visits, crosses)]
+    got = [visit(x, *way) for x, way in zip(sent, out_visits)]
     far, pair = call(
         far_kernel,
         (block(4), wide(8, LANES)),
@@ -344,10 +347,10 @@
         [pair, mine, other, far, swap(far), near],
         "tile",
     )
-    back = [visit(*three) for three in zip(parts, visits, crosses)]
+    back = [visit(x, *way) for x, way in zip(parts, back_visits)]
     keep, kept_loss, give = call(
         add_kernel,
-        (wide(2, rows, depth), wide(2, rows, LANES), two),
+        (wide(rows, depth), wide(rows, LANES), one),
         [parts[4], *back[:2]],
         "add",
     )

time: 25.5 us -> 25.5 us (level)
  waiting for transfers between devices: 6.21 us -> 8.08 us
  starting transfers between devices: 13.8 us -> 12.2 us
  Pallas kernels: 2.59 us -> 2.29 us
    ppermute x8, waiting for transfers between devices: 4.76 us -> 6.12 us  [visit(): return lax.ppermute(x, AXES, pairs)]
    ppermute x8, starting transfers between devices: 12.6 us -> 11.6 us  [visit(): return lax.ppermute(x, AXES, pairs)]
    ppermute x3, starting transfers between devices: 1.23 us -> 0.67 us  [swap(): return lax.ppermute(x, AXES, [(i, i ^ lanes) for i in range(n)])]
    ppermute x3, waiting for transfers between devices: 1.45 us -> 1.96 us  [swap(): return lax.ppermute(x, AXES, [(i, i ^ lanes) for i in range(n)])]
    pallas_call x9, Pallas kernels: 2.59 us -> 2.29 us  [call(): pl.pallas_call(kernel, cost_estimate=cost, out_shape=shapes, in_specs=[sm...]
  transfers between devices with their start and end apart: 11 -> 11, of which waited for: 7 -> 6; matrix products, arithmetic and copies ran while one was open for 0% -> 0% of each run, Pallas kernels for 2% -> 2%
where the time goes in v14:
time: 25.5 us; the launch traced here: 25.3 us
  starting transfers between devices  12.2 us (48%)
  waiting for transfers between devices  8.08 us (32%)
  Pallas kernels  2.29 us (9%)
  between operations  2.05 us (8%)
  local copies, waits for them, and re-layouts  0.67 us (3%)
    ppermute x8, starting transfers between devices, visit(): return lax.ppermute(x, AXES, pairs)  11.6 us
    ppermute x8, waiting for transfers between devices, visit(): return lax.ppermute(x, AXES, pairs)  6.12 us
    pallas_call x9, Pallas kernels, call(): pl.pallas_call(kernel, cost_estimate=cost, out_shape=shapes, in_specs=[sm...  2.29 us
    ppermute x3, waiting for transfers between devices, swap(): return lax.ppermute(x, AXES, [(i, i ^ lanes) for i in range(n)])  1.96 us
    unnamed x6, local copies, waits for them, and re-layouts  0.67 us
    ppermute x3, starting transfers between devices, swap(): return lax.ppermute(x, AXES, [(i, i ^ lanes) for i in range(n)])  0.67 us
  transfers between devices with their start and end apart: 11, of which 6 were waited for; matrix products, arithmetic and copies ran while one was open for 0% of the time, Pallas kernels for 2%

profile of v14, /device:TPU:0, one launch (start us, length us, event | category | flops | bytes accessed | tf_op | source)
XLA Modules:
  0.0 25.3 jit_solution(18324730229173019462)
XLA Ops:
  0.6 0.0 copy-start.1
  0.6 0.0 copy-start
  0.7 0.0 copy-start.2
  0.7 0.7 %copy-done.2 = s32[16]{0:T(128)S(1)} copy-done((s32[16]{0:T(128)S(1)}, s32[16]{0:T(128)}, u32[]{:S(2)}) %copy-start.2) | copy-done | bytes 88
  1.3 0.1 digits.1.digits_ref
  1.4 0.0 copy-done.1
  1.4 0.0 copy-done
  1.4 0.1 pack.1.own_ref
  1.5 0.5 %collective-permute-start = (bf16[32,1280]{1,0:T(8,128)(2,1)S(1)}, bf16[32,1280]{1,0:T(8,128)(2,1)S(1)}, u32[]{:S(2)}, u32[]{:S(2)}) collective-permute-start(bf16[32,1280]{1,0:T(8,128)(2,1)S(1)} %pack.1.own_ref), channel_id=1, source_target_pairs={{0,2},{1,3},{2,0},{3,1},{4,6},{5,7},{6,4},{7,5},{8,10},{9,11},{10,... | collective-permute-start | bytes 245768 | tf_op jit(solution)/shard_map/ppermute | solution.py:320
  2.1 0.9 %collective-permute-done.got_ref = bf16[32,1280]{1,0:T(8,128)(2,1)S(1)} collective-permute-done((bf16[32,1280]{1,0:T(8,128)(2,1)S(1)}, bf16[32,1280]{1,0:T(8,128)(2,1)S(1)}, u32[]{:S(2)}, u32[]{:S(2)}) %collective-permute-start) | collective-permute-done | bytes 81952 | tf_op jit(solution)/shard_map/ppermute | solution.py:320
  3.0 0.1 join.1
  3.1 5.0 %collective-permute-start.1 = (bf16[32,1280]{1,0:T(8,128)(2,1)S(1)}, bf16[32,1280]{1,0:T(8,128)(2,1)S(1)}, u32[]{:S(2)}, u32[]{:S(2)}) collective-permute-start(bf16[32,1280]{1,0:T(8,128)(2,1)S(1)} %get-tuple-element.26), channel_id=1, source_target_pairs={{0,24},{1,25},{2,7},{3,6},{4,28},{5,29},{6,3},{7,2},{8,16},{9,17},... | collective-permute-start | bytes 245768 | tf_op jit(solution)/shard_map/ppermute | solution.py:317
  8.1 1.5 %collective-permute-start.2 = (bf16[32,1280]{1,0:T(8,128)(2,1)S(1)}, bf16[32,1280]{1,0:T(8,128)(2,1)S(1)}, u32[]{:S(2)}, u32[]{:S(2)}) collective-permute-start(bf16[32,1280]{1,0:T(8,128)(2,1)S(1)} %get-tuple-element.27), channel_id=1, source_target_pairs={{0,4},{1,5},{2,18},{3,19},{4,0},{5,1},{6,22},{7,23},{8,12},{9,13},... | collective-permute-start | bytes 245768 | tf_op jit(solution)/shard_map/ppermute | solution.py:317
  9.6 0.0 collective-permute-start.4
  9.6 0.9 %collective-permute-start.5 = (bf16[32,1280]{1,0:T(8,128)(2,1)S(1)}, bf16[32,1280]{1,0:T(8,128)(2,1)S(1)}, u32[]{:S(2)}, u32[]{:S(2)}) collective-permute-start(bf16[32,1280]{1,0:T(8,128)(2,1)S(1)} %get-tuple-element.33), channel_id=1, source_target_pairs={{0,10},{1,11},{2,1},{3,0},{4,14},{5,15},{6,5},{7,4},{8,2},{9,3},{1... | collective-permute-start | bytes 245768 | tf_op jit(solution)/shard_map/ppermute | solution.py:317
  11.8 0.0 collective-permute-done.1.upper_ref
  11.8 0.7 %collective-permute-done.2.lower_ref = bf16[32,1280]{1,0:T(8,128)(2,1)S(1)} collective-permute-done((bf16[32,1280]{1,0:T(8,128)(2,1)S(1)}, bf16[32,1280]{1,0:T(8,128)(2,1)S(1)}, u32[]{:S(2)}, u32[]{:S(2)}) %collective-permute-start.2) | collective-permute-done | bytes 81952 | tf_op jit(solution)/shard_map/ppermute | solution.py:317
  12.5 0.1 collective-permute-start.3
  12.6 1.4 %collective-permute-done.4.upper_ref = bf16[32,1280]{1,0:T(8,128)(2,1)S(1)} collective-permute-done((bf16[32,1280]{1,0:T(8,128)(2,1)S(1)}, bf16[32,1280]{1,0:T(8,128)(2,1)S(1)}, u32[]{:S(2)}, u32[]{:S(2)}) %collective-permute-start.4) | collective-permute-done | bytes 81952 | tf_op jit(solution)/shard_map/ppermute | solution.py:317
  14.0 0.0 collective-permute-done.5.lower_ref
  14.0 0.0 collective-permute-done.3.swapped_ref
  14.0 0.7 %tile.1 = (s16[32,1280]{1,0:T(8,128)(2,1)S(1)}, s16[32,1280]{1,0:T(8,128)(2,1)S(1)}, s16[16,1280]{1,0:T(8,128)(2,1)S(1)}, s16[16,1280]{1,0:T(8,128)(2,1)S(1)}, s16[32,1280]{1,0:T(8,128)(2,1)S(1)}) custom-call(f32[8,128]{1,0:T(8,128)S(1)} %get-tuple-element.28.pair_ref, bf16[32,1280]{1,0:T(8,128)(2,1)S(1)} %get-tuple-element.29.mine_ref, ...), custom_call_target="tpu_custom_call" | custom-call | tf_op jit(solution)/shard_map/tile/pallas_call | solution.py:293
  14.8 3.1 %collective-permute-start.6 = (s16[32,1280]{1,0:T(8,128)(2,1)S(1)}, s16[32,1280]{1,0:T(8,128)(2,1)S(1)}, u32[]{:S(2)}, u32[]{:S(2)}) collective-permute-start(s16[32,1280]{1,0:T(8,128)(2,1)S(1)} %get-tuple-element.35), channel_id=1, source_target_pairs={{0,24},{1,25},{2,7},{3,6},{4,28},{5,29},{6,3},{7,2},{8,16},{9,17},... | collective-permute-start | bytes 245768 | tf_op jit(solution)/shard_map/ppermute | solution.py:317
  17.9 0.0 collective-permute-start.7
  17.9 0.9 %collective-permute-start.8 = (s16[16,1280]{1,0:T(8,128)(2,1)S(1)}, s16[16,1280]{1,0:T(8,128)(2,1)S(1)}, u32[]{:S(2)}, u32[]{:S(2)}) collective-permute-start(s16[16,1280]{1,0:T(8,128)(2,1)S(1)} %get-tuple-element.39), channel_id=1, source_target_pairs={{0,4},{1,5},{2,18},{3,19},{4,0},{5,1},{6,22},{7,23},{8,12},{9,13},... | collective-permute-start | bytes 122888 | tf_op jit(solution)/shard_map/ppermute | solution.py:317
  18.7 0.1 collective-permute-start.9
  18.9 2.3 %collective-permute-done.6.back_0 = s16[32,1280]{1,0:T(8,128)(2,1)S(1)} collective-permute-done((s16[32,1280]{1,0:T(8,128)(2,1)S(1)}, s16[32,1280]{1,0:T(8,128)(2,1)S(1)}, u32[]{:S(2)}, u32[]{:S(2)}) %collective-permute-start.6) | collective-permute-done | bytes 81952 | tf_op jit(solution)/shard_map/ppermute | solution.py:317
  21.2 1.7 %collective-permute-done.7.back_1 = s16[32,1280]{1,0:T(8,128)(2,1)S(1)} collective-permute-done((s16[32,1280]{1,0:T(8,128)(2,1)S(1)}, s16[32,1280]{1,0:T(8,128)(2,1)S(1)}, u32[]{:S(2)}, u32[]{:S(2)}) %collective-permute-start.7) | collective-permute-done | bytes 81952 | tf_op jit(solution)/shard_map/ppermute | solution.py:317
  22.9 0.2 add.1
  23.1 0.1 collective-permute-start.10
  23.2 0.0 collective-permute-done.8.same_ref
  23.2 0.0 collective-permute-done.9.cross_ref
  23.2 0.2 more.1
  23.4 1.0 %collective-permute-done.10.got_ref = s16[16,1280]{1,0:T(8,128)(2,1)S(1)} collective-permute-done((s16[16,1280]{1,0:T(8,128)(2,1)S(1)}, s16[16,1280]{1,0:T(8,128)(2,1)S(1)}, u32[]{:S(2)}, u32[]{:S(2)}) %collective-permute-start.10) | collective-permute-done | bytes 40992 | tf_op jit(solution)/shard_map/ppermute | solution.py:320
  24.4 0.9 %final.1 = (f32[1,16]{1,0:T(1,128)}, f32[16,1152]{1,0:T(8,128)}, f32[16,1152]{1,0:T(8,128)}) custom-call(f32[2,16,1152]{2,1,0:T(8,128)S(1)} %get-tuple-element.41.sum_ref, f32[2,16,128]{2,1,0:T(8,128)S(1)} %get-tuple-element.42.sum_loss_ref, f32[2,16,1152]{2,1,0:T(8,128)S(1)} %get-tuple-element.43.unit_ref, f32[2,16,128]{2,1,0:T(8,128)S(1)} %get-tuple-element.44.inverse_ref, ...), custom_call_target="tpu_custom_call" | custom-call | tf_op jit(solution)/shard_map/final/pallas_call | solution.py:293
  (2 shorter events, 0.0 us)
Async XLA Ops:
  0.6 0.8 %copy-start.1 = (bf16[16,1152]{1,0:T(8,128)(2,1)S(1)}, bf16[16,1152]{1,0:T(8,128)(2,1)}, u32[]{:S(2)}) copy-start(bf16[16,1152]{1,0:T(8,128)(2,1)} %text_ref.3) | copy-start | bytes 110596
  0.6 0.8 %copy-start = (bf16[16,1152]{1,0:T(8,128)(2,1)S(1)}, bf16[16,1152]{1,0:T(8,128)(2,1)}, u32[]{:S(2)}) copy-start(bf16[16,1152]{1,0:T(8,128)(2,1)} %image_ref.3) | copy-start | bytes 110596
  0.7 0.7 %copy-start.2 = (s32[16]{0:T(128)S(1)}, s32[16]{0:T(128)}, u32[]{:S(2)}) copy-start(s32[16]{0:T(128)} %class_ref.1) | copy-start | bytes 196
  1.5 1.4 %collective-permute-start = (bf16[32,1280]{1,0:T(8,128)(2,1)S(1)}, bf16[32,1280]{1,0:T(8,128)(2,1)S(1)}, u32[]{:S(2)}, u32[]{:S(2)}) collective-permute-start(bf16[32,1280]{1,0:T(8,128)(2,1)S(1)} %pack.1.own_ref), channel_id=1, source_target_pairs={{0,2},{1,3},{2,0},{3,1},{4,6},{5,7},{6,4},{7,5},{8,10},{9,11},{10,... | collective-permute-start | bytes 245768 | tf_op jit(solution)/shard_map/ppermute | solution.py:320
  3.1 8.8 %collective-permute-start.1 = (bf16[32,1280]{1,0:T(8,128)(2,1)S(1)}, bf16[32,1280]{1,0:T(8,128)(2,1)S(1)}, u32[]{:S(2)}, u32[]{:S(2)}) collective-permute-start(bf16[32,1280]{1,0:T(8,128)(2,1)S(1)} %get-tuple-element.26), channel_id=1, source_target_pairs={{0,24},{1,25},{2,7},{3,6},{4,28},{5,29},{6,3},{7,2},{8,16},{9,17},... | collective-permute-start | bytes 245768 | tf_op jit(solution)/shard_map/ppermute | solution.py:317
  8.1 4.4 %collective-permute-start.2 = (bf16[32,1280]{1,0:T(8,128)(2,1)S(1)}, bf16[32,1280]{1,0:T(8,128)(2,1)S(1)}, u32[]{:S(2)}, u32[]{:S(2)}) collective-permute-start(bf16[32,1280]{1,0:T(8,128)(2,1)S(1)} %get-tuple-element.27), channel_id=1, source_target_pairs={{0,4},{1,5},{2,18},{3,19},{4,0},{5,1},{6,22},{7,23},{8,12},{9,13},... | collective-permute-start | bytes 245768 | tf_op jit(solution)/shard_map/ppermute | solution.py:317
  9.6 4.4 %collective-permute-start.4 = (bf16[32,1280]{1,0:T(8,128)(2,1)S(1)}, bf16[32,1280]{1,0:T(8,128)(2,1)S(1)}, u32[]{:S(2)}, u32[]{:S(2)}) collective-permute-start(bf16[32,1280]{1,0:T(8,128)(2,1)S(1)} %get-tuple-element.32), channel_id=1, source_target_pairs={{0,8},{1,9},{2,3},{3,2},{4,12},{5,13},{6,7},{7,6},{8,0},{9,1},{10,... | collective-permute-start | bytes 245768 | tf_op jit(solution)/shard_map/ppermute | solution.py:317
  9.6 4.4 %collective-permute-start.5 = (bf16[32,1280]{1,0:T(8,128)(2,1)S(1)}, bf16[32,1280]{1,0:T(8,128)(2,1)S(1)}, u32[]{:S(2)}, u32[]{:S(2)}) collective-permute-start(bf16[32,1280]{1,0:T(8,128)(2,1)S(1)} %get-tuple-element.33), channel_id=1, source_target_pairs={{0,10},{1,11},{2,1},{3,0},{4,14},{5,15},{6,5},{7,4},{8,2},{9,3},{1... | collective-permute-start | bytes 245768 | tf_op jit(solution)/shard_map/ppermute | solution.py:317
  12.5 1.5 %collective-permute-start.3 = (bf16[64,1280]{1,0:T(8,128)(2,1)S(1)}, bf16[64,1280]{1,0:T(8,128)(2,1)S(1)}, u32[]{:S(2)}, u32[]{:S(2)}) collective-permute-start(bf16[64,1280]{1,0:T(8,128)(2,1)S(1)} %get-tuple-element.31.far_ref), channel_id=1, source_target_pairs={{0,2},{1,3},{2,0},{3,1},{4,6},{5,7},{6,4},{7,5},{8,10},{9,11},{10,... | collective-permute-start | bytes 491528 | tf_op jit(solution)/shard_map/ppermute | solution.py:320
  14.8 6.4 %collective-permute-start.6 = (s16[32,1280]{1,0:T(8,128)(2,1)S(1)}, s16[32,1280]{1,0:T(8,128)(2,1)S(1)}, u32[]{:S(2)}, u32[]{:S(2)}) collective-permute-start(s16[32,1280]{1,0:T(8,128)(2,1)S(1)} %get-tuple-element.35), channel_id=1, source_target_pairs={{0,24},{1,25},{2,7},{3,6},{4,28},{5,29},{6,3},{7,2},{8,16},{9,17},... | collective-permute-start | bytes 245768 | tf_op jit(solution)/shard_map/ppermute | solution.py:317
  17.9 5.0 %collective-permute-start.7 = (s16[32,1280]{1,0:T(8,128)(2,1)S(1)}, s16[32,1280]{1,0:T(8,128)(2,1)S(1)}, u32[]{:S(2)}, u32[]{:S(2)}) collective-permute-start(s16[32,1280]{1,0:T(8,128)(2,1)S(1)} %get-tuple-element.36), channel_id=1, source_target_pairs={{0,8},{1,9},{2,3},{3,2},{4,12},{5,13},{6,7},{7,6},{8,0},{9,1},{10,... | collective-permute-start | bytes 245768 | tf_op jit(solution)/shard_map/ppermute | solution.py:317
  17.9 5.3 %collective-permute-start.8 = (s16[16,1280]{1,0:T(8,128)(2,1)S(1)}, s16[16,1280]{1,0:T(8,128)(2,1)S(1)}, u32[]{:S(2)}, u32[]{:S(2)}) collective-permute-start(s16[16,1280]{1,0:T(8,128)(2,1)S(1)} %get-tuple-element.39), channel_id=1, source_target_pairs={{0,4},{1,5},{2,18},{3,19},{4,0},{5,1},{6,22},{7,23},{8,12},{9,13},... | collective-permute-start | bytes 122888 | tf_op jit(solution)/shard_map/ppermute | solution.py:317
  18.7 4.5 %collective-permute-start.9 = (s16[16,1280]{1,0:T(8,128)(2,1)S(1)}, s16[16,1280]{1,0:T(8,128)(2,1)S(1)}, u32[]{:S(2)}, u32[]{:S(2)}) collective-permute-start(s16[16,1280]{1,0:T(8,128)(2,1)S(1)} %get-tuple-element.40), channel_id=1, source_target_pairs={{0,6},{1,7},{2,16},{3,17},{4,2},{5,3},{6,20},{7,21},{8,14},{9,15},... | collective-permute-start | bytes 122888 | tf_op jit(solution)/shard_map/ppermute | solution.py:317
  23.1 1.3 %collective-permute-start.10 = (s16[16,1280]{1,0:T(8,128)(2,1)S(1)}, s16[16,1280]{1,0:T(8,128)(2,1)S(1)}, u32[]{:S(2)}, u32[]{:S(2)}) collective-permute-start(s16[16,1280]{1,0:T(8,128)(2,1)S(1)} %get-tuple-element.45), channel_id=1, source_target_pairs={{0,2},{1,3},{2,0},{3,1},{4,6},{5,7},{6,4},{7,5},{8,10},{9,11},{10,... | collective-permute-start | bytes 122888 | tf_op jit(solution)/shard_map/ppermute | solution.py:320

commit v15 on v14

--- a/solution.py
+++ b/solution.py
@@ -95,11 +95,13 @@
     digits_ref[...] = class_digits(class_ref)
 
 
-def pack_kernel(image_ref, text_ref, digits_ref, out_ref):
+def pack_kernel(image_ref, text_ref, digits_ref, both_ref, image_out, text_out):
     rows, depth = image_ref.shape
-    for start, source in ((0, image_ref), (rows, text_ref)):
-        out_ref[start : start + rows, :depth] = unit_rows(source[...])[0].astype(jnp.bfloat16)
-        out_ref[start : start + rows, depth:] = digits_ref[...]
+    for start, source, out in ((0, image_ref, image_out), (rows, text_ref, text_out)):
+        half = unit_rows(source[...])[0].astype(jnp.bfloat16)
+        for ref in (both_ref.at[start : start + rows, :], out):
+            ref[:, :depth] = half
+            ref[:, depth:] = digits_ref[...]
 
 
 def join_kernel(own_ref, got_ref, *refs):
@@ -111,20 +113,25 @@
     texts = jnp.concatenate([low[rows:], high[rows:]], axis=0)
     mine = jnp.where(first, images, texts).astype(jnp.bfloat16)
     other = jnp.where(first, texts, images).astype(jnp.bfloat16)
-    for ref, block in zip(refs, (mine, other, mine, mine, mine, other)):
+    for ref, block in zip(refs, (mine, mine, mine, mine, other)):
         ref[...] = block
 
 
-def put_pair(upper_ref, lower_ref, out_ref):
-    rows = upper_ref.shape[0]
-    out_ref[:rows, :] = upper_ref[...]
-    out_ref[rows:, :] = lower_ref[...]
-
-
-def far_kernel(scale_ref, shift_ref, upper_ref, lower_ref, out_ref, pair_ref):
-    put_pair(upper_ref, lower_ref, out_ref)
-    row = lax.broadcasted_iota(jnp.int32, pair_ref.shape, 0)
-    pair_ref[...] = jnp.where(row == 0, scale_ref[0], shift_ref[0])
+def stack(refs, out_ref):
+    start = 0
+    for ref in refs:
+        out_ref[start : start + ref.shape[0], :] = ref[...]
+        start += ref.shape[0]
+
+
+def near_kernel(scale_ref, shift_ref, *refs):
+    stack(refs[:-2], refs[-2])
+    row = lax.broadcasted_iota(jnp.int32, refs[-1].shape, 0)
+    refs[-1][...] = jnp.where(row == 0, scale_ref[0], shift_ref[0])
+
+
+def stack_kernel(*refs):
+    stack(refs[:-1], refs[-1])
 
 
 def power_above(size):
@@ -204,23 +211,37 @@
 
 def tile_kernel(pair_ref, mine_ref, other_ref, far_ref, swapped_ref, near_ref, *outs):
     rows = mine_ref.shape[0]
+    half = rows // 2
+    first = on_first_core()
     scale, shift = pair_ref[0:1, 0:1], pair_ref[1:2, 0:1]
+
+    def pick(one, two):
+        return jnp.where(first, one.astype(jnp.float32), two.astype(jnp.float32))
+
+    def parted(ref):
+        image, text = ref[:half, :], ref[half:rows, :]
+        return pick(image, text).astype(jnp.bfloat16), pick(text, image).astype(jnp.bfloat16)
+
+    (line_half, column_half), (line_rest, column_rest) = parted(far_ref), parted(swapped_ref)
     lines = jnp.concatenate(
-        [far_ref[:rows, :], near_ref[:rows, :], mine_ref[...], swapped_ref[rows:, :]], axis=0
+        [far_ref[rows:, :], near_ref[:rows, :], line_half, mine_ref[...], line_rest], axis=0
     )
     columns = jnp.concatenate(
-        [far_ref[rows:, :], swapped_ref[:rows, :], near_ref[rows:, :], other_ref[...]], axis=0
+        [column_half, column_rest, swapped_ref[rows:, :], near_ref[rows:, :], other_ref[...]], axis=0
     )
     loss, coef = tile_terms_of(lines, columns, scale, shift)
-    put_rows([outs[0], outs[1], outs[4]], *pulls_of(loss[: 3 * rows], coef[: 3 * rows], columns))
-    first = on_first_core()
-    half = rows // 2
-    halves = []
-    for part in pulls_of(loss.T[:rows], coef.T[:rows], lines):
-        low, high = part[:half], part[half:]
-        halves.append((jnp.where(first, low, high), jnp.where(first, high, low)))
-    for out, pull, part_loss in zip(outs[2:4], *halves):
-        put_rows([out], pull, part_loss)
+    used = 3 * rows + half
+    pull, loss_sum = pulls_of(loss[:used], coef[:used], columns)
+    column_pull, column_loss = pulls_of(loss.T[:half], coef.T[:half], lines)
+    put_rows([outs[0]], pull[:rows], loss_sum[:rows])
+    line_pull, line_loss = pull[2 * rows : 2 * rows + half], loss_sum[2 * rows : 2 * rows + half]
+    put_rows([outs[1]], pick(line_pull, column_pull), pick(line_loss, column_loss))
+    put_rows([outs[2]], pick(column_pull, line_pull), pick(column_loss, line_loss))
+    low, high = pull[rows : rows + half], pull[rows + half : 2 * rows]
+    low_loss, high_loss = loss_sum[rows : rows + half], loss_sum[rows + half : 2 * rows]
+    put_rows([outs[3]], pick(low, high), pick(low_loss, high_loss))
+    put_rows([outs[4]], pick(high, low), pick(high_loss, low_loss))
+    put_rows([outs[5]], pull[2 * rows + half : used], loss_sum[2 * rows + half : used])
 
 
 def total(parts, rows, depth):
@@ -238,45 +259,44 @@
     return pl.ds(own, rows), pl.ds(pl.multiple_of(rows - own, rows), rows)
 
 
-def add_kernel(own_ref, back_0, back_1, keep_ref, loss_ref, give_ref):
+def add_kernel(own_ref, back_ref, keep_ref, loss_ref, give_ref):
     rows, depth = keep_ref.shape
     own, other = place_of(on_first_core(), rows)
-    parts = (own_ref, back_0, back_1)
-    pull, loss = total([part[other, :] for part in parts], rows, depth)
+    pull, loss = total([own_ref[other, :], back_ref[other, :]], rows, depth)
     put_rows([give_ref], pull, loss)
-    keep_ref[...], loss = total([part[own, :] for part in parts], rows, depth)
+    keep_ref[...], loss = total([own_ref[own, :], back_ref[own, :]], rows, depth)
     loss_ref[...] = jnp.broadcast_to(loss, loss_ref.shape)
 
 
-def more_kernel(keep_ref, kept_loss_ref, same_ref, cross_ref, image_ref, text_ref, sum_ref, sum_loss_ref, *units):
+def more_kernel(keep_ref, kept_loss_ref, image_back, text_back, same_ref, cross_ref, image_ref, text_ref, *outs):
+    sum_ref, sum_loss_ref, unit_ref, inverse_ref = outs
+    first = on_first_core()
     rows, depth = keep_ref.shape
-    pull, loss = total([cross_ref], rows, depth)
-    sum_ref[0] = keep_ref[...] + pull
-    sum_loss_ref[0] = kept_loss_ref[...] + loss
-    sum_ref[1], loss = total([same_ref], rows, depth)
-    sum_loss_ref[1] = jnp.broadcast_to(loss, sum_loss_ref.shape[1:])
-    for side, ref in enumerate((image_ref, text_ref)):
-        unit, inverse = unit_rows(ref[...])
-        units[0][side] = unit
-        units[1][side] = jnp.broadcast_to(inverse, units[1].shape[1:])
+    pull, loss = total([same_ref], rows, depth)
+    mine = (keep_ref[...] + pull, kept_loss_ref[:, 0:1] + loss)
+    other = total([cross_ref], rows, depth)
+    for side, (back, source) in enumerate(((image_back, image_ref), (text_back, text_ref))):
+        pull, loss = total([back], rows, depth)
+        here, there = (mine, other) if side == 0 else (other, mine)
+        sum_ref[side] = pull + jnp.where(first, here[0], there[0])
+        loss = loss + jnp.where(first, here[1], there[1])
+        sum_loss_ref[side] = jnp.broadcast_to(loss, sum_loss_ref.shape[1:])
+        unit, inverse = unit_rows(source[...])
+        unit_ref[side] = unit
+        inverse_ref[side] = jnp.broadcast_to(inverse, inverse_ref.shape[1:])
 
 
 def final_kernel(pairs, sum_ref, sum_loss_ref, unit_ref, inverse_ref, got_ref, loss_ref, grad_image_ref, grad_text_ref):
     first = on_first_core()
     rows, depth = sum_ref.shape[1:]
     pull, loss = total([got_ref], rows, depth)
-    pulls = (sum_ref[0], sum_ref[1] + pull)
-    losses = (sum_loss_ref[0][:, 0:1], sum_loss_ref[1][:, 0:1] + loss)
-    for side, (pull, out) in enumerate(
-        (
-            (jnp.where(first, pulls[0], pulls[1]), grad_image_ref),
-            (jnp.where(first, pulls[1], pulls[0]), grad_text_ref),
-        )
-    ):
-        out[...] = project_back(unit_ref[side], inverse_ref[side][:, 0:1], pull)
+    image_pull = sum_ref[0] + jnp.where(first, 0.0, pull)
+    text_pull = sum_ref[1] + jnp.where(first, pull, 0.0)
+    grad_image_ref[...] = project_back(unit_ref[0], inverse_ref[0][:, 0:1], image_pull)
+    grad_text_ref[...] = project_back(unit_ref[1], inverse_ref[1][:, 0:1], text_pull)
     row = lax.broadcasted_iota(jnp.int32, (rows, rows), 0)
     column = lax.broadcasted_iota(jnp.int32, (rows, rows), 1)
-    loss = jnp.where(first, losses[0], losses[1])
+    loss = sum_loss_ref[0][:, 0:1] + jnp.where(first, 0.0, loss)
     across = jnp.where(row == column, loss / pairs, 0.0)
     loss_ref[...] = jnp.sum(across, axis=0, keepdims=True)
 
@@ -319,8 +339,8 @@
     def swap(x):
         return lax.ppermute(x, AXES, [(i, i ^ lanes) for i in range(n)])
 
-    out_visits = (((12, 3), 0), ((2, 8), 0), ((4, 1), 0), ((4, 1), 1))
-    back_visits = (((12, 3), 0), ((4, 1), 0), ((2, 8), 0), ((2, 8), 1))
+    across, beside = ((12, 12), 0), ((3, 3), 0)
+    second, near_same, near_cross = ((8, 2), 0), ((4, 1), 0), ((4, 1), 1)
     late = pl.CostEstimate(flops=10**9, bytes_accessed=10**7, transcendentals=0)
     digits = call(
         digits_kernel,
@@ -329,35 +349,38 @@
         "digits",
         cost=late,
     )
-    own = call(pack_kernel, block(2), [image_emb, text_emb, digits], "pack")
-    *sent, mine, other = call(join_kernel, (block(2),) * 6, [own, swap(own)], "join")
-    got = [visit(x, *way) for x, way in zip(sent, out_visits)]
-    far, pair = call(
-        far_kernel,
+    own, own_images, own_texts = call(
+        pack_kernel, (block(2), block(1), block(1)), [image_emb, text_emb, digits], "pack"
+    )
+    halves = [visit(own_images, *across), visit(own_texts, *beside)]
+    *sent, mine, other = call(join_kernel, (block(2),) * 5, [own, swap(own)], "join")
+    got = [visit(x, *way) for x, way in zip(sent, (second, near_same, near_cross))]
+    halves = call(stack_kernel, block(2), halves, "halves", cost=late)
+    far = call(stack_kernel, block(4), [halves, got[0]], "far", cost=late)
+    near, pair = call(
+        near_kernel,
         (block(4), wide(8, LANES)),
-        [scale[None], shift[None], *got[:2]],
-        "far",
+        [scale[None], shift[None], *got[1:]],
+        "near",
         2,
-    )
-    near = call(put_pair, block(4), got[2:], "near", cost=late)
+        late,
+    )
     one, two = block(1, jnp.int16), block(2, jnp.int16)
     parts = call(
         tile_kernel,
-        (two, two, one, one, two),
+        (two, one, one, one, one, two),
         [pair, mine, other, far, swap(far), near],
         "tile",
     )
-    back = [visit(x, *way) for x, way in zip(parts, back_visits)]
+    ways = (second, across, beside, near_same, near_cross)
+    back = [visit(x, *way) for x, way in zip(parts, ways)]
     keep, kept_loss, give = call(
-        add_kernel,
-        (wide(rows, depth), wide(rows, LANES), one),
-        [parts[4], *back[:2]],
-        "add",
+        add_kernel, (wide(rows, depth), wide(rows, LANES), one), [parts[5], back[0]], "add"
     )
     sums = call(
         more_kernel,
         (wide(2, rows, depth), wide(2, rows, LANES)) * 2,
-        [keep, kept_loss, *back[2:], image_emb, text_emb],
+        [keep, kept_loss, *back[1:], image_emb, text_emb],
         "more",
         cost=late,
     )

time: 25.5 us -> 29.1 us (1.14)
  starting transfers between devices: 12.2 us -> 14.6 us
  waiting for transfers between devices: 8.08 us -> 9.01 us
    ppermute x8 -> x10, waiting for transfers between devices: 6.12 us -> 8.98 us  [visit(): return lax.ppermute(x, AXES, pairs)]
    ppermute x8 -> x10, starting transfers between devices: 11.6 us -> 14 us  [visit(): return lax.ppermute(x, AXES, pairs)]
    ppermute x3, waiting for transfers between devices: 1.96 us -> 0.03 us  [swap(): return lax.ppermute(x, AXES, [(i, i ^ lanes) for i in range(n)])]
    pallas_call x9 -> x10, Pallas kernels: 2.29 us -> 2.48 us  [call(): pl.pallas_call(kernel, cost_estimate=cost, out_shape=shapes, in_specs=[sm...]
  transfers between devices with their start and end apart: 11 -> 13, of which waited for: 6 -> 5; matrix products, arithmetic and copies ran while one was open for 0% -> 0% of each run, Pallas kernels for 2% -> 2%
where the time goes in v15:
time: 29.1 us; the launch traced here: 28.9 us
  starting transfers between devices  14.6 us (50%)
  waiting for transfers between devices  9.01 us (31%)
  Pallas kernels  2.48 us (9%)
  between operations  2.08 us (7%)
  local copies, waits for them, and re-layouts  0.67 us (2%)
    ppermute x10, starting transfers between devices, visit(): return lax.ppermute(x, AXES, pairs)  14 us
    ppermute x10, waiting for transfers between devices, visit(): return lax.ppermute(x, AXES, pairs)  8.98 us
    pallas_call x10, Pallas kernels, call(): pl.pallas_call(kernel, cost_estimate=cost, out_shape=shapes, in_specs=[sm...  2.48 us
    unnamed x6, local copies, waits for them, and re-layouts  0.67 us
    ppermute x3, starting transfers between devices, swap(): return lax.ppermute(x, AXES, [(i, i ^ lanes) for i in range(n)])  0.66 us
  transfers between devices with their start and end apart: 13, of which 5 were waited for; matrix products, arithmetic and copies ran while one was open for 0% of the time, Pallas kernels for 2%

profile of v15, /device:TPU:0, one launch (start us, length us, event | category | flops | bytes accessed | tf_op | source)
XLA Modules:
  0.0 28.9 jit_solution(5682446561078648270)
XLA Ops:
  0.6 0.0 copy-start.1
  0.6 0.0 copy-start
  0.7 0.0 copy-start.2
  0.7 0.7 %copy-done.2 = s32[16]{0:T(128)S(1)} copy-done((s32[16]{0:T(128)S(1)}, s32[16]{0:T(128)}, u32[]{:S(2)}) %copy-start.2) | copy-done | bytes 88
  1.3 0.1 digits.1.digits_ref
  1.4 0.0 copy-done.1
  1.4 0.0 copy-done
  1.4 0.1 pack.1
  1.5 0.5 %collective-permute-start = (bf16[32,1280]{1,0:T(8,128)(2,1)S(1)}, bf16[32,1280]{1,0:T(8,128)(2,1)S(1)}, u32[]{:S(2)}, u32[]{:S(2)}) collective-permute-start(bf16[32,1280]{1,0:T(8,128)(2,1)S(1)} %get-tuple-element.29.own_ref), channel_id=1, source_target_pairs={{0,2},{1,3},{2,0},{3,1},{4,6},{5,7},{6,4},{7,5},{8,10},{9,11},{10,... | collective-permute-start | bytes 245768 | tf_op jit(solution)/shard_map/ppermute | solution.py:340
  2.1 4.7 %collective-permute-start.3 = (bf16[16,1280]{1,0:T(8,128)(2,1)S(1)}, bf16[16,1280]{1,0:T(8,128)(2,1)S(1)}, u32[]{:S(2)}, u32[]{:S(2)}) collective-permute-start(bf16[16,1280]{1,0:T(8,128)(2,1)S(1)} %get-tuple-element.35), channel_id=1, source_target_pairs={{0,24},{1,25},{2,26},{3,27},{4,28},{5,29},{6,30},{7,31},{8,16},{9,... | collective-permute-start | bytes 122888 | tf_op jit(solution)/shard_map/ppermute | solution.py:337
  6.7 2.4 %collective-permute-start.4 = (bf16[16,1280]{1,0:T(8,128)(2,1)S(1)}, bf16[16,1280]{1,0:T(8,128)(2,1)S(1)}, u32[]{:S(2)}, u32[]{:S(2)}) collective-permute-start(bf16[16,1280]{1,0:T(8,128)(2,1)S(1)} %get-tuple-element.36), channel_id=1, source_target_pairs={{0,5},{1,4},{2,7},{3,6},{4,1},{5,0},{6,3},{7,2},{8,13},{9,12},{10,... | collective-permute-start | bytes 122888 | tf_op jit(solution)/shard_map/ppermute | solution.py:337
  9.2 0.0 collective-permute-done.got_ref
  9.2 0.1 join.1
  9.3 0.1 collective-permute-start.5
  9.3 0.0 collective-permute-done.3.refs_0_
  9.4 2.3 %collective-permute-done.4.refs_1_ = bf16[16,1280]{1,0:T(8,128)(2,1)S(1)} collective-permute-done((bf16[16,1280]{1,0:T(8,128)(2,1)S(1)}, bf16[16,1280]{1,0:T(8,128)(2,1)S(1)}, u32[]{:S(2)}, u32[]{:S(2)}) %collective-permute-start.4) | collective-permute-done | bytes 40992 | tf_op jit(solution)/shard_map/ppermute | solution.py:337
  11.7 0.0 collective-permute-start.1
  11.7 0.1 collective-permute-start.2
  11.7 2.9 %collective-permute-done.5.refs_1_ = bf16[32,1280]{1,0:T(8,128)(2,1)S(1)} collective-permute-done((bf16[32,1280]{1,0:T(8,128)(2,1)S(1)}, bf16[32,1280]{1,0:T(8,128)(2,1)S(1)}, u32[]{:S(2)}, u32[]{:S(2)}) %collective-permute-start.5) | collective-permute-done | bytes 81952 | tf_op jit(solution)/shard_map/ppermute | solution.py:337
  14.7 0.1 collective-permute-start.6
  16.1 0.0 collective-permute-done.1.refs_0_
  16.1 0.0 collective-permute-done.2.refs_1_
  16.1 0.0 collective-permute-done.6.swapped_ref
  16.1 0.8 %tile.1 = (s16[32,1280]{1,0:T(8,128)(2,1)S(1)}, s16[16,1280]{1,0:T(8,128)(2,1)S(1)}, s16[16,1280]{1,0:T(8,128)(2,1)S(1)}, s16[16,1280]{1,0:T(8,128)(2,1)S(1)}, s...) custom-call(f32[8,128]{1,0:T(8,128)S(1)} %get-tuple-element.32.pair_ref, ...), custom_call_target="tpu_custom_call" | custom-call | tf_op jit(solution)/shard_map/tile/pallas_call | solution.py:313
  16.9 1.0 %collective-permute-start.7 = (s16[32,1280]{1,0:T(8,128)(2,1)S(1)}, s16[32,1280]{1,0:T(8,128)(2,1)S(1)}, u32[]{:S(2)}, u32[]{:S(2)}) collective-permute-start(s16[32,1280]{1,0:T(8,128)(2,1)S(1)} %get-tuple-element.40), channel_id=1, source_target_pairs={{0,16},{1,17},{2,6},{3,7},{4,20},{5,21},{6,2},{7,3},{8,24},{9,25},... | collective-permute-start | bytes 245768 | tf_op jit(solution)/shard_map/ppermute | solution.py:337
  18.0 2.9 %collective-permute-start.8 = (s16[16,1280]{1,0:T(8,128)(2,1)S(1)}, s16[16,1280]{1,0:T(8,128)(2,1)S(1)}, u32[]{:S(2)}, u32[]{:S(2)}) collective-permute-start(s16[16,1280]{1,0:T(8,128)(2,1)S(1)} %get-tuple-element.43), channel_id=1, source_target_pairs={{0,24},{1,25},{2,26},{3,27},{4,28},{5,29},{6,30},{7,31},{8,16},{9,... | collective-permute-start | bytes 122888 | tf_op jit(solution)/shard_map/ppermute | solution.py:337
  20.8 2.9 %collective-permute-start.9 = (s16[16,1280]{1,0:T(8,128)(2,1)S(1)}, s16[16,1280]{1,0:T(8,128)(2,1)S(1)}, u32[]{:S(2)}, u32[]{:S(2)}) collective-permute-start(s16[16,1280]{1,0:T(8,128)(2,1)S(1)} %get-tuple-element.44), channel_id=1, source_target_pairs={{0,5},{1,4},{2,7},{3,6},{4,1},{5,0},{6,3},{7,2},{8,13},{9,12},{10,... | collective-permute-start | bytes 122888 | tf_op jit(solution)/shard_map/ppermute | solution.py:337
  23.7 0.0 collective-permute-start.10
  23.7 0.0 collective-permute-start.11
  23.7 0.9 %collective-permute-done.7.back_ref = s16[32,1280]{1,0:T(8,128)(2,1)S(1)} collective-permute-done((s16[32,1280]{1,0:T(8,128)(2,1)S(1)}, s16[32,1280]{1,0:T(8,128)(2,1)S(1)}, u32[]{:S(2)}, u32[]{:S(2)}) %collective-permute-start.7) | collective-permute-done | bytes 81952 | tf_op jit(solution)/shard_map/ppermute | solution.py:337
  24.5 0.2 add.1
  24.7 0.1 collective-permute-start.12
  24.8 0.0 collective-permute-done.8.image_back
  24.8 0.9 %collective-permute-done.9.text_back = s16[16,1280]{1,0:T(8,128)(2,1)S(1)} collective-permute-done((s16[16,1280]{1,0:T(8,128)(2,1)S(1)}, s16[16,1280]{1,0:T(8,128)(2,1)S(1)}, u32[]{:S(2)}, u32[]{:S(2)}) %collective-permute-start.9) | collective-permute-done | bytes 40992 | tf_op jit(solution)/shard_map/ppermute | solution.py:337
  25.7 2.0 %collective-permute-done.10.same_ref = s16[16,1280]{1,0:T(8,128)(2,1)S(1)} collective-permute-done((s16[16,1280]{1,0:T(8,128)(2,1)S(1)}, s16[16,1280]{1,0:T(8,128)(2,1)S(1)}, u32[]{:S(2)}, u32[]{:S(2)}) %collective-permute-start.10) | collective-permute-done | bytes 40992 | tf_op jit(solution)/shard_map/ppermute | solution.py:337
  27.7 0.0 collective-permute-done.11.cross_ref
  27.7 0.3 more.1
  28.0 0.0 collective-permute-done.12.got_ref
  28.0 0.9 %final.1 = (f32[1,16]{1,0:T(1,128)}, f32[16,1152]{1,0:T(8,128)}, f32[16,1152]{1,0:T(8,128)}) custom-call(f32[2,16,1152]{2,1,0:T(8,128)S(1)} %get-tuple-element.47.sum_ref, f32[2,16,128]{2,1,0:T(8,128)S(1)} %get-tuple-element.48.sum_loss_ref, f32[2,16,1152]{2,1,0:T(8,128)S(1)} %get-tuple-element.49.unit_ref, f32[2,16,128]{2,1,0:T(8,128)S(1)} %get-tuple-element.50.inverse_ref, ...), custom_call_target="tpu_custom_call" | custom-call | tf_op jit(solution)/shard_map/final/pallas_call | solution.py:313
  (3 shorter events, 0.0 us)
Async XLA Ops:
  0.6 0.8 %copy-start.1 = (bf16[16,1152]{1,0:T(8,128)(2,1)S(1)}, bf16[16,1152]{1,0:T(8,128)(2,1)}, u32[]{:S(2)}) copy-start(bf16[16,1152]{1,0:T(8,128)(2,1)} %text_ref.3) | copy-start | bytes 110596
  0.6 0.8 %copy-start = (bf16[16,1152]{1,0:T(8,128)(2,1)S(1)}, bf16[16,1152]{1,0:T(8,128)(2,1)}, u32[]{:S(2)}) copy-start(bf16[16,1152]{1,0:T(8,128)(2,1)} %image_ref.3) | copy-start | bytes 110596
  0.7 0.7 %copy-start.2 = (s32[16]{0:T(128)S(1)}, s32[16]{0:T(128)}, u32[]{:S(2)}) copy-start(s32[16]{0:T(128)} %class_ref.1) | copy-start | bytes 196
  1.5 7.6 %collective-permute-start = (bf16[32,1280]{1,0:T(8,128)(2,1)S(1)}, bf16[32,1280]{1,0:T(8,128)(2,1)S(1)}, u32[]{:S(2)}, u32[]{:S(2)}) collective-permute-start(bf16[32,1280]{1,0:T(8,128)(2,1)S(1)} %get-tuple-element.29.own_ref), channel_id=1, source_target_pairs={{0,2},{1,3},{2,0},{3,1},{4,6},{5,7},{6,4},{7,5},{8,10},{9,11},{10,... | collective-permute-start | bytes 245768 | tf_op jit(solution)/shard_map/ppermute | solution.py:340
  2.1 7.3 %collective-permute-start.3 = (bf16[16,1280]{1,0:T(8,128)(2,1)S(1)}, bf16[16,1280]{1,0:T(8,128)(2,1)S(1)}, u32[]{:S(2)}, u32[]{:S(2)}) collective-permute-start(bf16[16,1280]{1,0:T(8,128)(2,1)S(1)} %get-tuple-element.35), channel_id=1, source_target_pairs={{0,24},{1,25},{2,26},{3,27},{4,28},{5,29},{6,30},{7,31},{8,16},{9,... | collective-permute-start | bytes 122888 | tf_op jit(solution)/shard_map/ppermute | solution.py:337
  6.7 4.9 %collective-permute-start.4 = (bf16[16,1280]{1,0:T(8,128)(2,1)S(1)}, bf16[16,1280]{1,0:T(8,128)(2,1)S(1)}, u32[]{:S(2)}, u32[]{:S(2)}) collective-permute-start(bf16[16,1280]{1,0:T(8,128)(2,1)S(1)} %get-tuple-element.36), channel_id=1, source_target_pairs={{0,5},{1,4},{2,7},{3,6},{4,1},{5,0},{6,3},{7,2},{8,13},{9,12},{10,... | collective-permute-start | bytes 122888 | tf_op jit(solution)/shard_map/ppermute | solution.py:337
  9.3 5.4 %collective-permute-start.5 = (bf16[32,1280]{1,0:T(8,128)(2,1)S(1)}, bf16[32,1280]{1,0:T(8,128)(2,1)S(1)}, u32[]{:S(2)}, u32[]{:S(2)}) collective-permute-start(bf16[32,1280]{1,0:T(8,128)(2,1)S(1)} %get-tuple-element.37), channel_id=1, source_target_pairs={{0,16},{1,17},{2,6},{3,7},{4,20},{5,21},{6,2},{7,3},{8,24},{9,25},... | collective-permute-start | bytes 245768 | tf_op jit(solution)/shard_map/ppermute | solution.py:337
  11.7 4.4 %collective-permute-start.1 = (bf16[32,1280]{1,0:T(8,128)(2,1)S(1)}, bf16[32,1280]{1,0:T(8,128)(2,1)S(1)}, u32[]{:S(2)}, u32[]{:S(2)}) collective-permute-start(bf16[32,1280]{1,0:T(8,128)(2,1)S(1)} %get-tuple-element.30), channel_id=1, source_target_pairs={{0,8},{1,9},{2,3},{3,2},{4,12},{5,13},{6,7},{7,6},{8,0},{9,1},{10,... | collective-permute-start | bytes 245768 | tf_op jit(solution)/shard_map/ppermute | solution.py:337
  11.7 4.4 %collective-permute-start.2 = (bf16[32,1280]{1,0:T(8,128)(2,1)S(1)}, bf16[32,1280]{1,0:T(8,128)(2,1)S(1)}, u32[]{:S(2)}, u32[]{:S(2)}) collective-permute-start(bf16[32,1280]{1,0:T(8,128)(2,1)S(1)} %get-tuple-element.31), channel_id=1, source_target_pairs={{0,10},{1,11},{2,1},{3,0},{4,14},{5,15},{6,5},{7,4},{8,2},{9,3},{1... | collective-permute-start | bytes 245768 | tf_op jit(solution)/shard_map/ppermute | solution.py:337
  14.7 1.5 %collective-permute-start.6 = (bf16[64,1280]{1,0:T(8,128)(2,1)S(1)}, bf16[64,1280]{1,0:T(8,128)(2,1)S(1)}, u32[]{:S(2)}, u32[]{:S(2)}) collective-permute-start(bf16[64,1280]{1,0:T(8,128)(2,1)S(1)} %far.1.far_ref), channel_id=1, source_target_pairs={{0,2},{1,3},{2,0},{3,1},{4,6},{5,7},{6,4},{7,5},{8,10},{9,11},{10,... | collective-permute-start | bytes 491528 | tf_op jit(solution)/shard_map/ppermute | solution.py:340
  16.9 7.6 %collective-permute-start.7 = (s16[32,1280]{1,0:T(8,128)(2,1)S(1)}, s16[32,1280]{1,0:T(8,128)(2,1)S(1)}, u32[]{:S(2)}, u32[]{:S(2)}) collective-permute-start(s16[32,1280]{1,0:T(8,128)(2,1)S(1)} %get-tuple-element.40), channel_id=1, source_target_pairs={{0,16},{1,17},{2,6},{3,7},{4,20},{5,21},{6,2},{7,3},{8,24},{9,25},... | collective-permute-start | bytes 245768 | tf_op jit(solution)/shard_map/ppermute | solution.py:337
  18.0 6.9 %collective-permute-start.8 = (s16[16,1280]{1,0:T(8,128)(2,1)S(1)}, s16[16,1280]{1,0:T(8,128)(2,1)S(1)}, u32[]{:S(2)}, u32[]{:S(2)}) collective-permute-start(s16[16,1280]{1,0:T(8,128)(2,1)S(1)} %get-tuple-element.43), channel_id=1, source_target_pairs={{0,24},{1,25},{2,26},{3,27},{4,28},{5,29},{6,30},{7,31},{8,16},{9,... | collective-permute-start | bytes 122888 | tf_op jit(solution)/shard_map/ppermute | solution.py:337
  20.8 4.9 %collective-permute-start.9 = (s16[16,1280]{1,0:T(8,128)(2,1)S(1)}, s16[16,1280]{1,0:T(8,128)(2,1)S(1)}, u32[]{:S(2)}, u32[]{:S(2)}) collective-permute-start(s16[16,1280]{1,0:T(8,128)(2,1)S(1)} %get-tuple-element.44), channel_id=1, source_target_pairs={{0,5},{1,4},{2,7},{3,6},{4,1},{5,0},{6,3},{7,2},{8,13},{9,12},{10,... | collective-permute-start | bytes 122888 | tf_op jit(solution)/shard_map/ppermute | solution.py:337
  23.7 4.0 %collective-permute-start.10 = (s16[16,1280]{1,0:T(8,128)(2,1)S(1)}, s16[16,1280]{1,0:T(8,128)(2,1)S(1)}, u32[]{:S(2)}, u32[]{:S(2)}) collective-permute-start(s16[16,1280]{1,0:T(8,128)(2,1)S(1)} %get-tuple-element.45), channel_id=1, source_target_pairs={{0,8},{1,9},{2,3},{3,2},{4,12},{5,13},{6,7},{7,6},{8,0},{9,1},{10,... | collective-permute-start | bytes 122888 | tf_op jit(solution)/shard_map/ppermute | solution.py:337
  23.7 4.0 %collective-permute-start.11 = (s16[16,1280]{1,0:T(8,128)(2,1)S(1)}, s16[16,1280]{1,0:T(8,128)(2,1)S(1)}, u32[]{:S(2)}, u32[]{:S(2)}) collective-permute-start(s16[16,1280]{1,0:T(8,128)(2,1)S(1)} %get-tuple-element.46), channel_id=1, source_target_pairs={{0,10},{1,11},{2,1},{3,0},{4,14},{5,15},{6,5},{7,4},{8,2},{9,3},{1... | collective-permute-start | bytes 122888 | tf_op jit(solution)/shard_map/ppermute | solution.py:337
  24.7 3.2 %collective-permute-start.12 = (s16[16,1280]{1,0:T(8,128)(2,1)S(1)}, s16[16,1280]{1,0:T(8,128)(2,1)S(1)}, u32[]{:S(2)}, u32[]{:S(2)}) collective-permute-start(s16[16,1280]{1,0:T(8,128)(2,1)S(1)} %get-tuple-element.51), channel_id=1, source_target_pairs={{0,2},{1,3},{2,0},{3,1},{4,6},{5,7},{6,4},{7,5},{8,10},{9,11},{10,... | collective-permute-start | bytes 122888 | tf_op jit(solution)/shard_map/ppermute | solution.py:340

commit v16 on v14

--- a/solution.py
+++ b/solution.py
@@ -115,14 +115,10 @@
         ref[...] = block
 
 
-def put_pair(upper_ref, lower_ref, out_ref):
+def near_kernel(scale_ref, shift_ref, upper_ref, lower_ref, out_ref, pair_ref):
     rows = upper_ref.shape[0]
     out_ref[:rows, :] = upper_ref[...]
     out_ref[rows:, :] = lower_ref[...]
-
-
-def far_kernel(scale_ref, shift_ref, upper_ref, lower_ref, out_ref, pair_ref):
-    put_pair(upper_ref, lower_ref, out_ref)
     row = lax.broadcasted_iota(jnp.int32, pair_ref.shape, 0)
     pair_ref[...] = jnp.where(row == 0, scale_ref[0], shift_ref[0])
 
@@ -202,25 +198,28 @@
     return pull, jnp.sum(loss, axis=1, keepdims=True)
 
 
-def tile_kernel(pair_ref, mine_ref, other_ref, far_ref, swapped_ref, near_ref, *outs):
+def tile_kernel(pair_ref, mine_ref, other_ref, got_0, got_1, swapped_0, swapped_1, near_ref, *outs):
     rows = mine_ref.shape[0]
     scale, shift = pair_ref[0:1, 0:1], pair_ref[1:2, 0:1]
     lines = jnp.concatenate(
-        [far_ref[:rows, :], near_ref[:rows, :], mine_ref[...], swapped_ref[rows:, :]], axis=0
+        [got_0[...], near_ref[:rows, :], mine_ref[...], swapped_1[...]], axis=0
     )
     columns = jnp.concatenate(
-        [far_ref[rows:, :], swapped_ref[:rows, :], near_ref[rows:, :], other_ref[...]], axis=0
+        [got_1[...], swapped_0[...], near_ref[rows:, :], other_ref[...]], axis=0
     )
     loss, coef = tile_terms_of(lines, columns, scale, shift)
-    put_rows([outs[0], outs[1], outs[4]], *pulls_of(loss[: 3 * rows], coef[: 3 * rows], columns))
+    pull, loss_sum = pulls_of(loss[: 3 * rows], coef[: 3 * rows], columns)
+    put_rows([outs[0]], pull[:rows], loss_sum[:rows])
+    put_rows([outs[1]], *pulls_of(loss.T[:rows], coef.T[:rows], lines))
     first = on_first_core()
     half = rows // 2
     halves = []
-    for part in pulls_of(loss.T[:rows], coef.T[:rows], lines):
-        low, high = part[:half], part[half:]
+    for part in (pull, loss_sum):
+        low, high = part[rows : rows + half], part[rows + half : 2 * rows]
         halves.append((jnp.where(first, low, high), jnp.where(first, high, low)))
-    for out, pull, part_loss in zip(outs[2:4], *halves):
-        put_rows([out], pull, part_loss)
+    for out, part, part_loss in zip(outs[2:4], *halves):
+        put_rows([out], part, part_loss)
+    put_rows([outs[4]], pull[2 * rows :], loss_sum[2 * rows :])
 
 
 def total(parts, rows, depth):
@@ -238,35 +237,37 @@
     return pl.ds(own, rows), pl.ds(pl.multiple_of(rows - own, rows), rows)
 
 
-def add_kernel(own_ref, back_0, back_1, keep_ref, loss_ref, give_ref):
+def add_kernel(own_ref, back_ref, keep_ref, loss_ref, give_ref):
     rows, depth = keep_ref.shape
     own, other = place_of(on_first_core(), rows)
-    parts = (own_ref, back_0, back_1)
-    pull, loss = total([part[other, :] for part in parts], rows, depth)
+    pull, loss = total([own_ref[other, :], back_ref[other, :]], rows, depth)
     put_rows([give_ref], pull, loss)
-    keep_ref[...], loss = total([part[own, :] for part in parts], rows, depth)
+    keep_ref[...], loss = total([own_ref[own, :], back_ref[own, :]], rows, depth)
     loss_ref[...] = jnp.broadcast_to(loss, loss_ref.shape)
 
 
-def more_kernel(keep_ref, kept_loss_ref, same_ref, cross_ref, image_ref, text_ref, sum_ref, sum_loss_ref, *units):
+def more_kernel(keep_ref, kept_loss_ref, back_ref, got_ref, same_ref, cross_ref, image_ref, text_ref, *outs):
+    sum_ref, sum_loss_ref, unit_ref, inverse_ref = outs
     rows, depth = keep_ref.shape
-    pull, loss = total([cross_ref], rows, depth)
+    own, _ = place_of(on_first_core(), rows)
+    pull, loss = total([same_ref], rows, depth)
     sum_ref[0] = keep_ref[...] + pull
     sum_loss_ref[0] = kept_loss_ref[...] + loss
-    sum_ref[1], loss = total([same_ref], rows, depth)
+    sum_ref[1], loss = total([back_ref[own, :], got_ref, cross_ref], rows, depth)
     sum_loss_ref[1] = jnp.broadcast_to(loss, sum_loss_ref.shape[1:])
     for side, ref in enumerate((image_ref, text_ref)):
         unit, inverse = unit_rows(ref[...])
-        units[0][side] = unit
-        units[1][side] = jnp.broadcast_to(inverse, units[1].shape[1:])
+        unit_ref[side] = unit
+        inverse_ref[side] = jnp.broadcast_to(inverse, inverse_ref.shape[1:])
 
 
 def final_kernel(pairs, sum_ref, sum_loss_ref, unit_ref, inverse_ref, got_ref, loss_ref, grad_image_ref, grad_text_ref):
     first = on_first_core()
     rows, depth = sum_ref.shape[1:]
-    pull, loss = total([got_ref], rows, depth)
-    pulls = (sum_ref[0], sum_ref[1] + pull)
-    losses = (sum_loss_ref[0][:, 0:1], sum_loss_ref[1][:, 0:1] + loss)
+    own, _ = place_of(first, rows)
+    pull, loss = total([got_ref[own, :]], rows, depth)
+    pulls = (sum_ref[0] + pull, sum_ref[1])
+    losses = (sum_loss_ref[0][:, 0:1] + loss, sum_loss_ref[1][:, 0:1])
     for side, (pull, out) in enumerate(
         (
             (jnp.where(first, pulls[0], pulls[1]), grad_image_ref),
@@ -319,8 +320,7 @@
     def swap(x):
         return lax.ppermute(x, AXES, [(i, i ^ lanes) for i in range(n)])
 
-    out_visits = (((12, 3), 0), ((2, 8), 0), ((4, 1), 0), ((4, 1), 1))
-    back_visits = (((12, 3), 0), ((4, 1), 0), ((2, 8), 0), ((2, 8), 1))
+    visits = (((12, 3), 0), ((2, 8), 0), ((4, 1), 0), ((4, 1), 1))
     late = pl.CostEstimate(flops=10**9, bytes_accessed=10**7, transcendentals=0)
     digits = call(
         digits_kernel,
@@ -331,40 +331,37 @@
     )
     own = call(pack_kernel, block(2), [image_emb, text_emb, digits], "pack")
     *sent, mine, other = call(join_kernel, (block(2),) * 6, [own, swap(own)], "join")
-    got = [visit(x, *way) for x, way in zip(sent, out_visits)]
-    far, pair = call(
-        far_kernel,
+    got = [visit(x, *way) for x, way in zip(sent, visits)]
+    near, pair = call(
+        near_kernel,
         (block(4), wide(8, LANES)),
-        [scale[None], shift[None], *got[:2]],
-        "far",
+        [scale[None], shift[None], *got[2:]],
+        "near",
         2,
-    )
-    near = call(put_pair, block(4), got[2:], "near", cost=late)
+        late,
+    )
     one, two = block(1, jnp.int16), block(2, jnp.int16)
     parts = call(
         tile_kernel,
         (two, two, one, one, two),
-        [pair, mine, other, far, swap(far), near],
+        [pair, mine, other, *got[:2], swap(got[0]), swap(got[1]), near],
         "tile",
     )
-    back = [visit(x, *way) for x, way in zip(parts, back_visits)]
+    back = [visit(x, *way) for x, way in zip(parts, visits)]
     keep, kept_loss, give = call(
-        add_kernel,
-        (wide(rows, depth), wide(rows, LANES), one),
-        [parts[4], *back[:2]],
-        "add",
+        add_kernel, (wide(rows, depth), wide(rows, LANES), one), [parts[4], back[0]], "add"
     )
     sums = call(
         more_kernel,
         (wide(2, rows, depth), wide(2, rows, LANES)) * 2,
-        [keep, kept_loss, *back[2:], image_emb, text_emb],
+        [keep, kept_loss, back[1], swap(give), *back[2:], image_emb, text_emb],
         "more",
         cost=late,
     )
     loss, grad_image, grad_text = call(
         functools.partial(final_kernel, n * rows),
         (wide(1, rows), wide(rows, depth), wide(rows, depth)),
-        [*sums, swap(give)],
+        [*sums, swap(back[1])],
         "final",
     )
     return (loss[0], grad_image, grad_text)

time: 25.5 us -> 25.2 us (0.988)
  waiting for transfers between devices: 8.08 us -> 5.31 us
  starting transfers between devices: 12.2 us -> 14.7 us
    ppermute x8, waiting for transfers between devices: 6.12 us -> 3.88 us  [visit(): return lax.ppermute(x, AXES, pairs)]
    ppermute x3 -> x5, starting transfers between devices: 0.67 us -> 2.3 us  [swap(): return lax.ppermute(x, AXES, [(i, i ^ lanes) for i in range(n)])]
    ppermute x8, starting transfers between devices: 11.6 us -> 12.4 us  [visit(): return lax.ppermute(x, AXES, pairs)]
    ppermute x3 -> x5, waiting for transfers between devices: 1.96 us -> 1.43 us  [swap(): return lax.ppermute(x, AXES, [(i, i ^ lanes) for i in range(n)])]
    pallas_call x9 -> x8, Pallas kernels: 2.29 us -> 2.3 us  [call(): pl.pallas_call(kernel, cost_estimate=cost, out_shape=shapes, in_specs=[sm...]
  transfers between devices with their start and end apart: 11 -> 13, of which waited for: 6 -> 6; matrix products, arithmetic and copies ran while one was open for 0% -> 0% of each run, Pallas kernels for 2% -> 2%
where the time goes in v16:
time: 25.2 us; the launch traced here: 25 us
  starting transfers between devices  14.7 us (58%)
  waiting for transfers between devices  5.31 us (21%)
  Pallas kernels  2.3 us (9%)
  between operations  2.04 us (8%)
  local copies, waits for them, and re-layouts  0.67 us (3%)
    ppermute x8, starting transfers between devices, visit(): return lax.ppermute(x, AXES, pairs)  12.4 us
    ppermute x8, waiting for transfers between devices, visit(): return lax.ppermute(x, AXES, pairs)  3.88 us
    pallas_call x8, Pallas kernels, call(): pl.pallas_call(kernel, cost_estimate=cost, out_shape=shapes, in_specs=[sm...  2.3 us
    ppermute x5, starting transfers between devices, swap(): return lax.ppermute(x, AXES, [(i, i ^ lanes) for i in range(n)])  2.3 us
    ppermute x5, waiting for transfers between devices, swap(): return lax.ppermute(x, AXES, [(i, i ^ lanes) for i in range(n)])  1.43 us
    unnamed x6, local copies, waits for them, and re-layouts  0.67 us
  transfers between devices with their start and end apart: 13, of which 6 were waited for; matrix products, arithmetic and copies ran while one was open for 0% of the time, Pallas kernels for 2%

profile of v16, /device:TPU:0, one launch (start us, length us, event | category | flops | bytes accessed | tf_op | source)
XLA Modules:
  0.0 25.0 jit_solution(16455636346607903781)
XLA Ops:
  0.6 0.0 copy-start.1
  0.6 0.0 copy-start
  0.7 0.0 copy-start.2
  0.7 0.7 %copy-done.2 = s32[16]{0:T(128)S(1)} copy-done((s32[16]{0:T(128)S(1)}, s32[16]{0:T(128)}, u32[]{:S(2)}) %copy-start.2) | copy-done | bytes 88
  1.3 0.1 digits.1.digits_ref
  1.4 0.0 copy-done.1
  1.4 0.0 copy-done
  1.4 0.1 pack.1.own_ref
  1.5 0.5 %collective-permute-start = (bf16[32,1280]{1,0:T(8,128)(2,1)S(1)}, bf16[32,1280]{1,0:T(8,128)(2,1)S(1)}, u32[]{:S(2)}, u32[]{:S(2)}) collective-permute-start(bf16[32,1280]{1,0:T(8,128)(2,1)S(1)} %pack.1.own_ref), channel_id=1, source_target_pairs={{0,2},{1,3},{2,0},{3,1},{4,6},{5,7},{6,4},{7,5},{8,10},{9,11},{10,... | collective-permute-start | bytes 245768 | tf_op jit(solution)/shard_map/ppermute | solution.py:321
  2.1 0.9 %collective-permute-done.got_ref = bf16[32,1280]{1,0:T(8,128)(2,1)S(1)} collective-permute-done((bf16[32,1280]{1,0:T(8,128)(2,1)S(1)}, bf16[32,1280]{1,0:T(8,128)(2,1)S(1)}, u32[]{:S(2)}, u32[]{:S(2)}) %collective-permute-start) | collective-permute-done | bytes 81952 | tf_op jit(solution)/shard_map/ppermute | solution.py:321
  3.0 0.1 join.1
  3.1 5.0 %collective-permute-start.3 = (bf16[32,1280]{1,0:T(8,128)(2,1)S(1)}, bf16[32,1280]{1,0:T(8,128)(2,1)S(1)}, u32[]{:S(2)}, u32[]{:S(2)}) collective-permute-start(bf16[32,1280]{1,0:T(8,128)(2,1)S(1)} %get-tuple-element.31), channel_id=1, source_target_pairs={{0,24},{1,25},{2,7},{3,6},{4,28},{5,29},{6,3},{7,2},{8,16},{9,17},... | collective-permute-start | bytes 245768 | tf_op jit(solution)/shard_map/ppermute | solution.py:318
  8.1 1.5 %collective-permute-start.4 = (bf16[32,1280]{1,0:T(8,128)(2,1)S(1)}, bf16[32,1280]{1,0:T(8,128)(2,1)S(1)}, u32[]{:S(2)}, u32[]{:S(2)}) collective-permute-start(bf16[32,1280]{1,0:T(8,128)(2,1)S(1)} %get-tuple-element.32), channel_id=1, source_target_pairs={{0,4},{1,5},{2,18},{3,19},{4,0},{5,1},{6,22},{7,23},{8,12},{9,13},... | collective-permute-start | bytes 245768 | tf_op jit(solution)/shard_map/ppermute | solution.py:318
  9.6 0.0 collective-permute-start.1
  9.6 0.9 %collective-permute-start.2 = (bf16[32,1280]{1,0:T(8,128)(2,1)S(1)}, bf16[32,1280]{1,0:T(8,128)(2,1)S(1)}, u32[]{:S(2)}, u32[]{:S(2)}) collective-permute-start(bf16[32,1280]{1,0:T(8,128)(2,1)S(1)} %get-tuple-element.27), channel_id=1, source_target_pairs={{0,10},{1,11},{2,1},{3,0},{4,14},{5,15},{6,5},{7,4},{8,2},{9,3},{1... | collective-permute-start | bytes 245768 | tf_op jit(solution)/shard_map/ppermute | solution.py:318
  11.8 0.0 collective-permute-done.3.got_0
  11.8 0.8 %collective-permute-start.5 = (bf16[32,1280]{1,0:T(8,128)(2,1)S(1)}, bf16[32,1280]{1,0:T(8,128)(2,1)S(1)}, u32[]{:S(2)}, u32[]{:S(2)}) collective-permute-start(bf16[32,1280]{1,0:T(8,128)(2,1)S(1)} %collective-permute-done.3.got_0), channel_id=1, source_target_pairs={{0,2},{1,3},{2,0},{3,1},{4,6},{5,7},{6,4},{7,5},{8,10},{9,11},{10,... | collective-permute-start | bytes 245768 | tf_op jit(solution)/shard_map/ppermute | solution.py:321
  12.6 0.0 collective-permute-done.4.got_1
  12.6 0.1 collective-permute-start.6
  12.7 1.3 %collective-permute-done.1.upper_ref = bf16[32,1280]{1,0:T(8,128)(2,1)S(1)} collective-permute-done((bf16[32,1280]{1,0:T(8,128)(2,1)S(1)}, bf16[32,1280]{1,0:T(8,128)(2,1)S(1)}, u32[]{:S(2)}, u32[]{:S(2)}) %collective-permute-start.1) | collective-permute-done | bytes 81952 | tf_op jit(solution)/shard_map/ppermute | solution.py:318
  14.0 0.0 collective-permute-done.2.lower_ref
  14.0 0.0 collective-permute-done.5.swapped_0
  14.0 0.0 collective-permute-done.6.swapped_1
  14.1 0.7 %tile.1 = (s16[32,1280]{1,0:T(8,128)(2,1)S(1)}, s16[32,1280]{1,0:T(8,128)(2,1)S(1)}, s16[16,1280]{1,0:T(8,128)(2,1)S(1)}, s16[16,1280]{1,0:T(8,128)(2,1)S(1)}, s16[32,1280]{1,0:T(8,128)(2,1)S(1)}) custom-call(f32[8,128]{1,0:T(8,128)S(1)} %get-tuple-element.28.pair_ref, bf16[32,1280]{1,0:T(8,128)(2,1)S(1)} %get-tuple-element.29.mine_ref, ...), custom_call_target="tpu_custom_call" | custom-call | tf_op jit(solution)/shard_map/tile/pallas_call | solution.py:294
  14.8 2.9 %collective-permute-start.7 = (s16[32,1280]{1,0:T(8,128)(2,1)S(1)}, s16[32,1280]{1,0:T(8,128)(2,1)S(1)}, u32[]{:S(2)}, u32[]{:S(2)}) collective-permute-start(s16[32,1280]{1,0:T(8,128)(2,1)S(1)} %get-tuple-element.35), channel_id=1, source_target_pairs={{0,24},{1,25},{2,7},{3,6},{4,28},{5,29},{6,3},{7,2},{8,16},{9,17},... | collective-permute-start | bytes 245768 | tf_op jit(solution)/shard_map/ppermute | solution.py:318
  17.7 0.9 %collective-permute-start.8 = (s16[32,1280]{1,0:T(8,128)(2,1)S(1)}, s16[32,1280]{1,0:T(8,128)(2,1)S(1)}, u32[]{:S(2)}, u32[]{:S(2)}) collective-permute-start(s16[32,1280]{1,0:T(8,128)(2,1)S(1)} %get-tuple-element.38), channel_id=1, source_target_pairs={{0,4},{1,5},{2,18},{3,19},{4,0},{5,1},{6,22},{7,23},{8,12},{9,13},... | collective-permute-start | bytes 245768 | tf_op jit(solution)/shard_map/ppermute | solution.py:318
  18.6 0.0 collective-permute-start.10
  18.6 1.1 %collective-permute-start.11 = (s16[16,1280]{1,0:T(8,128)(2,1)S(1)}, s16[16,1280]{1,0:T(8,128)(2,1)S(1)}, u32[]{:S(2)}, u32[]{:S(2)}) collective-permute-start(s16[16,1280]{1,0:T(8,128)(2,1)S(1)} %get-tuple-element.41), channel_id=1, source_target_pairs={{0,10},{1,11},{2,1},{3,0},{4,14},{5,15},{6,5},{7,4},{8,2},{9,3},{1... | collective-permute-start | bytes 122888 | tf_op jit(solution)/shard_map/ppermute | solution.py:318
  19.7 2.3 %collective-permute-done.7.back_ref = s16[32,1280]{1,0:T(8,128)(2,1)S(1)} collective-permute-done((s16[32,1280]{1,0:T(8,128)(2,1)S(1)}, s16[32,1280]{1,0:T(8,128)(2,1)S(1)}, u32[]{:S(2)}, u32[]{:S(2)}) %collective-permute-start.7) | collective-permute-done | bytes 81952 | tf_op jit(solution)/shard_map/ppermute | solution.py:318
  22.0 0.2 add.1
  22.2 0.1 collective-permute-start.9
  22.3 0.0 collective-permute-done.8.back_ref
  22.3 0.9 %collective-permute-start.12 = (s16[32,1280]{1,0:T(8,128)(2,1)S(1)}, s16[32,1280]{1,0:T(8,128)(2,1)S(1)}, u32[]{:S(2)}, u32[]{:S(2)}) collective-permute-start(s16[32,1280]{1,0:T(8,128)(2,1)S(1)} %collective-permute-done.8.back_ref), channel_id=1, source_target_pairs={{0,2},{1,3},{2,0},{3,1},{4,6},{5,7},{6,4},{7,5},{8,10},{9,11},{10,... | collective-permute-start | bytes 245768 | tf_op jit(solution)/shard_map/ppermute | solution.py:321
  23.1 0.3 %collective-permute-done.10.same_ref = s16[16,1280]{1,0:T(8,128)(2,1)S(1)} collective-permute-done((s16[16,1280]{1,0:T(8,128)(2,1)S(1)}, s16[16,1280]{1,0:T(8,128)(2,1)S(1)}, u32[]{:S(2)}, u32[]{:S(2)}) %collective-permute-start.10) | collective-permute-done | bytes 40992 | tf_op jit(solution)/shard_map/ppermute | solution.py:318
  23.4 0.0 collective-permute-done.11.cross_ref
  23.4 0.1 collective-permute-done.9.got_ref
  23.5 0.2 more.1
  23.6 0.4 %collective-permute-done.12.got_ref = s16[32,1280]{1,0:T(8,128)(2,1)S(1)} collective-permute-done((s16[32,1280]{1,0:T(8,128)(2,1)S(1)}, s16[32,1280]{1,0:T(8,128)(2,1)S(1)}, u32[]{:S(2)}, u32[]{:S(2)}) %collective-permute-start.12) | collective-permute-done | bytes 81952 | tf_op jit(solution)/shard_map/ppermute | solution.py:321
  24.1 0.9 %final.1 = (f32[1,16]{1,0:T(1,128)}, f32[16,1152]{1,0:T(8,128)}, f32[16,1152]{1,0:T(8,128)}) custom-call(f32[2,16,1152]{2,1,0:T(8,128)S(1)} %get-tuple-element.42.sum_ref, f32[2,16,128]{2,1,0:T(8,128)S(1)} %get-tuple-element.43.sum_loss_ref, f32[2,16,1152]{2,1,0:T(8,128)S(1)} %get-tuple-element.44.unit_ref, f32[2,16,128]{2,1,0:T(8,128)S(1)} %get-tuple-element.45.inverse_ref, ...), custom_call_target="tpu_custom_call" | custom-call | tf_op jit(solution)/shard_map/final/pallas_call | solution.py:294
  (1 shorter events, 0.0 us)
Async XLA Ops:
  0.6 0.8 %copy-start.1 = (bf16[16,1152]{1,0:T(8,128)(2,1)S(1)}, bf16[16,1152]{1,0:T(8,128)(2,1)}, u32[]{:S(2)}) copy-start(bf16[16,1152]{1,0:T(8,128)(2,1)} %text_ref.3) | copy-start | bytes 110596
  0.6 0.8 %copy-start = (bf16[16,1152]{1,0:T(8,128)(2,1)S(1)}, bf16[16,1152]{1,0:T(8,128)(2,1)}, u32[]{:S(2)}) copy-start(bf16[16,1152]{1,0:T(8,128)(2,1)} %image_ref.3) | copy-start | bytes 110596
  0.7 0.7 %copy-start.2 = (s32[16]{0:T(128)S(1)}, s32[16]{0:T(128)}, u32[]{:S(2)}) copy-start(s32[16]{0:T(128)} %class_ref.1) | copy-start | bytes 196
  1.5 1.4 %collective-permute-start = (bf16[32,1280]{1,0:T(8,128)(2,1)S(1)}, bf16[32,1280]{1,0:T(8,128)(2,1)S(1)}, u32[]{:S(2)}, u32[]{:S(2)}) collective-permute-start(bf16[32,1280]{1,0:T(8,128)(2,1)S(1)} %pack.1.own_ref), channel_id=1, source_target_pairs={{0,2},{1,3},{2,0},{3,1},{4,6},{5,7},{6,4},{7,5},{8,10},{9,11},{10,... | collective-permute-start | bytes 245768 | tf_op jit(solution)/shard_map/ppermute | solution.py:321
  3.1 8.8 %collective-permute-start.3 = (bf16[32,1280]{1,0:T(8,128)(2,1)S(1)}, bf16[32,1280]{1,0:T(8,128)(2,1)S(1)}, u32[]{:S(2)}, u32[]{:S(2)}) collective-permute-start(bf16[32,1280]{1,0:T(8,128)(2,1)S(1)} %get-tuple-element.31), channel_id=1, source_target_pairs={{0,24},{1,25},{2,7},{3,6},{4,28},{5,29},{6,3},{7,2},{8,16},{9,17},... | collective-permute-start | bytes 245768 | tf_op jit(solution)/shard_map/ppermute | solution.py:318
  8.1 4.5 %collective-permute-start.4 = (bf16[32,1280]{1,0:T(8,128)(2,1)S(1)}, bf16[32,1280]{1,0:T(8,128)(2,1)S(1)}, u32[]{:S(2)}, u32[]{:S(2)}) collective-permute-start(bf16[32,1280]{1,0:T(8,128)(2,1)S(1)} %get-tuple-element.32), channel_id=1, source_target_pairs={{0,4},{1,5},{2,18},{3,19},{4,0},{5,1},{6,22},{7,23},{8,12},{9,13},... | collective-permute-start | bytes 245768 | tf_op jit(solution)/shard_map/ppermute | solution.py:318
  9.6 4.4 %collective-permute-start.1 = (bf16[32,1280]{1,0:T(8,128)(2,1)S(1)}, bf16[32,1280]{1,0:T(8,128)(2,1)S(1)}, u32[]{:S(2)}, u32[]{:S(2)}) collective-permute-start(bf16[32,1280]{1,0:T(8,128)(2,1)S(1)} %get-tuple-element.26), channel_id=1, source_target_pairs={{0,8},{1,9},{2,3},{3,2},{4,12},{5,13},{6,7},{7,6},{8,0},{9,1},{10,... | collective-permute-start | bytes 245768 | tf_op jit(solution)/shard_map/ppermute | solution.py:318
  9.6 4.4 %collective-permute-start.2 = (bf16[32,1280]{1,0:T(8,128)(2,1)S(1)}, bf16[32,1280]{1,0:T(8,128)(2,1)S(1)}, u32[]{:S(2)}, u32[]{:S(2)}) collective-permute-start(bf16[32,1280]{1,0:T(8,128)(2,1)S(1)} %get-tuple-element.27), channel_id=1, source_target_pairs={{0,10},{1,11},{2,1},{3,0},{4,14},{5,15},{6,5},{7,4},{8,2},{9,3},{1... | collective-permute-start | bytes 245768 | tf_op jit(solution)/shard_map/ppermute | solution.py:318
  11.8 2.2 %collective-permute-start.5 = (bf16[32,1280]{1,0:T(8,128)(2,1)S(1)}, bf16[32,1280]{1,0:T(8,128)(2,1)S(1)}, u32[]{:S(2)}, u32[]{:S(2)}) collective-permute-start(bf16[32,1280]{1,0:T(8,128)(2,1)S(1)} %collective-permute-done.3.got_0), channel_id=1, source_target_pairs={{0,2},{1,3},{2,0},{3,1},{4,6},{5,7},{6,4},{7,5},{8,10},{9,11},{10,... | collective-permute-start | bytes 245768 | tf_op jit(solution)/shard_map/ppermute | solution.py:321
  12.6 1.5 %collective-permute-start.6 = (bf16[32,1280]{1,0:T(8,128)(2,1)S(1)}, bf16[32,1280]{1,0:T(8,128)(2,1)S(1)}, u32[]{:S(2)}, u32[]{:S(2)}) collective-permute-start(bf16[32,1280]{1,0:T(8,128)(2,1)S(1)} %collective-permute-done.4.got_1), channel_id=1, source_target_pairs={{0,2},{1,3},{2,0},{3,1},{4,6},{5,7},{6,4},{7,5},{8,10},{9,11},{10,... | collective-permute-start | bytes 245768 | tf_op jit(solution)/shard_map/ppermute | solution.py:321
  14.8 7.2 %collective-permute-start.7 = (s16[32,1280]{1,0:T(8,128)(2,1)S(1)}, s16[32,1280]{1,0:T(8,128)(2,1)S(1)}, u32[]{:S(2)}, u32[]{:S(2)}) collective-permute-start(s16[32,1280]{1,0:T(8,128)(2,1)S(1)} %get-tuple-element.35), channel_id=1, source_target_pairs={{0,24},{1,25},{2,7},{3,6},{4,28},{5,29},{6,3},{7,2},{8,16},{9,17},... | collective-permute-start | bytes 245768 | tf_op jit(solution)/shard_map/ppermute | solution.py:318
  17.7 4.6 %collective-permute-start.8 = (s16[32,1280]{1,0:T(8,128)(2,1)S(1)}, s16[32,1280]{1,0:T(8,128)(2,1)S(1)}, u32[]{:S(2)}, u32[]{:S(2)}) collective-permute-start(s16[32,1280]{1,0:T(8,128)(2,1)S(1)} %get-tuple-element.38), channel_id=1, source_target_pairs={{0,4},{1,5},{2,18},{3,19},{4,0},{5,1},{6,22},{7,23},{8,12},{9,13},... | collective-permute-start | bytes 245768 | tf_op jit(solution)/shard_map/ppermute | solution.py:318
  18.6 4.8 %collective-permute-start.10 = (s16[16,1280]{1,0:T(8,128)(2,1)S(1)}, s16[16,1280]{1,0:T(8,128)(2,1)S(1)}, u32[]{:S(2)}, u32[]{:S(2)}) collective-permute-start(s16[16,1280]{1,0:T(8,128)(2,1)S(1)} %get-tuple-element.40), channel_id=1, source_target_pairs={{0,8},{1,9},{2,3},{3,2},{4,12},{5,13},{6,7},{7,6},{8,0},{9,1},{10,... | collective-permute-start | bytes 122888 | tf_op jit(solution)/shard_map/ppermute | solution.py:318
  18.6 4.8 %collective-permute-start.11 = (s16[16,1280]{1,0:T(8,128)(2,1)S(1)}, s16[16,1280]{1,0:T(8,128)(2,1)S(1)}, u32[]{:S(2)}, u32[]{:S(2)}) collective-permute-start(s16[16,1280]{1,0:T(8,128)(2,1)S(1)} %get-tuple-element.41), channel_id=1, source_target_pairs={{0,10},{1,11},{2,1},{3,0},{4,14},{5,15},{6,5},{7,4},{8,2},{9,3},{1... | collective-permute-start | bytes 122888 | tf_op jit(solution)/shard_map/ppermute | solution.py:318
  22.2 1.3 %collective-permute-start.9 = (s16[16,1280]{1,0:T(8,128)(2,1)S(1)}, s16[16,1280]{1,0:T(8,128)(2,1)S(1)}, u32[]{:S(2)}, u32[]{:S(2)}) collective-permute-start(s16[16,1280]{1,0:T(8,128)(2,1)S(1)} %get-tuple-element.39), channel_id=1, source_target_pairs={{0,2},{1,3},{2,0},{3,1},{4,6},{5,7},{6,4},{7,5},{8,10},{9,11},{10,... | collective-permute-start | bytes 122888 | tf_op jit(solution)/shard_map/ppermute | solution.py:321
  22.3 1.8 %collective-permute-start.12 = (s16[32,1280]{1,0:T(8,128)(2,1)S(1)}, s16[32,1280]{1,0:T(8,128)(2,1)S(1)}, u32[]{:S(2)}, u32[]{:S(2)}) collective-permute-start(s16[32,1280]{1,0:T(8,128)(2,1)S(1)} %collective-permute-done.8.back_ref), channel_id=1, source_target_pairs={{0,2},{1,3},{2,0},{3,1},{4,6},{5,7},{6,4},{7,5},{8,10},{9,11},{10,... | collective-permute-start | bytes 245768 | tf_op jit(solution)/shard_map/ppermute | solution.py:321

commit v17 on v16

--- a/solution.py
+++ b/solution.py
@@ -77,9 +77,9 @@
     return lax.rem(lax.axis_index("img"), 2) == 0
 
 
-def class_digits(class_ref):
-    rows = class_ref.shape[0]
-    across = jnp.broadcast_to(class_ref[...][None, :], (rows, rows))
+def class_digits(classes):
+    rows = classes.shape[1]
+    across = jnp.broadcast_to(classes, (rows, rows))
     row = lax.broadcasted_iota(jnp.int32, (rows, rows), 0)
     column = lax.broadcasted_iota(jnp.int32, (rows, rows), 1)
     lane = lax.broadcasted_iota(jnp.int32, (rows, LANES), 1)
@@ -92,17 +92,23 @@
 
 
 def digits_kernel(class_ref, digits_ref):
-    digits_ref[...] = class_digits(class_ref)
-
-
-def pack_kernel(image_ref, text_ref, digits_ref, out_ref):
+    digits_ref[...] = class_digits(class_ref[...][None, :])
+
+
+def put_rows_of(image_ref, text_ref, digits, out_ref):
     rows, depth = image_ref.shape
     for start, source in ((0, image_ref), (rows, text_ref)):
         out_ref[start : start + rows, :depth] = unit_rows(source[...])[0].astype(jnp.bfloat16)
-        out_ref[start : start + rows, depth:] = digits_ref[...]
-
-
-def join_kernel(own_ref, got_ref, *refs):
+        out_ref[start : start + rows, depth:] = digits
+
+
+def pack_kernel(image_ref, text_ref, digits_ref, out_ref):
+    put_rows_of(image_ref, text_ref, digits_ref[...], out_ref)
+
+
+def join_kernel(own_ref, got_image, got_text, got_class, *refs):
+    *refs, got_ref = refs
+    put_rows_of(got_image, got_text, class_digits(got_class[...][None, :]), got_ref)
     first = on_first_core()
     rows = own_ref.shape[0] // 2
     own, got = own_ref[...].astype(jnp.float32), got_ref[...].astype(jnp.float32)
@@ -330,7 +336,8 @@
         cost=late,
     )
     own = call(pack_kernel, block(2), [image_emb, text_emb, digits], "pack")
-    *sent, mine, other = call(join_kernel, (block(2),) * 6, [own, swap(own)], "join")
+    swapped = [swap(x) for x in (image_emb, text_emb, pair_class)]
+    *sent, mine, other, _ = call(join_kernel, (block(2),) * 7, [own, *swapped], "join")
     got = [visit(x, *way) for x, way in zip(sent, visits)]
     near, pair = call(
         near_kernel,

time: 25.2 us -> 25.5 us (1.012)
  waiting for transfers between devices: 5.31 us -> 4.56 us
  Pallas kernels: 2.3 us -> 3 us
  starting transfers between devices: 14.7 us -> 15.1 us
    ppermute x5 -> x7, waiting for transfers between devices: 1.43 us -> 0.68 us  [swap(): return lax.ppermute(x, AXES, [(i, i ^ lanes) for i in range(n)])]
    pallas_call x8, Pallas kernels: 2.3 us -> 3 us  [call(): pl.pallas_call(kernel, cost_estimate=cost, out_shape=shapes, in_specs=[sm...]
    ppermute x5 -> x7, starting transfers between devices: 2.3 us -> 2.8 us  [swap(): return lax.ppermute(x, AXES, [(i, i ^ lanes) for i in range(n)])]
  transfers between devices with their start and end apart: 13 -> 15, of which waited for: 6 -> 6; matrix products, arithmetic and copies ran while one was open for 0% -> 0% of each run, Pallas kernels for 2% -> 2%
where the time goes in v17:
time: 25.5 us; the launch traced here: 25.4 us
  starting transfers between devices  15.1 us (59%)
  waiting for transfers between devices  4.56 us (18%)
  Pallas kernels  3 us (12%)
  between operations  2.04 us (8%)
  local copies, waits for them, and re-layouts  0.66 us (3%)
    ppermute x8, starting transfers between devices, visit(): return lax.ppermute(x, AXES, pairs)  12.3 us
    ppermute x8, waiting for transfers between devices, visit(): return lax.ppermute(x, AXES, pairs)  3.88 us
    pallas_call x8, Pallas kernels, call(): pl.pallas_call(kernel, cost_estimate=cost, out_shape=shapes, in_specs=[sm...  3 us
    ppermute x7, starting transfers between devices, swap(): return lax.ppermute(x, AXES, [(i, i ^ lanes) for i in range(n)])  2.8 us
    ppermute x7, waiting for transfers between devices, swap(): return lax.ppermute(x, AXES, [(i, i ^ lanes) for i in range(n)])  0.68 us
    unnamed x6, local copies, waits for them, and re-layouts  0.66 us
  transfers between devices with their start and end apart: 15, of which 6 were waited for; matrix products, arithmetic and copies ran while one was open for 0% of the time, Pallas kernels for 2%

profile of v17, /device:TPU:0, one launch (start us, length us, event | category | flops | bytes accessed | tf_op | source)
XLA Modules:
  0.0 25.4 jit_solution(17791667486842404690)
XLA Ops:
  0.6 0.0 copy-start
  0.6 0.0 copy-start.1
  0.7 0.5 %collective-permute-start.2 = (s32[16]{0:T(128)}, s32[16]{0:T(128)S(1)}, u32[]{:S(2)}, u32[]{:S(2)}) collective-permute-start(s32[16]{0:T(128)} %class_ref.1), channel_id=1, source_target_pairs={{0,2},{1,3},{2,0},{3,1},{4,6},{5,7},{6,4},{7,5},{8,10},{9,11},{10,... | collective-permute-start | bytes 200 | tf_op jit(solution)/shard_map/ppermute | solution.py:327
  1.2 0.1 collective-permute-start
  1.2 0.4 %collective-permute-start.1 = (bf16[16,1152]{1,0:T(8,128)(2,1)}, bf16[16,1152]{1,0:T(8,128)(2,1)S(1)}, u32[]{:S(2)}, u32[]{:S(2)}) collective-permute-start(bf16[16,1152]{1,0:T(8,128)(2,1)} %text_ref.3), channel_id=1, source_target_pairs={{0,2},{1,3},{2,0},{3,1},{4,6},{5,7},{6,4},{7,5},{8,10},{9,11},{10,... | collective-permute-start | bytes 110600 | tf_op jit(solution)/shard_map/ppermute | solution.py:327
  1.7 0.0 copy-start.2
  1.7 0.7 %copy-done.2 = s32[16]{0:T(128)S(1)} copy-done((s32[16]{0:T(128)S(1)}, s32[16]{0:T(128)}, u32[]{:S(2)}) %copy-start.2) | copy-done | bytes 88
  2.3 0.1 digits.1.digits_ref
  2.4 0.0 copy-done
  2.4 0.0 copy-done.1
  2.4 0.1 pack.1.own_ref
  2.6 0.0 collective-permute-done.2.got_class
  2.6 0.0 collective-permute-done.got_image
  2.6 0.2 collective-permute-done.1.got_text
  2.8 0.8 %join.1 = (bf16[32,1280]{1,0:T(8,128)(2,1)S(1)}, bf16[32,1280]{1,0:T(8,128)(2,1)S(1)}, bf16[32,1280]{1,0:T(8,128)(2,1)S(1)}, bf16[32,1280]{1,0:T(8,128)(2,1)S(1)...) custom-call(bf16[32,1280]{1,0:T(8,128)(2,1)S(1)} %pack.1.own_ref, ...), custom_call_target="tpu_custom_call" | custom-call | tf_op jit(solution)/shard_map/join/pallas_call | solution.py:300
  3.5 4.9 %collective-permute-start.5 = (bf16[32,1280]{1,0:T(8,128)(2,1)S(1)}, bf16[32,1280]{1,0:T(8,128)(2,1)S(1)}, u32[]{:S(2)}, u32[]{:S(2)}) collective-permute-start(bf16[32,1280]{1,0:T(8,128)(2,1)S(1)} %get-tuple-element.31), channel_id=1, source_target_pairs={{0,24},{1,25},{2,7},{3,6},{4,28},{5,29},{6,3},{7,2},{8,16},{9,17},... | collective-permute-start | bytes 245768 | tf_op jit(solution)/shard_map/ppermute | solution.py:324
  8.5 1.5 %collective-permute-start.6 = (bf16[32,1280]{1,0:T(8,128)(2,1)S(1)}, bf16[32,1280]{1,0:T(8,128)(2,1)S(1)}, u32[]{:S(2)}, u32[]{:S(2)}) collective-permute-start(bf16[32,1280]{1,0:T(8,128)(2,1)S(1)} %get-tuple-element.32), channel_id=1, source_target_pairs={{0,4},{1,5},{2,18},{3,19},{4,0},{5,1},{6,22},{7,23},{8,12},{9,13},... | collective-permute-start | bytes 245768 | tf_op jit(solution)/shard_map/ppermute | solution.py:324
  10.0 0.0 collective-permute-start.3
  10.0 0.9 %collective-permute-start.4 = (bf16[32,1280]{1,0:T(8,128)(2,1)S(1)}, bf16[32,1280]{1,0:T(8,128)(2,1)S(1)}, u32[]{:S(2)}, u32[]{:S(2)}) collective-permute-start(bf16[32,1280]{1,0:T(8,128)(2,1)S(1)} %get-tuple-element.27), channel_id=1, source_target_pairs={{0,10},{1,11},{2,1},{3,0},{4,14},{5,15},{6,5},{7,4},{8,2},{9,3},{1... | collective-permute-start | bytes 245768 | tf_op jit(solution)/shard_map/ppermute | solution.py:324
  12.2 0.0 collective-permute-done.5.got_0
  12.2 0.8 %collective-permute-start.7 = (bf16[32,1280]{1,0:T(8,128)(2,1)S(1)}, bf16[32,1280]{1,0:T(8,128)(2,1)S(1)}, u32[]{:S(2)}, u32[]{:S(2)}) collective-permute-start(bf16[32,1280]{1,0:T(8,128)(2,1)S(1)} %collective-permute-done.5.got_0), channel_id=1, source_target_pairs={{0,2},{1,3},{2,0},{3,1},{4,6},{5,7},{6,4},{7,5},{8,10},{9,11},{10,... | collective-permute-start | bytes 245768 | tf_op jit(solution)/shard_map/ppermute | solution.py:327
  13.0 0.0 collective-permute-done.6.got_1
  13.0 0.1 collective-permute-start.8
  13.1 1.3 %collective-permute-done.3.upper_ref = bf16[32,1280]{1,0:T(8,128)(2,1)S(1)} collective-permute-done((bf16[32,1280]{1,0:T(8,128)(2,1)S(1)}, bf16[32,1280]{1,0:T(8,128)(2,1)S(1)}, u32[]{:S(2)}, u32[]{:S(2)}) %collective-permute-start.3) | collective-permute-done | bytes 81952 | tf_op jit(solution)/shard_map/ppermute | solution.py:324
  14.4 0.0 collective-permute-done.4.lower_ref
  14.4 0.0 collective-permute-done.7.swapped_0
  14.4 0.0 collective-permute-done.8.swapped_1
  14.4 0.7 %tile.1 = (s16[32,1280]{1,0:T(8,128)(2,1)S(1)}, s16[32,1280]{1,0:T(8,128)(2,1)S(1)}, s16[16,1280]{1,0:T(8,128)(2,1)S(1)}, s16[16,1280]{1,0:T(8,128)(2,1)S(1)}, s16[32,1280]{1,0:T(8,128)(2,1)S(1)}) custom-call(f32[8,128]{1,0:T(8,128)S(1)} %get-tuple-element.28.pair_ref, bf16[32,1280]{1,0:T(8,128)(2,1)S(1)} %get-tuple-element.29.mine_ref, ...), custom_call_target="tpu_custom_call" | custom-call | tf_op jit(solution)/shard_map/tile/pallas_call | solution.py:300
  15.2 2.9 %collective-permute-start.9 = (s16[32,1280]{1,0:T(8,128)(2,1)S(1)}, s16[32,1280]{1,0:T(8,128)(2,1)S(1)}, u32[]{:S(2)}, u32[]{:S(2)}) collective-permute-start(s16[32,1280]{1,0:T(8,128)(2,1)S(1)} %get-tuple-element.35), channel_id=1, source_target_pairs={{0,24},{1,25},{2,7},{3,6},{4,28},{5,29},{6,3},{7,2},{8,16},{9,17},... | collective-permute-start | bytes 245768 | tf_op jit(solution)/shard_map/ppermute | solution.py:324
  18.1 0.9 %collective-permute-start.10 = (s16[32,1280]{1,0:T(8,128)(2,1)S(1)}, s16[32,1280]{1,0:T(8,128)(2,1)S(1)}, u32[]{:S(2)}, u32[]{:S(2)}) collective-permute-start(s16[32,1280]{1,0:T(8,128)(2,1)S(1)} %get-tuple-element.38), channel_id=1, source_target_pairs={{0,4},{1,5},{2,18},{3,19},{4,0},{5,1},{6,22},{7,23},{8,12},{9,13},... | collective-permute-start | bytes 245768 | tf_op jit(solution)/shard_map/ppermute | solution.py:324
  19.0 0.0 collective-permute-start.12
  19.0 1.1 %collective-permute-start.13 = (s16[16,1280]{1,0:T(8,128)(2,1)S(1)}, s16[16,1280]{1,0:T(8,128)(2,1)S(1)}, u32[]{:S(2)}, u32[]{:S(2)}) collective-permute-start(s16[16,1280]{1,0:T(8,128)(2,1)S(1)} %get-tuple-element.41), channel_id=1, source_target_pairs={{0,10},{1,11},{2,1},{3,0},{4,14},{5,15},{6,5},{7,4},{8,2},{9,3},{1... | collective-permute-start | bytes 122888 | tf_op jit(solution)/shard_map/ppermute | solution.py:324
  20.1 2.3 %collective-permute-done.9.back_ref = s16[32,1280]{1,0:T(8,128)(2,1)S(1)} collective-permute-done((s16[32,1280]{1,0:T(8,128)(2,1)S(1)}, s16[32,1280]{1,0:T(8,128)(2,1)S(1)}, u32[]{:S(2)}, u32[]{:S(2)}) %collective-permute-start.9) | collective-permute-done | bytes 81952 | tf_op jit(solution)/shard_map/ppermute | solution.py:324
  22.4 0.2 add.1
  22.6 0.1 collective-permute-start.11
  22.7 0.0 collective-permute-done.10.back_ref
  22.7 0.9 %collective-permute-start.14 = (s16[32,1280]{1,0:T(8,128)(2,1)S(1)}, s16[32,1280]{1,0:T(8,128)(2,1)S(1)}, u32[]{:S(2)}, u32[]{:S(2)}) collective-permute-start(s16[32,1280]{1,0:T(8,128)(2,1)S(1)} %collective-permute-done.10.back_ref), channel_id=1, source_target_pairs={{0,2},{1,3},{2,0},{3,1},{4,6},{5,7},{6,4},{7,5},{8,10},{9,11},{10,... | collective-permute-start | bytes 245768 | tf_op jit(solution)/shard_map/ppermute | solution.py:327
  23.5 0.3 %collective-permute-done.12.same_ref = s16[16,1280]{1,0:T(8,128)(2,1)S(1)} collective-permute-done((s16[16,1280]{1,0:T(8,128)(2,1)S(1)}, s16[16,1280]{1,0:T(8,128)(2,1)S(1)}, u32[]{:S(2)}, u32[]{:S(2)}) %collective-permute-start.12) | collective-permute-done | bytes 40992 | tf_op jit(solution)/shard_map/ppermute | solution.py:324
  23.8 0.0 collective-permute-done.13.cross_ref
  23.8 0.1 collective-permute-done.11.got_ref
  23.9 0.2 more.1
  24.0 0.4 %collective-permute-done.14.got_ref = s16[32,1280]{1,0:T(8,128)(2,1)S(1)} collective-permute-done((s16[32,1280]{1,0:T(8,128)(2,1)S(1)}, s16[32,1280]{1,0:T(8,128)(2,1)S(1)}, u32[]{:S(2)}, u32[]{:S(2)}) %collective-permute-start.14) | collective-permute-done | bytes 81952 | tf_op jit(solution)/shard_map/ppermute | solution.py:327
  24.4 0.9 %final.1 = (f32[1,16]{1,0:T(1,128)}, f32[16,1152]{1,0:T(8,128)}, f32[16,1152]{1,0:T(8,128)}) custom-call(f32[2,16,1152]{2,1,0:T(8,128)S(1)} %get-tuple-element.42.sum_ref, f32[2,16,128]{2,1,0:T(8,128)S(1)} %get-tuple-element.43.sum_loss_ref, f32[2,16,1152]{2,1,0:T(8,128)S(1)} %get-tuple-element.44.unit_ref, f32[2,16,128]{2,1,0:T(8,128)S(1)} %get-tuple-element.45.inverse_ref, ...), custom_call_target="tpu_custom_call" | custom-call | tf_op jit(solution)/shard_map/final/pallas_call | solution.py:300
  (1 shorter events, 0.0 us)
Async XLA Ops:
  0.6 1.8 %copy-start = (bf16[16,1152]{1,0:T(8,128)(2,1)S(1)}, bf16[16,1152]{1,0:T(8,128)(2,1)}, u32[]{:S(2)}) copy-start(bf16[16,1152]{1,0:T(8,128)(2,1)} %image_ref.3) | copy-start | bytes 110596
  0.6 1.8 %copy-start.1 = (bf16[16,1152]{1,0:T(8,128)(2,1)S(1)}, bf16[16,1152]{1,0:T(8,128)(2,1)}, u32[]{:S(2)}) copy-start(bf16[16,1152]{1,0:T(8,128)(2,1)} %text_ref.3) | copy-start | bytes 110596
  0.7 1.9 %collective-permute-start.2 = (s32[16]{0:T(128)}, s32[16]{0:T(128)S(1)}, u32[]{:S(2)}, u32[]{:S(2)}) collective-permute-start(s32[16]{0:T(128)} %class_ref.1), channel_id=1, source_target_pairs={{0,2},{1,3},{2,0},{3,1},{4,6},{5,7},{6,4},{7,5},{8,10},{9,11},{10,... | collective-permute-start | bytes 200 | tf_op jit(solution)/shard_map/ppermute | solution.py:327
  1.2 1.4 %collective-permute-start = (bf16[16,1152]{1,0:T(8,128)(2,1)}, bf16[16,1152]{1,0:T(8,128)(2,1)S(1)}, u32[]{:S(2)}, u32[]{:S(2)}) collective-permute-start(bf16[16,1152]{1,0:T(8,128)(2,1)} %image_ref.3), channel_id=1, source_target_pairs={{0,2},{1,3},{2,0},{3,1},{4,6},{5,7},{6,4},{7,5},{8,10},{9,11},{10,... | collective-permute-start | bytes 110600 | tf_op jit(solution)/shard_map/ppermute | solution.py:327
  1.2 1.5 %collective-permute-start.1 = (bf16[16,1152]{1,0:T(8,128)(2,1)}, bf16[16,1152]{1,0:T(8,128)(2,1)S(1)}, u32[]{:S(2)}, u32[]{:S(2)}) collective-permute-start(bf16[16,1152]{1,0:T(8,128)(2,1)} %text_ref.3), channel_id=1, source_target_pairs={{0,2},{1,3},{2,0},{3,1},{4,6},{5,7},{6,4},{7,5},{8,10},{9,11},{10,... | collective-permute-start | bytes 110600 | tf_op jit(solution)/shard_map/ppermute | solution.py:327
  1.7 0.7 %copy-start.2 = (s32[16]{0:T(128)S(1)}, s32[16]{0:T(128)}, u32[]{:S(2)}) copy-start(s32[16]{0:T(128)} %class_ref.1) | copy-start | bytes 196
  3.5 8.7 %collective-permute-start.5 = (bf16[32,1280]{1,0:T(8,128)(2,1)S(1)}, bf16[32,1280]{1,0:T(8,128)(2,1)S(1)}, u32[]{:S(2)}, u32[]{:S(2)}) collective-permute-start(bf16[32,1280]{1,0:T(8,128)(2,1)S(1)} %get-tuple-element.31), channel_id=1, source_target_pairs={{0,24},{1,25},{2,7},{3,6},{4,28},{5,29},{6,3},{7,2},{8,16},{9,17},... | collective-permute-start | bytes 245768 | tf_op jit(solution)/shard_map/ppermute | solution.py:324
  8.5 4.5 %collective-permute-start.6 = (bf16[32,1280]{1,0:T(8,128)(2,1)S(1)}, bf16[32,1280]{1,0:T(8,128)(2,1)S(1)}, u32[]{:S(2)}, u32[]{:S(2)}) collective-permute-start(bf16[32,1280]{1,0:T(8,128)(2,1)S(1)} %get-tuple-element.32), channel_id=1, source_target_pairs={{0,4},{1,5},{2,18},{3,19},{4,0},{5,1},{6,22},{7,23},{8,12},{9,13},... | collective-permute-start | bytes 245768 | tf_op jit(solution)/shard_map/ppermute | solution.py:324
  10.0 4.4 %collective-permute-start.3 = (bf16[32,1280]{1,0:T(8,128)(2,1)S(1)}, bf16[32,1280]{1,0:T(8,128)(2,1)S(1)}, u32[]{:S(2)}, u32[]{:S(2)}) collective-permute-start(bf16[32,1280]{1,0:T(8,128)(2,1)S(1)} %get-tuple-element.26), channel_id=1, source_target_pairs={{0,8},{1,9},{2,3},{3,2},{4,12},{5,13},{6,7},{7,6},{8,0},{9,1},{10,... | collective-permute-start | bytes 245768 | tf_op jit(solution)/shard_map/ppermute | solution.py:324
  10.0 4.4 %collective-permute-start.4 = (bf16[32,1280]{1,0:T(8,128)(2,1)S(1)}, bf16[32,1280]{1,0:T(8,128)(2,1)S(1)}, u32[]{:S(2)}, u32[]{:S(2)}) collective-permute-start(bf16[32,1280]{1,0:T(8,128)(2,1)S(1)} %get-tuple-element.27), channel_id=1, source_target_pairs={{0,10},{1,11},{2,1},{3,0},{4,14},{5,15},{6,5},{7,4},{8,2},{9,3},{1... | collective-permute-start | bytes 245768 | tf_op jit(solution)/shard_map/ppermute | solution.py:324
  12.2 2.2 %collective-permute-start.7 = (bf16[32,1280]{1,0:T(8,128)(2,1)S(1)}, bf16[32,1280]{1,0:T(8,128)(2,1)S(1)}, u32[]{:S(2)}, u32[]{:S(2)}) collective-permute-start(bf16[32,1280]{1,0:T(8,128)(2,1)S(1)} %collective-permute-done.5.got_0), channel_id=1, source_target_pairs={{0,2},{1,3},{2,0},{3,1},{4,6},{5,7},{6,4},{7,5},{8,10},{9,11},{10,... | collective-permute-start | bytes 245768 | tf_op jit(solution)/shard_map/ppermute | solution.py:327
  13.0 1.5 %collective-permute-start.8 = (bf16[32,1280]{1,0:T(8,128)(2,1)S(1)}, bf16[32,1280]{1,0:T(8,128)(2,1)S(1)}, u32[]{:S(2)}, u32[]{:S(2)}) collective-permute-start(bf16[32,1280]{1,0:T(8,128)(2,1)S(1)} %collective-permute-done.6.got_1), channel_id=1, source_target_pairs={{0,2},{1,3},{2,0},{3,1},{4,6},{5,7},{6,4},{7,5},{8,10},{9,11},{10,... | collective-permute-start | bytes 245768 | tf_op jit(solution)/shard_map/ppermute | solution.py:327
  15.2 7.2 %collective-permute-start.9 = (s16[32,1280]{1,0:T(8,128)(2,1)S(1)}, s16[32,1280]{1,0:T(8,128)(2,1)S(1)}, u32[]{:S(2)}, u32[]{:S(2)}) collective-permute-start(s16[32,1280]{1,0:T(8,128)(2,1)S(1)} %get-tuple-element.35), channel_id=1, source_target_pairs={{0,24},{1,25},{2,7},{3,6},{4,28},{5,29},{6,3},{7,2},{8,16},{9,17},... | collective-permute-start | bytes 245768 | tf_op jit(solution)/shard_map/ppermute | solution.py:324
  18.1 4.6 %collective-permute-start.10 = (s16[32,1280]{1,0:T(8,128)(2,1)S(1)}, s16[32,1280]{1,0:T(8,128)(2,1)S(1)}, u32[]{:S(2)}, u32[]{:S(2)}) collective-permute-start(s16[32,1280]{1,0:T(8,128)(2,1)S(1)} %get-tuple-element.38), channel_id=1, source_target_pairs={{0,4},{1,5},{2,18},{3,19},{4,0},{5,1},{6,22},{7,23},{8,12},{9,13},... | collective-permute-start | bytes 245768 | tf_op jit(solution)/shard_map/ppermute | solution.py:324
  19.0 4.8 %collective-permute-start.12 = (s16[16,1280]{1,0:T(8,128)(2,1)S(1)}, s16[16,1280]{1,0:T(8,128)(2,1)S(1)}, u32[]{:S(2)}, u32[]{:S(2)}) collective-permute-start(s16[16,1280]{1,0:T(8,128)(2,1)S(1)} %get-tuple-element.40), channel_id=1, source_target_pairs={{0,8},{1,9},{2,3},{3,2},{4,12},{5,13},{6,7},{7,6},{8,0},{9,1},{10,... | collective-permute-start | bytes 122888 | tf_op jit(solution)/shard_map/ppermute | solution.py:324
  19.0 4.8 %collective-permute-start.13 = (s16[16,1280]{1,0:T(8,128)(2,1)S(1)}, s16[16,1280]{1,0:T(8,128)(2,1)S(1)}, u32[]{:S(2)}, u32[]{:S(2)}) collective-permute-start(s16[16,1280]{1,0:T(8,128)(2,1)S(1)} %get-tuple-element.41), channel_id=1, source_target_pairs={{0,10},{1,11},{2,1},{3,0},{4,14},{5,15},{6,5},{7,4},{8,2},{9,3},{1... | collective-permute-start | bytes 122888 | tf_op jit(solution)/shard_map/ppermute | solution.py:324
  22.6 1.3 %collective-permute-start.11 = (s16[16,1280]{1,0:T(8,128)(2,1)S(1)}, s16[16,1280]{1,0:T(8,128)(2,1)S(1)}, u32[]{:S(2)}, u32[]{:S(2)}) collective-permute-start(s16[16,1280]{1,0:T(8,128)(2,1)S(1)} %get-tuple-element.39), channel_id=1, source_target_pairs={{0,2},{1,3},{2,0},{3,1},{4,6},{5,7},{6,4},{7,5},{8,10},{9,11},{10,... | collective-permute-start | bytes 122888 | tf_op jit(solution)/shard_map/ppermute | solution.py:327
  22.7 1.8 %collective-permute-start.14 = (s16[32,1280]{1,0:T(8,128)(2,1)S(1)}, s16[32,1280]{1,0:T(8,128)(2,1)S(1)}, u32[]{:S(2)}, u32[]{:S(2)}) collective-permute-start(s16[32,1280]{1,0:T(8,128)(2,1)S(1)} %collective-permute-done.10.back_ref), channel_id=1, source_target_pairs={{0,2},{1,3},{2,0},{3,1},{4,6},{5,7},{6,4},{7,5},{8,10},{9,11},{10,... | collective-permute-start | bytes 245768 | tf_op jit(solution)/shard_map/ppermute | solution.py:327

commit v18 on v17

--- a/solution.py
+++ b/solution.py
@@ -115,10 +115,9 @@
     low, high = jnp.where(first, own, got), jnp.where(first, got, own)
     images = jnp.concatenate([low[:rows], high[:rows]], axis=0)
     texts = jnp.concatenate([low[rows:], high[rows:]], axis=0)
-    mine = jnp.where(first, images, texts).astype(jnp.bfloat16)
-    other = jnp.where(first, texts, images).astype(jnp.bfloat16)
-    for ref, block in zip(refs, (mine, other, mine, mine, mine, other)):
-        ref[...] = block
+    mine, other = jnp.where(first, images, texts), jnp.where(first, texts, images)
+    for ref, block in zip(refs, (images, texts, mine, mine, mine, other)):
+        ref[...] = block.astype(jnp.bfloat16)
 
 
 def near_kernel(scale_ref, shift_ref, upper_ref, lower_ref, out_ref, pair_ref):
@@ -204,28 +203,35 @@
     return pull, jnp.sum(loss, axis=1, keepdims=True)
 
 
-def tile_kernel(pair_ref, mine_ref, other_ref, got_0, got_1, swapped_0, swapped_1, near_ref, *outs):
+def tile_kernel(pair_ref, mine_ref, other_ref, images, texts, other_images, other_texts, near_ref, *outs):
     rows = mine_ref.shape[0]
+    first = on_first_core()
     scale, shift = pair_ref[0:1, 0:1], pair_ref[1:2, 0:1]
-    lines = jnp.concatenate(
-        [got_0[...], near_ref[:rows, :], mine_ref[...], swapped_1[...]], axis=0
-    )
-    columns = jnp.concatenate(
-        [got_1[...], swapped_0[...], near_ref[rows:, :], other_ref[...]], axis=0
-    )
+
+    def pick(one, two):
+        return jnp.where(first, one, two)
+
+    def parted(image_ref, text_ref):
+        image, text = image_ref[...].astype(jnp.float32), text_ref[...].astype(jnp.float32)
+        return pick(image, text).astype(jnp.bfloat16), pick(text, image).astype(jnp.bfloat16)
+
+    (line, column), (other_line, other_column) = parted(images, texts), parted(other_images, other_texts)
+    lines = jnp.concatenate([line, near_ref[:rows, :], mine_ref[...], other_line], axis=0)
+    columns = jnp.concatenate([column, other_column, near_ref[rows:, :], other_ref[...]], axis=0)
     loss, coef = tile_terms_of(lines, columns, scale, shift)
     pull, loss_sum = pulls_of(loss[: 3 * rows], coef[: 3 * rows], columns)
-    put_rows([outs[0]], pull[:rows], loss_sum[:rows])
-    put_rows([outs[1]], *pulls_of(loss.T[:rows], coef.T[:rows], lines))
-    first = on_first_core()
+    column_pull, column_loss = pulls_of(loss.T[:rows], coef.T[:rows], lines)
+    line_pull, line_loss = pull[:rows], loss_sum[:rows]
+    put_rows([outs[0]], pick(line_pull, column_pull), pick(line_loss, column_loss))
+    put_rows([outs[1]], pick(column_pull, line_pull), pick(column_loss, line_loss))
     half = rows // 2
-    halves = []
-    for part in (pull, loss_sum):
-        low, high = part[rows : rows + half], part[rows + half : 2 * rows]
-        halves.append((jnp.where(first, low, high), jnp.where(first, high, low)))
-    for out, part, part_loss in zip(outs[2:4], *halves):
+    halves = [], []
+    for start in (rows, 2 * rows):
+        for part, listing in zip((pull, loss_sum), halves):
+            low, high = part[start : start + half], part[start + half : start + rows]
+            listing.extend((pick(low, high), pick(high, low)))
+    for out, part, part_loss in zip(outs[2:], *halves):
         put_rows([out], part, part_loss)
-    put_rows([outs[4]], pull[2 * rows :], loss_sum[2 * rows :])
 
 
 def total(parts, rows, depth):
@@ -243,48 +249,40 @@
     return pl.ds(own, rows), pl.ds(pl.multiple_of(rows - own, rows), rows)
 
 
-def add_kernel(own_ref, back_ref, keep_ref, loss_ref, give_ref):
-    rows, depth = keep_ref.shape
-    own, other = place_of(on_first_core(), rows)
-    pull, loss = total([own_ref[other, :], back_ref[other, :]], rows, depth)
-    put_rows([give_ref], pull, loss)
-    keep_ref[...], loss = total([own_ref[own, :], back_ref[own, :]], rows, depth)
-    loss_ref[...] = jnp.broadcast_to(loss, loss_ref.shape)
-
-
-def more_kernel(keep_ref, kept_loss_ref, back_ref, got_ref, same_ref, cross_ref, image_ref, text_ref, *outs):
+def give_kernel(back_ref, give_ref):
+    _, other = place_of(on_first_core(), give_ref.shape[0])
+    give_ref[...] = back_ref[other, :]
+
+
+def more_kernel(own_ref, text_back, got_own, got_text, same_ref, cross_ref, image_ref, text_ref, *outs):
     sum_ref, sum_loss_ref, unit_ref, inverse_ref = outs
-    rows, depth = keep_ref.shape
-    own, _ = place_of(on_first_core(), rows)
-    pull, loss = total([same_ref], rows, depth)
-    sum_ref[0] = keep_ref[...] + pull
-    sum_loss_ref[0] = kept_loss_ref[...] + loss
-    sum_ref[1], loss = total([back_ref[own, :], got_ref, cross_ref], rows, depth)
-    sum_loss_ref[1] = jnp.broadcast_to(loss, sum_loss_ref.shape[1:])
+    first = on_first_core()
+    rows, depth = sum_ref.shape[1:]
+    own, _ = place_of(first, rows)
+    mine = total([own_ref, same_ref], rows, depth)
+    other = total([got_own, cross_ref], rows, depth)
+    texts = total([text_back[own, :], got_text], rows, depth)
+    for side, (one, two, back) in enumerate(((mine, other, None), (other, mine, texts))):
+        pull, loss = (jnp.where(first, x, y) for x, y in zip(one, two))
+        sum_ref[side] = pull if back is None else pull + back[0]
+        loss = loss if back is None else loss + back[1]
+        sum_loss_ref[side] = jnp.broadcast_to(loss, sum_loss_ref.shape[1:])
     for side, ref in enumerate((image_ref, text_ref)):
         unit, inverse = unit_rows(ref[...])
         unit_ref[side] = unit
         inverse_ref[side] = jnp.broadcast_to(inverse, inverse_ref.shape[1:])
 
 
-def final_kernel(pairs, sum_ref, sum_loss_ref, unit_ref, inverse_ref, got_ref, loss_ref, grad_image_ref, grad_text_ref):
-    first = on_first_core()
+def final_kernel(pairs, sum_ref, sum_loss_ref, unit_ref, inverse_ref, back_ref, got_ref, *outs):
+    loss_ref, grad_image_ref, grad_text_ref = outs
     rows, depth = sum_ref.shape[1:]
-    own, _ = place_of(first, rows)
-    pull, loss = total([got_ref[own, :]], rows, depth)
-    pulls = (sum_ref[0] + pull, sum_ref[1])
-    losses = (sum_loss_ref[0][:, 0:1] + loss, sum_loss_ref[1][:, 0:1])
-    for side, (pull, out) in enumerate(
-        (
-            (jnp.where(first, pulls[0], pulls[1]), grad_image_ref),
-            (jnp.where(first, pulls[1], pulls[0]), grad_text_ref),
-        )
-    ):
-        out[...] = project_back(unit_ref[side], inverse_ref[side][:, 0:1], pull)
+    own, _ = place_of(on_first_core(), rows)
+    pull, loss = total([back_ref[own, :], got_ref[own, :]], rows, depth)
+    for side, (side_pull, out) in enumerate(((sum_ref[0] + pull, grad_image_ref), (sum_ref[1], grad_text_ref))):
+        out[...] = project_back(unit_ref[side], inverse_ref[side][:, 0:1], side_pull)
     row = lax.broadcasted_iota(jnp.int32, (rows, rows), 0)
     column = lax.broadcasted_iota(jnp.int32, (rows, rows), 1)
-    loss = jnp.where(first, losses[0], losses[1])
-    across = jnp.where(row == column, loss / pairs, 0.0)
+    across = jnp.where(row == column, (sum_loss_ref[0][:, 0:1] + loss) / pairs, 0.0)
     loss_ref[...] = jnp.sum(across, axis=0, keepdims=True)
 
 
@@ -296,9 +294,10 @@
     vmem = pl.BlockSpec(memory_space=pltpu.VMEM)
     smem = pl.BlockSpec(memory_space=pltpu.SMEM)
 
-    def call(kernel, shapes, operands, name, scalars=0, cost=None):
+    def call(kernel, shapes, operands, name, scalars=0, cost=None, scratch=()):
         return pl.pallas_call(
             kernel,
+            scratch_shapes=scratch,
             cost_estimate=cost,
             out_shape=shapes,
             in_specs=[smem] * scalars + [vmem] * (len(operands) - scalars),
@@ -326,7 +325,7 @@
     def swap(x):
         return lax.ppermute(x, AXES, [(i, i ^ lanes) for i in range(n)])
 
-    visits = (((12, 3), 0), ((2, 8), 0), ((4, 1), 0), ((4, 1), 1))
+    visits = (((12, 8), 0), ((2, 3), 0), ((4, 1), 0), ((4, 1), 1))
     late = pl.CostEstimate(flops=10**9, bytes_accessed=10**7, transcendentals=0)
     digits = call(
         digits_kernel,
@@ -337,7 +336,13 @@
     )
     own = call(pack_kernel, block(2), [image_emb, text_emb, digits], "pack")
     swapped = [swap(x) for x in (image_emb, text_emb, pair_class)]
-    *sent, mine, other, _ = call(join_kernel, (block(2),) * 7, [own, *swapped], "join")
+    *sent, mine, other = call(
+        join_kernel,
+        (block(2),) * 6,
+        [own, *swapped],
+        "join",
+        scratch=[pltpu.VMEM((2 * rows, width), jnp.bfloat16)],
+    )
     got = [visit(x, *way) for x, way in zip(sent, visits)]
     near, pair = call(
         near_kernel,
@@ -350,25 +355,23 @@
     one, two = block(1, jnp.int16), block(2, jnp.int16)
     parts = call(
         tile_kernel,
-        (two, two, one, one, two),
+        (two, two, one, one, one, one),
         [pair, mine, other, *got[:2], swap(got[0]), swap(got[1]), near],
         "tile",
     )
     back = [visit(x, *way) for x, way in zip(parts, visits)]
-    keep, kept_loss, give = call(
-        add_kernel, (wide(rows, depth), wide(rows, LANES), one), [parts[4], back[0]], "add"
-    )
+    give = call(give_kernel, one, [back[1]], "give")
     sums = call(
         more_kernel,
         (wide(2, rows, depth), wide(2, rows, LANES)) * 2,
-        [keep, kept_loss, back[1], swap(give), *back[2:], image_emb, text_emb],
+        [parts[4], back[1], swap(parts[5]), swap(give), *back[2:], image_emb, text_emb],
         "more",
         cost=late,
     )
     loss, grad_image, grad_text = call(
         functools.partial(final_kernel, n * rows),
         (wide(1, rows), wide(rows, depth), wide(rows, depth)),
-        [*sums, swap(back[1])],
+        [*sums, back[0], swap(back[0])],
         "final",
     )
     return (loss[0], grad_image, grad_text)

time: 25.5 us -> 25.5 us (level)
  starting transfers between devices: 15.1 us -> 16 us
  Pallas kernels: 3 us -> 2.28 us
    ppermute x7 -> x8, starting transfers between devices: 2.8 us -> 3.76 us  [swap(): return lax.ppermute(x, AXES, [(i, i ^ lanes) for i in range(n)])]
    pallas_call x8, Pallas kernels: 3 us -> 2.28 us  [call(): pl.pallas_call(kernel, scratch_shapes=scratch, cost_estimate=cost, out_sh...]
    ppermute x8, waiting for transfers between devices: 3.88 us -> 3.41 us  [visit(): return lax.ppermute(x, AXES, pairs)]
    ppermute x7 -> x8, waiting for transfers between devices: 0.68 us -> 0.91 us  [swap(): return lax.ppermute(x, AXES, [(i, i ^ lanes) for i in range(n)])]
  transfers between devices with their start and end apart: 15 -> 16, of which waited for: 6 -> 4; matrix products, arithmetic and copies ran while one was open for 0% -> 0% of each run, Pallas kernels for 2% -> 2%
where the time goes in v18:
time: 25.5 us; the launch traced here: 25.3 us
  starting transfers between devices  16 us (63%)
  waiting for transfers between devices  4.32 us (17%)
  Pallas kernels  2.28 us (9%)
  between operations  2.04 us (8%)
  local copies, waits for them, and re-layouts  0.66 us (3%)
    ppermute x8, starting transfers between devices, visit(): return lax.ppermute(x, AXES, pairs)  12.3 us
    ppermute x8, starting transfers between devices, swap(): return lax.ppermute(x, AXES, [(i, i ^ lanes) for i in range(n)])  3.76 us
    ppermute x8, waiting for transfers between devices, visit(): return lax.ppermute(x, AXES, pairs)  3.41 us
    pallas_call x8, Pallas kernels, call(): pl.pallas_call(kernel, scratch_shapes=scratch, cost_estimate=cost, out_sh...  2.28 us
    ppermute x8, waiting for transfers between devices, swap(): return lax.ppermute(x, AXES, [(i, i ^ lanes) for i in range(n)])  0.91 us
    unnamed x6, local copies, waits for them, and re-layouts  0.66 us
  transfers between devices with their start and end apart: 16, of which 4 were waited for; matrix products, arithmetic and copies ran while one was open for 0% of the time, Pallas kernels for 2%

profile of v18, /device:TPU:0, one launch (start us, length us, event | category | flops | bytes accessed | tf_op | source)
XLA Modules:
  0.0 25.3 jit_solution(2616302660159277613)
XLA Ops:
  0.6 0.0 copy-start
  0.6 0.0 copy-start.1
  0.7 0.5 %collective-permute-start.2 = (s32[16]{0:T(128)}, s32[16]{0:T(128)S(1)}, u32[]{:S(2)}, u32[]{:S(2)}) collective-permute-start(s32[16]{0:T(128)} %class_ref.1), channel_id=1, source_target_pairs={{0,2},{1,3},{2,0},{3,1},{4,6},{5,7},{6,4},{7,5},{8,10},{9,11},{10,... | collective-permute-start | bytes 200 | tf_op jit(solution)/shard_map/ppermute | solution.py:326
  1.2 0.1 collective-permute-start
  1.2 0.4 %collective-permute-start.1 = (bf16[16,1152]{1,0:T(8,128)(2,1)}, bf16[16,1152]{1,0:T(8,128)(2,1)S(1)}, u32[]{:S(2)}, u32[]{:S(2)}) collective-permute-start(bf16[16,1152]{1,0:T(8,128)(2,1)} %text_ref.3), channel_id=1, source_target_pairs={{0,2},{1,3},{2,0},{3,1},{4,6},{5,7},{6,4},{7,5},{8,10},{9,11},{10,... | collective-permute-start | bytes 110600 | tf_op jit(solution)/shard_map/ppermute | solution.py:326
  1.7 0.0 copy-start.2
  1.7 0.7 %copy-done.2 = s32[16]{0:T(128)S(1)} copy-done((s32[16]{0:T(128)S(1)}, s32[16]{0:T(128)}, u32[]{:S(2)}) %copy-start.2) | copy-done | bytes 88
  2.3 0.1 digits.1.digits_ref
  2.4 0.0 copy-done
  2.4 0.0 copy-done.1
  2.4 0.1 pack.1.own_ref
  2.6 0.0 collective-permute-done.2.got_class
  2.6 0.0 collective-permute-done.got_image
  2.6 0.2 collective-permute-done.1.got_text
  2.8 0.2 join.1
  2.9 5.0 %collective-permute-start.5 = (bf16[32,1280]{1,0:T(8,128)(2,1)S(1)}, bf16[32,1280]{1,0:T(8,128)(2,1)S(1)}, u32[]{:S(2)}, u32[]{:S(2)}) collective-permute-start(bf16[32,1280]{1,0:T(8,128)(2,1)S(1)} %get-tuple-element.29), channel_id=1, source_target_pairs={{0,24},{1,25},{2,18},{3,19},{4,28},{5,29},{6,22},{7,23},{8,16},{9,... | collective-permute-start | bytes 245768 | tf_op jit(solution)/shard_map/ppermute | solution.py:323
  7.9 1.5 %collective-permute-start.6 = (bf16[32,1280]{1,0:T(8,128)(2,1)S(1)}, bf16[32,1280]{1,0:T(8,128)(2,1)S(1)}, u32[]{:S(2)}, u32[]{:S(2)}) collective-permute-start(bf16[32,1280]{1,0:T(8,128)(2,1)S(1)} %get-tuple-element.30), channel_id=1, source_target_pairs={{0,4},{1,5},{2,7},{3,6},{4,0},{5,1},{6,3},{7,2},{8,12},{9,13},{10,... | collective-permute-start | bytes 245768 | tf_op jit(solution)/shard_map/ppermute | solution.py:323
  9.4 0.0 collective-permute-start.3
  9.4 0.9 %collective-permute-start.4 = (bf16[32,1280]{1,0:T(8,128)(2,1)S(1)}, bf16[32,1280]{1,0:T(8,128)(2,1)S(1)}, u32[]{:S(2)}, u32[]{:S(2)}) collective-permute-start(bf16[32,1280]{1,0:T(8,128)(2,1)S(1)} %get-tuple-element.25), channel_id=1, source_target_pairs={{0,10},{1,11},{2,1},{3,0},{4,14},{5,15},{6,5},{7,4},{8,2},{9,3},{1... | collective-permute-start | bytes 245768 | tf_op jit(solution)/shard_map/ppermute | solution.py:323
  11.7 0.0 collective-permute-done.5.images
  11.7 0.8 %collective-permute-start.7 = (bf16[32,1280]{1,0:T(8,128)(2,1)S(1)}, bf16[32,1280]{1,0:T(8,128)(2,1)S(1)}, u32[]{:S(2)}, u32[]{:S(2)}) collective-permute-start(bf16[32,1280]{1,0:T(8,128)(2,1)S(1)} %collective-permute-done.5.images), channel_id=1, source_target_pairs={{0,2},{1,3},{2,0},{3,1},{4,6},{5,7},{6,4},{7,5},{8,10},{9,11},{10,... | collective-permute-start | bytes 245768 | tf_op jit(solution)/shard_map/ppermute | solution.py:326
  12.5 0.0 collective-permute-done.6.texts
  12.5 0.1 collective-permute-start.8
  12.5 1.3 %collective-permute-done.3.upper_ref = bf16[32,1280]{1,0:T(8,128)(2,1)S(1)} collective-permute-done((bf16[32,1280]{1,0:T(8,128)(2,1)S(1)}, bf16[32,1280]{1,0:T(8,128)(2,1)S(1)}, u32[]{:S(2)}, u32[]{:S(2)}) %collective-permute-start.3) | collective-permute-done | bytes 81952 | tf_op jit(solution)/shard_map/ppermute | solution.py:323
  13.9 0.0 collective-permute-done.4.lower_ref
  13.9 0.0 collective-permute-done.7.other_images
  13.9 0.0 collective-permute-done.8.other_texts
  13.9 0.8 %tile.1 = (s16[32,1280]{1,0:T(8,128)(2,1)S(1)}, s16[32,1280]{1,0:T(8,128)(2,1)S(1)}, s16[16,1280]{1,0:T(8,128)(2,1)S(1)}, s16[16,1280]{1,0:T(8,128)(2,1)S(1)}, s...) custom-call(f32[8,128]{1,0:T(8,128)S(1)} %get-tuple-element.26.pair_ref, ...), custom_call_target="tpu_custom_call" | custom-call | tf_op jit(solution)/shard_map/tile/pallas_call | solution.py:298
  14.7 1.3 %collective-permute-start.9 = (s16[32,1280]{1,0:T(8,128)(2,1)S(1)}, s16[32,1280]{1,0:T(8,128)(2,1)S(1)}, u32[]{:S(2)}, u32[]{:S(2)}) collective-permute-start(s16[32,1280]{1,0:T(8,128)(2,1)S(1)} %get-tuple-element.33), channel_id=1, source_target_pairs={{0,4},{1,5},{2,7},{3,6},{4,0},{5,1},{6,3},{7,2},{8,12},{9,13},{10,... | collective-permute-start | bytes 245768 | tf_op jit(solution)/shard_map/ppermute | solution.py:323
  16.0 2.4 %collective-permute-start.14 = (s16[32,1280]{1,0:T(8,128)(2,1)S(1)}, s16[32,1280]{1,0:T(8,128)(2,1)S(1)}, u32[]{:S(2)}, u32[]{:S(2)}) collective-permute-start(s16[32,1280]{1,0:T(8,128)(2,1)S(1)} %get-tuple-element.41), channel_id=1, source_target_pairs={{0,24},{1,25},{2,18},{3,19},{4,28},{5,29},{6,22},{7,23},{8,16},{9,... | collective-permute-start | bytes 245768 | tf_op jit(solution)/shard_map/ppermute | solution.py:323
  18.4 0.0 collective-permute-start.10
  18.4 1.1 %collective-permute-start.12 = (s16[16,1280]{1,0:T(8,128)(2,1)S(1)}, s16[16,1280]{1,0:T(8,128)(2,1)S(1)}, u32[]{:S(2)}, u32[]{:S(2)}) collective-permute-start(s16[16,1280]{1,0:T(8,128)(2,1)S(1)} %get-tuple-element.35), channel_id=1, source_target_pairs={{0,8},{1,9},{2,3},{3,2},{4,12},{5,13},{6,7},{7,6},{8,0},{9,1},{10,... | collective-permute-start | bytes 122888 | tf_op jit(solution)/shard_map/ppermute | solution.py:323
  19.5 0.0 collective-permute-start.13
  19.5 0.0 collective-permute-done.9.back_ref.text_back
  19.5 0.7 %collective-permute-start.11 = (s16[16,1280]{1,0:T(8,128)(2,1)S(1)}, s16[16,1280]{1,0:T(8,128)(2,1)S(1)}, u32[]{:S(2)}, u32[]{:S(2)}) collective-permute-start(s16[16,1280]{1,0:T(8,128)(2,1)S(1)} %give.1), channel_id=1, source_target_pairs={{0,2},{1,3},{2,0},{3,1},{4,6},{5,7},{6,4},{7,5},{8,10},{9,11},{10,... | collective-permute-start | bytes 122888 | tf_op jit(solution)/shard_map/ppermute | solution.py:326
  20.2 2.1 %collective-permute-done.14.back_ref = s16[32,1280]{1,0:T(8,128)(2,1)S(1)} collective-permute-done((s16[32,1280]{1,0:T(8,128)(2,1)S(1)}, s16[32,1280]{1,0:T(8,128)(2,1)S(1)}, u32[]{:S(2)}, u32[]{:S(2)}) %collective-permute-start.14) | collective-permute-done | bytes 81952 | tf_op jit(solution)/shard_map/ppermute | solution.py:323
  22.3 1.2 %collective-permute-start.15 = (s16[32,1280]{1,0:T(8,128)(2,1)S(1)}, s16[32,1280]{1,0:T(8,128)(2,1)S(1)}, u32[]{:S(2)}, u32[]{:S(2)}) collective-permute-start(s16[32,1280]{1,0:T(8,128)(2,1)S(1)} %collective-permute-done.14.back_ref), channel_id=1, source_target_pairs={{0,2},{1,3},{2,0},{3,1},{4,6},{5,7},{6,4},{7,5},{8,10},{9,11},{10,... | collective-permute-start | bytes 245768 | tf_op jit(solution)/shard_map/ppermute | solution.py:326
  23.5 0.0 collective-permute-done.10.got_own
  23.5 0.0 collective-permute-done.12.same_ref
  23.5 0.0 collective-permute-done.13.cross_ref
  23.5 0.0 collective-permute-done.11.got_text
  23.5 0.2 more.1
  23.7 0.7 %collective-permute-done.15.got_ref = s16[32,1280]{1,0:T(8,128)(2,1)S(1)} collective-permute-done((s16[32,1280]{1,0:T(8,128)(2,1)S(1)}, s16[32,1280]{1,0:T(8,128)(2,1)S(1)}, u32[]{:S(2)}, u32[]{:S(2)}) %collective-permute-start.15) | collective-permute-done | bytes 81952 | tf_op jit(solution)/shard_map/ppermute | solution.py:326
  24.4 0.9 %final.1 = (f32[1,16]{1,0:T(1,128)}, f32[16,1152]{1,0:T(8,128)}, f32[16,1152]{1,0:T(8,128)}) custom-call(f32[2,16,1152]{2,1,0:T(8,128)S(1)} %get-tuple-element.37.sum_ref, f32[2,16,128]{2,1,0:T(8,128)S(1)} %get-tuple-element.38.sum_loss_ref, f32[2,16,1152]{2,1,0:T(8,128)S(1)} %get-tuple-element.39.unit_ref, f32[2,16,128]{2,1,0:T(8,128)S(1)} %get-tuple-element.40.inverse_ref, ...), custom_call_target="tpu_custom_call" | custom-call | tf_op jit(solution)/shard_map/final/pallas_call | solution.py:298
  (2 shorter events, 0.0 us)
Async XLA Ops:
  0.6 1.8 %copy-start = (bf16[16,1152]{1,0:T(8,128)(2,1)S(1)}, bf16[16,1152]{1,0:T(8,128)(2,1)}, u32[]{:S(2)}) copy-start(bf16[16,1152]{1,0:T(8,128)(2,1)} %image_ref.3) | copy-start | bytes 110596
  0.6 1.8 %copy-start.1 = (bf16[16,1152]{1,0:T(8,128)(2,1)S(1)}, bf16[16,1152]{1,0:T(8,128)(2,1)}, u32[]{:S(2)}) copy-start(bf16[16,1152]{1,0:T(8,128)(2,1)} %text_ref.3) | copy-start | bytes 110596
  0.7 1.9 %collective-permute-start.2 = (s32[16]{0:T(128)}, s32[16]{0:T(128)S(1)}, u32[]{:S(2)}, u32[]{:S(2)}) collective-permute-start(s32[16]{0:T(128)} %class_ref.1), channel_id=1, source_target_pairs={{0,2},{1,3},{2,0},{3,1},{4,6},{5,7},{6,4},{7,5},{8,10},{9,11},{10,... | collective-permute-start | bytes 200 | tf_op jit(solution)/shard_map/ppermute | solution.py:326
  1.2 1.4 %collective-permute-start = (bf16[16,1152]{1,0:T(8,128)(2,1)}, bf16[16,1152]{1,0:T(8,128)(2,1)S(1)}, u32[]{:S(2)}, u32[]{:S(2)}) collective-permute-start(bf16[16,1152]{1,0:T(8,128)(2,1)} %image_ref.3), channel_id=1, source_target_pairs={{0,2},{1,3},{2,0},{3,1},{4,6},{5,7},{6,4},{7,5},{8,10},{9,11},{10,... | collective-permute-start | bytes 110600 | tf_op jit(solution)/shard_map/ppermute | solution.py:326
  1.2 1.5 %collective-permute-start.1 = (bf16[16,1152]{1,0:T(8,128)(2,1)}, bf16[16,1152]{1,0:T(8,128)(2,1)S(1)}, u32[]{:S(2)}, u32[]{:S(2)}) collective-permute-start(bf16[16,1152]{1,0:T(8,128)(2,1)} %text_ref.3), channel_id=1, source_target_pairs={{0,2},{1,3},{2,0},{3,1},{4,6},{5,7},{6,4},{7,5},{8,10},{9,11},{10,... | collective-permute-start | bytes 110600 | tf_op jit(solution)/shard_map/ppermute | solution.py:326
  1.7 0.7 %copy-start.2 = (s32[16]{0:T(128)S(1)}, s32[16]{0:T(128)}, u32[]{:S(2)}) copy-start(s32[16]{0:T(128)} %class_ref.1) | copy-start | bytes 196
  2.9 8.8 %collective-permute-start.5 = (bf16[32,1280]{1,0:T(8,128)(2,1)S(1)}, bf16[32,1280]{1,0:T(8,128)(2,1)S(1)}, u32[]{:S(2)}, u32[]{:S(2)}) collective-permute-start(bf16[32,1280]{1,0:T(8,128)(2,1)S(1)} %get-tuple-element.29), channel_id=1, source_target_pairs={{0,24},{1,25},{2,18},{3,19},{4,28},{5,29},{6,22},{7,23},{8,16},{9,... | collective-permute-start | bytes 245768 | tf_op jit(solution)/shard_map/ppermute | solution.py:323
  7.9 4.5 %collective-permute-start.6 = (bf16[32,1280]{1,0:T(8,128)(2,1)S(1)}, bf16[32,1280]{1,0:T(8,128)(2,1)S(1)}, u32[]{:S(2)}, u32[]{:S(2)}) collective-permute-start(bf16[32,1280]{1,0:T(8,128)(2,1)S(1)} %get-tuple-element.30), channel_id=1, source_target_pairs={{0,4},{1,5},{2,7},{3,6},{4,0},{5,1},{6,3},{7,2},{8,12},{9,13},{10,... | collective-permute-start | bytes 245768 | tf_op jit(solution)/shard_map/ppermute | solution.py:323
  9.4 4.4 %collective-permute-start.3 = (bf16[32,1280]{1,0:T(8,128)(2,1)S(1)}, bf16[32,1280]{1,0:T(8,128)(2,1)S(1)}, u32[]{:S(2)}, u32[]{:S(2)}) collective-permute-start(bf16[32,1280]{1,0:T(8,128)(2,1)S(1)} %get-tuple-element.24), channel_id=1, source_target_pairs={{0,8},{1,9},{2,3},{3,2},{4,12},{5,13},{6,7},{7,6},{8,0},{9,1},{10,... | collective-permute-start | bytes 245768 | tf_op jit(solution)/shard_map/ppermute | solution.py:323
  9.4 4.4 %collective-permute-start.4 = (bf16[32,1280]{1,0:T(8,128)(2,1)S(1)}, bf16[32,1280]{1,0:T(8,128)(2,1)S(1)}, u32[]{:S(2)}, u32[]{:S(2)}) collective-permute-start(bf16[32,1280]{1,0:T(8,128)(2,1)S(1)} %get-tuple-element.25), channel_id=1, source_target_pairs={{0,10},{1,11},{2,1},{3,0},{4,14},{5,15},{6,5},{7,4},{8,2},{9,3},{1... | collective-permute-start | bytes 245768 | tf_op jit(solution)/shard_map/ppermute | solution.py:323
  11.7 2.2 %collective-permute-start.7 = (bf16[32,1280]{1,0:T(8,128)(2,1)S(1)}, bf16[32,1280]{1,0:T(8,128)(2,1)S(1)}, u32[]{:S(2)}, u32[]{:S(2)}) collective-permute-start(bf16[32,1280]{1,0:T(8,128)(2,1)S(1)} %collective-permute-done.5.images), channel_id=1, source_target_pairs={{0,2},{1,3},{2,0},{3,1},{4,6},{5,7},{6,4},{7,5},{8,10},{9,11},{10,... | collective-permute-start | bytes 245768 | tf_op jit(solution)/shard_map/ppermute | solution.py:326
  12.5 1.5 %collective-permute-start.8 = (bf16[32,1280]{1,0:T(8,128)(2,1)S(1)}, bf16[32,1280]{1,0:T(8,128)(2,1)S(1)}, u32[]{:S(2)}, u32[]{:S(2)}) collective-permute-start(bf16[32,1280]{1,0:T(8,128)(2,1)S(1)} %collective-permute-done.6.texts), channel_id=1, source_target_pairs={{0,2},{1,3},{2,0},{3,1},{4,6},{5,7},{6,4},{7,5},{8,10},{9,11},{10,... | collective-permute-start | bytes 245768 | tf_op jit(solution)/shard_map/ppermute | solution.py:326
  14.7 4.8 %collective-permute-start.9 = (s16[32,1280]{1,0:T(8,128)(2,1)S(1)}, s16[32,1280]{1,0:T(8,128)(2,1)S(1)}, u32[]{:S(2)}, u32[]{:S(2)}) collective-permute-start(s16[32,1280]{1,0:T(8,128)(2,1)S(1)} %get-tuple-element.33), channel_id=1, source_target_pairs={{0,4},{1,5},{2,7},{3,6},{4,0},{5,1},{6,3},{7,2},{8,12},{9,13},{10,... | collective-permute-start | bytes 245768 | tf_op jit(solution)/shard_map/ppermute | solution.py:323
  16.0 6.3 %collective-permute-start.14 = (s16[32,1280]{1,0:T(8,128)(2,1)S(1)}, s16[32,1280]{1,0:T(8,128)(2,1)S(1)}, u32[]{:S(2)}, u32[]{:S(2)}) collective-permute-start(s16[32,1280]{1,0:T(8,128)(2,1)S(1)} %get-tuple-element.41), channel_id=1, source_target_pairs={{0,24},{1,25},{2,18},{3,19},{4,28},{5,29},{6,22},{7,23},{8,16},{9,... | collective-permute-start | bytes 245768 | tf_op jit(solution)/shard_map/ppermute | solution.py:323
  18.4 5.1 %collective-permute-start.10 = (s16[16,1280]{1,0:T(8,128)(2,1)S(1)}, s16[16,1280]{1,0:T(8,128)(2,1)S(1)}, u32[]{:S(2)}, u32[]{:S(2)}) collective-permute-start(s16[16,1280]{1,0:T(8,128)(2,1)S(1)} %get-tuple-element.34), channel_id=1, source_target_pairs={{0,2},{1,3},{2,0},{3,1},{4,6},{5,7},{6,4},{7,5},{8,10},{9,11},{10,... | collective-permute-start | bytes 122888 | tf_op jit(solution)/shard_map/ppermute | solution.py:326
  18.4 5.1 %collective-permute-start.12 = (s16[16,1280]{1,0:T(8,128)(2,1)S(1)}, s16[16,1280]{1,0:T(8,128)(2,1)S(1)}, u32[]{:S(2)}, u32[]{:S(2)}) collective-permute-start(s16[16,1280]{1,0:T(8,128)(2,1)S(1)} %get-tuple-element.35), channel_id=1, source_target_pairs={{0,8},{1,9},{2,3},{3,2},{4,12},{5,13},{6,7},{7,6},{8,0},{9,1},{10,... | collective-permute-start | bytes 122888 | tf_op jit(solution)/shard_map/ppermute | solution.py:323
  19.5 4.0 %collective-permute-start.13 = (s16[16,1280]{1,0:T(8,128)(2,1)S(1)}, s16[16,1280]{1,0:T(8,128)(2,1)S(1)}, u32[]{:S(2)}, u32[]{:S(2)}) collective-permute-start(s16[16,1280]{1,0:T(8,128)(2,1)S(1)} %get-tuple-element.36), channel_id=1, source_target_pairs={{0,10},{1,11},{2,1},{3,0},{4,14},{5,15},{6,5},{7,4},{8,2},{9,3},{1... | collective-permute-start | bytes 122888 | tf_op jit(solution)/shard_map/ppermute | solution.py:323
  19.5 4.0 %collective-permute-start.11 = (s16[16,1280]{1,0:T(8,128)(2,1)S(1)}, s16[16,1280]{1,0:T(8,128)(2,1)S(1)}, u32[]{:S(2)}, u32[]{:S(2)}) collective-permute-start(s16[16,1280]{1,0:T(8,128)(2,1)S(1)} %give.1), channel_id=1, source_target_pairs={{0,2},{1,3},{2,0},{3,1},{4,6},{5,7},{6,4},{7,5},{8,10},{9,11},{10,... | collective-permute-start | bytes 122888 | tf_op jit(solution)/shard_map/ppermute | solution.py:326
  22.3 2.1 %collective-permute-start.15 = (s16[32,1280]{1,0:T(8,128)(2,1)S(1)}, s16[32,1280]{1,0:T(8,128)(2,1)S(1)}, u32[]{:S(2)}, u32[]{:S(2)}) collective-permute-start(s16[32,1280]{1,0:T(8,128)(2,1)S(1)} %collective-permute-done.14.back_ref), channel_id=1, source_target_pairs={{0,2},{1,3},{2,0},{3,1},{4,6},{5,7},{6,4},{7,5},{8,10},{9,11},{10,... | collective-permute-start | bytes 245768 | tf_op jit(solution)/shard_map/ppermute | solution.py:326

commit v19 on v17

--- a/solution.py
+++ b/solution.py
@@ -115,10 +115,9 @@
     low, high = jnp.where(first, own, got), jnp.where(first, got, own)
     images = jnp.concatenate([low[:rows], high[:rows]], axis=0)
     texts = jnp.concatenate([low[rows:], high[rows:]], axis=0)
-    mine = jnp.where(first, images, texts).astype(jnp.bfloat16)
-    other = jnp.where(first, texts, images).astype(jnp.bfloat16)
-    for ref, block in zip(refs, (mine, other, mine, mine, mine, other)):
-        ref[...] = block
+    mine, other = jnp.where(first, images, texts), jnp.where(first, texts, images)
+    for ref, block in zip(refs, (images, texts, mine, mine, mine, other)):
+        ref[...] = block.astype(jnp.bfloat16)
 
 
 def near_kernel(scale_ref, shift_ref, upper_ref, lower_ref, out_ref, pair_ref):
@@ -204,25 +203,30 @@
     return pull, jnp.sum(loss, axis=1, keepdims=True)
 
 
-def tile_kernel(pair_ref, mine_ref, other_ref, got_0, got_1, swapped_0, swapped_1, near_ref, *outs):
+def tile_kernel(pair_ref, mine_ref, other_ref, images, texts, other_images, other_texts, near_ref, *outs):
     rows = mine_ref.shape[0]
+    first = on_first_core()
     scale, shift = pair_ref[0:1, 0:1], pair_ref[1:2, 0:1]
-    lines = jnp.concatenate(
-        [got_0[...], near_ref[:rows, :], mine_ref[...], swapped_1[...]], axis=0
-    )
-    columns = jnp.concatenate(
-        [got_1[...], swapped_0[...], near_ref[rows:, :], other_ref[...]], axis=0
-    )
+
+    def pick(one, two):
+        return jnp.where(first, one, two)
+
+    def parted(image_ref, text_ref):
+        image, text = image_ref[...].astype(jnp.float32), text_ref[...].astype(jnp.float32)
+        return pick(image, text).astype(jnp.bfloat16), pick(text, image).astype(jnp.bfloat16)
+
+    (line, column), (other_line, other_column) = parted(images, texts), parted(other_images, other_texts)
+    lines = jnp.concatenate([line, near_ref[:rows, :], mine_ref[...], other_line], axis=0)
+    columns = jnp.concatenate([column, other_column, near_ref[rows:, :], other_ref[...]], axis=0)
     loss, coef = tile_terms_of(lines, columns, scale, shift)
     pull, loss_sum = pulls_of(loss[: 3 * rows], coef[: 3 * rows], columns)
     put_rows([outs[0]], pull[:rows], loss_sum[:rows])
     put_rows([outs[1]], *pulls_of(loss.T[:rows], coef.T[:rows], lines))
-    first = on_first_core()
     half = rows // 2
     halves = []
     for part in (pull, loss_sum):
         low, high = part[rows : rows + half], part[rows + half : 2 * rows]
-        halves.append((jnp.where(first, low, high), jnp.where(first, high, low)))
+        halves.append((pick(low, high), pick(high, low)))
     for out, part, part_loss in zip(outs[2:4], *halves):
         put_rows([out], part, part_loss)
     put_rows([outs[4]], pull[2 * rows :], loss_sum[2 * rows :])
@@ -296,9 +300,10 @@
     vmem = pl.BlockSpec(memory_space=pltpu.VMEM)
     smem = pl.BlockSpec(memory_space=pltpu.SMEM)
 
-    def call(kernel, shapes, operands, name, scalars=0, cost=None):
+    def call(kernel, shapes, operands, name, scalars=0, cost=None, scratch=()):
         return pl.pallas_call(
             kernel,
+            scratch_shapes=scratch,
             cost_estimate=cost,
             out_shape=shapes,
             in_specs=[smem] * scalars + [vmem] * (len(operands) - scalars),
@@ -326,7 +331,8 @@
     def swap(x):
         return lax.ppermute(x, AXES, [(i, i ^ lanes) for i in range(n)])
 
-    visits = (((12, 3), 0), ((2, 8), 0), ((4, 1), 0), ((4, 1), 1))
+    out_visits = (((12, 8), 0), ((2, 3), 0), ((4, 1), 0), ((4, 1), 1))
+    back_visits = (((12, 3), 0), ((2, 8), 0), ((4, 1), 0), ((4, 1), 1))
     late = pl.CostEstimate(flops=10**9, bytes_accessed=10**7, transcendentals=0)
     digits = call(
         digits_kernel,
@@ -337,8 +343,14 @@
     )
     own = call(pack_kernel, block(2), [image_emb, text_emb, digits], "pack")
     swapped = [swap(x) for x in (image_emb, text_emb, pair_class)]
-    *sent, mine, other, _ = call(join_kernel, (block(2),) * 7, [own, *swapped], "join")
-    got = [visit(x, *way) for x, way in zip(sent, visits)]
+    *sent, mine, other = call(
+        join_kernel,
+        (block(2),) * 6,
+        [own, *swapped],
+        "join",
+        scratch=[pltpu.VMEM((2 * rows, width), jnp.bfloat16)],
+    )
+    got = [visit(x, *way) for x, way in zip(sent, out_visits)]
     near, pair = call(
         near_kernel,
         (block(4), wide(8, LANES)),
@@ -354,7 +366,7 @@
         [pair, mine, other, *got[:2], swap(got[0]), swap(got[1]), near],
         "tile",
     )
-    back = [visit(x, *way) for x, way in zip(parts, visits)]
+    back = [visit(x, *way) for x, way in zip(parts, back_visits)]
     keep, kept_loss, give = call(
         add_kernel, (wide(rows, depth), wide(rows, LANES), one), [parts[4], back[0]], "add"
     )

time: 25.5 us -> 25 us (0.980)
  Pallas kernels: 3 us -> 2.43 us
  waiting for transfers between devices: 4.56 us -> 4.87 us
  starting transfers between devices: 15.1 us -> 14.8 us
    pallas_call x8, Pallas kernels: 3 us -> 2.43 us  [call(): pl.pallas_call(kernel, scratch_shapes=scratch, cost_estimate=cost, out_sh...]
where the time goes in v19:
time: 25 us; the launch traced here: 24.9 us
  starting transfers between devices  14.8 us (59%)
  waiting for transfers between devices  4.87 us (19%)
  Pallas kernels  2.43 us (10%)
  between operations  2.05 us (8%)
  local copies, waits for them, and re-layouts  0.66 us (3%)
    ppermute x8, starting transfers between devices, visit(): return lax.ppermute(x, AXES, pairs)  12.1 us
    ppermute x8, waiting for transfers between devices, visit(): return lax.ppermute(x, AXES, pairs)  4.13 us
    ppermute x7, starting transfers between devices, swap(): return lax.ppermute(x, AXES, [(i, i ^ lanes) for i in range(n)])  2.79 us
    pallas_call x8, Pallas kernels, call(): pl.pallas_call(kernel, scratch_shapes=scratch, cost_estimate=cost, out_sh...  2.43 us
    ppermute x7, waiting for transfers between devices, swap(): return lax.ppermute(x, AXES, [(i, i ^ lanes) for i in range(n)])  0.74 us
    unnamed x6, local copies, waits for them, and re-layouts  0.66 us
  transfers between devices with their start and end apart: 15, of which 6 were waited for; matrix products, arithmetic and copies ran while one was open for 0% of the time, Pallas kernels for 2%

profile of v19, /device:TPU:0, one launch (start us, length us, event | category | flops | bytes accessed | tf_op | source)
XLA Modules:
  0.0 24.9 jit_solution(12966700104895747147)
XLA Ops:
  0.6 0.0 copy-start
  0.6 0.0 copy-start.1
  0.7 0.5 %collective-permute-start.2 = (s32[16]{0:T(128)}, s32[16]{0:T(128)S(1)}, u32[]{:S(2)}, u32[]{:S(2)}) collective-permute-start(s32[16]{0:T(128)} %class_ref.1), channel_id=1, source_target_pairs={{0,2},{1,3},{2,0},{3,1},{4,6},{5,7},{6,4},{7,5},{8,10},{9,11},{10,... | collective-permute-start | bytes 200 | tf_op jit(solution)/shard_map/ppermute | solution.py:332
  1.2 0.1 collective-permute-start
  1.2 0.4 %collective-permute-start.1 = (bf16[16,1152]{1,0:T(8,128)(2,1)}, bf16[16,1152]{1,0:T(8,128)(2,1)S(1)}, u32[]{:S(2)}, u32[]{:S(2)}) collective-permute-start(bf16[16,1152]{1,0:T(8,128)(2,1)} %text_ref.3), channel_id=1, source_target_pairs={{0,2},{1,3},{2,0},{3,1},{4,6},{5,7},{6,4},{7,5},{8,10},{9,11},{10,... | collective-permute-start | bytes 110600 | tf_op jit(solution)/shard_map/ppermute | solution.py:332
  1.7 0.0 copy-start.2
  1.7 0.7 %copy-done.2 = s32[16]{0:T(128)S(1)} copy-done((s32[16]{0:T(128)S(1)}, s32[16]{0:T(128)}, u32[]{:S(2)}) %copy-start.2) | copy-done | bytes 88
  2.3 0.1 digits.1.digits_ref
  2.4 0.0 copy-done
  2.4 0.0 copy-done.1
  2.4 0.1 pack.1.own_ref
  2.6 0.0 collective-permute-done.2.got_class
  2.6 0.0 collective-permute-done.got_image
  2.6 0.2 collective-permute-done.1.got_text
  2.8 0.2 join.1
  2.9 5.0 %collective-permute-start.5 = (bf16[32,1280]{1,0:T(8,128)(2,1)S(1)}, bf16[32,1280]{1,0:T(8,128)(2,1)S(1)}, u32[]{:S(2)}, u32[]{:S(2)}) collective-permute-start(bf16[32,1280]{1,0:T(8,128)(2,1)S(1)} %get-tuple-element.31), channel_id=1, source_target_pairs={{0,24},{1,25},{2,18},{3,19},{4,28},{5,29},{6,22},{7,23},{8,16},{9,... | collective-permute-start | bytes 245768 | tf_op jit(solution)/shard_map/ppermute | solution.py:329
  7.9 1.5 %collective-permute-start.6 = (bf16[32,1280]{1,0:T(8,128)(2,1)S(1)}, bf16[32,1280]{1,0:T(8,128)(2,1)S(1)}, u32[]{:S(2)}, u32[]{:S(2)}) collective-permute-start(bf16[32,1280]{1,0:T(8,128)(2,1)S(1)} %get-tuple-element.32), channel_id=1, source_target_pairs={{0,4},{1,5},{2,7},{3,6},{4,0},{5,1},{6,3},{7,2},{8,12},{9,13},{10,... | collective-permute-start | bytes 245768 | tf_op jit(solution)/shard_map/ppermute | solution.py:329
  9.4 0.0 collective-permute-start.3
  9.4 0.9 %collective-permute-start.4 = (bf16[32,1280]{1,0:T(8,128)(2,1)S(1)}, bf16[32,1280]{1,0:T(8,128)(2,1)S(1)}, u32[]{:S(2)}, u32[]{:S(2)}) collective-permute-start(bf16[32,1280]{1,0:T(8,128)(2,1)S(1)} %get-tuple-element.27), channel_id=1, source_target_pairs={{0,10},{1,11},{2,1},{3,0},{4,14},{5,15},{6,5},{7,4},{8,2},{9,3},{1... | collective-permute-start | bytes 245768 | tf_op jit(solution)/shard_map/ppermute | solution.py:329
  11.7 0.0 collective-permute-done.5.images
  11.7 0.8 %collective-permute-start.7 = (bf16[32,1280]{1,0:T(8,128)(2,1)S(1)}, bf16[32,1280]{1,0:T(8,128)(2,1)S(1)}, u32[]{:S(2)}, u32[]{:S(2)}) collective-permute-start(bf16[32,1280]{1,0:T(8,128)(2,1)S(1)} %collective-permute-done.5.images), channel_id=1, source_target_pairs={{0,2},{1,3},{2,0},{3,1},{4,6},{5,7},{6,4},{7,5},{8,10},{9,11},{10,... | collective-permute-start | bytes 245768 | tf_op jit(solution)/shard_map/ppermute | solution.py:332
  12.5 0.0 collective-permute-done.6.texts
  12.5 0.1 collective-permute-start.8
  12.5 1.3 %collective-permute-done.3.upper_ref = bf16[32,1280]{1,0:T(8,128)(2,1)S(1)} collective-permute-done((bf16[32,1280]{1,0:T(8,128)(2,1)S(1)}, bf16[32,1280]{1,0:T(8,128)(2,1)S(1)}, u32[]{:S(2)}, u32[]{:S(2)}) %collective-permute-start.3) | collective-permute-done | bytes 81952 | tf_op jit(solution)/shard_map/ppermute | solution.py:329
  13.9 0.0 collective-permute-done.4.lower_ref
  13.9 0.0 collective-permute-done.7.other_images
  13.9 0.0 collective-permute-done.8.other_texts
  13.9 0.8 %tile.1 = (s16[32,1280]{1,0:T(8,128)(2,1)S(1)}, s16[32,1280]{1,0:T(8,128)(2,1)S(1)}, s16[16,1280]{1,0:T(8,128)(2,1)S(1)}, s16[16,1280]{1,0:T(8,128)(2,1)S(1)}, s16[32,1280]{1,0:T(8,128)(2,1)S(1)}) custom-call(f32[8,128]{1,0:T(8,128)S(1)} %get-tuple-element.28.pair_ref, bf16[32,1280]{1,0:T(8,128)(2,1)S(1)} %get-tuple-element.29.mine_ref, ...), custom_call_target="tpu_custom_call" | custom-call | tf_op jit(solution)/shard_map/tile/pallas_call | solution.py:304
  14.7 2.2 %collective-permute-start.9 = (s16[32,1280]{1,0:T(8,128)(2,1)S(1)}, s16[32,1280]{1,0:T(8,128)(2,1)S(1)}, u32[]{:S(2)}, u32[]{:S(2)}) collective-permute-start(s16[32,1280]{1,0:T(8,128)(2,1)S(1)} %get-tuple-element.35), channel_id=1, source_target_pairs={{0,24},{1,25},{2,7},{3,6},{4,28},{5,29},{6,3},{7,2},{8,16},{9,17},... | collective-permute-start | bytes 245768 | tf_op jit(solution)/shard_map/ppermute | solution.py:329
  16.8 1.5 %collective-permute-start.10 = (s16[32,1280]{1,0:T(8,128)(2,1)S(1)}, s16[32,1280]{1,0:T(8,128)(2,1)S(1)}, u32[]{:S(2)}, u32[]{:S(2)}) collective-permute-start(s16[32,1280]{1,0:T(8,128)(2,1)S(1)} %get-tuple-element.38), channel_id=1, source_target_pairs={{0,4},{1,5},{2,18},{3,19},{4,0},{5,1},{6,22},{7,23},{8,12},{9,13},... | collective-permute-start | bytes 245768 | tf_op jit(solution)/shard_map/ppermute | solution.py:329
  18.3 0.0 collective-permute-start.12
  18.3 0.9 %collective-permute-start.13 = (s16[16,1280]{1,0:T(8,128)(2,1)S(1)}, s16[16,1280]{1,0:T(8,128)(2,1)S(1)}, u32[]{:S(2)}, u32[]{:S(2)}) collective-permute-start(s16[16,1280]{1,0:T(8,128)(2,1)S(1)} %get-tuple-element.41), channel_id=1, source_target_pairs={{0,10},{1,11},{2,1},{3,0},{4,14},{5,15},{6,5},{7,4},{8,2},{9,3},{1... | collective-permute-start | bytes 122888 | tf_op jit(solution)/shard_map/ppermute | solution.py:329
  19.3 2.6 %collective-permute-done.9.back_ref = s16[32,1280]{1,0:T(8,128)(2,1)S(1)} collective-permute-done((s16[32,1280]{1,0:T(8,128)(2,1)S(1)}, s16[32,1280]{1,0:T(8,128)(2,1)S(1)}, u32[]{:S(2)}, u32[]{:S(2)}) %collective-permute-start.9) | collective-permute-done | bytes 81952 | tf_op jit(solution)/shard_map/ppermute | solution.py:329
  21.9 0.2 add.1
  22.1 0.1 collective-permute-start.11
  22.2 0.0 collective-permute-done.10.back_ref
  22.2 0.9 %collective-permute-start.14 = (s16[32,1280]{1,0:T(8,128)(2,1)S(1)}, s16[32,1280]{1,0:T(8,128)(2,1)S(1)}, u32[]{:S(2)}, u32[]{:S(2)}) collective-permute-start(s16[32,1280]{1,0:T(8,128)(2,1)S(1)} %collective-permute-done.10.back_ref), channel_id=1, source_target_pairs={{0,2},{1,3},{2,0},{3,1},{4,6},{5,7},{6,4},{7,5},{8,10},{9,11},{10,... | collective-permute-start | bytes 245768 | tf_op jit(solution)/shard_map/ppermute | solution.py:332
  23.0 0.2 collective-permute-done.12.same_ref
  23.2 0.0 collective-permute-done.13.cross_ref
  23.2 0.1 collective-permute-done.11.got_ref
  23.4 0.2 more.1
  23.5 0.4 %collective-permute-done.14.got_ref = s16[32,1280]{1,0:T(8,128)(2,1)S(1)} collective-permute-done((s16[32,1280]{1,0:T(8,128)(2,1)S(1)}, s16[32,1280]{1,0:T(8,128)(2,1)S(1)}, u32[]{:S(2)}, u32[]{:S(2)}) %collective-permute-start.14) | collective-permute-done | bytes 81952 | tf_op jit(solution)/shard_map/ppermute | solution.py:332
  23.9 0.9 %final.1 = (f32[1,16]{1,0:T(1,128)}, f32[16,1152]{1,0:T(8,128)}, f32[16,1152]{1,0:T(8,128)}) custom-call(f32[2,16,1152]{2,1,0:T(8,128)S(1)} %get-tuple-element.42.sum_ref, f32[2,16,128]{2,1,0:T(8,128)S(1)} %get-tuple-element.43.sum_loss_ref, f32[2,16,1152]{2,1,0:T(8,128)S(1)} %get-tuple-element.44.unit_ref, f32[2,16,128]{2,1,0:T(8,128)S(1)} %get-tuple-element.45.inverse_ref, ...), custom_call_target="tpu_custom_call" | custom-call | tf_op jit(solution)/shard_map/final/pallas_call | solution.py:304
  (1 shorter events, 0.0 us)
Async XLA Ops:
  0.6 1.8 %copy-start = (bf16[16,1152]{1,0:T(8,128)(2,1)S(1)}, bf16[16,1152]{1,0:T(8,128)(2,1)}, u32[]{:S(2)}) copy-start(bf16[16,1152]{1,0:T(8,128)(2,1)} %image_ref.3) | copy-start | bytes 110596
  0.6 1.8 %copy-start.1 = (bf16[16,1152]{1,0:T(8,128)(2,1)S(1)}, bf16[16,1152]{1,0:T(8,128)(2,1)}, u32[]{:S(2)}) copy-start(bf16[16,1152]{1,0:T(8,128)(2,1)} %text_ref.3) | copy-start | bytes 110596
  0.7 1.9 %collective-permute-start.2 = (s32[16]{0:T(128)}, s32[16]{0:T(128)S(1)}, u32[]{:S(2)}, u32[]{:S(2)}) collective-permute-start(s32[16]{0:T(128)} %class_ref.1), channel_id=1, source_target_pairs={{0,2},{1,3},{2,0},{3,1},{4,6},{5,7},{6,4},{7,5},{8,10},{9,11},{10,... | collective-permute-start | bytes 200 | tf_op jit(solution)/shard_map/ppermute | solution.py:332
  1.2 1.4 %collective-permute-start = (bf16[16,1152]{1,0:T(8,128)(2,1)}, bf16[16,1152]{1,0:T(8,128)(2,1)S(1)}, u32[]{:S(2)}, u32[]{:S(2)}) collective-permute-start(bf16[16,1152]{1,0:T(8,128)(2,1)} %image_ref.3), channel_id=1, source_target_pairs={{0,2},{1,3},{2,0},{3,1},{4,6},{5,7},{6,4},{7,5},{8,10},{9,11},{10,... | collective-permute-start | bytes 110600 | tf_op jit(solution)/shard_map/ppermute | solution.py:332
  1.2 1.5 %collective-permute-start.1 = (bf16[16,1152]{1,0:T(8,128)(2,1)}, bf16[16,1152]{1,0:T(8,128)(2,1)S(1)}, u32[]{:S(2)}, u32[]{:S(2)}) collective-permute-start(bf16[16,1152]{1,0:T(8,128)(2,1)} %text_ref.3), channel_id=1, source_target_pairs={{0,2},{1,3},{2,0},{3,1},{4,6},{5,7},{6,4},{7,5},{8,10},{9,11},{10,... | collective-permute-start | bytes 110600 | tf_op jit(solution)/shard_map/ppermute | solution.py:332
  1.7 0.7 %copy-start.2 = (s32[16]{0:T(128)S(1)}, s32[16]{0:T(128)}, u32[]{:S(2)}) copy-start(s32[16]{0:T(128)} %class_ref.1) | copy-start | bytes 196
  2.9 8.8 %collective-permute-start.5 = (bf16[32,1280]{1,0:T(8,128)(2,1)S(1)}, bf16[32,1280]{1,0:T(8,128)(2,1)S(1)}, u32[]{:S(2)}, u32[]{:S(2)}) collective-permute-start(bf16[32,1280]{1,0:T(8,128)(2,1)S(1)} %get-tuple-element.31), channel_id=1, source_target_pairs={{0,24},{1,25},{2,18},{3,19},{4,28},{5,29},{6,22},{7,23},{8,16},{9,... | collective-permute-start | bytes 245768 | tf_op jit(solution)/shard_map/ppermute | solution.py:329
  7.9 4.5 %collective-permute-start.6 = (bf16[32,1280]{1,0:T(8,128)(2,1)S(1)}, bf16[32,1280]{1,0:T(8,128)(2,1)S(1)}, u32[]{:S(2)}, u32[]{:S(2)}) collective-permute-start(bf16[32,1280]{1,0:T(8,128)(2,1)S(1)} %get-tuple-element.32), channel_id=1, source_target_pairs={{0,4},{1,5},{2,7},{3,6},{4,0},{5,1},{6,3},{7,2},{8,12},{9,13},{10,... | collective-permute-start | bytes 245768 | tf_op jit(solution)/shard_map/ppermute | solution.py:329
  9.4 4.4 %collective-permute-start.3 = (bf16[32,1280]{1,0:T(8,128)(2,1)S(1)}, bf16[32,1280]{1,0:T(8,128)(2,1)S(1)}, u32[]{:S(2)}, u32[]{:S(2)}) collective-permute-start(bf16[32,1280]{1,0:T(8,128)(2,1)S(1)} %get-tuple-element.26), channel_id=1, source_target_pairs={{0,8},{1,9},{2,3},{3,2},{4,12},{5,13},{6,7},{7,6},{8,0},{9,1},{10,... | collective-permute-start | bytes 245768 | tf_op jit(solution)/shard_map/ppermute | solution.py:329
  9.4 4.4 %collective-permute-start.4 = (bf16[32,1280]{1,0:T(8,128)(2,1)S(1)}, bf16[32,1280]{1,0:T(8,128)(2,1)S(1)}, u32[]{:S(2)}, u32[]{:S(2)}) collective-permute-start(bf16[32,1280]{1,0:T(8,128)(2,1)S(1)} %get-tuple-element.27), channel_id=1, source_target_pairs={{0,10},{1,11},{2,1},{3,0},{4,14},{5,15},{6,5},{7,4},{8,2},{9,3},{1... | collective-permute-start | bytes 245768 | tf_op jit(solution)/shard_map/ppermute | solution.py:329
  11.7 2.2 %collective-permute-start.7 = (bf16[32,1280]{1,0:T(8,128)(2,1)S(1)}, bf16[32,1280]{1,0:T(8,128)(2,1)S(1)}, u32[]{:S(2)}, u32[]{:S(2)}) collective-permute-start(bf16[32,1280]{1,0:T(8,128)(2,1)S(1)} %collective-permute-done.5.images), channel_id=1, source_target_pairs={{0,2},{1,3},{2,0},{3,1},{4,6},{5,7},{6,4},{7,5},{8,10},{9,11},{10,... | collective-permute-start | bytes 245768 | tf_op jit(solution)/shard_map/ppermute | solution.py:332
  12.5 1.5 %collective-permute-start.8 = (bf16[32,1280]{1,0:T(8,128)(2,1)S(1)}, bf16[32,1280]{1,0:T(8,128)(2,1)S(1)}, u32[]{:S(2)}, u32[]{:S(2)}) collective-permute-start(bf16[32,1280]{1,0:T(8,128)(2,1)S(1)} %collective-permute-done.6.texts), channel_id=1, source_target_pairs={{0,2},{1,3},{2,0},{3,1},{4,6},{5,7},{6,4},{7,5},{8,10},{9,11},{10,... | collective-permute-start | bytes 245768 | tf_op jit(solution)/shard_map/ppermute | solution.py:332
  14.7 7.2 %collective-permute-start.9 = (s16[32,1280]{1,0:T(8,128)(2,1)S(1)}, s16[32,1280]{1,0:T(8,128)(2,1)S(1)}, u32[]{:S(2)}, u32[]{:S(2)}) collective-permute-start(s16[32,1280]{1,0:T(8,128)(2,1)S(1)} %get-tuple-element.35), channel_id=1, source_target_pairs={{0,24},{1,25},{2,7},{3,6},{4,28},{5,29},{6,3},{7,2},{8,16},{9,17},... | collective-permute-start | bytes 245768 | tf_op jit(solution)/shard_map/ppermute | solution.py:329
  16.8 5.3 %collective-permute-start.10 = (s16[32,1280]{1,0:T(8,128)(2,1)S(1)}, s16[32,1280]{1,0:T(8,128)(2,1)S(1)}, u32[]{:S(2)}, u32[]{:S(2)}) collective-permute-start(s16[32,1280]{1,0:T(8,128)(2,1)S(1)} %get-tuple-element.38), channel_id=1, source_target_pairs={{0,4},{1,5},{2,18},{3,19},{4,0},{5,1},{6,22},{7,23},{8,12},{9,13},... | collective-permute-start | bytes 245768 | tf_op jit(solution)/shard_map/ppermute | solution.py:329
  18.3 4.9 %collective-permute-start.12 = (s16[16,1280]{1,0:T(8,128)(2,1)S(1)}, s16[16,1280]{1,0:T(8,128)(2,1)S(1)}, u32[]{:S(2)}, u32[]{:S(2)}) collective-permute-start(s16[16,1280]{1,0:T(8,128)(2,1)S(1)} %get-tuple-element.40), channel_id=1, source_target_pairs={{0,8},{1,9},{2,3},{3,2},{4,12},{5,13},{6,7},{7,6},{8,0},{9,1},{10,... | collective-permute-start | bytes 122888 | tf_op jit(solution)/shard_map/ppermute | solution.py:329
  18.3 4.9 %collective-permute-start.13 = (s16[16,1280]{1,0:T(8,128)(2,1)S(1)}, s16[16,1280]{1,0:T(8,128)(2,1)S(1)}, u32[]{:S(2)}, u32[]{:S(2)}) collective-permute-start(s16[16,1280]{1,0:T(8,128)(2,1)S(1)} %get-tuple-element.41), channel_id=1, source_target_pairs={{0,10},{1,11},{2,1},{3,0},{4,14},{5,15},{6,5},{7,4},{8,2},{9,3},{1... | collective-permute-start | bytes 122888 | tf_op jit(solution)/shard_map/ppermute | solution.py:329
  22.1 1.3 %collective-permute-start.11 = (s16[16,1280]{1,0:T(8,128)(2,1)S(1)}, s16[16,1280]{1,0:T(8,128)(2,1)S(1)}, u32[]{:S(2)}, u32[]{:S(2)}) collective-permute-start(s16[16,1280]{1,0:T(8,128)(2,1)S(1)} %get-tuple-element.39), channel_id=1, source_target_pairs={{0,2},{1,3},{2,0},{3,1},{4,6},{5,7},{6,4},{7,5},{8,10},{9,11},{10,... | collective-permute-start | bytes 122888 | tf_op jit(solution)/shard_map/ppermute | solution.py:332
  22.2 1.8 %collective-permute-start.14 = (s16[32,1280]{1,0:T(8,128)(2,1)S(1)}, s16[32,1280]{1,0:T(8,128)(2,1)S(1)}, u32[]{:S(2)}, u32[]{:S(2)}) collective-permute-start(s16[32,1280]{1,0:T(8,128)(2,1)S(1)} %collective-permute-done.10.back_ref), channel_id=1, source_target_pairs={{0,2},{1,3},{2,0},{3,1},{4,6},{5,7},{6,4},{7,5},{8,10},{9,11},{10,... | collective-permute-start | bytes 245768 | tf_op jit(solution)/shard_map/ppermute | solution.py:332

commit v20 on v19

--- a/solution.py
+++ b/solution.py
@@ -102,13 +102,14 @@
         out_ref[start : start + rows, depth:] = digits
 
 
-def pack_kernel(image_ref, text_ref, digits_ref, out_ref):
-    put_rows_of(image_ref, text_ref, digits_ref[...], out_ref)
-
-
-def join_kernel(own_ref, got_image, got_text, got_class, *refs):
-    *refs, got_ref = refs
-    put_rows_of(got_image, got_text, class_digits(got_class[...][None, :]), got_ref)
+def pack_kernel(image_ref, text_ref, digits_ref, both_ref, image_out, text_out):
+    rows = image_ref.shape[0]
+    put_rows_of(image_ref, text_ref, digits_ref[...], both_ref)
+    image_out[...] = both_ref[:rows, :]
+    text_out[...] = both_ref[rows:, :]
+
+
+def join_kernel(own_ref, got_ref, *refs):
     first = on_first_core()
     rows = own_ref.shape[0] // 2
     own, got = own_ref[...].astype(jnp.float32), got_ref[...].astype(jnp.float32)
@@ -116,14 +117,17 @@
     images = jnp.concatenate([low[:rows], high[:rows]], axis=0)
     texts = jnp.concatenate([low[rows:], high[rows:]], axis=0)
     mine, other = jnp.where(first, images, texts), jnp.where(first, texts, images)
-    for ref, block in zip(refs, (images, texts, mine, mine, mine, other)):
+    for ref, block in zip(refs, (other, mine, mine, other)):
         ref[...] = block.astype(jnp.bfloat16)
 
 
-def near_kernel(scale_ref, shift_ref, upper_ref, lower_ref, out_ref, pair_ref):
-    rows = upper_ref.shape[0]
-    out_ref[:rows, :] = upper_ref[...]
-    out_ref[rows:, :] = lower_ref[...]
+def halves_kernel(image_ref, text_ref, out_ref):
+    rows = image_ref.shape[0]
+    out_ref[:rows, :] = image_ref[...]
+    out_ref[rows:, :] = text_ref[...]
+
+
+def pair_kernel(scale_ref, shift_ref, pair_ref):
     row = lax.broadcasted_iota(jnp.int32, pair_ref.shape, 0)
     pair_ref[...] = jnp.where(row == 0, scale_ref[0], shift_ref[0])
 
@@ -203,33 +207,34 @@
     return pull, jnp.sum(loss, axis=1, keepdims=True)
 
 
-def tile_kernel(pair_ref, mine_ref, other_ref, images, texts, other_images, other_texts, near_ref, *outs):
+def tile_kernel(pair_ref, mine_ref, other_ref, got_0, got_1, swapped_0, swapped_1, halves, other_halves, *outs):
     rows = mine_ref.shape[0]
+    half = rows // 2
     first = on_first_core()
     scale, shift = pair_ref[0:1, 0:1], pair_ref[1:2, 0:1]
 
     def pick(one, two):
         return jnp.where(first, one, two)
 
-    def parted(image_ref, text_ref):
-        image, text = image_ref[...].astype(jnp.float32), text_ref[...].astype(jnp.float32)
+    def parted(ref):
+        image, text = ref[:half, :].astype(jnp.float32), ref[half:, :].astype(jnp.float32)
         return pick(image, text).astype(jnp.bfloat16), pick(text, image).astype(jnp.bfloat16)
 
-    (line, column), (other_line, other_column) = parted(images, texts), parted(other_images, other_texts)
-    lines = jnp.concatenate([line, near_ref[:rows, :], mine_ref[...], other_line], axis=0)
-    columns = jnp.concatenate([column, other_column, near_ref[rows:, :], other_ref[...]], axis=0)
+    (line, column), (other_line, other_column) = parted(halves), parted(other_halves)
+    lines = jnp.concatenate([got_1[...], mine_ref[...], line, other_line, swapped_0[...]], axis=0)
+    columns = jnp.concatenate([got_0[...], column, other_column, swapped_1[...], other_ref[...]], axis=0)
     loss, coef = tile_terms_of(lines, columns, scale, shift)
-    pull, loss_sum = pulls_of(loss[: 3 * rows], coef[: 3 * rows], columns)
-    put_rows([outs[0]], pull[:rows], loss_sum[:rows])
-    put_rows([outs[1]], *pulls_of(loss.T[:rows], coef.T[:rows], lines))
-    half = rows // 2
-    halves = []
-    for part in (pull, loss_sum):
-        low, high = part[rows : rows + half], part[rows + half : 2 * rows]
-        halves.append((pick(low, high), pick(high, low)))
-    for out, part, part_loss in zip(outs[2:4], *halves):
-        put_rows([out], part, part_loss)
-    put_rows([outs[4]], pull[2 * rows :], loss_sum[2 * rows :])
+    used = 2 * rows + half
+    pull, loss_sum = pulls_of(loss[:used], coef[:used], columns)
+    used = rows + half
+    column_pull, column_loss = pulls_of(loss.T[:used], coef.T[:used], lines)
+    put_rows([outs[0], outs[4]], pull[: 2 * rows], loss_sum[: 2 * rows])
+    put_rows([outs[1]], column_pull[:rows], column_loss[:rows])
+    line_half, column_half = (
+        (x[start:], y[start:]) for x, y, start in ((pull, loss_sum, 2 * rows), (column_pull, column_loss, rows))
+    )
+    for out, (one, two) in zip(outs[2:4], ((line_half, column_half), (column_half, line_half))):
+        put_rows([out], *(pick(x, y) for x, y in zip(one, two)))
 
 
 def total(parts, rows, depth):
@@ -256,38 +261,38 @@
     loss_ref[...] = jnp.broadcast_to(loss, loss_ref.shape)
 
 
-def more_kernel(keep_ref, kept_loss_ref, back_ref, got_ref, same_ref, cross_ref, image_ref, text_ref, *outs):
+def more_kernel(keep_ref, kept_loss_ref, back_ref, got_ref, image_back, text_back, image_ref, text_ref, *outs):
     sum_ref, sum_loss_ref, unit_ref, inverse_ref = outs
+    first = on_first_core()
     rows, depth = keep_ref.shape
-    own, _ = place_of(on_first_core(), rows)
-    pull, loss = total([same_ref], rows, depth)
-    sum_ref[0] = keep_ref[...] + pull
-    sum_loss_ref[0] = kept_loss_ref[...] + loss
-    sum_ref[1], loss = total([back_ref[own, :], got_ref, cross_ref], rows, depth)
-    sum_loss_ref[1] = jnp.broadcast_to(loss, sum_loss_ref.shape[1:])
+    own, _ = place_of(first, rows)
+    mine = (keep_ref[...], kept_loss_ref[:, 0:1])
+    other = total([back_ref[own, :], got_ref], rows, depth)
+    for side, (one, two, back) in enumerate(((mine, other, image_back), (other, mine, text_back))):
+        pull, loss = total([back], rows, depth)
+        sum_ref[side] = pull + jnp.where(first, one[0], two[0])
+        sum_loss_ref[side] = jnp.broadcast_to(
+            loss + jnp.where(first, one[1], two[1]), sum_loss_ref.shape[1:]
+        )
     for side, ref in enumerate((image_ref, text_ref)):
         unit, inverse = unit_rows(ref[...])
         unit_ref[side] = unit
         inverse_ref[side] = jnp.broadcast_to(inverse, inverse_ref.shape[1:])
 
 
-def final_kernel(pairs, sum_ref, sum_loss_ref, unit_ref, inverse_ref, got_ref, loss_ref, grad_image_ref, grad_text_ref):
+def final_kernel(pairs, sum_ref, sum_loss_ref, unit_ref, inverse_ref, got_ref, *outs):
+    loss_ref, grad_image_ref, grad_text_ref = outs
     first = on_first_core()
     rows, depth = sum_ref.shape[1:]
     own, _ = place_of(first, rows)
     pull, loss = total([got_ref[own, :]], rows, depth)
-    pulls = (sum_ref[0] + pull, sum_ref[1])
-    losses = (sum_loss_ref[0][:, 0:1] + loss, sum_loss_ref[1][:, 0:1])
-    for side, (pull, out) in enumerate(
-        (
-            (jnp.where(first, pulls[0], pulls[1]), grad_image_ref),
-            (jnp.where(first, pulls[1], pulls[0]), grad_text_ref),
-        )
-    ):
-        out[...] = project_back(unit_ref[side], inverse_ref[side][:, 0:1], pull)
+    image_pull = sum_ref[0] + jnp.where(first, pull, 0.0)
+    text_pull = sum_ref[1] + jnp.where(first, 0.0, pull)
+    grad_image_ref[...] = project_back(unit_ref[0], inverse_ref[0][:, 0:1], image_pull)
+    grad_text_ref[...] = project_back(unit_ref[1], inverse_ref[1][:, 0:1], text_pull)
     row = lax.broadcasted_iota(jnp.int32, (rows, rows), 0)
     column = lax.broadcasted_iota(jnp.int32, (rows, rows), 1)
-    loss = jnp.where(first, losses[0], losses[1])
+    loss = sum_loss_ref[0][:, 0:1] + jnp.where(first, loss, 0.0)
     across = jnp.where(row == column, loss / pairs, 0.0)
     loss_ref[...] = jnp.sum(across, axis=0, keepdims=True)
 
@@ -321,18 +326,17 @@
     def core(i):
         return i // lanes % 2
 
-    def visit(x, masks, cross):
+    def visit(x, masks):
         pairs = []
         for i in range(n):
             chip = (i // (2 * lanes) * lanes + i % lanes) ^ masks[core(i)]
-            pairs.append((i, (chip // lanes * 2 + (core(i) ^ cross)) * lanes + chip % lanes))
+            pairs.append((i, (chip // lanes * 2 + core(i)) * lanes + chip % lanes))
         return lax.ppermute(x, AXES, pairs)
 
     def swap(x):
         return lax.ppermute(x, AXES, [(i, i ^ lanes) for i in range(n)])
 
-    out_visits = (((12, 8), 0), ((2, 3), 0), ((4, 1), 0), ((4, 1), 1))
-    back_visits = (((12, 3), 0), ((2, 8), 0), ((4, 1), 0), ((4, 1), 1))
+    across, beside, second, third = (12, 12), (1, 1), (2, 8), (4, 3)
     late = pl.CostEstimate(flops=10**9, bytes_accessed=10**7, transcendentals=0)
     digits = call(
         digits_kernel,
@@ -341,32 +345,22 @@
         "digits",
         cost=late,
     )
-    own = call(pack_kernel, block(2), [image_emb, text_emb, digits], "pack")
-    swapped = [swap(x) for x in (image_emb, text_emb, pair_class)]
-    *sent, mine, other = call(
-        join_kernel,
-        (block(2),) * 6,
-        [own, *swapped],
-        "join",
-        scratch=[pltpu.VMEM((2 * rows, width), jnp.bfloat16)],
-    )
-    got = [visit(x, *way) for x, way in zip(sent, out_visits)]
-    near, pair = call(
-        near_kernel,
-        (block(4), wide(8, LANES)),
-        [scale[None], shift[None], *got[2:]],
-        "near",
-        2,
-        late,
-    )
+    own, own_images, own_texts = call(
+        pack_kernel, (block(2), block(1), block(1)), [image_emb, text_emb, digits], "pack"
+    )
+    halves = [visit(own_images, across), visit(own_texts, beside)]
+    halves = call(halves_kernel, block(2), halves, "halves", cost=late)
+    *sent, mine, other = call(join_kernel, (block(2),) * 4, [own, swap(own)], "join")
+    got = [visit(x, masks) for x, masks in zip(sent, (second, third))]
+    pair = call(pair_kernel, wide(8, LANES), [scale[None], shift[None]], "pair", 2)
     one, two = block(1, jnp.int16), block(2, jnp.int16)
     parts = call(
         tile_kernel,
         (two, two, one, one, two),
-        [pair, mine, other, *got[:2], swap(got[0]), swap(got[1]), near],
+        [pair, mine, other, *got, swap(got[0]), swap(got[1]), halves, swap(halves)],
         "tile",
     )
-    back = [visit(x, *way) for x, way in zip(parts, back_visits)]
+    back = [visit(x, masks) for x, masks in zip(parts, (third, second, across, beside))]
     keep, kept_loss, give = call(
         add_kernel, (wide(rows, depth), wide(rows, LANES), one), [parts[4], back[0]], "add"
     )

time: 25 us -> 25.7 us (1.028)
  waiting for transfers between devices: 4.87 us -> 6.6 us
  starting transfers between devices: 14.8 us -> 13.7 us
    ppermute x8, waiting for transfers between devices: 4.13 us -> 6.59 us  [visit(): return lax.ppermute(x, AXES, pairs)]
    ppermute x7 -> x6, starting transfers between devices: 2.79 us -> 1.63 us  [swap(): return lax.ppermute(x, AXES, [(i, i ^ lanes) for i in range(n)])]
    ppermute x7 -> x6, waiting for transfers between devices: 0.74 us -> 0.02 us  [swap(): return lax.ppermute(x, AXES, [(i, i ^ lanes) for i in range(n)])]
    pallas_call x8 -> x9, Pallas kernels: 2.43 us -> 2.46 us  [call(): pl.pallas_call(kernel, scratch_shapes=scratch, cost_estimate=cost, out_sh...]
  transfers between devices with their start and end apart: 15 -> 14, of which waited for: 6 -> 6; matrix products, arithmetic and copies ran while one was open for 0% -> 0% of each run, Pallas kernels for 2% -> 2%
where the time goes in v20:
time: 25.7 us; the launch traced here: 25.5 us
  starting transfers between devices  13.7 us (53%)
  waiting for transfers between devices  6.6 us (26%)
  Pallas kernels  2.46 us (10%)
  between operations  2.06 us (8%)
  local copies, waits for them, and re-layouts  0.67 us (3%)
    ppermute x8, starting transfers between devices, visit(): return lax.ppermute(x, AXES, pairs)  12.1 us
    ppermute x8, waiting for transfers between devices, visit(): return lax.ppermute(x, AXES, pairs)  6.59 us
    pallas_call x9, Pallas kernels, call(): pl.pallas_call(kernel, scratch_shapes=scratch, cost_estimate=cost, out_sh...  2.46 us
    ppermute x6, starting transfers between devices, swap(): return lax.ppermute(x, AXES, [(i, i ^ lanes) for i in range(n)])  1.63 us
    unnamed x6, local copies, waits for them, and re-layouts  0.67 us
  transfers between devices with their start and end apart: 14, of which 6 were waited for; matrix products, arithmetic and copies ran while one was open for 0% of the time, Pallas kernels for 2%

profile of v20, /device:TPU:0, one launch (start us, length us, event | category | flops | bytes accessed | tf_op | source)
XLA Modules:
  0.0 25.5 jit_solution(11390870155830528630)
XLA Ops:
  0.6 0.0 copy-start.1
  0.6 0.0 copy-start
  0.7 0.0 copy-start.2
  0.7 0.7 %copy-done.2 = s32[16]{0:T(128)S(1)} copy-done((s32[16]{0:T(128)S(1)}, s32[16]{0:T(128)}, u32[]{:S(2)}) %copy-start.2) | copy-done | bytes 88
  1.3 0.1 digits.1.digits_ref
  1.4 0.0 copy-done.1
  1.4 0.0 copy-done
  1.4 0.1 pack.1
  1.6 0.5 %collective-permute-start = (bf16[32,1280]{1,0:T(8,128)(2,1)S(1)}, bf16[32,1280]{1,0:T(8,128)(2,1)S(1)}, u32[]{:S(2)}, u32[]{:S(2)}) collective-permute-start(bf16[32,1280]{1,0:T(8,128)(2,1)S(1)} %get-tuple-element.25.own_ref), channel_id=1, source_target_pairs={{0,2},{1,3},{2,0},{3,1},{4,6},{5,7},{6,4},{7,5},{8,10},{9,11},{10,... | collective-permute-start | bytes 245768 | tf_op jit(solution)/shard_map/ppermute | solution.py:337
  2.1 4.7 %collective-permute-start.5 = (bf16[16,1280]{1,0:T(8,128)(2,1)S(1)}, bf16[16,1280]{1,0:T(8,128)(2,1)S(1)}, u32[]{:S(2)}, u32[]{:S(2)}) collective-permute-start(bf16[16,1280]{1,0:T(8,128)(2,1)S(1)} %get-tuple-element.30), channel_id=1, source_target_pairs={{0,24},{1,25},{2,26},{3,27},{4,28},{5,29},{6,30},{7,31},{8,16},{9,... | collective-permute-start | bytes 122888 | tf_op jit(solution)/shard_map/ppermute | solution.py:334
  6.7 1.5 %collective-permute-start.6 = (bf16[16,1280]{1,0:T(8,128)(2,1)S(1)}, bf16[16,1280]{1,0:T(8,128)(2,1)S(1)}, u32[]{:S(2)}, u32[]{:S(2)}) collective-permute-start(bf16[16,1280]{1,0:T(8,128)(2,1)S(1)} %get-tuple-element.31), channel_id=1, source_target_pairs={{0,1},{1,0},{2,3},{3,2},{4,5},{5,4},{6,7},{7,6},{8,9},{9,8},{10,11... | collective-permute-start | bytes 122888 | tf_op jit(solution)/shard_map/ppermute | solution.py:334
  8.3 0.0 collective-permute-done.got_ref
  8.3 0.1 join.1
  8.3 1.6 %collective-permute-start.1 = (bf16[32,1280]{1,0:T(8,128)(2,1)S(1)}, bf16[32,1280]{1,0:T(8,128)(2,1)S(1)}, u32[]{:S(2)}, u32[]{:S(2)}) collective-permute-start(bf16[32,1280]{1,0:T(8,128)(2,1)S(1)} %get-tuple-element.28), channel_id=1, source_target_pairs={{0,4},{1,5},{2,18},{3,19},{4,0},{5,1},{6,22},{7,23},{8,12},{9,13},... | collective-permute-start | bytes 245768 | tf_op jit(solution)/shard_map/ppermute | solution.py:334
  9.9 0.0 collective-permute-start.2
  9.9 0.0 collective-permute-done.5.image_ref
  9.9 0.8 %collective-permute-done.6.text_ref = bf16[16,1280]{1,0:T(8,128)(2,1)S(1)} collective-permute-done((bf16[16,1280]{1,0:T(8,128)(2,1)S(1)}, bf16[16,1280]{1,0:T(8,128)(2,1)S(1)}, u32[]{:S(2)}, u32[]{:S(2)}) %collective-permute-start.6) | collective-permute-done | bytes 40992 | tf_op jit(solution)/shard_map/ppermute | solution.py:334
  10.8 0.0 collective-permute-start.7
  10.8 2.1 %collective-permute-done.1.got_0 = bf16[32,1280]{1,0:T(8,128)(2,1)S(1)} collective-permute-done((bf16[32,1280]{1,0:T(8,128)(2,1)S(1)}, bf16[32,1280]{1,0:T(8,128)(2,1)S(1)}, u32[]{:S(2)}, u32[]{:S(2)}) %collective-permute-start.1) | collective-permute-done | bytes 81952 | tf_op jit(solution)/shard_map/ppermute | solution.py:334
  12.8 0.0 collective-permute-start.3
  12.8 1.5 %collective-permute-done.2.got_1 = bf16[32,1280]{1,0:T(8,128)(2,1)S(1)} collective-permute-done((bf16[32,1280]{1,0:T(8,128)(2,1)S(1)}, bf16[32,1280]{1,0:T(8,128)(2,1)S(1)}, u32[]{:S(2)}, u32[]{:S(2)}) %collective-permute-start.2) | collective-permute-done | bytes 81952 | tf_op jit(solution)/shard_map/ppermute | solution.py:334
  14.3 0.0 collective-permute-start.4
  15.7 0.0 collective-permute-done.7.other_halves
  15.7 0.0 collective-permute-done.3.swapped_0
  15.7 0.0 collective-permute-done.4.swapped_1
  15.7 0.7 %tile.1 = (s16[32,1280]{1,0:T(8,128)(2,1)S(1)}, s16[32,1280]{1,0:T(8,128)(2,1)S(1)}, s16[16,1280]{1,0:T(8,128)(2,1)S(1)}, s16[16,1280]{1,0:T(8,128)(2,1)S(1)}, s16[32,1280]{1,0:T(8,128)(2,1)S(1)}) custom-call(f32[8,128]{1,0:T(8,128)S(1)} %pair.1.pair_ref, bf16[32,1280]{1,0:T(8,128)(2,1)S(1)} %get-tuple-element.26.mine_ref, ...), custom_call_target="tpu_custom_call" | custom-call | tf_op jit(solution)/shard_map/tile/pallas_call | solution.py:309
  16.4 0.1 collective-permute-start.8
  16.5 0.9 %collective-permute-start.9 = (s16[32,1280]{1,0:T(8,128)(2,1)S(1)}, s16[32,1280]{1,0:T(8,128)(2,1)S(1)}, u32[]{:S(2)}, u32[]{:S(2)}) collective-permute-start(s16[32,1280]{1,0:T(8,128)(2,1)S(1)} %get-tuple-element.36), channel_id=1, source_target_pairs={{0,4},{1,5},{2,18},{3,19},{4,0},{5,1},{6,22},{7,23},{8,12},{9,13},... | collective-permute-start | bytes 245768 | tf_op jit(solution)/shard_map/ppermute | solution.py:334
  17.4 2.9 %collective-permute-start.11 = (s16[16,1280]{1,0:T(8,128)(2,1)S(1)}, s16[16,1280]{1,0:T(8,128)(2,1)S(1)}, u32[]{:S(2)}, u32[]{:S(2)}) collective-permute-start(s16[16,1280]{1,0:T(8,128)(2,1)S(1)} %get-tuple-element.38), channel_id=1, source_target_pairs={{0,24},{1,25},{2,26},{3,27},{4,28},{5,29},{6,30},{7,31},{8,16},{9,... | collective-permute-start | bytes 122888 | tf_op jit(solution)/shard_map/ppermute | solution.py:334
  20.2 0.5 %collective-permute-start.12 = (s16[16,1280]{1,0:T(8,128)(2,1)S(1)}, s16[16,1280]{1,0:T(8,128)(2,1)S(1)}, u32[]{:S(2)}, u32[]{:S(2)}) collective-permute-start(s16[16,1280]{1,0:T(8,128)(2,1)S(1)} %get-tuple-element.39), channel_id=1, source_target_pairs={{0,1},{1,0},{2,3},{3,2},{4,5},{5,4},{6,7},{7,6},{8,9},{9,8},{10,11... | collective-permute-start | bytes 122888 | tf_op jit(solution)/shard_map/ppermute | solution.py:334
  20.7 0.2 collective-permute-done.8.back_ref
  20.9 0.2 add.1
  21.2 0.8 %collective-permute-start.10 = (s16[16,1280]{1,0:T(8,128)(2,1)S(1)}, s16[16,1280]{1,0:T(8,128)(2,1)S(1)}, u32[]{:S(2)}, u32[]{:S(2)}) collective-permute-start(s16[16,1280]{1,0:T(8,128)(2,1)S(1)} %get-tuple-element.37), channel_id=1, source_target_pairs={{0,2},{1,3},{2,0},{3,1},{4,6},{5,7},{6,4},{7,5},{8,10},{9,11},{10,... | collective-permute-start | bytes 122888 | tf_op jit(solution)/shard_map/ppermute | solution.py:337
  21.9 0.0 collective-permute-done.9.back_ref
  21.9 0.3 %collective-permute-start.13 = (s16[32,1280]{1,0:T(8,128)(2,1)S(1)}, s16[32,1280]{1,0:T(8,128)(2,1)S(1)}, u32[]{:S(2)}, u32[]{:S(2)}) collective-permute-start(s16[32,1280]{1,0:T(8,128)(2,1)S(1)} %collective-permute-done.9.back_ref), channel_id=1, source_target_pairs={{0,2},{1,3},{2,0},{3,1},{4,6},{5,7},{6,4},{7,5},{8,10},{9,11},{10,... | collective-permute-start | bytes 245768 | tf_op jit(solution)/shard_map/ppermute | solution.py:337
  22.3 1.2 %collective-permute-done.11.image_back = s16[16,1280]{1,0:T(8,128)(2,1)S(1)} collective-permute-done((s16[16,1280]{1,0:T(8,128)(2,1)S(1)}, s16[16,1280]{1,0:T(8,128)(2,1)S(1)}, u32[]{:S(2)}, u32[]{:S(2)}) %collective-permute-start.11) | collective-permute-done | bytes 40992 | tf_op jit(solution)/shard_map/ppermute | solution.py:334
  23.5 0.8 %collective-permute-done.12.text_back = s16[16,1280]{1,0:T(8,128)(2,1)S(1)} collective-permute-done((s16[16,1280]{1,0:T(8,128)(2,1)S(1)}, s16[16,1280]{1,0:T(8,128)(2,1)S(1)}, u32[]{:S(2)}, u32[]{:S(2)}) %collective-permute-start.12) | collective-permute-done | bytes 40992 | tf_op jit(solution)/shard_map/ppermute | solution.py:334
  24.2 0.0 collective-permute-done.10.got_ref
  24.2 0.3 %more.1 = (f32[2,16,1152]{2,1,0:T(8,128)S(1)}, f32[2,16,128]{2,1,0:T(8,128)S(1)}, f32[2,16,1152]{2,1,0:T(8,128)S(1)}, f32[2,16,128]{2,1,0:T(8,128)S(1)}) custom-call(f32[16,1152]{1,0:T(8,128)S(1)} %get-tuple-element.34.keep_ref, f32[16,128]{1,0:T(8,128)S(1)} %get-tuple-element.35.kept_loss_ref, s16[32,1280]{1,0:T(8,128)(2,1)S(1)} %collective-permute-done.9.back_ref, ...), custom_call_target="tpu_custom_call" | custom-call | flops 1000000000 | bytes 10000000 | tf_op jit(solution)/shard_map/more/pallas_call | solution.py:309
  24.5 0.0 collective-permute-done.13.got_ref
  24.6 0.9 %final.1 = (f32[1,16]{1,0:T(1,128)}, f32[16,1152]{1,0:T(8,128)}, f32[16,1152]{1,0:T(8,128)}) custom-call(f32[2,16,1152]{2,1,0:T(8,128)S(1)} %get-tuple-element.40.sum_ref, f32[2,16,128]{2,1,0:T(8,128)S(1)} %get-tuple-element.41.sum_loss_ref, f32[2,16,1152]{2,1,0:T(8,128)S(1)} %get-tuple-element.42.unit_ref, f32[2,16,128]{2,1,0:T(8,128)S(1)} %get-tuple-element.43.inverse_ref, ...), custom_call_target="tpu_custom_call" | custom-call | tf_op jit(solution)/shard_map/final/pallas_call | solution.py:309
  (2 shorter events, 0.0 us)
Async XLA Ops:
  0.6 0.8 %copy-start.1 = (bf16[16,1152]{1,0:T(8,128)(2,1)S(1)}, bf16[16,1152]{1,0:T(8,128)(2,1)}, u32[]{:S(2)}) copy-start(bf16[16,1152]{1,0:T(8,128)(2,1)} %text_ref.3) | copy-start | bytes 110596
  0.6 0.8 %copy-start = (bf16[16,1152]{1,0:T(8,128)(2,1)S(1)}, bf16[16,1152]{1,0:T(8,128)(2,1)}, u32[]{:S(2)}) copy-start(bf16[16,1152]{1,0:T(8,128)(2,1)} %image_ref.3) | copy-start | bytes 110596
  0.7 0.7 %copy-start.2 = (s32[16]{0:T(128)S(1)}, s32[16]{0:T(128)}, u32[]{:S(2)}) copy-start(s32[16]{0:T(128)} %class_ref.1) | copy-start | bytes 196
  1.6 6.7 %collective-permute-start = (bf16[32,1280]{1,0:T(8,128)(2,1)S(1)}, bf16[32,1280]{1,0:T(8,128)(2,1)S(1)}, u32[]{:S(2)}, u32[]{:S(2)}) collective-permute-start(bf16[32,1280]{1,0:T(8,128)(2,1)S(1)} %get-tuple-element.25.own_ref), channel_id=1, source_target_pairs={{0,2},{1,3},{2,0},{3,1},{4,6},{5,7},{6,4},{7,5},{8,10},{9,11},{10,... | collective-permute-start | bytes 245768 | tf_op jit(solution)/shard_map/ppermute | solution.py:337
  2.1 7.8 %collective-permute-start.5 = (bf16[16,1280]{1,0:T(8,128)(2,1)S(1)}, bf16[16,1280]{1,0:T(8,128)(2,1)S(1)}, u32[]{:S(2)}, u32[]{:S(2)}) collective-permute-start(bf16[16,1280]{1,0:T(8,128)(2,1)S(1)} %get-tuple-element.30), channel_id=1, source_target_pairs={{0,24},{1,25},{2,26},{3,27},{4,28},{5,29},{6,30},{7,31},{8,16},{9,... | collective-permute-start | bytes 122888 | tf_op jit(solution)/shard_map/ppermute | solution.py:334
  6.7 4.0 %collective-permute-start.6 = (bf16[16,1280]{1,0:T(8,128)(2,1)S(1)}, bf16[16,1280]{1,0:T(8,128)(2,1)S(1)}, u32[]{:S(2)}, u32[]{:S(2)}) collective-permute-start(bf16[16,1280]{1,0:T(8,128)(2,1)S(1)} %get-tuple-element.31), channel_id=1, source_target_pairs={{0,1},{1,0},{2,3},{3,2},{4,5},{5,4},{6,7},{7,6},{8,9},{9,8},{10,11... | collective-permute-start | bytes 122888 | tf_op jit(solution)/shard_map/ppermute | solution.py:334
  8.3 4.5 %collective-permute-start.1 = (bf16[32,1280]{1,0:T(8,128)(2,1)S(1)}, bf16[32,1280]{1,0:T(8,128)(2,1)S(1)}, u32[]{:S(2)}, u32[]{:S(2)}) collective-permute-start(bf16[32,1280]{1,0:T(8,128)(2,1)S(1)} %get-tuple-element.28), channel_id=1, source_target_pairs={{0,4},{1,5},{2,18},{3,19},{4,0},{5,1},{6,22},{7,23},{8,12},{9,13},... | collective-permute-start | bytes 245768 | tf_op jit(solution)/shard_map/ppermute | solution.py:334
  9.9 4.4 %collective-permute-start.2 = (bf16[32,1280]{1,0:T(8,128)(2,1)S(1)}, bf16[32,1280]{1,0:T(8,128)(2,1)S(1)}, u32[]{:S(2)}, u32[]{:S(2)}) collective-permute-start(bf16[32,1280]{1,0:T(8,128)(2,1)S(1)} %get-tuple-element.29), channel_id=1, source_target_pairs={{0,8},{1,9},{2,7},{3,6},{4,12},{5,13},{6,3},{7,2},{8,0},{9,1},{10,... | collective-permute-start | bytes 245768 | tf_op jit(solution)/shard_map/ppermute | solution.py:334
  10.8 4.9 %collective-permute-start.7 = (bf16[32,1280]{1,0:T(8,128)(2,1)S(1)}, bf16[32,1280]{1,0:T(8,128)(2,1)S(1)}, u32[]{:S(2)}, u32[]{:S(2)}) collective-permute-start(bf16[32,1280]{1,0:T(8,128)(2,1)S(1)} %halves.1), channel_id=1, source_target_pairs={{0,2},{1,3},{2,0},{3,1},{4,6},{5,7},{6,4},{7,5},{8,10},{9,11},{10,... | collective-permute-start | bytes 245768 | tf_op jit(solution)/shard_map/ppermute | solution.py:337
  12.8 2.8 %collective-permute-start.3 = (bf16[32,1280]{1,0:T(8,128)(2,1)S(1)}, bf16[32,1280]{1,0:T(8,128)(2,1)S(1)}, u32[]{:S(2)}, u32[]{:S(2)}) collective-permute-start(bf16[32,1280]{1,0:T(8,128)(2,1)S(1)} %collective-permute-done.1.got_0), channel_id=1, source_target_pairs={{0,2},{1,3},{2,0},{3,1},{4,6},{5,7},{6,4},{7,5},{8,10},{9,11},{10,... | collective-permute-start | bytes 245768 | tf_op jit(solution)/shard_map/ppermute | solution.py:337
  14.3 1.3 %collective-permute-start.4 = (bf16[32,1280]{1,0:T(8,128)(2,1)S(1)}, bf16[32,1280]{1,0:T(8,128)(2,1)S(1)}, u32[]{:S(2)}, u32[]{:S(2)}) collective-permute-start(bf16[32,1280]{1,0:T(8,128)(2,1)S(1)} %collective-permute-done.2.got_1), channel_id=1, source_target_pairs={{0,2},{1,3},{2,0},{3,1},{4,6},{5,7},{6,4},{7,5},{8,10},{9,11},{10,... | collective-permute-start | bytes 245768 | tf_op jit(solution)/shard_map/ppermute | solution.py:337
  16.4 4.5 %collective-permute-start.8 = (s16[32,1280]{1,0:T(8,128)(2,1)S(1)}, s16[32,1280]{1,0:T(8,128)(2,1)S(1)}, u32[]{:S(2)}, u32[]{:S(2)}) collective-permute-start(s16[32,1280]{1,0:T(8,128)(2,1)S(1)} %get-tuple-element.33), channel_id=1, source_target_pairs={{0,8},{1,9},{2,7},{3,6},{4,12},{5,13},{6,3},{7,2},{8,0},{9,1},{10,... | collective-permute-start | bytes 245768 | tf_op jit(solution)/shard_map/ppermute | solution.py:334
  16.5 5.4 %collective-permute-start.9 = (s16[32,1280]{1,0:T(8,128)(2,1)S(1)}, s16[32,1280]{1,0:T(8,128)(2,1)S(1)}, u32[]{:S(2)}, u32[]{:S(2)}) collective-permute-start(s16[32,1280]{1,0:T(8,128)(2,1)S(1)} %get-tuple-element.36), channel_id=1, source_target_pairs={{0,4},{1,5},{2,18},{3,19},{4,0},{5,1},{6,22},{7,23},{8,12},{9,13},... | collective-permute-start | bytes 245768 | tf_op jit(solution)/shard_map/ppermute | solution.py:334
  17.4 6.1 %collective-permute-start.11 = (s16[16,1280]{1,0:T(8,128)(2,1)S(1)}, s16[16,1280]{1,0:T(8,128)(2,1)S(1)}, u32[]{:S(2)}, u32[]{:S(2)}) collective-permute-start(s16[16,1280]{1,0:T(8,128)(2,1)S(1)} %get-tuple-element.38), channel_id=1, source_target_pairs={{0,24},{1,25},{2,26},{3,27},{4,28},{5,29},{6,30},{7,31},{8,16},{9,... | collective-permute-start | bytes 122888 | tf_op jit(solution)/shard_map/ppermute | solution.py:334
  20.2 4.0 %collective-permute-start.12 = (s16[16,1280]{1,0:T(8,128)(2,1)S(1)}, s16[16,1280]{1,0:T(8,128)(2,1)S(1)}, u32[]{:S(2)}, u32[]{:S(2)}) collective-permute-start(s16[16,1280]{1,0:T(8,128)(2,1)S(1)} %get-tuple-element.39), channel_id=1, source_target_pairs={{0,1},{1,0},{2,3},{3,2},{4,5},{5,4},{6,7},{7,6},{8,9},{9,8},{10,11... | collective-permute-start | bytes 122888 | tf_op jit(solution)/shard_map/ppermute | solution.py:334
  21.2 3.1 %collective-permute-start.10 = (s16[16,1280]{1,0:T(8,128)(2,1)S(1)}, s16[16,1280]{1,0:T(8,128)(2,1)S(1)}, u32[]{:S(2)}, u32[]{:S(2)}) collective-permute-start(s16[16,1280]{1,0:T(8,128)(2,1)S(1)} %get-tuple-element.37), channel_id=1, source_target_pairs={{0,2},{1,3},{2,0},{3,1},{4,6},{5,7},{6,4},{7,5},{8,10},{9,11},{10,... | collective-permute-start | bytes 122888 | tf_op jit(solution)/shard_map/ppermute | solution.py:337
  21.9 2.6 %collective-permute-start.13 = (s16[32,1280]{1,0:T(8,128)(2,1)S(1)}, s16[32,1280]{1,0:T(8,128)(2,1)S(1)}, u32[]{:S(2)}, u32[]{:S(2)}) collective-permute-start(s16[32,1280]{1,0:T(8,128)(2,1)S(1)} %collective-permute-done.9.back_ref), channel_id=1, source_target_pairs={{0,2},{1,3},{2,0},{3,1},{4,6},{5,7},{6,4},{7,5},{8,10},{9,11},{10,... | collective-permute-start | bytes 245768 | tf_op jit(solution)/shard_map/ppermute | solution.py:337

commit v21 on v19

--- a/solution.py
+++ b/solution.py
@@ -118,6 +118,12 @@
     mine, other = jnp.where(first, images, texts), jnp.where(first, texts, images)
     for ref, block in zip(refs, (images, texts, mine, mine, mine, other)):
         ref[...] = block.astype(jnp.bfloat16)
+
+
+def far_kernel(upper_ref, lower_ref, out_ref):
+    rows = upper_ref.shape[0]
+    out_ref[:rows, :] = upper_ref[...]
+    out_ref[rows:, :] = lower_ref[...]
 
 
 def near_kernel(scale_ref, shift_ref, upper_ref, lower_ref, out_ref, pair_ref):
@@ -203,7 +209,7 @@
     return pull, jnp.sum(loss, axis=1, keepdims=True)
 
 
-def tile_kernel(pair_ref, mine_ref, other_ref, images, texts, other_images, other_texts, near_ref, *outs):
+def tile_kernel(pair_ref, mine_ref, other_ref, far_ref, swapped_ref, near_ref, *outs):
     rows = mine_ref.shape[0]
     first = on_first_core()
     scale, shift = pair_ref[0:1, 0:1], pair_ref[1:2, 0:1]
@@ -211,11 +217,11 @@
     def pick(one, two):
         return jnp.where(first, one, two)
 
-    def parted(image_ref, text_ref):
-        image, text = image_ref[...].astype(jnp.float32), text_ref[...].astype(jnp.float32)
+    def parted(ref):
+        image, text = ref[:rows, :].astype(jnp.float32), ref[rows:, :].astype(jnp.float32)
         return pick(image, text).astype(jnp.bfloat16), pick(text, image).astype(jnp.bfloat16)
 
-    (line, column), (other_line, other_column) = parted(images, texts), parted(other_images, other_texts)
+    (line, column), (other_line, other_column) = parted(far_ref), parted(swapped_ref)
     lines = jnp.concatenate([line, near_ref[:rows, :], mine_ref[...], other_line], axis=0)
     columns = jnp.concatenate([column, other_column, near_ref[rows:, :], other_ref[...]], axis=0)
     loss, coef = tile_terms_of(lines, columns, scale, shift)
@@ -351,6 +357,7 @@
         scratch=[pltpu.VMEM((2 * rows, width), jnp.bfloat16)],
     )
     got = [visit(x, *way) for x, way in zip(sent, out_visits)]
+    far = call(far_kernel, block(4), got[:2], "far")
     near, pair = call(
         near_kernel,
         (block(4), wide(8, LANES)),
@@ -363,7 +370,7 @@
     parts = call(
         tile_kernel,
         (two, two, one, one, two),
-        [pair, mine, other, *got[:2], swap(got[0]), swap(got[1]), near],
+        [pair, mine, other, far, swap(far), near],
         "tile",
     )
     back = [visit(x, *way) for x, way in zip(parts, back_visits)]

time: 25 us -> 24.7 us (0.988)
  starting transfers between devices: 14.8 us -> 14.2 us
  waiting for transfers between devices: 4.87 us -> 5.2 us
    ppermute x7 -> x6, starting transfers between devices: 2.79 us -> 1.98 us  [swap(): return lax.ppermute(x, AXES, [(i, i ^ lanes) for i in range(n)])]
    ppermute x8, waiting for transfers between devices: 4.13 us -> 4.71 us  [visit(): return lax.ppermute(x, AXES, pairs)]
    ppermute x7 -> x6, waiting for transfers between devices: 0.74 us -> 0.48 us  [swap(): return lax.ppermute(x, AXES, [(i, i ^ lanes) for i in range(n)])]
    pallas_call x8 -> x9, Pallas kernels: 2.43 us -> 2.44 us  [call(): pl.pallas_call(kernel, scratch_shapes=scratch, cost_estimate=cost, out_sh...]
  transfers between devices with their start and end apart: 15 -> 14, of which waited for: 6 -> 7; matrix products, arithmetic and copies ran while one was open for 0% -> 0% of each run, Pallas kernels for 2% -> 2%
where the time goes in v21:
time: 24.7 us; the launch traced here: 24.5 us
  starting transfers between devices  14.2 us (57%)
  waiting for transfers between devices  5.2 us (21%)
  Pallas kernels  2.44 us (10%)
  between operations  2.04 us (8%)
  local copies, waits for them, and re-layouts  0.66 us (3%)
    ppermute x8, starting transfers between devices, visit(): return lax.ppermute(x, AXES, pairs)  12.2 us
    ppermute x8, waiting for transfers between devices, visit(): return lax.ppermute(x, AXES, pairs)  4.71 us
    pallas_call x9, Pallas kernels, call(): pl.pallas_call(kernel, scratch_shapes=scratch, cost_estimate=cost, out_sh...  2.44 us
    ppermute x6, starting transfers between devices, swap(): return lax.ppermute(x, AXES, [(i, i ^ lanes) for i in range(n)])  1.98 us
    unnamed x6, local copies, waits for them, and re-layouts  0.66 us
  transfers between devices with their start and end apart: 14, of which 7 were waited for; matrix products, arithmetic and copies ran while one was open for 0% of the time, Pallas kernels for 2%

profile of v21, /device:TPU:0, one launch (start us, length us, event | category | flops | bytes accessed | tf_op | source)
XLA Modules:
  0.0 24.5 jit_solution(8453386350605236380)
XLA Ops:
  0.6 0.0 copy-start
  0.6 0.0 copy-start.1
  0.7 0.5 %collective-permute-start.2 = (s32[16]{0:T(128)}, s32[16]{0:T(128)S(1)}, u32[]{:S(2)}, u32[]{:S(2)}) collective-permute-start(s32[16]{0:T(128)} %class_ref.1), channel_id=1, source_target_pairs={{0,2},{1,3},{2,0},{3,1},{4,6},{5,7},{6,4},{7,5},{8,10},{9,11},{10,... | collective-permute-start | bytes 200 | tf_op jit(solution)/shard_map/ppermute | solution.py:338
  1.2 0.1 collective-permute-start
  1.2 0.4 %collective-permute-start.1 = (bf16[16,1152]{1,0:T(8,128)(2,1)}, bf16[16,1152]{1,0:T(8,128)(2,1)S(1)}, u32[]{:S(2)}, u32[]{:S(2)}) collective-permute-start(bf16[16,1152]{1,0:T(8,128)(2,1)} %text_ref.3), channel_id=1, source_target_pairs={{0,2},{1,3},{2,0},{3,1},{4,6},{5,7},{6,4},{7,5},{8,10},{9,11},{10,... | collective-permute-start | bytes 110600 | tf_op jit(solution)/shard_map/ppermute | solution.py:338
  1.7 0.0 copy-start.2
  1.7 0.7 %copy-done.2 = s32[16]{0:T(128)S(1)} copy-done((s32[16]{0:T(128)S(1)}, s32[16]{0:T(128)}, u32[]{:S(2)}) %copy-start.2) | copy-done | bytes 88
  2.3 0.1 digits.1.digits_ref
  2.4 0.0 copy-done
  2.4 0.0 copy-done.1
  2.4 0.1 pack.1.own_ref
  2.6 0.0 collective-permute-done.2.got_class
  2.6 0.0 collective-permute-done.got_image
  2.6 0.2 collective-permute-done.1.got_text
  2.8 0.2 join.1
  2.9 5.0 %collective-permute-start.5 = (bf16[32,1280]{1,0:T(8,128)(2,1)S(1)}, bf16[32,1280]{1,0:T(8,128)(2,1)S(1)}, u32[]{:S(2)}, u32[]{:S(2)}) collective-permute-start(bf16[32,1280]{1,0:T(8,128)(2,1)S(1)} %get-tuple-element.31), channel_id=1, source_target_pairs={{0,24},{1,25},{2,18},{3,19},{4,28},{5,29},{6,22},{7,23},{8,16},{9,... | collective-permute-start | bytes 245768 | tf_op jit(solution)/shard_map/ppermute | solution.py:335
  7.9 1.5 %collective-permute-start.6 = (bf16[32,1280]{1,0:T(8,128)(2,1)S(1)}, bf16[32,1280]{1,0:T(8,128)(2,1)S(1)}, u32[]{:S(2)}, u32[]{:S(2)}) collective-permute-start(bf16[32,1280]{1,0:T(8,128)(2,1)S(1)} %get-tuple-element.32), channel_id=1, source_target_pairs={{0,4},{1,5},{2,7},{3,6},{4,0},{5,1},{6,3},{7,2},{8,12},{9,13},{10,... | collective-permute-start | bytes 245768 | tf_op jit(solution)/shard_map/ppermute | solution.py:335
  9.4 0.0 collective-permute-start.3
  9.4 0.9 %collective-permute-start.4 = (bf16[32,1280]{1,0:T(8,128)(2,1)S(1)}, bf16[32,1280]{1,0:T(8,128)(2,1)S(1)}, u32[]{:S(2)}, u32[]{:S(2)}) collective-permute-start(bf16[32,1280]{1,0:T(8,128)(2,1)S(1)} %get-tuple-element.27), channel_id=1, source_target_pairs={{0,10},{1,11},{2,1},{3,0},{4,14},{5,15},{6,5},{7,4},{8,2},{9,3},{1... | collective-permute-start | bytes 245768 | tf_op jit(solution)/shard_map/ppermute | solution.py:335
  10.4 0.5 %collective-permute-done.5.upper_ref = bf16[32,1280]{1,0:T(8,128)(2,1)S(1)} collective-permute-done((bf16[32,1280]{1,0:T(8,128)(2,1)S(1)}, bf16[32,1280]{1,0:T(8,128)(2,1)S(1)}, u32[]{:S(2)}, u32[]{:S(2)}) %collective-permute-start.5) | collective-permute-done | bytes 81952 | tf_op jit(solution)/shard_map/ppermute | solution.py:335
  10.9 1.5 %collective-permute-done.6.lower_ref = bf16[32,1280]{1,0:T(8,128)(2,1)S(1)} collective-permute-done((bf16[32,1280]{1,0:T(8,128)(2,1)S(1)}, bf16[32,1280]{1,0:T(8,128)(2,1)S(1)}, u32[]{:S(2)}, u32[]{:S(2)}) %collective-permute-start.6) | collective-permute-done | bytes 81952 | tf_op jit(solution)/shard_map/ppermute | solution.py:335
  12.4 0.1 collective-permute-start.7
  13.8 0.1 collective-permute-done.3.upper_ref
  13.9 0.0 collective-permute-done.4.lower_ref
  13.9 0.0 collective-permute-done.7.swapped_ref
  13.9 0.8 %tile.1 = (s16[32,1280]{1,0:T(8,128)(2,1)S(1)}, s16[32,1280]{1,0:T(8,128)(2,1)S(1)}, s16[16,1280]{1,0:T(8,128)(2,1)S(1)}, s16[16,1280]{1,0:T(8,128)(2,1)S(1)}, s16[32,1280]{1,0:T(8,128)(2,1)S(1)}) custom-call(f32[8,128]{1,0:T(8,128)S(1)} %get-tuple-element.28.pair_ref, bf16[32,1280]{1,0:T(8,128)(2,1)S(1)} %get-tuple-element.29.mine_ref, ...), custom_call_target="tpu_custom_call" | custom-call | tf_op jit(solution)/shard_map/tile/pallas_call | solution.py:310
  14.7 2.3 %collective-permute-start.8 = (s16[32,1280]{1,0:T(8,128)(2,1)S(1)}, s16[32,1280]{1,0:T(8,128)(2,1)S(1)}, u32[]{:S(2)}, u32[]{:S(2)}) collective-permute-start(s16[32,1280]{1,0:T(8,128)(2,1)S(1)} %get-tuple-element.35), channel_id=1, source_target_pairs={{0,24},{1,25},{2,7},{3,6},{4,28},{5,29},{6,3},{7,2},{8,16},{9,17},... | collective-permute-start | bytes 245768 | tf_op jit(solution)/shard_map/ppermute | solution.py:335
  17.0 1.5 %collective-permute-start.9 = (s16[32,1280]{1,0:T(8,128)(2,1)S(1)}, s16[32,1280]{1,0:T(8,128)(2,1)S(1)}, u32[]{:S(2)}, u32[]{:S(2)}) collective-permute-start(s16[32,1280]{1,0:T(8,128)(2,1)S(1)} %get-tuple-element.38), channel_id=1, source_target_pairs={{0,4},{1,5},{2,18},{3,19},{4,0},{5,1},{6,22},{7,23},{8,12},{9,13},... | collective-permute-start | bytes 245768 | tf_op jit(solution)/shard_map/ppermute | solution.py:335
  18.5 0.0 collective-permute-start.11
  18.5 0.9 %collective-permute-start.12 = (s16[16,1280]{1,0:T(8,128)(2,1)S(1)}, s16[16,1280]{1,0:T(8,128)(2,1)S(1)}, u32[]{:S(2)}, u32[]{:S(2)}) collective-permute-start(s16[16,1280]{1,0:T(8,128)(2,1)S(1)} %get-tuple-element.41), channel_id=1, source_target_pairs={{0,10},{1,11},{2,1},{3,0},{4,14},{5,15},{6,5},{7,4},{8,2},{9,3},{1... | collective-permute-start | bytes 122888 | tf_op jit(solution)/shard_map/ppermute | solution.py:335
  19.4 2.1 %collective-permute-done.8.back_ref = s16[32,1280]{1,0:T(8,128)(2,1)S(1)} collective-permute-done((s16[32,1280]{1,0:T(8,128)(2,1)S(1)}, s16[32,1280]{1,0:T(8,128)(2,1)S(1)}, u32[]{:S(2)}, u32[]{:S(2)}) %collective-permute-start.8) | collective-permute-done | bytes 81952 | tf_op jit(solution)/shard_map/ppermute | solution.py:335
  21.6 0.2 add.1
  21.8 0.1 collective-permute-start.10
  21.8 0.0 collective-permute-done.9.back_ref
  21.9 0.8 %collective-permute-start.13 = (s16[32,1280]{1,0:T(8,128)(2,1)S(1)}, s16[32,1280]{1,0:T(8,128)(2,1)S(1)}, u32[]{:S(2)}, u32[]{:S(2)}) collective-permute-start(s16[32,1280]{1,0:T(8,128)(2,1)S(1)} %collective-permute-done.9.back_ref), channel_id=1, source_target_pairs={{0,2},{1,3},{2,0},{3,1},{4,6},{5,7},{6,4},{7,5},{8,10},{9,11},{10,... | collective-permute-start | bytes 245768 | tf_op jit(solution)/shard_map/ppermute | solution.py:338
  22.7 0.5 %collective-permute-done.11.same_ref = s16[16,1280]{1,0:T(8,128)(2,1)S(1)} collective-permute-done((s16[16,1280]{1,0:T(8,128)(2,1)S(1)}, s16[16,1280]{1,0:T(8,128)(2,1)S(1)}, u32[]{:S(2)}, u32[]{:S(2)}) %collective-permute-start.11) | collective-permute-done | bytes 40992 | tf_op jit(solution)/shard_map/ppermute | solution.py:335
  23.1 0.0 collective-permute-done.12.cross_ref
  23.1 0.0 collective-permute-done.10.got_ref
  23.1 0.2 more.1
  23.3 0.3 %collective-permute-done.13.got_ref = s16[32,1280]{1,0:T(8,128)(2,1)S(1)} collective-permute-done((s16[32,1280]{1,0:T(8,128)(2,1)S(1)}, s16[32,1280]{1,0:T(8,128)(2,1)S(1)}, u32[]{:S(2)}, u32[]{:S(2)}) %collective-permute-start.13) | collective-permute-done | bytes 81952 | tf_op jit(solution)/shard_map/ppermute | solution.py:338
  23.6 0.9 %final.1 = (f32[1,16]{1,0:T(1,128)}, f32[16,1152]{1,0:T(8,128)}, f32[16,1152]{1,0:T(8,128)}) custom-call(f32[2,16,1152]{2,1,0:T(8,128)S(1)} %get-tuple-element.42.sum_ref, f32[2,16,128]{2,1,0:T(8,128)S(1)} %get-tuple-element.43.sum_loss_ref, f32[2,16,1152]{2,1,0:T(8,128)S(1)} %get-tuple-element.44.unit_ref, f32[2,16,128]{2,1,0:T(8,128)S(1)} %get-tuple-element.45.inverse_ref, ...), custom_call_target="tpu_custom_call" | custom-call | tf_op jit(solution)/shard_map/final/pallas_call | solution.py:310
  (2 shorter events, 0.0 us)
Async XLA Ops:
  0.6 1.8 %copy-start = (bf16[16,1152]{1,0:T(8,128)(2,1)S(1)}, bf16[16,1152]{1,0:T(8,128)(2,1)}, u32[]{:S(2)}) copy-start(bf16[16,1152]{1,0:T(8,128)(2,1)} %image_ref.3) | copy-start | bytes 110596
  0.6 1.8 %copy-start.1 = (bf16[16,1152]{1,0:T(8,128)(2,1)S(1)}, bf16[16,1152]{1,0:T(8,128)(2,1)}, u32[]{:S(2)}) copy-start(bf16[16,1152]{1,0:T(8,128)(2,1)} %text_ref.3) | copy-start | bytes 110596
  0.7 1.9 %collective-permute-start.2 = (s32[16]{0:T(128)}, s32[16]{0:T(128)S(1)}, u32[]{:S(2)}, u32[]{:S(2)}) collective-permute-start(s32[16]{0:T(128)} %class_ref.1), channel_id=1, source_target_pairs={{0,2},{1,3},{2,0},{3,1},{4,6},{5,7},{6,4},{7,5},{8,10},{9,11},{10,... | collective-permute-start | bytes 200 | tf_op jit(solution)/shard_map/ppermute | solution.py:338
  1.2 1.4 %collective-permute-start = (bf16[16,1152]{1,0:T(8,128)(2,1)}, bf16[16,1152]{1,0:T(8,128)(2,1)S(1)}, u32[]{:S(2)}, u32[]{:S(2)}) collective-permute-start(bf16[16,1152]{1,0:T(8,128)(2,1)} %image_ref.3), channel_id=1, source_target_pairs={{0,2},{1,3},{2,0},{3,1},{4,6},{5,7},{6,4},{7,5},{8,10},{9,11},{10,... | collective-permute-start | bytes 110600 | tf_op jit(solution)/shard_map/ppermute | solution.py:338
  1.2 1.5 %collective-permute-start.1 = (bf16[16,1152]{1,0:T(8,128)(2,1)}, bf16[16,1152]{1,0:T(8,128)(2,1)S(1)}, u32[]{:S(2)}, u32[]{:S(2)}) collective-permute-start(bf16[16,1152]{1,0:T(8,128)(2,1)} %text_ref.3), channel_id=1, source_target_pairs={{0,2},{1,3},{2,0},{3,1},{4,6},{5,7},{6,4},{7,5},{8,10},{9,11},{10,... | collective-permute-start | bytes 110600 | tf_op jit(solution)/shard_map/ppermute | solution.py:338
  1.7 0.7 %copy-start.2 = (s32[16]{0:T(128)S(1)}, s32[16]{0:T(128)}, u32[]{:S(2)}) copy-start(s32[16]{0:T(128)} %class_ref.1) | copy-start | bytes 196
  2.9 7.9 %collective-permute-start.5 = (bf16[32,1280]{1,0:T(8,128)(2,1)S(1)}, bf16[32,1280]{1,0:T(8,128)(2,1)S(1)}, u32[]{:S(2)}, u32[]{:S(2)}) collective-permute-start(bf16[32,1280]{1,0:T(8,128)(2,1)S(1)} %get-tuple-element.31), channel_id=1, source_target_pairs={{0,24},{1,25},{2,18},{3,19},{4,28},{5,29},{6,22},{7,23},{8,16},{9,... | collective-permute-start | bytes 245768 | tf_op jit(solution)/shard_map/ppermute | solution.py:335
  7.9 4.4 %collective-permute-start.6 = (bf16[32,1280]{1,0:T(8,128)(2,1)S(1)}, bf16[32,1280]{1,0:T(8,128)(2,1)S(1)}, u32[]{:S(2)}, u32[]{:S(2)}) collective-permute-start(bf16[32,1280]{1,0:T(8,128)(2,1)S(1)} %get-tuple-element.32), channel_id=1, source_target_pairs={{0,4},{1,5},{2,7},{3,6},{4,0},{5,1},{6,3},{7,2},{8,12},{9,13},{10,... | collective-permute-start | bytes 245768 | tf_op jit(solution)/shard_map/ppermute | solution.py:335
  9.4 4.4 %collective-permute-start.3 = (bf16[32,1280]{1,0:T(8,128)(2,1)S(1)}, bf16[32,1280]{1,0:T(8,128)(2,1)S(1)}, u32[]{:S(2)}, u32[]{:S(2)}) collective-permute-start(bf16[32,1280]{1,0:T(8,128)(2,1)S(1)} %get-tuple-element.26), channel_id=1, source_target_pairs={{0,8},{1,9},{2,3},{3,2},{4,12},{5,13},{6,7},{7,6},{8,0},{9,1},{10,... | collective-permute-start | bytes 245768 | tf_op jit(solution)/shard_map/ppermute | solution.py:335
  9.4 4.4 %collective-permute-start.4 = (bf16[32,1280]{1,0:T(8,128)(2,1)S(1)}, bf16[32,1280]{1,0:T(8,128)(2,1)S(1)}, u32[]{:S(2)}, u32[]{:S(2)}) collective-permute-start(bf16[32,1280]{1,0:T(8,128)(2,1)S(1)} %get-tuple-element.27), channel_id=1, source_target_pairs={{0,10},{1,11},{2,1},{3,0},{4,14},{5,15},{6,5},{7,4},{8,2},{9,3},{1... | collective-permute-start | bytes 245768 | tf_op jit(solution)/shard_map/ppermute | solution.py:335
  12.4 1.5 %collective-permute-start.7 = (bf16[64,1280]{1,0:T(8,128)(2,1)S(1)}, bf16[64,1280]{1,0:T(8,128)(2,1)S(1)}, u32[]{:S(2)}, u32[]{:S(2)}) collective-permute-start(bf16[64,1280]{1,0:T(8,128)(2,1)S(1)} %far.1.far_ref), channel_id=1, source_target_pairs={{0,2},{1,3},{2,0},{3,1},{4,6},{5,7},{6,4},{7,5},{8,10},{9,11},{10,... | collective-permute-start | bytes 491528 | tf_op jit(solution)/shard_map/ppermute | solution.py:338
  14.7 6.9 %collective-permute-start.8 = (s16[32,1280]{1,0:T(8,128)(2,1)S(1)}, s16[32,1280]{1,0:T(8,128)(2,1)S(1)}, u32[]{:S(2)}, u32[]{:S(2)}) collective-permute-start(s16[32,1280]{1,0:T(8,128)(2,1)S(1)} %get-tuple-element.35), channel_id=1, source_target_pairs={{0,24},{1,25},{2,7},{3,6},{4,28},{5,29},{6,3},{7,2},{8,16},{9,17},... | collective-permute-start | bytes 245768 | tf_op jit(solution)/shard_map/ppermute | solution.py:335
  17.0 4.8 %collective-permute-start.9 = (s16[32,1280]{1,0:T(8,128)(2,1)S(1)}, s16[32,1280]{1,0:T(8,128)(2,1)S(1)}, u32[]{:S(2)}, u32[]{:S(2)}) collective-permute-start(s16[32,1280]{1,0:T(8,128)(2,1)S(1)} %get-tuple-element.38), channel_id=1, source_target_pairs={{0,4},{1,5},{2,18},{3,19},{4,0},{5,1},{6,22},{7,23},{8,12},{9,13},... | collective-permute-start | bytes 245768 | tf_op jit(solution)/shard_map/ppermute | solution.py:335
  18.5 4.6 %collective-permute-start.11 = (s16[16,1280]{1,0:T(8,128)(2,1)S(1)}, s16[16,1280]{1,0:T(8,128)(2,1)S(1)}, u32[]{:S(2)}, u32[]{:S(2)}) collective-permute-start(s16[16,1280]{1,0:T(8,128)(2,1)S(1)} %get-tuple-element.40), channel_id=1, source_target_pairs={{0,8},{1,9},{2,3},{3,2},{4,12},{5,13},{6,7},{7,6},{8,0},{9,1},{10,... | collective-permute-start | bytes 122888 | tf_op jit(solution)/shard_map/ppermute | solution.py:335
  18.5 4.6 %collective-permute-start.12 = (s16[16,1280]{1,0:T(8,128)(2,1)S(1)}, s16[16,1280]{1,0:T(8,128)(2,1)S(1)}, u32[]{:S(2)}, u32[]{:S(2)}) collective-permute-start(s16[16,1280]{1,0:T(8,128)(2,1)S(1)} %get-tuple-element.41), channel_id=1, source_target_pairs={{0,10},{1,11},{2,1},{3,0},{4,14},{5,15},{6,5},{7,4},{8,2},{9,3},{1... | collective-permute-start | bytes 122888 | tf_op jit(solution)/shard_map/ppermute | solution.py:335
  21.8 1.4 %collective-permute-start.10 = (s16[16,1280]{1,0:T(8,128)(2,1)S(1)}, s16[16,1280]{1,0:T(8,128)(2,1)S(1)}, u32[]{:S(2)}, u32[]{:S(2)}) collective-permute-start(s16[16,1280]{1,0:T(8,128)(2,1)S(1)} %get-tuple-element.39), channel_id=1, source_target_pairs={{0,2},{1,3},{2,0},{3,1},{4,6},{5,7},{6,4},{7,5},{8,10},{9,11},{10,... | collective-permute-start | bytes 122888 | tf_op jit(solution)/shard_map/ppermute | solution.py:338
  21.9 1.7 %collective-permute-start.13 = (s16[32,1280]{1,0:T(8,128)(2,1)S(1)}, s16[32,1280]{1,0:T(8,128)(2,1)S(1)}, u32[]{:S(2)}, u32[]{:S(2)}) collective-permute-start(s16[32,1280]{1,0:T(8,128)(2,1)S(1)} %collective-permute-done.9.back_ref), channel_id=1, source_target_pairs={{0,2},{1,3},{2,0},{3,1},{4,6},{5,7},{6,4},{7,5},{8,10},{9,11},{10,... | collective-permute-start | bytes 245768 | tf_op jit(solution)/shard_map/ppermute | solution.py:338

commit v22 on v21

--- a/solution.py
+++ b/solution.py
@@ -120,16 +120,14 @@
         ref[...] = block.astype(jnp.bfloat16)
 
 
-def far_kernel(upper_ref, lower_ref, out_ref):
+def near_kernel(upper_ref, lower_ref, out_ref):
     rows = upper_ref.shape[0]
     out_ref[:rows, :] = upper_ref[...]
     out_ref[rows:, :] = lower_ref[...]
 
 
-def near_kernel(scale_ref, shift_ref, upper_ref, lower_ref, out_ref, pair_ref):
-    rows = upper_ref.shape[0]
-    out_ref[:rows, :] = upper_ref[...]
-    out_ref[rows:, :] = lower_ref[...]
+def far_kernel(scale_ref, shift_ref, upper_ref, lower_ref, out_ref, pair_ref):
+    near_kernel(upper_ref, lower_ref, out_ref)
     row = lax.broadcasted_iota(jnp.int32, pair_ref.shape, 0)
     pair_ref[...] = jnp.where(row == 0, scale_ref[0], shift_ref[0])
 
@@ -357,15 +355,10 @@
         scratch=[pltpu.VMEM((2 * rows, width), jnp.bfloat16)],
     )
     got = [visit(x, *way) for x, way in zip(sent, out_visits)]
-    far = call(far_kernel, block(4), got[:2], "far")
-    near, pair = call(
-        near_kernel,
-        (block(4), wide(8, LANES)),
-        [scale[None], shift[None], *got[2:]],
-        "near",
-        2,
-        late,
-    )
+    far, pair = call(
+        far_kernel, (block(4), wide(8, LANES)), [scale[None], shift[None], *got[:2]], "far", 2
+    )
+    near = call(near_kernel, block(4), got[2:], "near", cost=late)
     one, two = block(1, jnp.int16), block(2, jnp.int16)
     parts = call(
         tile_kernel,

time: 24.7 us -> 24.8 us (level)
  waiting for transfers between devices: 5.2 us -> 5.54 us
  starting transfers between devices: 14.2 us -> 13.9 us
where the time goes in v22:
time: 24.8 us; the launch traced here: 24.6 us
  starting transfers between devices  13.9 us (56%)
  waiting for transfers between devices  5.54 us (22%)
  Pallas kernels  2.44 us (10%)
  between operations  2.04 us (8%)
  local copies, waits for them, and re-layouts  0.66 us (3%)
    ppermute x8, starting transfers between devices, visit(): return lax.ppermute(x, AXES, pairs)  12.1 us
    ppermute x8, waiting for transfers between devices, visit(): return lax.ppermute(x, AXES, pairs)  4.92 us
    pallas_call x9, Pallas kernels, call(): pl.pallas_call(kernel, scratch_shapes=scratch, cost_estimate=cost, out_sh...  2.44 us
    ppermute x6, starting transfers between devices, swap(): return lax.ppermute(x, AXES, [(i, i ^ lanes) for i in range(n)])  1.83 us
    unnamed x6, local copies, waits for them, and re-layouts  0.66 us
    ppermute x6, waiting for transfers between devices, swap(): return lax.ppermute(x, AXES, [(i, i ^ lanes) for i in range(n)])  0.63 us
  transfers between devices with their start and end apart: 14, of which 7 were waited for; matrix products, arithmetic and copies ran while one was open for 0% of the time, Pallas kernels for 2%

profile of v22, /device:TPU:0, one launch (start us, length us, event | category | flops | bytes accessed | tf_op | source)
XLA Modules:
  0.0 24.6 jit_solution(12682581836281819314)
XLA Ops:
  0.6 0.0 copy-start
  0.6 0.0 copy-start.1
  0.7 0.5 %collective-permute-start.2 = (s32[16]{0:T(128)}, s32[16]{0:T(128)S(1)}, u32[]{:S(2)}, u32[]{:S(2)}) collective-permute-start(s32[16]{0:T(128)} %class_ref.1), channel_id=1, source_target_pairs={{0,2},{1,3},{2,0},{3,1},{4,6},{5,7},{6,4},{7,5},{8,10},{9,11},{10,... | collective-permute-start | bytes 200 | tf_op jit(solution)/shard_map/ppermute | solution.py:336
  1.2 0.1 collective-permute-start
  1.2 0.4 %collective-permute-start.1 = (bf16[16,1152]{1,0:T(8,128)(2,1)}, bf16[16,1152]{1,0:T(8,128)(2,1)S(1)}, u32[]{:S(2)}, u32[]{:S(2)}) collective-permute-start(bf16[16,1152]{1,0:T(8,128)(2,1)} %text_ref.3), channel_id=1, source_target_pairs={{0,2},{1,3},{2,0},{3,1},{4,6},{5,7},{6,4},{7,5},{8,10},{9,11},{10,... | collective-permute-start | bytes 110600 | tf_op jit(solution)/shard_map/ppermute | solution.py:336
  1.7 0.0 copy-start.2
  1.7 0.7 %copy-done.2 = s32[16]{0:T(128)S(1)} copy-done((s32[16]{0:T(128)S(1)}, s32[16]{0:T(128)}, u32[]{:S(2)}) %copy-start.2) | copy-done | bytes 88
  2.3 0.1 digits.1.digits_ref
  2.4 0.0 copy-done
  2.4 0.0 copy-done.1
  2.4 0.1 pack.1.own_ref
  2.6 0.0 collective-permute-done.2.got_class
  2.6 0.0 collective-permute-done.got_image
  2.6 0.2 collective-permute-done.1.got_text
  2.8 0.2 join.1
  2.9 5.0 %collective-permute-start.3 = (bf16[32,1280]{1,0:T(8,128)(2,1)S(1)}, bf16[32,1280]{1,0:T(8,128)(2,1)S(1)}, u32[]{:S(2)}, u32[]{:S(2)}) collective-permute-start(bf16[32,1280]{1,0:T(8,128)(2,1)S(1)} %get-tuple-element.26), channel_id=1, source_target_pairs={{0,24},{1,25},{2,18},{3,19},{4,28},{5,29},{6,22},{7,23},{8,16},{9,... | collective-permute-start | bytes 245768 | tf_op jit(solution)/shard_map/ppermute | solution.py:333
  7.9 1.5 %collective-permute-start.4 = (bf16[32,1280]{1,0:T(8,128)(2,1)S(1)}, bf16[32,1280]{1,0:T(8,128)(2,1)S(1)}, u32[]{:S(2)}, u32[]{:S(2)}) collective-permute-start(bf16[32,1280]{1,0:T(8,128)(2,1)S(1)} %get-tuple-element.27), channel_id=1, source_target_pairs={{0,4},{1,5},{2,7},{3,6},{4,0},{5,1},{6,3},{7,2},{8,12},{9,13},{10,... | collective-permute-start | bytes 245768 | tf_op jit(solution)/shard_map/ppermute | solution.py:333
  9.4 0.0 collective-permute-start.6
  9.4 0.9 %collective-permute-start.7 = (bf16[32,1280]{1,0:T(8,128)(2,1)S(1)}, bf16[32,1280]{1,0:T(8,128)(2,1)S(1)}, u32[]{:S(2)}, u32[]{:S(2)}) collective-permute-start(bf16[32,1280]{1,0:T(8,128)(2,1)S(1)} %get-tuple-element.33), channel_id=1, source_target_pairs={{0,10},{1,11},{2,1},{3,0},{4,14},{5,15},{6,5},{7,4},{8,2},{9,3},{1... | collective-permute-start | bytes 245768 | tf_op jit(solution)/shard_map/ppermute | solution.py:333
  11.7 0.0 collective-permute-done.3.upper_ref
  11.7 0.7 %collective-permute-done.4.lower_ref = bf16[32,1280]{1,0:T(8,128)(2,1)S(1)} collective-permute-done((bf16[32,1280]{1,0:T(8,128)(2,1)S(1)}, bf16[32,1280]{1,0:T(8,128)(2,1)S(1)}, u32[]{:S(2)}, u32[]{:S(2)}) %collective-permute-start.4) | collective-permute-done | bytes 81952 | tf_op jit(solution)/shard_map/ppermute | solution.py:333
  12.4 0.1 collective-permute-start.5
  12.5 1.4 %collective-permute-done.6.upper_ref = bf16[32,1280]{1,0:T(8,128)(2,1)S(1)} collective-permute-done((bf16[32,1280]{1,0:T(8,128)(2,1)S(1)}, bf16[32,1280]{1,0:T(8,128)(2,1)S(1)}, u32[]{:S(2)}, u32[]{:S(2)}) %collective-permute-start.6) | collective-permute-done | bytes 81952 | tf_op jit(solution)/shard_map/ppermute | solution.py:333
  13.9 0.0 collective-permute-done.7.lower_ref
  13.9 0.0 collective-permute-done.5.swapped_ref
  13.9 0.8 %tile.1 = (s16[32,1280]{1,0:T(8,128)(2,1)S(1)}, s16[32,1280]{1,0:T(8,128)(2,1)S(1)}, s16[16,1280]{1,0:T(8,128)(2,1)S(1)}, s16[16,1280]{1,0:T(8,128)(2,1)S(1)}, s16[32,1280]{1,0:T(8,128)(2,1)S(1)}) custom-call(f32[8,128]{1,0:T(8,128)S(1)} %get-tuple-element.28.pair_ref, bf16[32,1280]{1,0:T(8,128)(2,1)S(1)} %get-tuple-element.29.mine_ref, ...), custom_call_target="tpu_custom_call" | custom-call | tf_op jit(solution)/shard_map/tile/pallas_call | solution.py:308
  14.7 2.0 %collective-permute-start.8 = (s16[32,1280]{1,0:T(8,128)(2,1)S(1)}, s16[32,1280]{1,0:T(8,128)(2,1)S(1)}, u32[]{:S(2)}, u32[]{:S(2)}) collective-permute-start(s16[32,1280]{1,0:T(8,128)(2,1)S(1)} %get-tuple-element.35), channel_id=1, source_target_pairs={{0,24},{1,25},{2,7},{3,6},{4,28},{5,29},{6,3},{7,2},{8,16},{9,17},... | collective-permute-start | bytes 245768 | tf_op jit(solution)/shard_map/ppermute | solution.py:333
  16.7 1.5 %collective-permute-start.9 = (s16[32,1280]{1,0:T(8,128)(2,1)S(1)}, s16[32,1280]{1,0:T(8,128)(2,1)S(1)}, u32[]{:S(2)}, u32[]{:S(2)}) collective-permute-start(s16[32,1280]{1,0:T(8,128)(2,1)S(1)} %get-tuple-element.38), channel_id=1, source_target_pairs={{0,4},{1,5},{2,18},{3,19},{4,0},{5,1},{6,22},{7,23},{8,12},{9,13},... | collective-permute-start | bytes 245768 | tf_op jit(solution)/shard_map/ppermute | solution.py:333
  18.2 0.0 collective-permute-start.11
  18.2 1.2 %collective-permute-start.12 = (s16[16,1280]{1,0:T(8,128)(2,1)S(1)}, s16[16,1280]{1,0:T(8,128)(2,1)S(1)}, u32[]{:S(2)}, u32[]{:S(2)}) collective-permute-start(s16[16,1280]{1,0:T(8,128)(2,1)S(1)} %get-tuple-element.41), channel_id=1, source_target_pairs={{0,10},{1,11},{2,1},{3,0},{4,14},{5,15},{6,5},{7,4},{8,2},{9,3},{1... | collective-permute-start | bytes 122888 | tf_op jit(solution)/shard_map/ppermute | solution.py:333
  19.3 2.5 %collective-permute-done.8.back_ref = s16[32,1280]{1,0:T(8,128)(2,1)S(1)} collective-permute-done((s16[32,1280]{1,0:T(8,128)(2,1)S(1)}, s16[32,1280]{1,0:T(8,128)(2,1)S(1)}, u32[]{:S(2)}, u32[]{:S(2)}) %collective-permute-start.8) | collective-permute-done | bytes 81952 | tf_op jit(solution)/shard_map/ppermute | solution.py:333
  21.8 0.2 add.1
  22.1 0.1 collective-permute-start.10
  22.1 0.0 collective-permute-done.9.back_ref
  22.1 0.7 %collective-permute-start.13 = (s16[32,1280]{1,0:T(8,128)(2,1)S(1)}, s16[32,1280]{1,0:T(8,128)(2,1)S(1)}, u32[]{:S(2)}, u32[]{:S(2)}) collective-permute-start(s16[32,1280]{1,0:T(8,128)(2,1)S(1)} %collective-permute-done.9.back_ref), channel_id=1, source_target_pairs={{0,2},{1,3},{2,0},{3,1},{4,6},{5,7},{6,4},{7,5},{8,10},{9,11},{10,... | collective-permute-start | bytes 245768 | tf_op jit(solution)/shard_map/ppermute | solution.py:336
  22.8 0.3 %collective-permute-done.11.same_ref = s16[16,1280]{1,0:T(8,128)(2,1)S(1)} collective-permute-done((s16[16,1280]{1,0:T(8,128)(2,1)S(1)}, s16[16,1280]{1,0:T(8,128)(2,1)S(1)}, u32[]{:S(2)}, u32[]{:S(2)}) %collective-permute-start.11) | collective-permute-done | bytes 40992 | tf_op jit(solution)/shard_map/ppermute | solution.py:333
  23.1 0.0 collective-permute-done.12.cross_ref
  23.1 0.2 collective-permute-done.10.got_ref
  23.3 0.2 more.1
  23.5 0.2 collective-permute-done.13.got_ref
  23.7 0.9 %final.1 = (f32[1,16]{1,0:T(1,128)}, f32[16,1152]{1,0:T(8,128)}, f32[16,1152]{1,0:T(8,128)}) custom-call(f32[2,16,1152]{2,1,0:T(8,128)S(1)} %get-tuple-element.42.sum_ref, f32[2,16,128]{2,1,0:T(8,128)S(1)} %get-tuple-element.43.sum_loss_ref, f32[2,16,1152]{2,1,0:T(8,128)S(1)} %get-tuple-element.44.unit_ref, f32[2,16,128]{2,1,0:T(8,128)S(1)} %get-tuple-element.45.inverse_ref, ...), custom_call_target="tpu_custom_call" | custom-call | tf_op jit(solution)/shard_map/final/pallas_call | solution.py:308
  (2 shorter events, 0.0 us)
Async XLA Ops:
  0.6 1.8 %copy-start = (bf16[16,1152]{1,0:T(8,128)(2,1)S(1)}, bf16[16,1152]{1,0:T(8,128)(2,1)}, u32[]{:S(2)}) copy-start(bf16[16,1152]{1,0:T(8,128)(2,1)} %image_ref.3) | copy-start | bytes 110596
  0.6 1.8 %copy-start.1 = (bf16[16,1152]{1,0:T(8,128)(2,1)S(1)}, bf16[16,1152]{1,0:T(8,128)(2,1)}, u32[]{:S(2)}) copy-start(bf16[16,1152]{1,0:T(8,128)(2,1)} %text_ref.3) | copy-start | bytes 110596
  0.7 1.9 %collective-permute-start.2 = (s32[16]{0:T(128)}, s32[16]{0:T(128)S(1)}, u32[]{:S(2)}, u32[]{:S(2)}) collective-permute-start(s32[16]{0:T(128)} %class_ref.1), channel_id=1, source_target_pairs={{0,2},{1,3},{2,0},{3,1},{4,6},{5,7},{6,4},{7,5},{8,10},{9,11},{10,... | collective-permute-start | bytes 200 | tf_op jit(solution)/shard_map/ppermute | solution.py:336
  1.2 1.4 %collective-permute-start = (bf16[16,1152]{1,0:T(8,128)(2,1)}, bf16[16,1152]{1,0:T(8,128)(2,1)S(1)}, u32[]{:S(2)}, u32[]{:S(2)}) collective-permute-start(bf16[16,1152]{1,0:T(8,128)(2,1)} %image_ref.3), channel_id=1, source_target_pairs={{0,2},{1,3},{2,0},{3,1},{4,6},{5,7},{6,4},{7,5},{8,10},{9,11},{10,... | collective-permute-start | bytes 110600 | tf_op jit(solution)/shard_map/ppermute | solution.py:336
  1.2 1.5 %collective-permute-start.1 = (bf16[16,1152]{1,0:T(8,128)(2,1)}, bf16[16,1152]{1,0:T(8,128)(2,1)S(1)}, u32[]{:S(2)}, u32[]{:S(2)}) collective-permute-start(bf16[16,1152]{1,0:T(8,128)(2,1)} %text_ref.3), channel_id=1, source_target_pairs={{0,2},{1,3},{2,0},{3,1},{4,6},{5,7},{6,4},{7,5},{8,10},{9,11},{10,... | collective-permute-start | bytes 110600 | tf_op jit(solution)/shard_map/ppermute | solution.py:336
  1.7 0.7 %copy-start.2 = (s32[16]{0:T(128)S(1)}, s32[16]{0:T(128)}, u32[]{:S(2)}) copy-start(s32[16]{0:T(128)} %class_ref.1) | copy-start | bytes 196
  2.9 8.8 %collective-permute-start.3 = (bf16[32,1280]{1,0:T(8,128)(2,1)S(1)}, bf16[32,1280]{1,0:T(8,128)(2,1)S(1)}, u32[]{:S(2)}, u32[]{:S(2)}) collective-permute-start(bf16[32,1280]{1,0:T(8,128)(2,1)S(1)} %get-tuple-element.26), channel_id=1, source_target_pairs={{0,24},{1,25},{2,18},{3,19},{4,28},{5,29},{6,22},{7,23},{8,16},{9,... | collective-permute-start | bytes 245768 | tf_op jit(solution)/shard_map/ppermute | solution.py:333
  7.9 4.4 %collective-permute-start.4 = (bf16[32,1280]{1,0:T(8,128)(2,1)S(1)}, bf16[32,1280]{1,0:T(8,128)(2,1)S(1)}, u32[]{:S(2)}, u32[]{:S(2)}) collective-permute-start(bf16[32,1280]{1,0:T(8,128)(2,1)S(1)} %get-tuple-element.27), channel_id=1, source_target_pairs={{0,4},{1,5},{2,7},{3,6},{4,0},{5,1},{6,3},{7,2},{8,12},{9,13},{10,... | collective-permute-start | bytes 245768 | tf_op jit(solution)/shard_map/ppermute | solution.py:333
  9.4 4.4 %collective-permute-start.6 = (bf16[32,1280]{1,0:T(8,128)(2,1)S(1)}, bf16[32,1280]{1,0:T(8,128)(2,1)S(1)}, u32[]{:S(2)}, u32[]{:S(2)}) collective-permute-start(bf16[32,1280]{1,0:T(8,128)(2,1)S(1)} %get-tuple-element.32), channel_id=1, source_target_pairs={{0,8},{1,9},{2,3},{3,2},{4,12},{5,13},{6,7},{7,6},{8,0},{9,1},{10,... | collective-permute-start | bytes 245768 | tf_op jit(solution)/shard_map/ppermute | solution.py:333
  9.4 4.4 %collective-permute-start.7 = (bf16[32,1280]{1,0:T(8,128)(2,1)S(1)}, bf16[32,1280]{1,0:T(8,128)(2,1)S(1)}, u32[]{:S(2)}, u32[]{:S(2)}) collective-permute-start(bf16[32,1280]{1,0:T(8,128)(2,1)S(1)} %get-tuple-element.33), channel_id=1, source_target_pairs={{0,10},{1,11},{2,1},{3,0},{4,14},{5,15},{6,5},{7,4},{8,2},{9,3},{1... | collective-permute-start | bytes 245768 | tf_op jit(solution)/shard_map/ppermute | solution.py:333
  12.4 1.5 %collective-permute-start.5 = (bf16[64,1280]{1,0:T(8,128)(2,1)S(1)}, bf16[64,1280]{1,0:T(8,128)(2,1)S(1)}, u32[]{:S(2)}, u32[]{:S(2)}) collective-permute-start(bf16[64,1280]{1,0:T(8,128)(2,1)S(1)} %get-tuple-element.31.far_ref), channel_id=1, source_target_pairs={{0,2},{1,3},{2,0},{3,1},{4,6},{5,7},{6,4},{7,5},{8,10},{9,11},{10,... | collective-permute-start | bytes 491528 | tf_op jit(solution)/shard_map/ppermute | solution.py:336
  14.7 7.2 %collective-permute-start.8 = (s16[32,1280]{1,0:T(8,128)(2,1)S(1)}, s16[32,1280]{1,0:T(8,128)(2,1)S(1)}, u32[]{:S(2)}, u32[]{:S(2)}) collective-permute-start(s16[32,1280]{1,0:T(8,128)(2,1)S(1)} %get-tuple-element.35), channel_id=1, source_target_pairs={{0,24},{1,25},{2,7},{3,6},{4,28},{5,29},{6,3},{7,2},{8,16},{9,17},... | collective-permute-start | bytes 245768 | tf_op jit(solution)/shard_map/ppermute | solution.py:333
  16.7 5.5 %collective-permute-start.9 = (s16[32,1280]{1,0:T(8,128)(2,1)S(1)}, s16[32,1280]{1,0:T(8,128)(2,1)S(1)}, u32[]{:S(2)}, u32[]{:S(2)}) collective-permute-start(s16[32,1280]{1,0:T(8,128)(2,1)S(1)} %get-tuple-element.38), channel_id=1, source_target_pairs={{0,4},{1,5},{2,18},{3,19},{4,0},{5,1},{6,22},{7,23},{8,12},{9,13},... | collective-permute-start | bytes 245768 | tf_op jit(solution)/shard_map/ppermute | solution.py:333
  18.2 4.9 %collective-permute-start.11 = (s16[16,1280]{1,0:T(8,128)(2,1)S(1)}, s16[16,1280]{1,0:T(8,128)(2,1)S(1)}, u32[]{:S(2)}, u32[]{:S(2)}) collective-permute-start(s16[16,1280]{1,0:T(8,128)(2,1)S(1)} %get-tuple-element.40), channel_id=1, source_target_pairs={{0,8},{1,9},{2,3},{3,2},{4,12},{5,13},{6,7},{7,6},{8,0},{9,1},{10,... | collective-permute-start | bytes 122888 | tf_op jit(solution)/shard_map/ppermute | solution.py:333
  18.2 4.9 %collective-permute-start.12 = (s16[16,1280]{1,0:T(8,128)(2,1)S(1)}, s16[16,1280]{1,0:T(8,128)(2,1)S(1)}, u32[]{:S(2)}, u32[]{:S(2)}) collective-permute-start(s16[16,1280]{1,0:T(8,128)(2,1)S(1)} %get-tuple-element.41), channel_id=1, source_target_pairs={{0,10},{1,11},{2,1},{3,0},{4,14},{5,15},{6,5},{7,4},{8,2},{9,3},{1... | collective-permute-start | bytes 122888 | tf_op jit(solution)/shard_map/ppermute | solution.py:333
  22.1 1.3 %collective-permute-start.10 = (s16[16,1280]{1,0:T(8,128)(2,1)S(1)}, s16[16,1280]{1,0:T(8,128)(2,1)S(1)}, u32[]{:S(2)}, u32[]{:S(2)}) collective-permute-start(s16[16,1280]{1,0:T(8,128)(2,1)S(1)} %get-tuple-element.39), channel_id=1, source_target_pairs={{0,2},{1,3},{2,0},{3,1},{4,6},{5,7},{6,4},{7,5},{8,10},{9,11},{10,... | collective-permute-start | bytes 122888 | tf_op jit(solution)/shard_map/ppermute | solution.py:336
  22.1 1.6 %collective-permute-start.13 = (s16[32,1280]{1,0:T(8,128)(2,1)S(1)}, s16[32,1280]{1,0:T(8,128)(2,1)S(1)}, u32[]{:S(2)}, u32[]{:S(2)}) collective-permute-start(s16[32,1280]{1,0:T(8,128)(2,1)S(1)} %collective-permute-done.9.back_ref), channel_id=1, source_target_pairs={{0,2},{1,3},{2,0},{3,1},{4,6},{5,7},{6,4},{7,5},{8,10},{9,11},{10,... | collective-permute-start | bytes 245768 | tf_op jit(solution)/shard_map/ppermute | solution.py:336

commit v23 on v21

--- a/solution.py
+++ b/solution.py
@@ -262,6 +262,11 @@
     loss_ref[...] = jnp.broadcast_to(loss, loss_ref.shape)
 
 
+def give_kernel(back_ref, give_ref):
+    _, other = place_of(on_first_core(), give_ref.shape[0])
+    give_ref[...] = back_ref[other, :]
+
+
 def more_kernel(keep_ref, kept_loss_ref, back_ref, got_ref, same_ref, cross_ref, image_ref, text_ref, *outs):
     sum_ref, sum_loss_ref, unit_ref, inverse_ref = outs
     rows, depth = keep_ref.shape
@@ -280,8 +285,7 @@
 def final_kernel(pairs, sum_ref, sum_loss_ref, unit_ref, inverse_ref, got_ref, loss_ref, grad_image_ref, grad_text_ref):
     first = on_first_core()
     rows, depth = sum_ref.shape[1:]
-    own, _ = place_of(first, rows)
-    pull, loss = total([got_ref[own, :]], rows, depth)
+    pull, loss = total([got_ref], rows, depth)
     pulls = (sum_ref[0] + pull, sum_ref[1])
     losses = (sum_loss_ref[0][:, 0:1] + loss, sum_loss_ref[1][:, 0:1])
     for side, (pull, out) in enumerate(
@@ -387,7 +391,7 @@
     loss, grad_image, grad_text = call(
         functools.partial(final_kernel, n * rows),
         (wide(1, rows), wide(rows, depth), wide(rows, depth)),
-        [*sums, swap(back[1])],
+        [*sums, swap(call(give_kernel, one, [back[1]], "give"))],
         "final",
     )
     return (loss[0], grad_image, grad_text)

time: 24.7 us -> 24.6 us (level)
    pallas_call x9 -> x10, Pallas kernels: 2.44 us -> 2.46 us  [call(): pl.pallas_call(kernel, scratch_shapes=scratch, cost_estimate=cost, out_sh...]
  transfers between devices with their start and end apart: 14 -> 14, of which waited for: 7 -> 7; matrix products, arithmetic and copies ran while one was open for 0% -> 0% of each run, Pallas kernels for 2% -> 3%
where the time goes in v23:
time: 24.6 us; the launch traced here: 24.4 us
  starting transfers between devices  14.1 us (57%)
  waiting for transfers between devices  5.14 us (21%)
  Pallas kernels  2.46 us (10%)
  between operations  2.05 us (8%)
  local copies, waits for them, and re-layouts  0.66 us (3%)
    ppermute x8, starting transfers between devices, visit(): return lax.ppermute(x, AXES, pairs)  12.2 us
    ppermute x8, waiting for transfers between devices, visit(): return lax.ppermute(x, AXES, pairs)  4.71 us
    pallas_call x10, Pallas kernels, call(): pl.pallas_call(kernel, scratch_shapes=scratch, cost_estimate=cost, out_sh...  2.46 us
    ppermute x6, starting transfers between devices, swap(): return lax.ppermute(x, AXES, [(i, i ^ lanes) for i in range(n)])  1.96 us
    unnamed x6, local copies, waits for them, and re-layouts  0.66 us
  transfers between devices with their start and end apart: 14, of which 7 were waited for; matrix products, arithmetic and copies ran while one was open for 0% of the time, Pallas kernels for 3%

profile of v23, /device:TPU:0, one launch (start us, length us, event | category | flops | bytes accessed | tf_op | source)
XLA Modules:
  0.0 24.4 jit_solution(16937957616205602702)
XLA Ops:
  0.6 0.0 copy-start
  0.6 0.0 copy-start.1
  0.7 0.5 %collective-permute-start.2 = (s32[16]{0:T(128)}, s32[16]{0:T(128)S(1)}, u32[]{:S(2)}, u32[]{:S(2)}) collective-permute-start(s32[16]{0:T(128)} %class_ref.1), channel_id=1, source_target_pairs={{0,2},{1,3},{2,0},{3,1},{4,6},{5,7},{6,4},{7,5},{8,10},{9,11},{10,... | collective-permute-start | bytes 200 | tf_op jit(solution)/shard_map/ppermute | solution.py:342
  1.2 0.1 collective-permute-start
  1.2 0.4 %collective-permute-start.1 = (bf16[16,1152]{1,0:T(8,128)(2,1)}, bf16[16,1152]{1,0:T(8,128)(2,1)S(1)}, u32[]{:S(2)}, u32[]{:S(2)}) collective-permute-start(bf16[16,1152]{1,0:T(8,128)(2,1)} %text_ref.3), channel_id=1, source_target_pairs={{0,2},{1,3},{2,0},{3,1},{4,6},{5,7},{6,4},{7,5},{8,10},{9,11},{10,... | collective-permute-start | bytes 110600 | tf_op jit(solution)/shard_map/ppermute | solution.py:342
  1.7 0.0 copy-start.2
  1.7 0.7 %copy-done.2 = s32[16]{0:T(128)S(1)} copy-done((s32[16]{0:T(128)S(1)}, s32[16]{0:T(128)}, u32[]{:S(2)}) %copy-start.2) | copy-done | bytes 88
  2.3 0.1 digits.1.digits_ref
  2.4 0.0 copy-done
  2.4 0.0 copy-done.1
  2.4 0.1 pack.1.own_ref
  2.6 0.0 collective-permute-done.2.got_class
  2.6 0.0 collective-permute-done.got_image
  2.6 0.2 collective-permute-done.1.got_text
  2.8 0.2 join.1
  2.9 5.0 %collective-permute-start.5 = (bf16[32,1280]{1,0:T(8,128)(2,1)S(1)}, bf16[32,1280]{1,0:T(8,128)(2,1)S(1)}, u32[]{:S(2)}, u32[]{:S(2)}) collective-permute-start(bf16[32,1280]{1,0:T(8,128)(2,1)S(1)} %get-tuple-element.31), channel_id=1, source_target_pairs={{0,24},{1,25},{2,18},{3,19},{4,28},{5,29},{6,22},{7,23},{8,16},{9,... | collective-permute-start | bytes 245768 | tf_op jit(solution)/shard_map/ppermute | solution.py:339
  7.9 1.5 %collective-permute-start.6 = (bf16[32,1280]{1,0:T(8,128)(2,1)S(1)}, bf16[32,1280]{1,0:T(8,128)(2,1)S(1)}, u32[]{:S(2)}, u32[]{:S(2)}) collective-permute-start(bf16[32,1280]{1,0:T(8,128)(2,1)S(1)} %get-tuple-element.32), channel_id=1, source_target_pairs={{0,4},{1,5},{2,7},{3,6},{4,0},{5,1},{6,3},{7,2},{8,12},{9,13},{10,... | collective-permute-start | bytes 245768 | tf_op jit(solution)/shard_map/ppermute | solution.py:339
  9.4 0.0 collective-permute-start.3
  9.4 0.9 %collective-permute-start.4 = (bf16[32,1280]{1,0:T(8,128)(2,1)S(1)}, bf16[32,1280]{1,0:T(8,128)(2,1)S(1)}, u32[]{:S(2)}, u32[]{:S(2)}) collective-permute-start(bf16[32,1280]{1,0:T(8,128)(2,1)S(1)} %get-tuple-element.27), channel_id=1, source_target_pairs={{0,10},{1,11},{2,1},{3,0},{4,14},{5,15},{6,5},{7,4},{8,2},{9,3},{1... | collective-permute-start | bytes 245768 | tf_op jit(solution)/shard_map/ppermute | solution.py:339
  10.4 0.5 %collective-permute-done.5.upper_ref = bf16[32,1280]{1,0:T(8,128)(2,1)S(1)} collective-permute-done((bf16[32,1280]{1,0:T(8,128)(2,1)S(1)}, bf16[32,1280]{1,0:T(8,128)(2,1)S(1)}, u32[]{:S(2)}, u32[]{:S(2)}) %collective-permute-start.5) | collective-permute-done | bytes 81952 | tf_op jit(solution)/shard_map/ppermute | solution.py:339
  10.9 1.5 %collective-permute-done.6.lower_ref = bf16[32,1280]{1,0:T(8,128)(2,1)S(1)} collective-permute-done((bf16[32,1280]{1,0:T(8,128)(2,1)S(1)}, bf16[32,1280]{1,0:T(8,128)(2,1)S(1)}, u32[]{:S(2)}, u32[]{:S(2)}) %collective-permute-start.6) | collective-permute-done | bytes 81952 | tf_op jit(solution)/shard_map/ppermute | solution.py:339
  12.4 0.1 collective-permute-start.7
  13.8 0.1 collective-permute-done.3.upper_ref
  13.9 0.0 collective-permute-done.4.lower_ref
  13.9 0.0 collective-permute-done.7.swapped_ref
  13.9 0.8 %tile.1 = (s16[32,1280]{1,0:T(8,128)(2,1)S(1)}, s16[32,1280]{1,0:T(8,128)(2,1)S(1)}, s16[16,1280]{1,0:T(8,128)(2,1)S(1)}, s16[16,1280]{1,0:T(8,128)(2,1)S(1)}, s16[32,1280]{1,0:T(8,128)(2,1)S(1)}) custom-call(f32[8,128]{1,0:T(8,128)S(1)} %get-tuple-element.28.pair_ref, bf16[32,1280]{1,0:T(8,128)(2,1)S(1)} %get-tuple-element.29.mine_ref, ...), custom_call_target="tpu_custom_call" | custom-call | tf_op jit(solution)/shard_map/tile/pallas_call | solution.py:314
  14.7 2.3 %collective-permute-start.8 = (s16[32,1280]{1,0:T(8,128)(2,1)S(1)}, s16[32,1280]{1,0:T(8,128)(2,1)S(1)}, u32[]{:S(2)}, u32[]{:S(2)}) collective-permute-start(s16[32,1280]{1,0:T(8,128)(2,1)S(1)} %get-tuple-element.35), channel_id=1, source_target_pairs={{0,24},{1,25},{2,7},{3,6},{4,28},{5,29},{6,3},{7,2},{8,16},{9,17},... | collective-permute-start | bytes 245768 | tf_op jit(solution)/shard_map/ppermute | solution.py:339
  17.0 1.5 %collective-permute-start.9 = (s16[32,1280]{1,0:T(8,128)(2,1)S(1)}, s16[32,1280]{1,0:T(8,128)(2,1)S(1)}, u32[]{:S(2)}, u32[]{:S(2)}) collective-permute-start(s16[32,1280]{1,0:T(8,128)(2,1)S(1)} %get-tuple-element.38), channel_id=1, source_target_pairs={{0,4},{1,5},{2,18},{3,19},{4,0},{5,1},{6,22},{7,23},{8,12},{9,13},... | collective-permute-start | bytes 245768 | tf_op jit(solution)/shard_map/ppermute | solution.py:339
  18.5 0.0 collective-permute-start.11
  18.5 0.9 %collective-permute-start.12 = (s16[16,1280]{1,0:T(8,128)(2,1)S(1)}, s16[16,1280]{1,0:T(8,128)(2,1)S(1)}, u32[]{:S(2)}, u32[]{:S(2)}) collective-permute-start(s16[16,1280]{1,0:T(8,128)(2,1)S(1)} %get-tuple-element.41), channel_id=1, source_target_pairs={{0,10},{1,11},{2,1},{3,0},{4,14},{5,15},{6,5},{7,4},{8,2},{9,3},{1... | collective-permute-start | bytes 122888 | tf_op jit(solution)/shard_map/ppermute | solution.py:339
  19.4 2.1 %collective-permute-done.8.back_ref = s16[32,1280]{1,0:T(8,128)(2,1)S(1)} collective-permute-done((s16[32,1280]{1,0:T(8,128)(2,1)S(1)}, s16[32,1280]{1,0:T(8,128)(2,1)S(1)}, u32[]{:S(2)}, u32[]{:S(2)}) %collective-permute-start.8) | collective-permute-done | bytes 81952 | tf_op jit(solution)/shard_map/ppermute | solution.py:339
  21.6 0.2 add.1
  21.8 0.1 collective-permute-start.10
  21.8 0.0 collective-permute-done.9.back_ref
  21.9 0.8 %collective-permute-start.13 = (s16[16,1280]{1,0:T(8,128)(2,1)S(1)}, s16[16,1280]{1,0:T(8,128)(2,1)S(1)}, u32[]{:S(2)}, u32[]{:S(2)}) collective-permute-start(s16[16,1280]{1,0:T(8,128)(2,1)S(1)} %give.1), channel_id=1, source_target_pairs={{0,2},{1,3},{2,0},{3,1},{4,6},{5,7},{6,4},{7,5},{8,10},{9,11},{10,... | collective-permute-start | bytes 122888 | tf_op jit(solution)/shard_map/ppermute | solution.py:342
  22.7 0.5 %collective-permute-done.11.same_ref = s16[16,1280]{1,0:T(8,128)(2,1)S(1)} collective-permute-done((s16[16,1280]{1,0:T(8,128)(2,1)S(1)}, s16[16,1280]{1,0:T(8,128)(2,1)S(1)}, u32[]{:S(2)}, u32[]{:S(2)}) %collective-permute-start.11) | collective-permute-done | bytes 40992 | tf_op jit(solution)/shard_map/ppermute | solution.py:339
  23.1 0.0 collective-permute-done.12.cross_ref
  23.1 0.0 collective-permute-done.10.got_ref
  23.1 0.2 more.1
  23.3 0.2 collective-permute-done.13.got_ref
  23.5 0.9 %final.1 = (f32[1,16]{1,0:T(1,128)}, f32[16,1152]{1,0:T(8,128)}, f32[16,1152]{1,0:T(8,128)}) custom-call(f32[2,16,1152]{2,1,0:T(8,128)S(1)} %get-tuple-element.42.sum_ref, f32[2,16,128]{2,1,0:T(8,128)S(1)} %get-tuple-element.43.sum_loss_ref, f32[2,16,1152]{2,1,0:T(8,128)S(1)} %get-tuple-element.44.unit_ref, f32[2,16,128]{2,1,0:T(8,128)S(1)} %get-tuple-element.45.inverse_ref, ...), custom_call_target="tpu_custom_call" | custom-call | tf_op jit(solution)/shard_map/final/pallas_call | solution.py:314
  (3 shorter events, 0.0 us)
Async XLA Ops:
  0.6 1.8 %copy-start = (bf16[16,1152]{1,0:T(8,128)(2,1)S(1)}, bf16[16,1152]{1,0:T(8,128)(2,1)}, u32[]{:S(2)}) copy-start(bf16[16,1152]{1,0:T(8,128)(2,1)} %image_ref.3) | copy-start | bytes 110596
  0.6 1.8 %copy-start.1 = (bf16[16,1152]{1,0:T(8,128)(2,1)S(1)}, bf16[16,1152]{1,0:T(8,128)(2,1)}, u32[]{:S(2)}) copy-start(bf16[16,1152]{1,0:T(8,128)(2,1)} %text_ref.3) | copy-start | bytes 110596
  0.7 1.9 %collective-permute-start.2 = (s32[16]{0:T(128)}, s32[16]{0:T(128)S(1)}, u32[]{:S(2)}, u32[]{:S(2)}) collective-permute-start(s32[16]{0:T(128)} %class_ref.1), channel_id=1, source_target_pairs={{0,2},{1,3},{2,0},{3,1},{4,6},{5,7},{6,4},{7,5},{8,10},{9,11},{10,... | collective-permute-start | bytes 200 | tf_op jit(solution)/shard_map/ppermute | solution.py:342
  1.2 1.4 %collective-permute-start = (bf16[16,1152]{1,0:T(8,128)(2,1)}, bf16[16,1152]{1,0:T(8,128)(2,1)S(1)}, u32[]{:S(2)}, u32[]{:S(2)}) collective-permute-start(bf16[16,1152]{1,0:T(8,128)(2,1)} %image_ref.3), channel_id=1, source_target_pairs={{0,2},{1,3},{2,0},{3,1},{4,6},{5,7},{6,4},{7,5},{8,10},{9,11},{10,... | collective-permute-start | bytes 110600 | tf_op jit(solution)/shard_map/ppermute | solution.py:342
  1.2 1.5 %collective-permute-start.1 = (bf16[16,1152]{1,0:T(8,128)(2,1)}, bf16[16,1152]{1,0:T(8,128)(2,1)S(1)}, u32[]{:S(2)}, u32[]{:S(2)}) collective-permute-start(bf16[16,1152]{1,0:T(8,128)(2,1)} %text_ref.3), channel_id=1, source_target_pairs={{0,2},{1,3},{2,0},{3,1},{4,6},{5,7},{6,4},{7,5},{8,10},{9,11},{10,... | collective-permute-start | bytes 110600 | tf_op jit(solution)/shard_map/ppermute | solution.py:342
  1.7 0.7 %copy-start.2 = (s32[16]{0:T(128)S(1)}, s32[16]{0:T(128)}, u32[]{:S(2)}) copy-start(s32[16]{0:T(128)} %class_ref.1) | copy-start | bytes 196
  2.9 7.9 %collective-permute-start.5 = (bf16[32,1280]{1,0:T(8,128)(2,1)S(1)}, bf16[32,1280]{1,0:T(8,128)(2,1)S(1)}, u32[]{:S(2)}, u32[]{:S(2)}) collective-permute-start(bf16[32,1280]{1,0:T(8,128)(2,1)S(1)} %get-tuple-element.31), channel_id=1, source_target_pairs={{0,24},{1,25},{2,18},{3,19},{4,28},{5,29},{6,22},{7,23},{8,16},{9,... | collective-permute-start | bytes 245768 | tf_op jit(solution)/shard_map/ppermute | solution.py:339
  7.9 4.4 %collective-permute-start.6 = (bf16[32,1280]{1,0:T(8,128)(2,1)S(1)}, bf16[32,1280]{1,0:T(8,128)(2,1)S(1)}, u32[]{:S(2)}, u32[]{:S(2)}) collective-permute-start(bf16[32,1280]{1,0:T(8,128)(2,1)S(1)} %get-tuple-element.32), channel_id=1, source_target_pairs={{0,4},{1,5},{2,7},{3,6},{4,0},{5,1},{6,3},{7,2},{8,12},{9,13},{10,... | collective-permute-start | bytes 245768 | tf_op jit(solution)/shard_map/ppermute | solution.py:339
  9.4 4.4 %collective-permute-start.3 = (bf16[32,1280]{1,0:T(8,128)(2,1)S(1)}, bf16[32,1280]{1,0:T(8,128)(2,1)S(1)}, u32[]{:S(2)}, u32[]{:S(2)}) collective-permute-start(bf16[32,1280]{1,0:T(8,128)(2,1)S(1)} %get-tuple-element.26), channel_id=1, source_target_pairs={{0,8},{1,9},{2,3},{3,2},{4,12},{5,13},{6,7},{7,6},{8,0},{9,1},{10,... | collective-permute-start | bytes 245768 | tf_op jit(solution)/shard_map/ppermute | solution.py:339
  9.4 4.4 %collective-permute-start.4 = (bf16[32,1280]{1,0:T(8,128)(2,1)S(1)}, bf16[32,1280]{1,0:T(8,128)(2,1)S(1)}, u32[]{:S(2)}, u32[]{:S(2)}) collective-permute-start(bf16[32,1280]{1,0:T(8,128)(2,1)S(1)} %get-tuple-element.27), channel_id=1, source_target_pairs={{0,10},{1,11},{2,1},{3,0},{4,14},{5,15},{6,5},{7,4},{8,2},{9,3},{1... | collective-permute-start | bytes 245768 | tf_op jit(solution)/shard_map/ppermute | solution.py:339
  12.4 1.5 %collective-permute-start.7 = (bf16[64,1280]{1,0:T(8,128)(2,1)S(1)}, bf16[64,1280]{1,0:T(8,128)(2,1)S(1)}, u32[]{:S(2)}, u32[]{:S(2)}) collective-permute-start(bf16[64,1280]{1,0:T(8,128)(2,1)S(1)} %far.1.far_ref), channel_id=1, source_target_pairs={{0,2},{1,3},{2,0},{3,1},{4,6},{5,7},{6,4},{7,5},{8,10},{9,11},{10,... | collective-permute-start | bytes 491528 | tf_op jit(solution)/shard_map/ppermute | solution.py:342
  14.7 6.9 %collective-permute-start.8 = (s16[32,1280]{1,0:T(8,128)(2,1)S(1)}, s16[32,1280]{1,0:T(8,128)(2,1)S(1)}, u32[]{:S(2)}, u32[]{:S(2)}) collective-permute-start(s16[32,1280]{1,0:T(8,128)(2,1)S(1)} %get-tuple-element.35), channel_id=1, source_target_pairs={{0,24},{1,25},{2,7},{3,6},{4,28},{5,29},{6,3},{7,2},{8,16},{9,17},... | collective-permute-start | bytes 245768 | tf_op jit(solution)/shard_map/ppermute | solution.py:339
  17.0 4.8 %collective-permute-start.9 = (s16[32,1280]{1,0:T(8,128)(2,1)S(1)}, s16[32,1280]{1,0:T(8,128)(2,1)S(1)}, u32[]{:S(2)}, u32[]{:S(2)}) collective-permute-start(s16[32,1280]{1,0:T(8,128)(2,1)S(1)} %get-tuple-element.38), channel_id=1, source_target_pairs={{0,4},{1,5},{2,18},{3,19},{4,0},{5,1},{6,22},{7,23},{8,12},{9,13},... | collective-permute-start | bytes 245768 | tf_op jit(solution)/shard_map/ppermute | solution.py:339
  18.5 4.6 %collective-permute-start.11 = (s16[16,1280]{1,0:T(8,128)(2,1)S(1)}, s16[16,1280]{1,0:T(8,128)(2,1)S(1)}, u32[]{:S(2)}, u32[]{:S(2)}) collective-permute-start(s16[16,1280]{1,0:T(8,128)(2,1)S(1)} %get-tuple-element.40), channel_id=1, source_target_pairs={{0,8},{1,9},{2,3},{3,2},{4,12},{5,13},{6,7},{7,6},{8,0},{9,1},{10,... | collective-permute-start | bytes 122888 | tf_op jit(solution)/shard_map/ppermute | solution.py:339
  18.5 4.6 %collective-permute-start.12 = (s16[16,1280]{1,0:T(8,128)(2,1)S(1)}, s16[16,1280]{1,0:T(8,128)(2,1)S(1)}, u32[]{:S(2)}, u32[]{:S(2)}) collective-permute-start(s16[16,1280]{1,0:T(8,128)(2,1)S(1)} %get-tuple-element.41), channel_id=1, source_target_pairs={{0,10},{1,11},{2,1},{3,0},{4,14},{5,15},{6,5},{7,4},{8,2},{9,3},{1... | collective-permute-start | bytes 122888 | tf_op jit(solution)/shard_map/ppermute | solution.py:339
  21.8 1.4 %collective-permute-start.10 = (s16[16,1280]{1,0:T(8,128)(2,1)S(1)}, s16[16,1280]{1,0:T(8,128)(2,1)S(1)}, u32[]{:S(2)}, u32[]{:S(2)}) collective-permute-start(s16[16,1280]{1,0:T(8,128)(2,1)S(1)} %get-tuple-element.39), channel_id=1, source_target_pairs={{0,2},{1,3},{2,0},{3,1},{4,6},{5,7},{6,4},{7,5},{8,10},{9,11},{10,... | collective-permute-start | bytes 122888 | tf_op jit(solution)/shard_map/ppermute | solution.py:342
  21.9 1.7 %collective-permute-start.13 = (s16[16,1280]{1,0:T(8,128)(2,1)S(1)}, s16[16,1280]{1,0:T(8,128)(2,1)S(1)}, u32[]{:S(2)}, u32[]{:S(2)}) collective-permute-start(s16[16,1280]{1,0:T(8,128)(2,1)S(1)} %give.1), channel_id=1, source_target_pairs={{0,2},{1,3},{2,0},{3,1},{4,6},{5,7},{6,4},{7,5},{8,10},{9,11},{10,... | collective-permute-start | bytes 122888 | tf_op jit(solution)/shard_map/ppermute | solution.py:342
